TPU v7x, 32 devices: a whole 2x2x4 slice. The times are simulated.
32 devices in a mesh: items: 4 (over y, core), rows: 8 (over z, x).
Axes of the slice: x: 2, y: 2, z: 4, core: 2. Of those that a mesh axis runs over, the one named last changes fastest.
Arguments:
- hidden_in: float32 [4, 1024, 1536], P('items', 'rows'), may hold values from -6 to 6
- cotangent: float32 [4, 1024, 1536], P('items', 'rows'), may hold values from -6 to 6
- text_states: bfloat16 [4, 2, 128, 4096], P('items', None, 'rows'), may hold values from -6 to 6
- time_embed: bfloat16 [4, 2, 1024], P('items'), may hold values from -6 to 6
- live_rows: int32 [4, 8, 2], P('items', 'rows'), may hold values from 1 to 2, as said below
- frame_rows: int32 [4, 2], P('items'), may hold values from 4 to 16
- text_len: int32 [4, 2], P('items'), may hold values from 64 to 128
- w_qkv: bfloat16 [1536, 4608], P('rows'), may hold values from -0.15625 to 0.15625
- w_out: bfloat16 [1536, 1536], P('rows'), may hold values from -0.15625 to 0.15625
- w_text: bfloat16 [4096, 3072], P('rows'), may hold values from -0.09375 to 0.09375
- w_gu: bfloat16 [1536, 8192], P('rows'), may hold values from -0.15625 to 0.15625
- w_down: bfloat16 [4096, 1536], P('rows'), may hold values from -0.09375 to 0.09375
- w_ada: bfloat16 [1024, 6144], P('rows'), may hold values from -0.1875 to 0.1875
- gains: float32 [7, 1536], replicated, may hold values from 0.1 to 1.9
- cross_gate: float32 [24], replicated, may hold values from -1.5 to 1.5
- ada_bias: float32 [6144], replicated, may hold values from -3 to 3
- text_gain: float32 [4096], replicated, may hold values from 0.1 to 1.9
Outputs:
- output: float32 [4, 1024, 1536], P('items', 'rows')
- grad_x: float32 [4, 1024, 1536], P('items', 'rows')
- grad_w_qkv: float32 [1536, 4608], P('rows')
- grad_w_out: float32 [1536, 1536], P('rows')
- grad_w_text: float32 [4096, 3072], P('rows')
- grad_w_gu: float32 [1536, 8192], P('rows')
- grad_w_down: float32 [4096, 1536], P('rows')
- grad_w_ada: float32 [1024, 6144], P('rows')
- grad_gains: float32 [7, 1536], replicated
- grad_cross_gate: float32 [24], replicated
- grad_ada_bias: float32 [6144], replicated
- grad_text_gain: float32 [4096], replicated
Inputs may be any that keep to these rules, and one draw needn't show every extreme that they name: The first live_rows[g, r, s] row slots of item s on device r hold its rows, in order of the devices; every item has at least one live row on every device of its group.
All inputs are finite; a program needn't handle non-finite values.
Results may differ from a plain program's by a relative error of at most 0.023.
Values may be sent and summed in bfloat16 or wider, within the bound.
A program may use at most 384 MiB of HBM per device.

v0:
```python
import jax
import jax.numpy as jnp
from jax import lax
from jax.sharding import PartitionSpec as P

COLS = 32


epsilon = 1e-06
masked_score = -1e30
group_heads = 4


def norm_gain(values, scaling):
    return values * lax.rsqrt(jnp.mean(values * values, axis=-1, keepdims=True) + epsilon) * scaling


def pre_norm(values, shift_scale, scaling):
    return norm_gain(values, scaling) * (1.0 + shift_scale)


def post_add(residual, branch, gate_in, scaling):
    return residual + jnp.tanh(gate_in) * norm_gain(branch, scaling)


def swiglu(gate_up):
    middle_col = gate_up.shape[-1] // 2
    return jax.nn.silu(gate_up[..., :middle_col]) * gate_up[..., middle_col:]


def freq_rates(number):
    return 10000.0 ** (-jnp.arange(number).astype(jnp.float32) / number)


def rotary_angles(frame_index, frame_row, column, head_size):
    frame_pairs = head_size // 8
    space_pairs = (head_size // 2 - frame_pairs) // 2
    return jnp.concatenate(
        [
            frame_index.astype(jnp.float32)[..., None] * freq_rates(frame_pairs),
            frame_row.astype(jnp.float32)[..., None] * freq_rates(space_pairs),
            column.astype(jnp.float32)[..., None] * freq_rates(space_pairs),
        ],
        axis=-1,
    )


def rotate(values, cos_table, sin_table, head_count):
    shaped = values.reshape(values.shape[:-1] + (head_count, values.shape[-1] // head_count))
    half_size = shaped.shape[-1] // 2
    upper_half = shaped[..., :half_size]
    lower_half = shaped[..., half_size:]
    cos_heads = cos_table[..., None, :]
    sin_heads = sin_table[..., None, :]
    turned = jnp.concatenate(
        [
            upper_half * cos_heads - lower_half * sin_heads,
            upper_half * sin_heads + lower_half * cos_heads,
        ],
        axis=-1,
    )
    return turned.reshape(values.shape)


def text_split(projected, key_gain):
    half_cols = projected.shape[-1] // 2
    return (norm_gain(projected[..., :half_cols], key_gain), projected[..., half_cols:])


def per_device(
    hidden_in,
    cotangent,
    text_states,
    time_embed,
    live_rows,
    frame_rows,
    text_len,
    w_qkv,
    w_out,
    w_text,
    w_gu,
    w_down,
    w_ada,
    gains,
    cross_gate,
    ada_bias,
    text_gain,
):
    single = jnp.float32
    narrow = jnp.bfloat16
    model_width = hidden_in.shape[2]
    head_count = cross_gate.shape[0]
    head_size = model_width // head_count
    score_scale = head_size ** (-0.5)
    item_count = time_embed.shape[1]
    item_slots = hidden_in.shape[1] // item_count
    row_devices = lax.axis_size("rows")
    seq_len = row_devices * item_slots
    text_local = text_states.shape[2]
    text_all = text_local * row_devices
    text_width = text_states.shape[3]
    group_span = group_heads * head_size
    block_count = head_count // group_heads
    token_count = item_count * item_slots

    def weight_term(left, right, accuracy):
        return jnp.einsum(
            "tk,tn->kn", left, right, precision=accuracy, preferred_element_type=single
        )

    def reduce_term(term):
        return lax.psum_scatter(
            term.astype(jnp.bfloat16), "rows", scatter_dimension=0, tiled=True
        ).astype(jnp.float32)

    full_qkv, full_out, full_text, full_gu, full_down, full_ada = (
        lax.all_gather(w_qkv, "rows", axis=0, tiled=True),
        lax.all_gather(w_out, "rows", axis=0, tiled=True),
        lax.all_gather(w_text, "rows", axis=0, tiled=True),
        lax.all_gather(w_gu, "rows", axis=0, tiled=True),
        lax.all_gather(w_down, "rows", axis=0, tiled=True),
        lax.all_gather(w_ada, "rows", axis=0, tiled=True),
    )
    counts_here = live_rows[0]
    every_count = lax.all_gather(counts_here, "rows", axis=0, tiled=True)
    device_place = lax.axis_index("rows")
    ranks = jnp.arange(row_devices)
    rows_below = jnp.sum(jnp.where(ranks[:, None] < device_place, every_count, 0), axis=0)
    slot_row = jnp.arange(item_slots) // COLS
    column = jnp.arange(item_slots) % COLS
    row_index = rows_below[:, None] + slot_row[None, :]
    heights = frame_rows[0][:, None]
    frame_index = row_index // heights
    frame_row = row_index % heights
    live_mask = (slot_row[None, :] < counts_here[0][:, None]).astype(single)
    key_live = (slot_row[None, None, :] < jnp.transpose(every_count)[:, :, None]).reshape(
        item_count, seq_len
    )
    text_live = jnp.arange(text_all)[None, :] < text_len[0][:, None]
    angles = rotary_angles(
        frame_index, frame_row, jnp.broadcast_to(column, row_index.shape), head_size
    )
    cos_table = jnp.cos(angles)
    sin_table = jnp.sin(angles)

    def qkv_split(projected, gain_query, gain_key):
        queries = rotate(
            norm_gain(projected[..., :model_width], gain_query), cos_table, sin_table, head_count
        )
        keys_here = rotate(
            norm_gain(projected[..., model_width : 2 * model_width], gain_key),
            cos_table,
            sin_table,
            head_count,
        )
        return (queries, keys_here, projected[..., 2 * model_width :])

    states = hidden_in[0].reshape(item_count, item_slots, model_width)
    time_silu = jax.nn.silu(time_embed[0].astype(single)).astype(narrow)
    modulation = jnp.dot(time_silu, full_ada, preferred_element_type=single) + ada_bias
    scale_attn = modulation[:, None, 0:model_width]
    gate_attn = modulation[:, None, model_width : 2 * model_width]
    scale_ffn = modulation[:, None, 2 * model_width : 3 * model_width]
    gate_ffn = modulation[:, None, 3 * model_width :]
    attn_in = (
        pre_norm(states, scale_attn, gains[0]).astype(narrow).reshape(token_count, model_width)
    )
    qkv_proj = jnp.dot(attn_in, full_qkv, preferred_element_type=single).reshape(
        item_count, item_slots, 3 * model_width
    )
    query_full, key_full, value_full = qkv_split(qkv_proj, gains[1], gains[2])
    query_low = query_full.astype(narrow)
    key_low = key_full.astype(narrow)
    value_low = value_full.astype(narrow)
    text_float = text_states[0].astype(single)
    text_norm = norm_gain(text_float, text_gain).astype(narrow)
    text_proj = jnp.einsum("ctd,dn->ctn", text_norm, full_text, preferred_element_type=single)
    tkey_full, tval_full = text_split(text_proj, gains[6])
    key_all, value_all, tkey_all, tval_all = (
        lax.all_gather(key_low, "rows", axis=1, tiled=True),
        lax.all_gather(value_low, "rows", axis=1, tiled=True),
        lax.all_gather(tkey_full.astype(narrow), "rows", axis=1, tiled=True),
        lax.all_gather(tval_full.astype(narrow), "rows", axis=1, tiled=True),
    )

    def block_slices(block_index, key_source, value_source):
        offset = block_index * group_span
        query_part = lax.dynamic_slice_in_dim(query_low, offset, group_span, 2).reshape(
            item_count, item_slots, group_heads, head_size
        )
        key_part = lax.dynamic_slice_in_dim(key_source, offset, group_span, 2).reshape(
            item_count, seq_len, group_heads, head_size
        )
        value_part = lax.dynamic_slice_in_dim(value_source, offset, group_span, 2).reshape(
            item_count, seq_len, group_heads, head_size
        )
        return (query_part, key_part, value_part)

    def self_step(carry, block_index):
        query_part, key_part, value_part = block_slices(block_index, key_all, value_all)
        scores = (
            jnp.einsum("iphe,ikhe->ihpk", query_part, key_part, preferred_element_type=single)
            * score_scale
        )
        scores = jnp.where(key_live[:, None, None, :], scores, masked_score)
        row_max = jnp.max(scores, axis=-1, keepdims=True)
        exp_terms = jnp.exp(scores - row_max)
        exp_total = jnp.sum(exp_terms, axis=-1, keepdims=True)
        probs_low = (exp_terms / exp_total).astype(narrow)
        attended = jnp.einsum(
            "ihpk,ikhe->iphe", probs_low, value_part, preferred_element_type=single
        )
        return (
            carry,
            (
                attended.reshape(item_count, item_slots, group_span),
                (row_max + jnp.log(exp_total))[..., 0],
            ),
        )

    _, (self_parts, log_totals) = lax.scan(
        self_step, jnp.zeros((), single), jnp.arange(block_count)
    )

    def heads_last(parts):
        return jnp.transpose(parts, (1, 2, 0, 3)).reshape(item_count, item_slots, model_width)

    self_out = heads_last(self_parts)
    query_heads = query_low.reshape(item_count, item_slots, head_count, head_size)
    tkey_heads = tkey_all.reshape(item_count, text_all, head_count, head_size)
    tval_heads = tval_all.reshape(item_count, text_all, head_count, head_size)
    cross_scores = (
        jnp.einsum("iphe,ikhe->ihpk", query_heads, tkey_heads, preferred_element_type=single)
        * score_scale
    )
    cross_scores = jnp.where(text_live[:, None, None, :], cross_scores, masked_score)
    cross_max = jnp.max(cross_scores, axis=-1, keepdims=True)
    cross_exp = jnp.exp(cross_scores - cross_max)
    cross_probs = cross_exp / jnp.sum(cross_exp, axis=-1, keepdims=True)
    cross_low = cross_probs.astype(narrow)
    cross_out = jnp.einsum("ihpk,ikhe->iphe", cross_low, tval_heads, preferred_element_type=single)
    tanh_gate = jnp.tanh(cross_gate)
    combined = (
        self_out.reshape(item_count, item_slots, head_count, head_size)
        + tanh_gate[:, None] * cross_out
    )
    combined = combined.reshape(token_count, model_width).astype(narrow)
    projected = jnp.dot(combined, full_out, preferred_element_type=single).reshape(
        item_count, item_slots, model_width
    )
    middle = post_add(states, projected, gate_attn, gains[3])
    ffn_in = pre_norm(middle, scale_ffn, gains[4]).astype(narrow).reshape(token_count, model_width)
    gate_up = jnp.dot(ffn_in, full_gu, preferred_element_type=single)
    inner_act = swiglu(gate_up).astype(narrow)
    ffn_out = jnp.dot(inner_act, full_down, preferred_element_type=single).reshape(
        item_count, item_slots, model_width
    )
    result = post_add(middle, ffn_out, gate_ffn, gains[5])
    output = (live_mask[..., None] * result).reshape(1, token_count, model_width)
    grad_result = live_mask[..., None] * cotangent[0].reshape(item_count, item_slots, model_width)
    _, back_ffn_out = jax.vjp(post_add, middle, ffn_out, gate_ffn, gains[5])
    grad_middle, grad_ffn_out, grad_gate_ffn, grad_gain_five = back_ffn_out(grad_result)
    ffn_low = grad_ffn_out.astype(narrow).reshape(token_count, model_width)
    shard_down = reduce_term(weight_term(inner_act, ffn_low, None))
    grad_inner = jnp.einsum("tn,kn->tk", ffn_low, full_down, preferred_element_type=single)
    _, back_glu = jax.vjp(swiglu, gate_up)
    gate_up_low = back_glu(grad_inner)[0].astype(narrow)
    shard_gu = reduce_term(weight_term(ffn_in, gate_up_low, None))
    grad_ffn_in = jnp.einsum("tn,kn->tk", gate_up_low, full_gu, preferred_element_type=single)
    _, back_ffn_in = jax.vjp(pre_norm, middle, scale_ffn, gains[4])
    part_middle, grad_scale_ffn, grad_gain_four = back_ffn_in(
        grad_ffn_in.reshape(item_count, item_slots, model_width)
    )
    grad_middle = grad_middle + part_middle
    _, back_attn_out = jax.vjp(post_add, states, projected, gate_attn, gains[3])
    grad_hidden, grad_projected, grad_gate_attn, grad_gain_three = back_attn_out(grad_middle)
    projected_low = grad_projected.astype(narrow).reshape(token_count, model_width)
    shard_out = reduce_term(weight_term(combined, projected_low, None))
    grad_combined = jnp.einsum("tn,kn->tk", projected_low, full_out, preferred_element_type=single)
    grad_combined = grad_combined.reshape(item_count, item_slots, head_count, head_size)
    self_low = grad_combined.reshape(item_count, item_slots, model_width).astype(narrow)
    cross_grad_low = (tanh_gate[:, None] * grad_combined).astype(narrow)
    grad_cross_gate = (1.0 - tanh_gate * tanh_gate) * jnp.sum(
        grad_combined * cross_out, axis=(0, 1, 3)
    )

    def self_back(carry, packed):
        block_index, log_total = packed
        query_part, key_part, value_part = block_slices(block_index, key_all, value_all)
        offset = block_index * group_span
        grad_part = lax.dynamic_slice_in_dim(self_low, offset, group_span, 2).reshape(
            item_count, item_slots, group_heads, head_size
        )
        scores = (
            jnp.einsum("iphe,ikhe->ihpk", query_part, key_part, preferred_element_type=single)
            * score_scale
        )
        scores = jnp.where(key_live[:, None, None, :], scores, masked_score)
        attn_probs = jnp.exp(scores - log_total[..., None])
        grad_probs = jnp.einsum(
            "iphe,ikhe->ihpk", grad_part, value_part, preferred_element_type=single
        )
        row_inner = jnp.sum(attn_probs * grad_probs, axis=-1, keepdims=True)
        score_low = (attn_probs * (grad_probs - row_inner)).astype(narrow)
        grad_query = (
            jnp.einsum("ihpk,ikhe->iphe", score_low, key_part, preferred_element_type=single)
            * score_scale
        )
        grad_value = jnp.einsum(
            "ihpk,iphe->ikhe", attn_probs.astype(narrow), grad_part, preferred_element_type=single
        )
        grad_key = (
            jnp.einsum("ihpk,iphe->ikhe", score_low, query_part, preferred_element_type=single)
            * score_scale
        )
        owned_key, owned_value = (
            lax.psum_scatter(
                grad_key.reshape(item_count, seq_len, group_span).astype(jnp.bfloat16),
                "rows",
                scatter_dimension=1,
                tiled=True,
            ).astype(jnp.float32),
            lax.psum_scatter(
                grad_value.reshape(item_count, seq_len, group_span).astype(jnp.bfloat16),
                "rows",
                scatter_dimension=1,
                tiled=True,
            ).astype(jnp.float32),
        )
        return (
            carry,
            (grad_query.reshape(item_count, item_slots, group_span), owned_key, owned_value),
        )

    _, (query_parts, key_parts, value_parts) = lax.scan(
        self_back, jnp.zeros((), single), (jnp.arange(block_count), log_totals)
    )
    cross_grad_probs = jnp.einsum(
        "iphe,ikhe->ihpk", cross_grad_low, tval_heads, preferred_element_type=single
    )
    cross_inner = jnp.sum(cross_probs * cross_grad_probs, axis=-1, keepdims=True)
    cross_score_low = (cross_probs * (cross_grad_probs - cross_inner)).astype(narrow)
    grad_query_cross = (
        jnp.einsum("ihpk,ikhe->iphe", cross_score_low, tkey_heads, preferred_element_type=single)
        * score_scale
    )
    grad_text_key = (
        jnp.einsum("ihpk,iphe->ikhe", cross_score_low, query_heads, preferred_element_type=single)
        * score_scale
    )
    grad_text_value = jnp.einsum(
        "ihpk,iphe->ikhe", cross_low, cross_grad_low, preferred_element_type=single
    )
    owned_tkey, owned_tval = (
        lax.psum_scatter(
            grad_text_key.reshape(item_count, text_all, model_width).astype(jnp.bfloat16),
            "rows",
            scatter_dimension=1,
            tiled=True,
        ).astype(jnp.float32),
        lax.psum_scatter(
            grad_text_value.reshape(item_count, text_all, model_width).astype(jnp.bfloat16),
            "rows",
            scatter_dimension=1,
            tiled=True,
        ).astype(jnp.float32),
    )
    grad_query_all = heads_last(query_parts) + grad_query_cross.reshape(
        item_count, item_slots, model_width
    )
    _, back_qkv = jax.vjp(qkv_split, qkv_proj, gains[1], gains[2])
    grad_qkv, grad_gain_one, grad_gain_two = back_qkv(
        (grad_query_all, heads_last(key_parts), heads_last(value_parts))
    )
    qkv_low = grad_qkv.astype(narrow).reshape(token_count, 3 * model_width)
    shard_qkv = reduce_term(weight_term(attn_in, qkv_low, None))
    grad_attn_in = jnp.einsum("tn,kn->tk", qkv_low, full_qkv, preferred_element_type=single)
    _, back_attn_in = jax.vjp(pre_norm, states, scale_attn, gains[0])
    part_states, grad_scale_attn, grad_gain_zero = back_attn_in(
        grad_attn_in.reshape(item_count, item_slots, model_width)
    )
    grad_x = (grad_hidden + part_states).reshape(1, token_count, model_width)
    _, back_text = jax.vjp(text_split, text_proj, gains[6])
    grad_text_proj, grad_gain_six = back_text((owned_tkey, owned_tval))
    text_low = grad_text_proj.astype(narrow).reshape(item_count * text_local, 2 * model_width)
    shard_text = reduce_term(
        weight_term(text_norm.reshape(item_count * text_local, text_width), text_low, None)
    )
    grad_text_norm = jnp.einsum("tn,kn->tk", text_low, full_text, preferred_element_type=single)
    _, back_text_norm = jax.vjp(norm_gain, text_float, text_gain)
    grad_text_gain = back_text_norm(grad_text_norm.reshape(text_float.shape))[1]
    grad_modulation = jnp.concatenate(
        [grad_scale_attn, grad_gate_attn, grad_scale_ffn, grad_gate_ffn], axis=-1
    )[:, 0, :]
    shard_ada = reduce_term(
        weight_term(time_silu.astype(single), grad_modulation, lax.Precision.HIGHEST)
    )
    grad_ada_bias = jnp.sum(grad_modulation, axis=0)
    grad_gains = jnp.stack(
        [
            grad_gain_zero,
            grad_gain_one,
            grad_gain_two,
            grad_gain_three,
            grad_gain_four,
            grad_gain_five,
            grad_gain_six,
        ],
        axis=0,
    )
    final_qkv, final_out, final_text, final_gu, final_down, final_ada = (
        lax.psum(shard_qkv.astype(jnp.bfloat16), "items").astype(jnp.float32),
        lax.psum(shard_out.astype(jnp.bfloat16), "items").astype(jnp.float32),
        lax.psum(shard_text.astype(jnp.bfloat16), "items").astype(jnp.float32),
        lax.psum(shard_gu.astype(jnp.bfloat16), "items").astype(jnp.float32),
        lax.psum(shard_down.astype(jnp.bfloat16), "items").astype(jnp.float32),
        lax.psum(shard_ada.astype(jnp.bfloat16), "items").astype(jnp.float32),
    )
    total_gains, total_gate, total_bias, total_text_gain = lax.psum(
        (grad_gains, grad_cross_gate, grad_ada_bias, grad_text_gain), ("items", "rows")
    )
    return (
        output,
        grad_x,
        final_qkv,
        final_out,
        final_text,
        final_gu,
        final_down,
        final_ada,
        total_gains,
        total_gate,
        total_bias,
        total_text_gain,
    )


def solution(mesh):
    in_specs = (
        P("items", "rows", None),
        P("items", "rows", None),
        P("items", None, "rows", None),
        P("items", None, None),
        P("items", "rows", None),
        P("items", None),
        P("items", None),
        P("rows", None),
        P("rows", None),
        P("rows", None),
        P("rows", None),
        P("rows", None),
        P("rows", None),
        P(),
        P(),
        P(),
        P(),
    )
    out_specs = (
        P("items", "rows", None),
        P("items", "rows", None),
        P("rows", None),
        P("rows", None),
        P("rows", None),
        P("rows", None),
        P("rows", None),
        P("rows", None),
        P(),
        P(),
        P(),
        P(),
    )
    return jax.shard_map(
        per_device, mesh=mesh, in_specs=in_specs, out_specs=out_specs, check_vma=False
    )
```

profile of v0, /device:TPU:0, one launch (start us, length us, event | category | flops | bytes accessed | tf_op | source)
XLA Modules:
  0.0 4407.8 jit_solution(14120854136439093524)
XLA Ops:
  8.8 22.3 all-gather
  33.1 156.2 %all-gather.10.cloned.1.call-done = bf16[1024,6144]{1,0:T(8,128)(2,1)} async-done(((bf16[128,6144]{1,0:T(8,128)(2,1)}), bf16[1024,6144]{1,0:T(8,128)(2,1)}) %all-gather.10.cloned.1.call-update) | async-done | bytes 12582928 | tf_op jit(solution)/shard_map/all_gather | solution.py:122
  189.4 6.3 convolution_add_fusion
  196.4 189.1 %all-gather.12.cloned.1.call-done = bf16[1536,4608]{1,0:T(8,128)(2,1)} async-done(((bf16[192,4608]{1,0:T(8,128)(2,1)}), bf16[1536,4608]{1,0:T(8,128)(2,1)}) %all-gather.12.cloned.1.call-update) | async-done | bytes 14155792 | tf_op jit(solution)/shard_map/all_gather | solution.py:117
  385.5 7.1 fusion.20
  414.6 48.7 %all-gather.16.cloned.1.call-done = bf16[2,512,1536]{2,1,0:T(8,128)(2,1)} async-done(((bf16[2,64,1536]{2,1,0:T(8,128)(2,1)}), bf16[2,512,1536]{2,1,0:T(8,128)(2,1)}) %all-gather.16.cloned.1.call-update) | async-done | bytes 3145744 | tf_op jit(solution)/shard_map/all_gather | solution.py:180
  463.4 4.6 copy.103
  468.0 57.1 %all-gather.14.cloned.1.call-done = bf16[2,512,1536]{2,1,0:T(8,128)(2,1)} async-done(((bf16[2,64,1536]{2,1,0:T(8,128)(2,1)}), bf16[2,512,1536]{2,1,0:T(8,128)(2,1)}) %all-gather.14.cloned.1.call-update) | async-done | bytes 3145744 | tf_op jit(solution)/shard_map/all_gather | solution.py:181
  525.1 4.6 copy.102
  531.0 36.9 while.28
  570.6 434.9 %all-gather.18.cloned.1.call-done = bf16[4096,3072]{1,0:T(8,128)(2,1)} async-done(((bf16[512,3072]{1,0:T(8,128)(2,1)}), bf16[4096,3072]{1,0:T(8,128)(2,1)}) %all-gather.18.cloned.1.call-update) | async-done | bytes 25165840 | tf_op jit(solution)/shard_map/all_gather | solution.py:119
  1005.6 10.5 fusion.16
  1016.3 36.1 all_gather.40
  1053.9 36.3 all_gather.39
  1094.3 4.0 fusion.32
  1098.3 9.5 all-gather.20.cloned.1.call-done
  1113.3 475.8 %all-gather.22.cloned.1.call-done = bf16[1536,8192]{1,0:T(8,128)(2,1)} async-done(((bf16[192,8192]{1,0:T(8,128)(2,1)}), bf16[1536,8192]{1,0:T(8,128)(2,1)}) %all-gather.22.cloned.1.call-update) | async-done | bytes 25165840 | tf_op jit(solution)/shard_map/all_gather | solution.py:120
  1589.1 10.2 fusion.100
  1602.0 165.8 %all-gather.24.cloned.1.call-done = bf16[4096,1536]{1,0:T(8,128)(2,1)} async-done(((bf16[512,1536]{1,0:T(8,128)(2,1)}), bf16[4096,1536]{1,0:T(8,128)(2,1)}) %all-gather.24.cloned.1.call-update) | async-done | bytes 12582928 | tf_op jit(solution)/shard_map/all_gather | solution.py:121
  1767.8 6.5 multiply_reduce_fusion.18
  1776.8 12.3 fusion.50
  1789.1 15.5 fusion.49
  1823.3 537.2 %while.29 = (s32[]{:T(128)}, f32[6,2,64,256]{2,3,1,0:T(8,128)}, f32[6,2,64,256]{3,1,2,0:T(2,128)}, f32[6,2,64,256]{3,1,2,0:T(2,128)}, s32[6]{0:T(128)S(1)}, /*in...) while((s32[]{:T(128)}, f32[6,2,64,256]{2,3,1,0:T(8,128)}, ...), condition=%wide.region_22.23_spmd.clone, body=%wide.region_18.22_spmd.clone.sunk | while | flops 171540992 | bytes 22690472 | solution.py:335
  1835.7 74.5 %all-reduce.26.cloned.1.call-done = (bf16[2,512,256]{2,0,1:T(2,128)(2,1)}, bf16[2,512,256]{2,0,1:T(2,128)(2,1)}) async-done(((bf16[2,512,256]{2,0,1:T(2,128)(2,1)}, bf16[2,512,256]{2,0,1:T(2,128)(2,1)}), (bf16[2,512,256]{2,0,1:T(2,128)(2,1)}, bf16[2,512,256]{2,0,1:T(2,128)(2,1)})) %all-reduce.26.cloned.1.call-update) | async-done | bytes 1048592 | tf_op jit(solution)/shard_map/while
  1924.2 75.7 %all-reduce.26.cloned.1.call-done = (bf16[2,512,256]{2,0,1:T(2,128)(2,1)}, bf16[2,512,256]{2,0,1:T(2,128)(2,1)}) async-done(((bf16[2,512,256]{2,0,1:T(2,128)(2,1)}, bf16[2,512,256]{2,0,1:T(2,128)(2,1)}), (bf16[2,512,256]{2,0,1:T(2,128)(2,1)}, bf16[2,512,256]{2,0,1:T(2,128)(2,1)})) %all-reduce.26.cloned.1.call-update) | async-done | bytes 1048592 | tf_op jit(solution)/shard_map/while
  2013.9 75.7 %all-reduce.26.cloned.1.call-done = (bf16[2,512,256]{2,0,1:T(2,128)(2,1)}, bf16[2,512,256]{2,0,1:T(2,128)(2,1)}) async-done(((bf16[2,512,256]{2,0,1:T(2,128)(2,1)}, bf16[2,512,256]{2,0,1:T(2,128)(2,1)}), (bf16[2,512,256]{2,0,1:T(2,128)(2,1)}, bf16[2,512,256]{2,0,1:T(2,128)(2,1)})) %all-reduce.26.cloned.1.call-update) | async-done | bytes 1048592 | tf_op jit(solution)/shard_map/while
  2103.6 75.7 %all-reduce.26.cloned.1.call-done = (bf16[2,512,256]{2,0,1:T(2,128)(2,1)}, bf16[2,512,256]{2,0,1:T(2,128)(2,1)}) async-done(((bf16[2,512,256]{2,0,1:T(2,128)(2,1)}, bf16[2,512,256]{2,0,1:T(2,128)(2,1)}), (bf16[2,512,256]{2,0,1:T(2,128)(2,1)}, bf16[2,512,256]{2,0,1:T(2,128)(2,1)})) %all-reduce.26.cloned.1.call-update) | async-done | bytes 1048592 | tf_op jit(solution)/shard_map/while
  2193.3 75.7 %all-reduce.26.cloned.1.call-done = (bf16[2,512,256]{2,0,1:T(2,128)(2,1)}, bf16[2,512,256]{2,0,1:T(2,128)(2,1)}) async-done(((bf16[2,512,256]{2,0,1:T(2,128)(2,1)}, bf16[2,512,256]{2,0,1:T(2,128)(2,1)}), (bf16[2,512,256]{2,0,1:T(2,128)(2,1)}, bf16[2,512,256]{2,0,1:T(2,128)(2,1)})) %all-reduce.26.cloned.1.call-update) | async-done | bytes 1048592 | tf_op jit(solution)/shard_map/while
  2283.1 75.7 %all-reduce.26.cloned.1.call-done = (bf16[2,512,256]{2,0,1:T(2,128)(2,1)}, bf16[2,512,256]{2,0,1:T(2,128)(2,1)}) async-done(((bf16[2,512,256]{2,0,1:T(2,128)(2,1)}, bf16[2,512,256]{2,0,1:T(2,128)(2,1)}), (bf16[2,512,256]{2,0,1:T(2,128)(2,1)}, bf16[2,512,256]{2,0,1:T(2,128)(2,1)})) %all-reduce.26.cloned.1.call-update) | async-done | bytes 1048592 | tf_op jit(solution)/shard_map/while
  2365.8 3.6 convolution_convert_fusion.4
  2402.2 11.2 multiply_reduce_fusion.7
  2414.0 12.8 convolution_convert_fusion.3
  2428.1 6.4 convolution_convert_fusion.2
  2436.2 8.0 bitcast_convert_fusion.1
  2445.7 13.5 convolution_convert_fusion.1
  2462.2 28.9 reduce-scatter.13.cloned.1.call-done
  2491.1 13.4 bitcast_convert_fusion
  2504.6 84.8 %reduce-scatter.11.cloned.1.call-done = bf16[192,1536]{1,0:T(8,128)(2,1)} async-done(((bf16[1536,1536]{1,0:T(8,128)(2,1)}), bf16[192,1536]{1,0:T(8,128)(2,1)}) %reduce-scatter.11.cloned.1.call-update) | async-done | bytes 589840 | tf_op jit(solution)/shard_map/reduce_scatter | solution.py:112
  2589.4 210.6 %reduce-scatter.23.cloned.1.call-done = bf16[128,6144]{1,0:T(8,128)(2,1)} async-done(((bf16[1024,6144]{1,0:T(8,128)(2,1)}), bf16[128,6144]{1,0:T(8,128)(2,1)}) %reduce-scatter.23.cloned.1.call-update) | async-done | bytes 1572880 | tf_op jit(solution)/shard_map/reduce_scatter | solution.py:112
  2800.0 210.1 %reduce-scatter.21.cloned.1.call-done = bf16[512,1536]{1,0:T(8,128)(2,1)} async-done(((bf16[4096,1536]{1,0:T(8,128)(2,1)}), bf16[512,1536]{1,0:T(8,128)(2,1)}) %reduce-scatter.21.cloned.1.call-update) | async-done | bytes 1572880 | tf_op jit(solution)/shard_map/reduce_scatter | solution.py:112
  3010.1 231.8 %reduce-scatter.9.cloned.1.call-done = bf16[192,4608]{1,0:T(8,128)(2,1)} async-done(((bf16[1536,4608]{1,0:T(8,128)(2,1)}), bf16[192,4608]{1,0:T(8,128)(2,1)}) %reduce-scatter.9.cloned.1.call-update) | async-done | bytes 1769488 | tf_op jit(solution)/shard_map/reduce_scatter | solution.py:112
  3241.9 406.8 %reduce-scatter.19.cloned.1.call-done = bf16[192,8192]{1,0:T(8,128)(2,1)} async-done(((bf16[1536,8192]{1,0:T(8,128)(2,1)}), bf16[192,8192]{1,0:T(8,128)(2,1)}) %reduce-scatter.19.cloned.1.call-update) | async-done | bytes 3145744 | tf_op jit(solution)/shard_map/reduce_scatter | solution.py:112
  3648.7 406.7 %reduce-scatter.17.cloned.1.call-done = bf16[512,3072]{1,0:T(8,128)(2,1)} async-done(((bf16[4096,3072]{1,0:T(8,128)(2,1)}), bf16[512,3072]{1,0:T(8,128)(2,1)}) %reduce-scatter.17.cloned.1.call-update) | async-done | bytes 3145744 | tf_op jit(solution)/shard_map/reduce_scatter | solution.py:112
  4059.9 14.1 fusion.35
  4075.1 192.2 %all-reduce.24.cloned.1.call-done = (bf16[192,4608]{1,0:T(8,128)(2,1)}, bf16[192,1536]{1,0:T(8,128)(2,1)}, bf16[512,3072]{1,0:T(8,128)(2,1)}, bf16[192,8192]{1,0...) async-done(((bf16[192,4608]{1,0:T(8,128)(2,1)}, bf16[192,1536]{1,0:T(8,128)(2,1)}, bf16[512,3072]{1,0:T(8,128)(2,1)}, bf16[192,8192]{1,0:T(8,128)(2,1)}, ...) | async-done | bytes 11796496 | tf_op jit(solution)/shard_map/psum | solution.py:412
  4267.4 5.5 convert_element_type.284
  4272.9 3.4 convert_element_type.286
  4283.8 111.5 %all-reduce.22.cloned.1.call-done = (f32[7,1536]{1,0:T(8,128)}, f32[24]{0:T(128)}, f32[6144]{0:T(1024)}, f32[4096]{0:T(1024)}) async-done(((f32[7,1536]{1,0:T(8,128)}, f32[24]{0:T(128)}, f32[6144]{0:T(1024)}, f32[4096]{0:T(1024)}), (f32[7,1536]{1,0:T(8,128)}, f32[24]{0:T(128)}, f32[6144]{0:T(1024)}, f32[4096]{0:T(1024)})) %all-reduce.22.cloned.1.call-update) | async-done | bytes 84080 | tf_op jit(solution)/shard_map/psum | solution.py:419
  (640 shorter events, 237.3 us)
Async XLA Ops:
  7.2 182.2 %all-gather.10.cloned.1.call-start = ((), (), s32[]{:S(2)}) async-start(), calls=%async_computation.8 | async-start | bytes 14155776 | tf_op jit(solution)/shard_map/all_gather | solution.py:122
  8.0 181.4 %copy-start.99 = (bf16[1,2,1024]{2,1,0:T(2,128)(2,1)S(1)}, bf16[1,2,1024]{2,1,0:T(2,128)(2,1)}, u32[]{:S(2)}) copy-start(bf16[1,2,1024]{2,1,0:T(2,128)(2,1)} %param.24) | copy-start | bytes 12292
  8.0 181.4 %copy-start.101 = (f32[6144]{0:T(1024)S(1)}, f32[6144]{0:T(1024)}, u32[]{:S(2)}) copy-start(f32[6144]{0:T(1024)} %param.36) | copy-start | bytes 73732
  8.0 377.5 %all-gather.12.cloned.1.call-start = ((), (), s32[]{:S(2)}) async-start(), calls=%async_computation.9 | async-start | bytes 15925248 | tf_op jit(solution)/shard_map/all_gather | solution.py:117
  8.7 454.6 %all-gather.16.cloned.1.call-start = ((), (), s32[]{:S(2)}) async-start(), calls=%async_computation.11 | async-start | bytes 3538944 | tf_op jit(solution)/shard_map/all_gather | solution.py:180
  31.3 354.2 %copy-start.86 = (f32[2,64]{1,0:T(2,128)}, f32[2,64]{1,0:T(2,128)S(1)}, u32[]{:S(2)}) copy-start(f32[2,64]{1,0:T(2,128)S(1)} %rsqrt.91) | copy-start | bytes 1540
  31.4 378.9 %copy-start.83 = (s32[64]{0:T(128)}, s32[64]{0:T(128)S(1)}, u32[]{:S(2)}) copy-start(s32[64]{0:T(128)S(1)} %and_select_fusion.3) | copy-start | bytes 772
  32.4 379.4 %copy-start.47 = (f32[2,64,32]{2,1,0:T(8,128)}, f32[2,64,32]{2,1,0:T(8,128)S(1)}, u32[]{:S(2)}) copy-start(f32[2,64,32]{2,1,0:T(8,128)S(1)} %get-tuple-element.347) | copy-start | bytes 49156
  32.4 379.4 %copy-start.49 = (f32[2,64,32]{2,1,0:T(8,128)}, f32[2,64,32]{2,1,0:T(8,128)S(1)}, u32[]{:S(2)}) copy-start(f32[2,64,32]{2,1,0:T(8,128)S(1)} %get-tuple-element.348) | copy-start | bytes 49156
  33.1 359.7 %copy-start.66 = (f32[1536]{0:T(1024)}, f32[1536]{0:T(1024)S(1)}, u32[]{:S(2)}) copy-start(f32[1536]{0:T(1024)S(1)} %get-tuple-element.256) | copy-start | bytes 18436
  33.1 359.7 %copy-start.68 = (f32[1536]{0:T(1024)}, f32[1536]{0:T(1024)S(1)}, u32[]{:S(2)}) copy-start(f32[1536]{0:T(1024)S(1)} %get-tuple-element.257) | copy-start | bytes 18436
  195.7 196.9 %copy-start.58 = (f32[2,6144]{1,0:T(2,128)}, f32[2,6144]{1,0:T(2,128)S(1)}, u32[]{:S(2)}) copy-start(f32[2,6144]{1,0:T(2,128)S(1)} %convolution_add_fusion) | copy-start | bytes 147460
  196.4 196.3 %copy-start.60 = (f32[2,1536]{1,0:T(2,128)}, f32[2,1536]{1,0:T(2,128)S(1)}, u32[]{:S(2)}) copy-start(f32[2,1536]{1,0:T(2,128)S(1)} %get-tuple-element.355) | copy-start | bytes 36868
  404.5 120.6 %all-gather.14.cloned.1.call-start = ((), (), s32[]{:S(2)}) async-start(), calls=%async_computation.10 | async-start | bytes 3538944 | tf_op jit(solution)/shard_map/all_gather | solution.py:181
  405.4 600.2 %all-gather.18.cloned.1.call-start = ((), (), s32[]{:S(2)}) async-start(), calls=%async_computation.12 | async-start | bytes 28311552 | tf_op jit(solution)/shard_map/all_gather | solution.py:119
  406.0 701.8 %all-gather.20.cloned.1.call-start = ((), (), s32[]{:S(2)}) async-start(), calls=%async_computation.13 | async-start | bytes 5308416 | tf_op jit(solution)/shard_map/all_gather | solution.py:118
  406.6 1182.6 %all-gather.22.cloned.1.call-start = ((), (), s32[]{:S(2)}) async-start(), calls=%async_computation.14 | async-start | bytes 28311552 | tf_op jit(solution)/shard_map/all_gather | solution.py:120
  407.4 1360.4 %all-gather.24.cloned.1.call-start = ((), (), s32[]{:S(2)}) async-start(), calls=%async_computation.15 | async-start | bytes 14155776 | tf_op jit(solution)/shard_map/all_gather | solution.py:121
  410.9 594.6 %copy-start.81 = (f32[2,16]{1,0:T(2,128)}, f32[2,16]{1,0:T(2,128)S(1)}, u32[]{:S(2)}) copy-start(f32[2,16]{1,0:T(2,128)S(1)} %add_rsqrt_fusion) | copy-start | bytes 388
  412.9 679.6 %copy-start.16 = (bf16[2,64,24,64]{3,1,2,0:T(8,128)(2,1)}, bf16[2,64,24,64]{3,1,2,0:T(8,128)(2,1)S(1)}, u32[]{:S(2)}) copy-start(bf16[2,64,24,64]{3,1,2,0:T(8,128)(2,1)S(1)} %maximum_convert_fusion) | copy-start | bytes 1179652
  568.0 437.6 %copy-start.55 = (f32[4096]{0:T(1024)S(1)}, f32[4096]{0:T(1024)}, u32[]{:S(2)}) copy-start(f32[4096]{0:T(1024)} %param.37) | copy-start | bytes 49156
  570.6 445.5 %copy-start.73 = (f32[1536]{0:T(1024)S(1)}, f32[1536]{0:T(1024)}, u32[]{:S(2)}) copy-start(f32[1536]{0:T(1024)} %get-tuple-element.255) | copy-start | bytes 18436
  1016.0 37.8 copy-start.26
  1016.2 74.0 %copy-start.111 = (f32[2,16]{1,0:T(2,128)}, f32[2,16]{1,0:T(2,128)S(1)}, u32[]{:S(2)}) copy-start(f32[2,16]{1,0:T(2,128)S(1)} %multiply_reduce_fusion.24) | copy-start | bytes 388
  1016.2 74.0 %copy-start.105 = (f32[2,16]{1,0:T(2,128)}, f32[2,16]{1,0:T(2,128)S(1)}, u32[]{:S(2)}) copy-start(f32[2,16]{1,0:T(2,128)S(1)} %fusion.76) | copy-start | bytes 388
  1053.9 40.4 copy-start.36
  1053.9 38.6 copy-start.130
  1601.9 172.3 %copy-start.4 = (bf16[128,4096]{1,0:T(8,128)(2,1)}, bf16[128,4096]{1,0:T(8,128)(2,1)S(1)}, u32[]{:S(2)}) copy-start(bf16[128,4096]{1,0:T(8,128)(2,1)S(1)} %multiply_convert_fusion.1) | copy-start | bytes 3145732
  1601.9 172.4 %copy-start.64 = (f32[2,1536]{1,0:T(2,128)S(1)}, f32[2,1536]{1,0:T(2,128)}, u32[]{:S(2)}) copy-start(f32[2,1536]{1,0:T(2,128)} %get-tuple-element.353) | copy-start | bytes 36868
  1601.9 172.4 %copy-start.71 = (f32[1536]{0:T(1024)S(1)}, f32[1536]{0:T(1024)}, u32[]{:S(2)}) copy-start(f32[1536]{0:T(1024)} %get-tuple-element.253) | copy-start | bytes 18436
  1601.9 172.4 %copy-start.123 = (f32[128]{0:T(128)S(1)}, f32[128]{0:T(128)}, u32[]{:S(2)}) copy-start(f32[128]{0:T(128)} %compare_convert_fusion) | copy-start | bytes 1540
  1823.3 537.8 %copy-start.104 = (f32[2,24,64]{2,1,0:T(8,128)S(1)}, f32[2,24,64]{2,1,0:T(8,128)}, u32[]{:S(2)}) copy-start(f32[2,24,64]{2,1,0:T(8,128)} %copy-done.102) | copy-start | bytes 36868
  1823.3 86.9 %all-reduce.26.cloned.1.call-start = ((), (), s32[]{:S(2)}) async-start(), calls=%async_computation.26 | async-start | bytes 2097152 | tf_op jit(solution)/shard_map/while
  1911.9 88.1 %all-reduce.26.cloned.1.call-start = ((), (), s32[]{:S(2)}) async-start(), calls=%async_computation.26 | async-start | bytes 2097152 | tf_op jit(solution)/shard_map/while
  2001.6 88.0 %all-reduce.26.cloned.1.call-start = ((), (), s32[]{:S(2)}) async-start(), calls=%async_computation.26 | async-start | bytes 2097152 | tf_op jit(solution)/shard_map/while
  2091.3 88.1 %all-reduce.26.cloned.1.call-start = ((), (), s32[]{:S(2)}) async-start(), calls=%async_computation.26 | async-start | bytes 2097152 | tf_op jit(solution)/shard_map/while
  2181.0 88.1 %all-reduce.26.cloned.1.call-start = ((), (), s32[]{:S(2)}) async-start(), calls=%async_computation.26 | async-start | bytes 2097152 | tf_op jit(solution)/shard_map/while
  2270.7 88.1 %all-reduce.26.cloned.1.call-start = ((), (), s32[]{:S(2)}) async-start(), calls=%async_computation.26 | async-start | bytes 2097152 | tf_op jit(solution)/shard_map/while
  2360.4 98.9 %reduce-scatter.15.cloned.1.call-start = ((), (), s32[]{:S(2)}) async-start(), calls=%async_computation.19 | async-start | bytes 884736 | tf_op jit(solution)/shard_map/reduce_scatter | solution.py:355
  2361.0 130.1 %reduce-scatter.13.cloned.1.call-start = ((), (), s32[]{:S(2)}) async-start(), calls=%async_computation.18 | async-start | bytes 884736 | tf_op jit(solution)/shard_map/reduce_scatter | solution.py:361
  2364.8 224.6 %reduce-scatter.11.cloned.1.call-start = ((), (), s32[]{:S(2)}) async-start(), calls=%async_computation.17 | async-start | bytes 5308416 | tf_op jit(solution)/shard_map/reduce_scatter | solution.py:112
  2369.4 430.6 %reduce-scatter.23.cloned.1.call-start = ((), (), s32[]{:S(2)}) async-start(), calls=%async_computation.23 | async-start | bytes 14155776 | tf_op jit(solution)/shard_map/reduce_scatter | solution.py:112
  2426.8 583.2 %reduce-scatter.21.cloned.1.call-start = ((), (), s32[]{:S(2)}) async-start(), calls=%async_computation.22 | async-start | bytes 14155776 | tf_op jit(solution)/shard_map/reduce_scatter | solution.py:112
  2434.5 807.3 %reduce-scatter.9.cloned.1.call-start = ((), (), s32[]{:S(2)}) async-start(), calls=%async_computation.16 | async-start | bytes 15925248 | tf_op jit(solution)/shard_map/reduce_scatter | solution.py:112
  2444.2 1204.5 %reduce-scatter.19.cloned.1.call-start = ((), (), s32[]{:S(2)}) async-start(), calls=%async_computation.21 | async-start | bytes 28311552 | tf_op jit(solution)/shard_map/reduce_scatter | solution.py:112
  2459.3 1596.1 %reduce-scatter.17.cloned.1.call-start = ((), (), s32[]{:S(2)}) async-start(), calls=%async_computation.20 | async-start | bytes 28311552 | tf_op jit(solution)/shard_map/reduce_scatter | solution.py:112
  2504.6 1762.8 %all-reduce.24.cloned.1.call-start = ((), (), s32[]{:S(2)}) async-start(), calls=%async_computation.25 | async-start | bytes 23592960 | tf_op jit(solution)/shard_map/psum | solution.py:412
  4055.5 339.8 %all-reduce.22.cloned.1.call-start = ((), (), s32[]{:S(2)}) async-start(), calls=%async_computation.24 | async-start | bytes 181248 | tf_op jit(solution)/shard_map/psum | solution.py:419
  (109 other events, 514.9 us)
Sparse Core Ops, SparseCore 0:
  10.2 179.1 all-gather.9
  191.6 193.8 all-gather.11
  404.6 58.6 all-gather.15
  466.0 59.0 all-gather.13
  526.5 479.0 all-gather.17
  1007.6 100.1 all-gather.19
  1109.3 479.8 all-gather.21
  1591.3 176.3 all-gather.23
  1833.5 76.6 all-reduce.25
  1922.1 77.8 all-reduce.25
  2011.8 77.7 all-reduce.25
  2101.5 77.8 all-reduce.25
  2191.2 77.8 all-reduce.25
  2280.9 77.8 all-reduce.25
  2364.3 61.7 reduce-scatter.14
  2429.6 61.4 reduce-scatter.12
  2495.2 94.1 reduce-scatter.10
  2592.8 207.1 reduce-scatter.22
  2803.6 206.4 reduce-scatter.20
  3013.6 228.2 reduce-scatter.8
  3245.8 402.8 reduce-scatter.18
  3652.5 402.7 reduce-scatter.16
  4058.5 208.8 all-reduce.23
  4273.9 121.3 all-reduce.21
where the time goes:
time: 4420 us; the launch traced here: 4410 us
  waiting for transfers between devices  3880 us (88%)
  matrix products  186 us (4%)
  local copies, waits for them, and re-layouts  153 us (3%)
  blocking collectives  94.6 us (2%)
  other arithmetic  66 us (1%)
    reduce_scatter x6, waiting for transfers between devices, reduce_term(): lax.psum_scatter(term.astype(jnp.bfloat16), 'rows', scatter_dimension=0,...  1550 us
    all_gather x1, waiting for transfers between devices, per_device(): lax.all_gather(w_gu, 'rows', axis=0, tiled=True)  476 us
    while x12, waiting for transfers between devices  453 us
    all_gather x1, waiting for transfers between devices, per_device(): lax.all_gather(w_text, 'rows', axis=0, tiled=True)  435 us
    psum x1, waiting for transfers between devices, per_device(): lax.psum(shard_qkv.astype(jnp.bfloat16), 'items').astype(jnp.float32)  192 us
    all_gather x1, waiting for transfers between devices, per_device(): lax.all_gather(w_qkv, 'rows', axis=0, tiled=True)  189 us
    all_gather x1, waiting for transfers between devices, per_device(): lax.all_gather(w_down, 'rows', axis=0, tiled=True)  166 us
    all_gather x1, waiting for transfers between devices, per_device(): lax.all_gather(w_ada, 'rows', axis=0, tiled=True)  156 us
  transfers between devices with their start and end apart: 24, of which 23 were waited for; matrix products, arithmetic and copies ran while one was open for 6% of the time, Pallas kernels for 0%

commit v1 on v0

--- a/solution.py
+++ b/solution.py
@@ -67,7 +67,7 @@
     return (norm_gain(projected[..., :half_cols], key_gain), projected[..., half_cols:])
 
 
-def per_device(
+def gathered_plan(
     hidden_in,
     cotangent,
     text_states,
@@ -435,6 +435,381 @@
     )
 
 
+def norm_parts(values):
+    inverse = lax.rsqrt(jnp.mean(values * values, axis=-1, keepdims=True) + epsilon)
+    return values * inverse, inverse
+
+
+def norm_back(unit, inverse, scaled_grad):
+    return inverse * (scaled_grad - unit * jnp.mean(scaled_grad * unit, axis=-1, keepdims=True))
+
+
+def gather_tokens(block):
+    return lax.all_gather(block, "rows", axis=1, tiled=True)
+
+
+def scatter_tokens(partial):
+    return lax.psum_scatter(
+        partial.astype(jnp.bfloat16), "rows", scatter_dimension=1, tiled=True
+    ).astype(jnp.float32)
+
+
+def columns_here(weight, pieces):
+    ranks = lax.axis_size("rows")
+    depth, width = weight.shape
+    shaped = weight.reshape(depth, pieces, ranks, width // (pieces * ranks))
+    moved = lax.all_to_all(shaped, "rows", split_axis=2, concat_axis=0, tiled=True)
+    return moved.reshape(depth * ranks, width // ranks)
+
+
+def rows_here(grad, pieces):
+    ranks = lax.axis_size("rows")
+    depth, width = grad.shape
+    low = grad.astype(jnp.bfloat16).reshape(depth, pieces, 1, width // pieces)
+    moved = lax.all_to_all(low, "rows", split_axis=0, concat_axis=2, tiled=True)
+    return moved.reshape(depth // ranks, width * ranks)
+
+
+def head_parallel_plan(
+    hidden_in,
+    cotangent,
+    text_states,
+    time_embed,
+    live_rows,
+    frame_rows,
+    text_len,
+    w_qkv,
+    w_out,
+    w_text,
+    w_gu,
+    w_down,
+    w_ada,
+    gains,
+    cross_gate,
+    ada_bias,
+    text_gain,
+):
+    single = jnp.float32
+    narrow = jnp.bfloat16
+    ranks = lax.axis_size("rows")
+    place = lax.axis_index("rows")
+    width = hidden_in.shape[2]
+    heads = cross_gate.shape[0]
+    head_size = width // heads
+    score_scale = head_size ** (-0.5)
+    items = time_embed.shape[1]
+    slots = hidden_in.shape[1] // items
+    row_slots = slots // COLS
+    seq_len = ranks * slots
+    text_local = text_states.shape[2]
+    text_all = text_local * ranks
+    text_width = text_states.shape[3]
+    span = width // ranks
+    heads_here = heads // ranks
+    tokens = items * seq_len
+
+    def dot(left, right):
+        return jnp.dot(left, right, preferred_element_type=single)
+
+    def dot_back(left, weight):
+        return jnp.einsum("tn,kn->tk", left, weight, preferred_element_type=single)
+
+    def weight_grad(left, right):
+        return jnp.einsum("tk,tn->kn", left, right, preferred_element_type=single)
+
+    time_silu = jax.nn.silu(time_embed[0].astype(single)).astype(narrow)
+    ada_depth = w_ada.shape[0]
+    time_here = lax.dynamic_slice_in_dim(time_silu, place * ada_depth, ada_depth, 1)
+    modulation = lax.psum(dot(time_here, w_ada), "rows") + ada_bias
+    scale_attn = modulation[:, None, 0:width]
+    gate_attn = jnp.tanh(modulation[:, None, width : 2 * width])
+    scale_ffn = modulation[:, None, 2 * width : 3 * width]
+    gate_ffn = jnp.tanh(modulation[:, None, 3 * width :])
+
+    counts_here = live_rows[0]
+    counts = lax.all_gather(counts_here, "rows", axis=0, tiled=True)
+    below = jnp.cumsum(counts, axis=0) - counts
+    slot_row = jnp.arange(row_slots)
+    row_index = jnp.transpose(below)[:, :, None] + slot_row
+    heights = frame_rows[0][:, None, None]
+    frame_pairs = head_size // 8
+    space_pairs = (head_size // 2 - frame_pairs) // 2
+    row_angles = jnp.concatenate(
+        [
+            (row_index // heights).astype(single)[..., None] * freq_rates(frame_pairs),
+            (row_index % heights).astype(single)[..., None] * freq_rates(space_pairs),
+        ],
+        axis=-1,
+    )
+    column_angles = jnp.arange(COLS).astype(single)[:, None] * freq_rates(space_pairs)
+
+    def table(function):
+        by_row = function(row_angles)
+        by_column = function(column_angles)
+        shape = (items, ranks, row_slots, COLS)
+        whole = jnp.concatenate(
+            [
+                jnp.broadcast_to(by_row[:, :, :, None, :], shape + by_row.shape[-1:]),
+                jnp.broadcast_to(by_column, shape + by_column.shape[-1:]),
+            ],
+            axis=-1,
+        )
+        return whole.reshape(tokens, 1, head_size // 2)
+
+    cos_table = table(jnp.cos)
+    sin_table = table(jnp.sin)
+
+    def turn(values, sign):
+        shaped = values.reshape(tokens, heads_here, head_size)
+        upper = shaped[..., : head_size // 2]
+        lower = shaped[..., head_size // 2 :]
+        sines = sign * sin_table
+        turned = jnp.concatenate(
+            [upper * cos_table - lower * sines, upper * sines + lower * cos_table], axis=-1
+        )
+        return turned.reshape(tokens, width // ranks)
+
+    slot_in_row = jnp.arange(slots) // COLS
+    live_mask = (slot_in_row[None, :] < counts_here[0][:, None]).astype(single)[..., None]
+    key_live = (slot_in_row < jnp.transpose(counts)[:, :, None]).reshape(items, seq_len)
+    text_live = jnp.arange(text_all)[None, :] < text_len[0][:, None]
+
+    def gain_here(index):
+        return lax.dynamic_slice_in_dim(gains[index], place * span, span, 0)
+
+    states = hidden_in[0].reshape(items, slots, width)
+    unit_in, inverse_in = norm_parts(states)
+    norm_in = unit_in * gains[0]
+    attn_in = gather_tokens((norm_in * (1.0 + scale_attn)).astype(narrow)).reshape(tokens, width)
+    qkv_here = columns_here(w_qkv, 3)
+    qkv_proj = dot(attn_in, qkv_here)
+    query_proj, key_proj, value_proj = jnp.split(qkv_proj, 3, axis=1)
+
+    text_in = lax.all_gather(text_states[0], "rows", axis=1, tiled=True)
+    text_unit, _ = norm_parts(text_in.astype(single).reshape(items * text_all, text_width))
+    text_norm = (text_unit * text_gain).astype(narrow)
+    text_here = columns_here(w_text, 2)
+    text_proj = dot(text_norm, text_here)
+    tkey_proj, tval_proj = jnp.split(text_proj, 2, axis=1)
+
+    def squares(values):
+        return jnp.sum(values * values, axis=-1)
+
+    totals = lax.psum(
+        jnp.concatenate([squares(query_proj), squares(key_proj), squares(tkey_proj)]), "rows"
+    )
+    inverses = lax.rsqrt(totals / width + epsilon)[:, None]
+    inverse_q, inverse_k, inverse_t = (
+        inverses[:tokens],
+        inverses[tokens : 2 * tokens],
+        inverses[2 * tokens :],
+    )
+    gain_q, gain_k, gain_t = gain_here(1), gain_here(2), gain_here(6)
+    unit_q, unit_k, unit_t = query_proj * inverse_q, key_proj * inverse_k, tkey_proj * inverse_t
+
+    def by_head(values):
+        return values.reshape(items, -1, heads_here, head_size)
+
+    query = by_head(turn(unit_q * gain_q, 1.0).astype(narrow))
+    key = by_head(turn(unit_k * gain_k, 1.0).astype(narrow))
+    value = by_head(value_proj.astype(narrow))
+    tkey = by_head((unit_t * gain_t).astype(narrow))
+    tval = by_head(tval_proj.astype(narrow))
+
+    def soft(keys, mask):
+        scores = jnp.einsum("iphe,ikhe->ihpk", query, keys, preferred_element_type=single)
+        scores = jnp.where(mask[:, None, None, :], scores * score_scale, masked_score)
+        terms = jnp.exp(scores - jnp.max(scores, axis=-1, keepdims=True))
+        return terms / jnp.sum(terms, axis=-1, keepdims=True)
+
+    def mix(weights, values):
+        return jnp.einsum("ihpk,ikhe->iphe", weights, values, preferred_element_type=single)
+
+    probs = soft(key, key_live)
+    self_out = mix(probs.astype(narrow), value)
+    cross_probs = soft(tkey, text_live)
+    cross_out = mix(cross_probs.astype(narrow), tval)
+    gate_here = jnp.tanh(lax.dynamic_slice_in_dim(cross_gate, place * heads_here, heads_here, 0))
+    combined = (self_out + gate_here[:, None] * cross_out).astype(narrow).reshape(tokens, span)
+    projected = scatter_tokens(dot(combined, w_out).reshape(items, seq_len, width))
+
+    unit_proj, inverse_proj = norm_parts(projected)
+    norm_proj = unit_proj * gains[3]
+    middle = states + gate_attn * norm_proj
+    unit_mid, inverse_mid = norm_parts(middle)
+    norm_mid = unit_mid * gains[4]
+    ffn_in = gather_tokens((norm_mid * (1.0 + scale_ffn)).astype(narrow)).reshape(tokens, width)
+    gu_here = columns_here(w_gu, 2)
+    gate_up = dot(ffn_in, gu_here)
+    gate_part, up_part = jnp.split(gate_up, 2, axis=1)
+    sigmoid = 1.0 / (1.0 + jnp.exp(-gate_part))
+    inner_act = (gate_part * sigmoid * up_part).astype(narrow)
+    ffn_out = scatter_tokens(dot(inner_act, w_down).reshape(items, seq_len, width))
+    unit_ffn, inverse_ffn = norm_parts(ffn_out)
+    norm_ffn = unit_ffn * gains[5]
+    output = live_mask * (middle + gate_ffn * norm_ffn)
+
+    def over_tokens(values):
+        return jnp.sum(values, axis=(0, 1))
+
+    grad_result = live_mask * cotangent[0].reshape(items, slots, width)
+    grad_gate_ffn = (1.0 - gate_ffn * gate_ffn)[:, 0] * jnp.sum(grad_result * norm_ffn, axis=1)
+    grad_norm = gate_ffn * grad_result
+    grad_five = over_tokens(grad_norm * unit_ffn)
+    ffn_low = gather_tokens(
+        norm_back(unit_ffn, inverse_ffn, grad_norm * gains[5]).astype(narrow)
+    ).reshape(tokens, width)
+    grad_down = weight_grad(inner_act, ffn_low)
+    grad_inner = dot_back(ffn_low, w_down)
+    gate_up_low = jnp.concatenate(
+        [
+            grad_inner * up_part * sigmoid * (1.0 + gate_part * (1.0 - sigmoid)),
+            grad_inner * gate_part * sigmoid,
+        ],
+        axis=1,
+    ).astype(narrow)
+    grad_gu = weight_grad(ffn_in, gate_up_low)
+    grad_ffn_in = scatter_tokens(
+        dot_back(gate_up_low, gu_here).reshape(items, seq_len, width)
+    )
+    grad_scale_ffn = jnp.sum(grad_ffn_in * norm_mid, axis=1)
+    grad_norm = grad_ffn_in * (1.0 + scale_ffn)
+    grad_four = over_tokens(grad_norm * unit_mid)
+    grad_middle = grad_result + norm_back(unit_mid, inverse_mid, grad_norm * gains[4])
+
+    grad_gate_attn = (1.0 - gate_attn * gate_attn)[:, 0] * jnp.sum(grad_middle * norm_proj, axis=1)
+    grad_norm = gate_attn * grad_middle
+    grad_three = over_tokens(grad_norm * unit_proj)
+    projected_low = gather_tokens(
+        norm_back(unit_proj, inverse_proj, grad_norm * gains[3]).astype(narrow)
+    ).reshape(tokens, width)
+    grad_out = weight_grad(combined, projected_low)
+    grad_combined = by_head(dot_back(projected_low, w_out))
+    self_low = grad_combined.astype(narrow)
+    cross_grad_low = (gate_here[:, None] * grad_combined).astype(narrow)
+    grad_gate = (1.0 - gate_here * gate_here) * jnp.sum(grad_combined * cross_out, axis=(0, 1, 3))
+
+    def soft_back(weights, low_grad, keys, values):
+        grad_weights = jnp.einsum(
+            "iphe,ikhe->ihpk", low_grad, values, preferred_element_type=single
+        )
+        inner = jnp.sum(weights * grad_weights, axis=-1, keepdims=True)
+        score_low = (weights * (grad_weights - inner)).astype(narrow)
+        grad_values = jnp.einsum(
+            "ihpk,iphe->ikhe", weights.astype(narrow), low_grad, preferred_element_type=single
+        )
+        grad_keys = jnp.einsum(
+            "ihpk,iphe->ikhe", score_low, query, preferred_element_type=single
+        )
+        grad_queries = mix(score_low, keys)
+        return (
+            grad_queries * score_scale,
+            (grad_keys * score_scale).reshape(-1, span),
+            grad_values.reshape(-1, span),
+        )
+
+    grad_query, grad_key, grad_value = soft_back(probs, self_low, key, value)
+    grad_query_text, grad_tkey, grad_tval = soft_back(cross_probs, cross_grad_low, tkey, tval)
+    grad_query = (grad_query + grad_query_text).reshape(tokens, span)
+    grad_query = turn(grad_query, -1.0)
+    grad_key = turn(grad_key, -1.0)
+    scaled_q, scaled_k, scaled_t = grad_query * gain_q, grad_key * gain_k, grad_tkey * gain_t
+    means = (
+        lax.psum(
+            jnp.concatenate(
+                [
+                    jnp.sum(scaled_q * unit_q, axis=-1),
+                    jnp.sum(scaled_k * unit_k, axis=-1),
+                    jnp.sum(scaled_t * unit_t, axis=-1),
+                ]
+            ),
+            "rows",
+        )[:, None]
+        / width
+    )
+    qkv_low = jnp.concatenate(
+        [
+            inverse_q * (scaled_q - unit_q * means[:tokens]),
+            inverse_k * (scaled_k - unit_k * means[tokens : 2 * tokens]),
+            grad_value,
+        ],
+        axis=1,
+    ).astype(narrow)
+    text_low = jnp.concatenate(
+        [inverse_t * (scaled_t - unit_t * means[2 * tokens :]), grad_tval], axis=1
+    ).astype(narrow)
+    grad_qkv = weight_grad(attn_in, qkv_low)
+    grad_attn_in = scatter_tokens(dot_back(qkv_low, qkv_here).reshape(items, seq_len, width))
+    grad_scale_attn = jnp.sum(grad_attn_in * norm_in, axis=1)
+    grad_norm = grad_attn_in * (1.0 + scale_attn)
+    grad_zero = over_tokens(grad_norm * unit_in)
+    grad_x = grad_middle + norm_back(unit_in, inverse_in, grad_norm * gains[0])
+
+    grad_text = weight_grad(text_norm, text_low)
+    grad_text_gain = jnp.sum(dot_back(text_low, text_here) * text_unit, axis=0)
+    grad_modulation = jnp.concatenate(
+        [grad_scale_attn, grad_gate_attn, grad_scale_ffn, grad_gate_ffn], axis=-1
+    )
+    all_modulation = lax.all_gather(
+        lax.psum(grad_modulation, "rows"), "items", axis=0, tiled=True
+    )
+    all_time = lax.all_gather(time_here, "items", axis=0, tiled=True)
+    final_ada = jnp.einsum(
+        "tk,tn->kn",
+        all_time.astype(single),
+        all_modulation,
+        precision=lax.Precision.HIGHEST,
+        preferred_element_type=single,
+    )
+    total_bias = jnp.sum(all_modulation, axis=0)
+
+    def spread(part, whole):
+        return lax.dynamic_update_slice_in_dim(
+            jnp.zeros((whole,), single), part, place * part.shape[0], 0
+        )
+
+    grad_gains = jnp.stack(
+        [
+            grad_zero,
+            spread(jnp.sum(grad_query * unit_q, axis=0), width),
+            spread(jnp.sum(grad_key * unit_k, axis=0), width),
+            grad_three,
+            grad_four,
+            grad_five,
+            spread(jnp.sum(grad_tkey * unit_t, axis=0), width),
+        ]
+    )
+    total_gains, total_gate, total_text_gain = lax.psum(
+        (grad_gains, spread(grad_gate, heads), grad_text_gain), ("items", "rows")
+    )
+    sums = [
+        lax.psum(part.astype(narrow), "items").astype(single)
+        for part in (
+            rows_here(grad_qkv, 3),
+            grad_out,
+            rows_here(grad_text, 2),
+            rows_here(grad_gu, 2),
+            grad_down,
+        )
+    ]
+    return (
+        output.reshape(1, items * slots, width),
+        grad_x.reshape(1, items * slots, width),
+        *sums,
+        final_ada,
+        total_gains,
+        total_gate,
+        total_bias,
+        total_text_gain,
+    )
+
+
+def per_device(*arrays):
+    heads = arrays[14].shape[0]
+    plan = gathered_plan if heads % lax.axis_size("rows") else head_parallel_plan
+    return plan(*arrays)
+
+
 def solution(mesh):
     in_specs = (
         P("items", "rows", None),

time: 4420 us -> 1370 us (0.31)
  waiting for transfers between devices: 3880 us -> 661 us
  blocking collectives: 94.6 us -> 365 us
  matrix products: 186 us -> 90.1 us
    all_gather x8 -> x5, waiting for transfers between devices: 1540 us -> 191 us  [the longest x4 191 us: gather_tokens(): return lax.all_gather(block, 'rows', axis=1, tiled=True)]
    reduce_scatter x8 -> x4, waiting for transfers between devices: 1580 us -> 252 us  [scatter_tokens(): lax.psum_scatter(partial.astype(jnp.bfloat16), 'rows', scatter_dimension=...]
    while x12 -> x0, waiting for transfers between devices: 453 us -> none
    psum x0 -> x5, blocking collectives: none -> 272 us  [the longest x1 98 us: head_parallel_plan(): modulation = lax.psum(dot(time_here, w_ada), 'rows') + ada_bias]
    psum x2 -> x1, waiting for transfers between devices: 304 us -> 84.5 us  [head_parallel_plan(): lax.psum(part.astype(narrow), 'items').astype(single)]
    all_to_all x0 -> x6, waiting for transfers between devices: none -> 133 us  [the longest x3 133 us: rows_here(): moved = lax.all_to_all(low, 'rows', split_axis=0, concat_axis=2, tiled=True)]
    dot_general x64 -> x27, matrix products: 185 us -> 84 us  [the longest x5 22.9 us: dot_back(): return jnp.einsum('tn,kn->tk', left, weight, preferred_element_type=single)]
    reshape x26 -> x15, local copies, waits for them, and re-layouts: 16.1 us -> 69.2 us  [the longest x3 25.1 us: rows_here(): low = grad.astype(jnp.bfloat16).reshape(depth, pieces, 1, width // pieces)]
  transfers between devices with their start and end apart: 24 -> 16, of which waited for: 23 -> 9; matrix products, arithmetic and copies ran while one was open for 6% -> 15% of each run, Pallas kernels for 0% -> 0%
where the time goes in v1:
time: 1370 us; the launch traced here: 1360 us
  waiting for transfers between devices  661 us (48%)
  blocking collectives  365 us (27%)
  local copies, waits for them, and re-layouts  143 us (10%)
  matrix products  90.1 us (7%)
  other arithmetic  55.5 us (4%)
  starting transfers between devices  31.2 us (2%)
  between operations  16.1 us (1%)
    reduce_scatter x4, waiting for transfers between devices, scatter_tokens(): lax.psum_scatter(partial.astype(jnp.bfloat16), 'rows', scatter_dimension=...  252 us
    all_gather x4, waiting for transfers between devices, gather_tokens(): return lax.all_gather(block, 'rows', axis=1, tiled=True)  191 us
    all_to_all x3, waiting for transfers between devices, rows_here(): moved = lax.all_to_all(low, 'rows', split_axis=0, concat_axis=2, tiled=True)  133 us
    psum x1, blocking collectives, head_parallel_plan(): modulation = lax.psum(dot(time_here, w_ada), 'rows') + ada_bias  98 us
    psum x1, waiting for transfers between devices, head_parallel_plan(): lax.psum(part.astype(narrow), 'items').astype(single)  84.5 us
    all_gather x1, blocking collectives, head_parallel_plan(): counts = lax.all_gather(counts_here, 'rows', axis=0, tiled=True)  80.7 us
    psum x1, blocking collectives, head_parallel_plan(): lax.psum(jnp.concatenate([squares(query_proj), squares(key_proj), squares...  65.4 us
    psum x1, blocking collectives, head_parallel_plan(): lax.psum((grad_gains, spread(grad_gate, heads), grad_text_gain), ('items'...  39.3 us
  transfers between devices with their start and end apart: 16, of which 9 were waited for; matrix products, arithmetic and copies ran while one was open for 15% of the time, Pallas kernels for 0%

profile of v1, /device:TPU:0, one launch (start us, length us, event | category | flops | bytes accessed | tf_op | source)
XLA Modules:
  0.0 1361.5 jit_solution(15530656957947362020)
XLA Ops:
  7.9 4.5 reshape.498
  12.4 4.6 copy.239
  17.0 7.4 all-to-all-start
  26.6 98.0 %psum.84 = f32[2,6144]{1,0:T(2,128)S(1)} all-reduce(f32[2,6144]{1,0:T(2,128)S(1)} %fusion.189), channel_id=1, replica_groups=mesh['items'=4,'rows'=8] {'rows'}, use_global_device_ids=true, to_apply=%region_0.1 | all-reduce | flops 12288 | bytes 98304 | tf_op jit(solution)/shard_map/psum | solution.py:523
  126.8 4.6 copy.242
  135.3 4.6 all-to-all-start.1
  140.0 80.7 %all-gather = s32[8,1,2]{2,1,0:T(1,128)S(1)} all-gather(s32[1,1,2]{2,1,0:T(1,128)S(1)} %copy-done.94), channel_id=2, replica_groups=mesh['items'=4,'rows'=8] {'rows'}, dimensions={0}, use_global_device_ids=true | all-gather | bytes 72 | tf_op jit(solution)/shard_map/all_gather | solution.py:530
  228.6 4.4 copy.240
  233.0 4.8 reshape.499
  242.6 4.4 fusion.190
  257.5 65.4 %psum.85 = f32[2304]{0:T(1024)S(1)} all-reduce(f32[2304]{0:T(1024)S(1)} %pad_maximum_fusion.11), channel_id=1, replica_groups=mesh['items'=4,'rows'=8] {'rows'}, use_global_device_ids=true, to_apply=%region_6.7 | all-reduce | flops 2304 | bytes 18432 | tf_op jit(solution)/shard_map/psum | solution.py:598
  349.8 4.5 all-to-all-start.2
  354.4 106.3 %reduce-scatter.5.cloned.1.call-done = bf16[2,64,1536]{2,1,0:T(8,128)(2,1)} async-done(((bf16[2,512,1536]{2,1,0:T(8,128)(2,1)}), bf16[2,64,1536]{2,1,0:T(8,128)(2,1)}) %reduce-scatter.5.cloned.1.call-update) | async-done | bytes 393232 | tf_op jit(solution)/shard_map/reduce_scatter | solution.py:452
  464.3 4.4 copy.307
  468.7 55.1 %all-gather.12.cloned.1.call-done = bf16[2,512,1536]{2,1,0:T(8,128)(2,1)} async-done(((bf16[2,64,1536]{2,1,0:T(8,128)(2,1)}), bf16[2,512,1536]{2,1,0:T(8,128)(2,1)}) %all-gather.12.cloned.1.call-update) | async-done | bytes 3145744 | tf_op jit(solution)/shard_map/all_gather | solution.py:448
  523.8 6.2 fusion.192
  537.0 72.5 %reduce-scatter.7.cloned.1.call-done = bf16[2,64,1536]{2,1,0:T(8,128)(2,1)} async-done(((bf16[2,512,1536]{2,1,0:T(8,128)(2,1)}), bf16[2,64,1536]{2,1,0:T(8,128)(2,1)}) %reduce-scatter.7.cloned.1.call-update) | async-done | bytes 393232 | tf_op jit(solution)/shard_map/reduce_scatter | solution.py:452
  615.4 6.1 reshape.537
  621.5 53.9 %all-gather.14.cloned.1.call-done = bf16[2,512,1536]{2,1,0:T(8,128)(2,1)} async-done(((bf16[2,64,1536]{2,1,0:T(8,128)(2,1)}), bf16[2,512,1536]{2,1,0:T(8,128)(2,1)}) %all-gather.14.cloned.1.call-update) | async-done | bytes 3145744 | tf_op jit(solution)/shard_map/all_gather | solution.py:448
  675.4 5.8 multiply_convert_fusion.4
  682.5 4.8 convolution_convert_fusion.5
  687.4 73.0 %reduce-scatter.9.cloned.1.call-done = bf16[2,64,1536]{2,1,0:T(8,128)(2,1)} async-done(((bf16[2,512,1536]{2,1,0:T(8,128)(2,1)}), bf16[2,64,1536]{2,1,0:T(8,128)(2,1)}) %reduce-scatter.9.cloned.1.call-update) | async-done | bytes 393232 | tf_op jit(solution)/shard_map/reduce_scatter | solution.py:452
  768.6 7.6 convolution_convert_fusion.4
  776.3 8.7 copy.283
  784.9 5.0 all-to-all-start.5
  789.9 81.8 %all-gather.16.cloned.1.call-done = bf16[2,512,1536]{2,1,0:T(8,128)(2,1)} async-done(((bf16[2,64,1536]{2,1,0:T(8,128)(2,1)}), bf16[2,512,1536]{2,1,0:T(8,128)(2,1)}) %all-gather.16.cloned.1.call-update) | async-done | bytes 3145744 | tf_op jit(solution)/shard_map/all_gather | solution.py:448
  891.4 33.0 %psum.86 = f32[2304]{0:T(1024)S(1)} all-reduce(f32[2304]{0:T(1024)S(1)} %pad_maximum_fusion.12), channel_id=1, replica_groups=mesh['items'=4,'rows'=8] {'rows'}, use_global_device_ids=true, to_apply=%region_26.27 | all-reduce | flops 2304 | bytes 18432 | tf_op jit(solution)/shard_map/psum | solution.py:718
  927.0 4.2 convolution_convert_fusion.6
  931.2 5.5 copy.275
  936.7 4.4 all-to-all-start.3
  941.4 4.6 reshape.540
  946.0 4.3 bitcast_multiply_fusion
  961.0 11.0 copy.280
  972.0 59.0 %all-to-all-done.3 = bf16[1536,3,1,192]{3,1,2,0:T(4,128)(2,1)} async-done(((bf16[1536,3,1,192]{3,1,2,0:T(4,128)(2,1)}), bf16[1536,3,1,192]{3,1,2,0:T(4,128)(2,1)}, u32[]{:S(2)}, u32[]{:S(2)}) %all-to-all-start.3) | async-done | bytes 1769504 | tf_op jit(solution)/shard_map/all_to_all | solution.py:469
  1031.0 4.6 all-to-all-start.4
  1036.1 4.9 convolution_convert_fusion.7
  1046.8 5.9 reshape.526
  1056.1 5.8 copy.276
  1062.0 4.6 reshape.518
  1066.5 74.0 %all-to-all-done.4 = bf16[4096,2,1,192]{3,1,2,0:T(2,128)(2,1)} async-done(((bf16[4096,2,1,192]{3,1,2,0:T(2,128)(2,1)}), bf16[4096,2,1,192]{3,1,2,0:T(2,128)(2,1)}, u32[]{:S(2)}, u32[]{:S(2)}) %all-to-all-start.4) | async-done | bytes 3145760 | tf_op jit(solution)/shard_map/all_to_all | solution.py:469
  1140.5 10.9 copy.297
  1152.2 5.0 all-gather.2
  1158.2 4.5 fusion.19
  1164.3 36.4 %psum.92 = f32[2,6144]{1,0:T(2,128)S(1)} all-reduce(f32[2,6144]{1,0:T(2,128)S(1)} %pad_maximum_fusion.9), channel_id=1, replica_groups=mesh['items'=4,'rows'=8] {'rows'}, use_global_device_ids=true, to_apply=%region_38.39 | all-reduce | flops 12288 | bytes 98304 | tf_op jit(solution)/shard_map/psum | solution.py:754
  1200.8 6.9 all-gather.3
  1208.6 39.3 %all-reduce = (f32[7,1536]{1,0:T(8,128)}, f32[24]{0:T(128)}, f32[4096]{0:T(1024)}) all-reduce(f32[7,1536]{1,0:T(8,128)S(1)} %stack.34, f32[24]{0:T(128)S(1)} %multiply_dynamic-update-slice_fusion, f32[4096]{0:T(1024)S(1)} %fusion.19), channel_id=1, replica_groups=mesh['items'=4,'rows'=8] {'items','rows'}, use_global_device_ids=true, to_apply=%region_46.47 | all-reduce | flops 14872 | bytes 118976 | tf_op jit(solution)/shard_map/psum | solution.py:782
  1252.1 84.5 %all-reduce.4.cloned.1.call-done = (bf16[512,3072]{0,1:T(8,128)(2,1)}, bf16[192,4608]{1,0:T(8,128)(2,1)}, bf16[192,1536]{1,0:T(8,128)(2,1)}, bf16[192,8192]{1,0:T(8,128)(2,1)}, bf16[512,1536]{1,0:T(8,128)(2,1)}) async-done(((bf16[512,3072]{0,1:T(8,128)(2,1)}, bf16[192,4608]{1,0:T(8,128)(2,1)}, bf16[192,1536]{1,0:T(8,128)(2,1)}, bf16[192,8192]{1,0:T(8,128)(2,1)}, bf16[512,1536]{1,0:T(8,128)(2,1)}), ...) | async-done | bytes 10223632 | tf_op jit(solution)/shard_map/psum | solution.py:786
  1338.8 5.4 copy.286
  (419 shorter events, 147.8 us)
Async XLA Ops:
  7.2 525.6 %copy-start = (bf16[512,1536]{1,0:T(8,128)(2,1)S(1)}, bf16[512,1536]{1,0:T(8,128)(2,1)}, u32[]{:S(2)}) copy-start(bf16[512,1536]{1,0:T(8,128)(2,1)} %param.28) | copy-start | bytes 4718596
  7.2 230.6 %all-gather.18.cloned.1.call-start = ((), (), s32[]{:S(2)}) async-start(), calls=%async_computation.18 | async-start | bytes 2359296 | tf_op jit(solution)/shard_map/all_gather | solution.py:588
  17.0 107.6 %copy-start.69 = (f32[6144]{0:T(1024)S(1)}, f32[6144]{0:T(1024)}, u32[]{:S(2)}) copy-start(f32[6144]{0:T(1024)} %param.32) | copy-start | bytes 73732
  17.0 118.3 %all-to-all-start = ((bf16[192,3,8,192]{0,3,1,2:T(8,128)(2,1)}), bf16[192,3,8,192]{0,3,1,2:T(8,128)(2,1)}, u32[]{:S(2)}, u32[]{:S(2)}) async-start(bf16[192,3,8,192]{0,3,1,2:T(8,128)(2,1)} %copy.239), calls=%async_computation | async-start | bytes 4718592 | tf_op jit(solution)/shard_map/all_to_all | solution.py:461
  24.4 218.1 %all-gather.10.cloned.1.call-start = ((), (), s32[]{:S(2)}) async-start(), calls=%async_computation.10 | async-start | bytes 3538944 | tf_op jit(solution)/shard_map/all_gather | solution.py:448
  24.7 106.8 %copy-start.86 = (f32[2,1024]{1,0:T(2,128)}, f32[2,1024]{1,0:T(2,128)S(1)}, u32[]{:S(2)}) copy-start(f32[2,1024]{1,0:T(2,128)S(1)} %bitcast_convert_fusion) | copy-start | bytes 24580
  24.8 106.7 %copy-start.49 = (f32[1536]{0:T(1024)}, f32[1536]{0:T(1024)S(1)}, u32[]{:S(2)}) copy-start(f32[1536]{0:T(1024)S(1)} %get-tuple-element.138) | copy-start | bytes 18436
  24.8 437.0 %copy-start.51 = (f32[1536]{0:T(1024)}, f32[1536]{0:T(1024)S(1)}, u32[]{:S(2)}) copy-start(f32[1536]{0:T(1024)S(1)} %get-tuple-element.139) | copy-start | bytes 18436
  24.8 438.4 %copy-start.52 = (f32[1536]{0:T(1024)}, f32[1536]{0:T(1024)S(1)}, u32[]{:S(2)}) copy-start(f32[1536]{0:T(1024)S(1)} %get-tuple-element.137) | copy-start | bytes 18436
  24.8 588.3 %copy-start.54 = (f32[1536]{0:T(1024)}, f32[1536]{0:T(1024)S(1)}, u32[]{:S(2)}) copy-start(f32[1536]{0:T(1024)S(1)} %get-tuple-element.140) | copy-start | bytes 18436
  26.6 104.8 %copy-start.87 = (f32[2,64]{1,0:T(2,128)}, f32[2,64]{1,0:T(2,128)S(1)}, u32[]{:S(2)}) copy-start(f32[2,64]{1,0:T(2,128)S(1)} %rsqrt.51) | copy-start | bytes 1540
  125.3 337.8 %copy-start.47 = (f32[2,1536]{1,0:T(2,128)}, f32[2,1536]{1,0:T(2,128)S(1)}, u32[]{:S(2)}) copy-start(f32[2,1536]{1,0:T(2,128)S(1)} %get-tuple-element.131) | copy-start | bytes 36868
  125.3 487.8 %copy-start.46 = (f32[2,1536]{1,0:T(2,128)}, f32[2,1536]{1,0:T(2,128)S(1)}, u32[]{:S(2)}) copy-start(f32[2,1536]{1,0:T(2,128)S(1)} %get-tuple-element.130) | copy-start | bytes 36868
  135.3 86.1 %copy-start.99 = (s32[1,2]{1,0:T(1,128)S(1)}, s32[1,2]{1,0:T(1,128)}, u32[]{:S(2)}) copy-start(s32[1,2]{1,0:T(1,128)} %param.22) | copy-start | bytes 28
  135.3 113.2 %all-to-all-start.1 = ((bf16[512,2,8,192]{0,3,1,2:T(8,128)(2,1)}), bf16[512,2,8,192]{0,3,1,2:T(8,128)(2,1)}, u32[]{:S(2)}, u32[]{:S(2)}) async-start(bf16[512,2,8,192]{0,3,1,2:T(8,128)(2,1)} %copy.243), calls=%async_computation.1 | async-start | bytes 6291456 | tf_op jit(solution)/shard_map/all_to_all | solution.py:461
  139.9 85.5 %copy-start.100 = (f32[24]{0:T(128)S(1)}, f32[24]{0:T(128)}, u32[]{:S(2)}) copy-start(f32[24]{0:T(128)} %param.31) | copy-start | bytes 292
  139.9 87.5 %copy-start.104 = (s32[1,2]{1,0:T(1,128)S(1)}, s32[1,2]{1,0:T(1,128)}, u32[]{:S(2)}) copy-start(s32[1,2]{1,0:T(1,128)} %param.23) | copy-start | bytes 28
  139.9 320.7 %reduce-scatter.5.cloned.1.call-start = ((), (), s32[]{:S(2)}) async-start(), calls=%async_computation.11 | async-start | bytes 3538944 | tf_op jit(solution)/shard_map/reduce_scatter | solution.py:452
  224.0 102.8 %copy-start.30 = (f32[1024,32]{0,1:T(8,128)}, f32[1024,32]{0,1:T(8,128)S(1)}, u32[]{:S(2)}) copy-start(f32[1024,32]{0,1:T(8,128)S(1)} %mul.769) | copy-start | bytes 393220
  225.4 101.4 %copy-start.29 = (f32[1024,32]{0,1:T(8,128)}, f32[1024,32]{0,1:T(8,128)S(1)}, u32[]{:S(2)}) copy-start(f32[1024,32]{0,1:T(8,128)S(1)} %mul.772) | copy-start | bytes 393220
  227.4 97.6 %copy-start.76 = (f32[1,192]{1,0:T(1,128)}, f32[1,192]{1,0:T(1,128)S(1)}, u32[]{:S(2)}) copy-start(f32[1,192]{1,0:T(1,128)S(1)} %get-tuple-element.165) | copy-start | bytes 2308
  257.5 69.6 %copy-start.12 = (f32[256,192]{0,1:T(8,128)}, f32[256,192]{0,1:T(8,128)S(1)}, u32[]{:S(2)}) copy-start(f32[256,192]{0,1:T(8,128)S(1)} %copy.298) | copy-start | bytes 589828
  349.8 114.5 %all-to-all-start.2 = ((bf16[192,2,8,512]{3,1,0,2:T(2,128)(2,1)}), bf16[192,2,8,512]{3,1,0,2:T(2,128)(2,1)}, u32[]{:S(2)}, u32[]{:S(2)}) async-start(bf16[192,2,8,512]{3,1,0,2:T(2,128)(2,1)} %copy.257), calls=%async_computation.3 | async-start | bytes 6291456 | tf_op jit(solution)/shard_map/all_to_all | solution.py:461
  354.3 169.5 %all-gather.12.cloned.1.call-start = ((), (), s32[]{:S(2)}) async-start(), calls=%async_computation.12 | async-start | bytes 3538944 | tf_op jit(solution)/shard_map/all_gather | solution.py:448
  464.1 145.4 %reduce-scatter.7.cloned.1.call-start = ((), (), s32[]{:S(2)}) async-start(), calls=%async_computation.13 | async-start | bytes 3538944 | tf_op jit(solution)/shard_map/reduce_scatter | solution.py:452
  536.3 139.1 %all-gather.14.cloned.1.call-start = ((), (), s32[]{:S(2)}) async-start(), calls=%async_computation.14 | async-start | bytes 3538944 | tf_op jit(solution)/shard_map/all_gather | solution.py:448
  537.0 84.5 %copy-start.80 = (f32[2,64]{1,0:T(2,128)}, f32[2,64]{1,0:T(2,128)S(1)}, u32[]{:S(2)}) copy-start(f32[2,64]{1,0:T(2,128)S(1)} %compare_convert_fusion) | copy-start | bytes 1540
  610.7 10.8 copy-start.81
  615.4 145.0 %reduce-scatter.9.cloned.1.call-start = ((), (), s32[]{:S(2)}) async-start(), calls=%async_computation.15 | async-start | bytes 3538944 | tf_op jit(solution)/shard_map/reduce_scatter | solution.py:452
  687.3 73.1 %copy-start.48 = (f32[2,1536]{1,0:T(2,128)S(1)}, f32[2,1536]{1,0:T(2,128)}, u32[]{:S(2)}) copy-start(f32[2,1536]{1,0:T(2,128)} %copy-done.47) | copy-start | bytes 36868
  687.3 73.1 %copy-start.53 = (f32[1536]{0:T(1024)S(1)}, f32[1536]{0:T(1024)}, u32[]{:S(2)}) copy-start(f32[1536]{0:T(1024)} %copy-done.52) | copy-start | bytes 18436
  687.3 73.1 %copy-start.79 = (f32[2,64]{1,0:T(2,128)S(1)}, f32[2,64]{1,0:T(2,128)}, u32[]{:S(2)}) copy-start(f32[2,64]{1,0:T(2,128)} %copy-done.78) | copy-start | bytes 1540
  687.3 75.1 %copy-start.10 = (f32[1,128,1536]{2,1,0:T(8,128)S(1)}, f32[1,128,1536]{2,1,0:T(8,128)}, u32[]{:S(2)}) copy-start(f32[1,128,1536]{2,1,0:T(8,128)} %param.18) | copy-start | bytes 2359300
  687.3 75.1 %copy-start.11 = (bf16[2,64,1536]{2,1,0:T(8,128)(2,1)S(1)}, bf16[2,64,1536]{2,1,0:T(8,128)(2,1)}, u32[]{:S(2)}) copy-start(bf16[2,64,1536]{2,1,0:T(8,128)(2,1)} %reduce-scatter.5.cloned.1.call-done) | copy-start | bytes 1179652
  687.4 184.4 %all-gather.16.cloned.1.call-start = ((), (), s32[]{:S(2)}) async-start(), calls=%async_computation.16 | async-start | bytes 3538944 | tf_op jit(solution)/shard_map/all_gather | solution.py:448
  765.9 10.3 copy-start.8
  784.9 86.8 %copy-start.35 = (bf16[192,1536]{1,0:T(8,128)(2,1)S(1)}, bf16[192,1536]{1,0:T(8,128)(2,1)}, u32[]{:S(2)}) copy-start(bf16[192,1536]{1,0:T(8,128)(2,1)} %param.25) | copy-start | bytes 1769476
  784.9 86.8 %copy-start.112 = (f32[2,512,3,64]{1,3,2,0:T(8,128)S(1)}, f32[2,512,3,64]{1,3,2,0:T(8,128)}, u32[]{:S(2)}) copy-start(f32[2,512,3,64]{1,3,2,0:T(8,128)} %copy-done.111) | copy-start | bytes 2359300
  784.9 151.8 %all-to-all-start.5 = ((bf16[1536,2,1,512]{3,1,2,0:T(2,128)(2,1)}), bf16[1536,2,1,512]{3,1,2,0:T(2,128)(2,1)}, u32[]{:S(2)}, u32[]{:S(2)}) async-start(bf16[1536,2,1,512]{3,1,2,0:T(2,128)(2,1)} %copy.283), calls=%async_computation.9 | async-start | bytes 6291456 | tf_op jit(solution)/shard_map/all_to_all | solution.py:469
  871.8 10.8 slice-start
  936.7 94.3 %all-to-all-start.3 = ((bf16[1536,3,1,192]{3,1,2,0:T(4,128)(2,1)}), bf16[1536,3,1,192]{3,1,2,0:T(4,128)(2,1)}, u32[]{:S(2)}, u32[]{:S(2)}) async-start(bf16[1536,3,1,192]{3,1,2,0:T(4,128)(2,1)} %copy.275), calls=%async_computation.7 | async-start | bytes 6291456 | tf_op jit(solution)/shard_map/all_to_all | solution.py:469
  941.2 221.5 %reduce-scatter.11.cloned.1.call-start = ((), (), s32[]{:S(2)}) async-start(), calls=%async_computation.17 | async-start | bytes 3538944 | tf_op jit(solution)/shard_map/reduce_scatter | solution.py:452
  972.0 63.7 %copy-start.18 = (bf16[2,512,3,64]{1,3,2,0:T(8,128)(2,1)S(1)}, bf16[2,512,3,64]{1,3,2,0:T(8,128)(2,1)}, u32[]{:S(2)}) copy-start(bf16[2,512,3,64]{1,3,2,0:T(8,128)(2,1)} %copy-done.17) | copy-start | bytes 1179652
  972.0 64.1 %copy-start.33 = (bf16[1024,512]{1,0:T(8,128)(2,1)S(1)}, bf16[1024,512]{1,0:T(8,128)(2,1)}, u32[]{:S(2)}) copy-start(bf16[1024,512]{1,0:T(8,128)(2,1)} %copy-done.32) | copy-start | bytes 3145732
  1031.0 109.5 %all-to-all-start.4 = ((bf16[4096,2,1,192]{3,1,2,0:T(2,128)(2,1)}), bf16[4096,2,1,192]{3,1,2,0:T(2,128)(2,1)}, u32[]{:S(2)}, u32[]{:S(2)}) async-start(bf16[4096,2,1,192]{3,1,2,0:T(2,128)(2,1)} %copy.280), calls=%async_computation.8 | async-start | bytes 8388608 | tf_op jit(solution)/shard_map/all_to_all | solution.py:469
  1035.6 301.0 %all-reduce.4.cloned.1.call-start = ((), (), s32[]{:S(2)}) async-start(), calls=%async_computation.19 | async-start | bytes 20447232 | tf_op jit(solution)/shard_map/psum | solution.py:786
  1162.6 88.3 %copy-start.9 = (f32[2,64,1536]{2,1,0:T(8,128)S(1)}, f32[2,64,1536]{2,1,0:T(8,128)}, u32[]{:S(2)}) copy-start(f32[2,64,1536]{2,1,0:T(8,128)} %copy-done.8) | copy-start | bytes 2359300
  1162.7 88.2 %copy-start.26 = (bf16[2,64,1536]{2,1,0:T(8,128)(2,1)S(1)}, bf16[2,64,1536]{2,1,0:T(8,128)(2,1)}, u32[]{:S(2)}) copy-start(bf16[2,64,1536]{2,1,0:T(8,128)(2,1)} %reduce-scatter.11.cloned.1.call-done) | copy-start | bytes 1179652
  (85 other events, 312.4 us)
Sparse Core Ops, SparseCore 0:
  10.2 87.9 all-gather.17
  126.9 112.9 all-gather.9
  342.7 117.9 reduce-scatter.4
  464.2 59.5 all-gather.11
  536.4 73.0 reduce-scatter.6
  615.5 59.8 all-gather.13
  687.5 72.8 reduce-scatter.8
  767.8 103.8 all-gather.15
  954.6 171.8 reduce-scatter.10
  1151.6 184.9 all-reduce.3

commit v2 on v1

--- a/solution.py
+++ b/solution.py
@@ -1,6 +1,10 @@
+import functools
+
 import jax
 import jax.numpy as jnp
 from jax import lax
+from jax.experimental import pallas as pl
+from jax.experimental.pallas import tpu as pltpu
 from jax.sharding import PartitionSpec as P
 
 COLS = 32
@@ -444,14 +448,385 @@
     return inverse * (scaled_grad - unit * jnp.mean(scaled_grad * unit, axis=-1, keepdims=True))
 
 
-def gather_tokens(block):
-    return lax.all_gather(block, "rows", axis=1, tiled=True)
-
-
-def scatter_tokens(partial):
-    return lax.psum_scatter(
-        partial.astype(jnp.bfloat16), "rows", scatter_dimension=1, tiled=True
-    ).astype(jnp.float32)
+MESH = pl.DeviceIdType.MESH
+DEPTH, BREADTH = 4, 2
+
+
+def row_place():
+    place = lax.axis_index("rows")
+    return place // BREADTH, lax.rem(place, BREADTH)
+
+
+def on_rows(line, side):
+    return {"rows": line * BREADTH + side}
+
+
+def greet(devices):
+    barrier = pltpu.get_barrier_semaphore()
+    for condition, device in devices:
+
+        @pl.when(condition)
+        def _(device=device):
+            pl.semaphore_signal(barrier, inc=1, device_id=device, device_id_type=MESH)
+
+    count = 0
+    for condition, _ in devices:
+        count = count + jnp.where(condition, 1, 0)
+    pl.semaphore_wait(barrier, count)
+
+
+def remote(source, target, send, receive, device):
+    return pltpu.make_async_remote_copy(
+        src_ref=source,
+        dst_ref=target,
+        send_sem=send,
+        recv_sem=receive,
+        device_id=device,
+        device_id_type=MESH,
+    )
+
+
+def shard_of(ref, place, axis):
+    return ref.at[place] if axis == 0 else ref.at[:, place]
+
+
+def gather_kernel(axis, own, whole, local, z_send, z_recv, x_send, x_recv):
+    line, side = row_place()
+    above, below, across = on_rows(line + 1, side), on_rows(line - 1, side), on_rows(line, 1 - side)
+    has_above, has_below = line < DEPTH - 1, line > 0
+    greet([(has_above, above), (has_below, below), (line >= 0, across)])
+
+    def block(at, which):
+        return shard_of(whole, at * BREADTH + which, axis)
+
+    def pass_on(source, at, way, device):
+        return remote(source, block(at, side), z_send.at[way, at], z_recv.at[at], device)
+
+    def cross(source, at):
+        return remote(source, block(at, side), x_send.at[at], x_recv.at[at], across)
+
+    cross(own, line).start()
+
+    @pl.when(has_above)
+    def _():
+        pass_on(own, line, 0, above).start()
+
+    @pl.when(has_below)
+    def _():
+        pass_on(own, line, 1, below).start()
+
+    keep = pltpu.make_async_copy(own, block(line, side), local)
+    keep.start()
+    for step in range(1, DEPTH):
+
+        @pl.when(line - step >= 0)
+        def _(at=line - step):
+            pass_on(own, at, 0, below).wait_recv()
+
+            @pl.when(has_above)
+            def _():
+                pass_on(block(at, side), at, 0, above).start()
+
+            cross(block(at, side), at).start()
+
+        @pl.when(line + step < DEPTH)
+        def _(at=line + step):
+            pass_on(own, at, 1, above).wait_recv()
+
+            @pl.when(has_below)
+            def _():
+                pass_on(block(at, side), at, 1, below).start()
+
+            cross(block(at, side), at).start()
+
+    keep.wait()
+    for at in range(DEPTH):
+        cross(own, at).wait_recv()
+        cross(own, at).wait_send()
+
+        @pl.when(has_above & (at <= line))
+        def _(at=at):
+            pass_on(own, at, 0, above).wait_send()
+
+        @pl.when(has_below & (at >= line))
+        def _(at=at):
+            pass_on(own, at, 1, below).wait_send()
+
+
+def gather_rows(block, ident, axis):
+    ranks = DEPTH * BREADTH
+    shape = block.shape[:axis] + (ranks,) + block.shape[axis:]
+    anywhere = pl.BlockSpec(memory_space=pl.ANY)
+    return pl.pallas_call(
+        functools.partial(gather_kernel, axis),
+        out_shape=jax.ShapeDtypeStruct(shape, block.dtype),
+        in_specs=[anywhere],
+        out_specs=anywhere,
+        scratch_shapes=[
+            pltpu.SemaphoreType.DMA,
+            pltpu.SemaphoreType.DMA((2, DEPTH)),
+            pltpu.SemaphoreType.DMA((DEPTH,)),
+            pltpu.SemaphoreType.DMA((DEPTH,)),
+            pltpu.SemaphoreType.DMA((DEPTH,)),
+        ],
+        name=f"gather_rows_{ident}",
+        compiler_params=pltpu.CompilerParams(collective_id=ident, has_side_effects=True),
+    )(block)
+
+
+def scatter_kernel(axis, parts, total, crossed, risen, sunk, up, down, x_send, x_recv, z_send, z_recv):
+    line, side = row_place()
+    above, below, across = on_rows(line + 1, side), on_rows(line - 1, side), on_rows(line, 1 - side)
+    has_above, has_below = line < DEPTH - 1, line > 0
+    greet([(has_above, above), (has_below, below), (line >= 0, across)])
+
+    def part(at, which):
+        return shard_of(parts, at * BREADTH + which, axis)
+
+    def cross(at):
+        return remote(part(at, 1 - side), crossed.at[at], x_send.at[at], x_recv.at[at], across)
+
+    def rise(at):
+        return remote(up.at[at], risen.at[at], z_send.at[0, at], z_recv.at[0, at], above)
+
+    def sink(at):
+        return remote(down.at[at], sunk.at[at], z_send.at[1, at], z_recv.at[1, at], below)
+
+    def add_up(at, others, target):
+        mine = part(at, side)
+        whole = mine.shape
+        value = mine[...].astype(jnp.float32) + crossed[at].astype(jnp.float32)
+        for other in others:
+            value = value + other[at].astype(jnp.float32)
+        target[...] = value.astype(target.dtype)
+
+    for step in range(DEPTH - 1, 0, -1):
+        for at, there in ((line + step, line + step < DEPTH), (line - step, line - step >= 0)):
+
+            @pl.when(there)
+            def _(at=at):
+                cross(at).start()
+
+    cross(line).start()
+    for step in range(DEPTH - 1, 0, -1):
+
+        @pl.when(line + step < DEPTH)
+        def _(at=line + step):
+            cross(at).wait_recv()
+
+            @pl.when(has_below)
+            def _():
+                rise(at).wait_recv()
+                add_up(at, [risen], up.at[at])
+
+            @pl.when(jnp.logical_not(has_below))
+            def _():
+                add_up(at, [], up.at[at])
+
+            rise(at).start()
+
+        @pl.when(line - step >= 0)
+        def _(at=line - step):
+            cross(at).wait_recv()
+
+            @pl.when(has_above)
+            def _():
+                sink(at).wait_recv()
+                add_up(at, [sunk], down.at[at])
+
+            @pl.when(jnp.logical_not(has_above))
+            def _():
+                add_up(at, [], down.at[at])
+
+            sink(at).start()
+
+    cross(line).wait_recv()
+
+    @pl.when(has_below & has_above)
+    def _():
+        rise(line).wait_recv()
+        sink(line).wait_recv()
+        add_up(line, [risen, sunk], total)
+
+    @pl.when(jnp.logical_not(has_above))
+    def _():
+        rise(line).wait_recv()
+        add_up(line, [risen], total)
+
+    @pl.when(jnp.logical_not(has_below))
+    def _():
+        sink(line).wait_recv()
+        add_up(line, [sunk], total)
+
+    for at in range(DEPTH):
+        cross(at).wait_send()
+
+        @pl.when(at > line)
+        def _(at=at):
+            rise(at).wait_send()
+
+        @pl.when(at < line)
+        def _(at=at):
+            sink(at).wait_send()
+
+
+def scatter_rows(parts, ident, axis):
+    shape = parts.shape[:axis] + parts.shape[axis + 1 :]
+    near = pl.BlockSpec(memory_space=pltpu.VMEM)
+    slots = pltpu.VMEM((DEPTH,) + shape, parts.dtype)
+    return pl.pallas_call(
+        functools.partial(scatter_kernel, axis),
+        out_shape=jax.ShapeDtypeStruct(shape, jnp.float32),
+        in_specs=[near],
+        out_specs=near,
+        scratch_shapes=[slots] * 5
+        + [
+            pltpu.SemaphoreType.DMA((DEPTH,)),
+            pltpu.SemaphoreType.DMA((DEPTH,)),
+            pltpu.SemaphoreType.DMA((2, DEPTH)),
+            pltpu.SemaphoreType.DMA((2, DEPTH)),
+        ],
+        name=f"scatter_rows_{ident}",
+        compiler_params=pltpu.CompilerParams(
+            collective_id=ident, has_side_effects=True, vmem_limit_bytes=32 << 20
+        ),
+    )(parts)
+
+
+def sum_kernel(own, total, held, send, receive):
+    ranks = DEPTH * BREADTH
+    place = lax.axis_index("rows")
+    others = [lax.rem(place + step, ranks) for step in range(1, ranks)]
+    greet([(place >= 0, {"rows": other}) for other in others])
+
+    def push(step, other, slot):
+        return remote(own, held.at[slot], send.at[step], receive.at[slot], {"rows": other})
+
+    for step, other in enumerate(others):
+        push(step, other, place).start()
+    held[pl.ds(place, 1)] = own[...][None]
+    for step, other in enumerate(others):
+        push(step, other, other).wait_recv()
+    value = held[0]
+    for rank in range(1, ranks):
+        value = value + held[rank]
+    total[...] = value
+    for step, other in enumerate(others):
+        push(step, other, place).wait_send()
+
+
+def sum_rows(own, ident):
+    ranks = DEPTH * BREADTH
+    near = pl.BlockSpec(memory_space=pltpu.VMEM)
+    return pl.pallas_call(
+        sum_kernel,
+        out_shape=jax.ShapeDtypeStruct(own.shape, own.dtype),
+        in_specs=[near],
+        out_specs=near,
+        scratch_shapes=[
+            pltpu.VMEM((ranks,) + own.shape, own.dtype),
+            pltpu.SemaphoreType.DMA((ranks,)),
+            pltpu.SemaphoreType.DMA((ranks,)),
+        ],
+        name=f"sum_rows_{ident}",
+        compiler_params=pltpu.CompilerParams(collective_id=ident, has_side_effects=True),
+    )(own)
+
+
+def final_kernel(ranks, groups, sums, own, out, held, kept, part, h_send, h_recv, g_send, g_recv, o_send, o_recv):
+    place, group = lax.axis_index("rows"), lax.axis_index("items")
+    rows = [lax.rem(place + step, ranks) for step in range(1, ranks)]
+    items = [lax.rem(group + step, groups) for step in range(1, groups)]
+    greet([(place >= 0, {"rows": other}) for other in rows] + [(place >= 0, {"items": other}) for other in items])
+
+    def push(step, other, slot):
+        return remote(own.at[other], held.at[slot], h_send.at[step], h_recv.at[slot], {"rows": other})
+
+    def swap(step, other, slot):
+        return remote(part, kept.at[slot], g_send.at[step], g_recv.at[slot], {"items": other})
+
+    def share(step, other, slot):
+        return remote(out.at[place], out.at[slot], o_send.at[step], o_recv.at[slot], {"rows": other})
+
+    for step, other in enumerate(rows):
+        push(step, other, place).start()
+    held[pl.ds(place, 1)] = own[pl.ds(place, 1)]
+    for step, other in enumerate(rows):
+        push(step, other, other).wait_recv()
+    value = held[0]
+    for rank in range(1, ranks):
+        value = value + held[rank]
+    part[...] = value
+    for step, other in enumerate(items):
+        swap(step, other, group).start()
+    kept[pl.ds(group, 1)] = value[None]
+    for step, other in enumerate(items):
+        swap(step, other, other).wait_recv()
+    total = kept[0, :sums]
+    for item in range(1, groups):
+        total = total + kept[item, :sums]
+    depth = own.shape[1] - sums
+    out[pl.ds(place, 1), :sums] = total[None]
+    for item in range(groups):
+        out[pl.ds(place, 1), sums + item * depth : sums + (item + 1) * depth] = kept[item, sums:][None]
+    for step, other in enumerate(rows):
+        share(step, other, place).start()
+    for step, other in enumerate(rows):
+        share(step, other, other).wait_recv()
+    for step, other in enumerate(rows):
+        push(step, other, place).wait_send()
+        share(step, other, place).wait_send()
+    for step, other in enumerate(items):
+        swap(step, other, group).wait_send()
+
+
+def final_sums(own, sums, ident):
+    ranks, groups = lax.axis_size("rows"), lax.axis_size("items")
+    near = pl.BlockSpec(memory_space=pltpu.VMEM)
+    depth = own.shape[1]
+    return pl.pallas_call(
+        functools.partial(final_kernel, ranks, groups, sums),
+        out_shape=jax.ShapeDtypeStruct((ranks, sums + groups * (depth - sums), 128), own.dtype),
+        in_specs=[near],
+        out_specs=near,
+        scratch_shapes=[
+            pltpu.VMEM(own.shape, own.dtype),
+            pltpu.VMEM((groups,) + own.shape[1:], own.dtype),
+            pltpu.VMEM(own.shape[1:], own.dtype),
+            pltpu.SemaphoreType.DMA((ranks,)),
+            pltpu.SemaphoreType.DMA((ranks,)),
+            pltpu.SemaphoreType.DMA((groups,)),
+            pltpu.SemaphoreType.DMA((groups,)),
+            pltpu.SemaphoreType.DMA((ranks,)),
+            pltpu.SemaphoreType.DMA((ranks,)),
+        ],
+        name=f"final_sums_{ident}",
+        compiler_params=pltpu.CompilerParams(collective_id=ident, has_side_effects=True),
+    )(own)
+
+
+def gather_tokens(block, ident):
+    whole = gather_rows(block, ident, 1)
+    return whole.reshape(-1, block.shape[-1])
+
+
+def scatter_tokens(partial, items, ident):
+    ranks = lax.axis_size("rows")
+    blocks = partial.astype(jnp.bfloat16).reshape(items, ranks, -1, partial.shape[-1])
+    return scatter_rows(blocks, ident, 1)
+
+
+def sum_vectors(vectors, ident):
+    sizes = [vector.size for vector in vectors]
+    flat = jnp.concatenate([vector.reshape(-1) for vector in vectors])
+    rows = -(-flat.size // 1024) * 8
+    flat = jnp.pad(flat, (0, rows * 128 - flat.size))
+    total = sum_rows(flat.reshape(rows, 128), ident).reshape(-1)
+    parts, start = [], 0
+    for vector, size in zip(vectors, sizes):
+        parts.append(total[start : start + size].reshape(vector.shape))
+        start += size
+    return parts
 
 
 def columns_here(weight, pieces):
@@ -520,14 +895,31 @@
     time_silu = jax.nn.silu(time_embed[0].astype(single)).astype(narrow)
     ada_depth = w_ada.shape[0]
     time_here = lax.dynamic_slice_in_dim(time_silu, place * ada_depth, ada_depth, 1)
-    modulation = lax.psum(dot(time_here, w_ada), "rows") + ada_bias
+
+    def spread(part, whole):
+        return lax.dynamic_update_slice_in_dim(
+            jnp.zeros((whole,), single), part.reshape(-1), place * part.size, 0
+        )
+
+    counts_here = live_rows[0]
+    text_float = text_states[0].astype(single).reshape(items * text_local, text_width)
+    text_inverse = norm_parts(text_float)[1]
+    modulation, counts, text_inverse = sum_vectors(
+        [
+            dot(time_here, w_ada),
+            spread(counts_here.astype(single), ranks * items),
+            spread(text_inverse, ranks * items * text_local),
+        ],
+        0,
+    )
+    modulation = modulation + ada_bias
+    counts = counts.astype(jnp.int32).reshape(ranks, items)
+    text_inverse = text_inverse.reshape(-1, 1)
     scale_attn = modulation[:, None, 0:width]
     gate_attn = jnp.tanh(modulation[:, None, width : 2 * width])
     scale_ffn = modulation[:, None, 2 * width : 3 * width]
     gate_ffn = jnp.tanh(modulation[:, None, 3 * width :])
 
-    counts_here = live_rows[0]
-    counts = lax.all_gather(counts_here, "rows", axis=0, tiled=True)
     below = jnp.cumsum(counts, axis=0) - counts
     slot_row = jnp.arange(row_slots)
     row_index = jnp.transpose(below)[:, :, None] + slot_row
@@ -580,29 +972,40 @@
     states = hidden_in[0].reshape(items, slots, width)
     unit_in, inverse_in = norm_parts(states)
     norm_in = unit_in * gains[0]
-    attn_in = gather_tokens((norm_in * (1.0 + scale_attn)).astype(narrow)).reshape(tokens, width)
+    attn_in = gather_tokens((norm_in * (1.0 + scale_attn)).astype(narrow), 1)
     qkv_here = columns_here(w_qkv, 3)
     qkv_proj = dot(attn_in, qkv_here)
     query_proj, key_proj, value_proj = jnp.split(qkv_proj, 3, axis=1)
 
-    text_in = lax.all_gather(text_states[0], "rows", axis=1, tiled=True)
-    text_unit, _ = norm_parts(text_in.astype(single).reshape(items * text_all, text_width))
-    text_norm = (text_unit * text_gain).astype(narrow)
-    text_here = columns_here(w_text, 2)
-    text_proj = dot(text_norm, text_here)
-    tkey_proj, tval_proj = jnp.split(text_proj, 2, axis=1)
+    features = text_width // ranks
+    text_in = lax.all_to_all(
+        text_states[0].reshape(items * text_local, ranks, features),
+        "rows",
+        split_axis=1,
+        concat_axis=0,
+        tiled=True,
+    ).reshape(items * text_all, features)
+    text_unit = text_in.astype(single) * text_inverse
+    gain_text = lax.dynamic_slice_in_dim(text_gain, place * features, features, 0)
+    text_norm = (text_unit * gain_text).astype(narrow)
+
+    def by_rank(values):
+        pieces = values.reshape(-1, 2, ranks, span)
+        return jnp.transpose(pieces, (2, 0, 1, 3)).reshape(ranks, -1, 2 * span)
+
+    def text_rows(values):
+        shaped = values.reshape(ranks, items, text_local, -1)
+        return jnp.swapaxes(shaped, 0, 1).reshape(items * text_all, -1)
+
+    text_proj = scatter_rows(by_rank(dot(text_norm, w_text).astype(narrow)), 2, 0)
+    tkey_proj, tval_proj = jnp.split(text_rows(text_proj), 2, axis=1)
 
     def squares(values):
         return jnp.sum(values * values, axis=-1)
 
-    totals = lax.psum(
-        jnp.concatenate([squares(query_proj), squares(key_proj), squares(tkey_proj)]), "rows"
-    )
-    inverses = lax.rsqrt(totals / width + epsilon)[:, None]
+    totals = sum_vectors([squares(query_proj), squares(key_proj), squares(tkey_proj)], 3)
     inverse_q, inverse_k, inverse_t = (
-        inverses[:tokens],
-        inverses[tokens : 2 * tokens],
-        inverses[2 * tokens :],
+        lax.rsqrt(total / width + epsilon)[:, None] for total in totals
     )
     gain_q, gain_k, gain_t = gain_here(1), gain_here(2), gain_here(6)
     unit_q, unit_k, unit_t = query_proj * inverse_q, key_proj * inverse_k, tkey_proj * inverse_t
@@ -631,20 +1034,20 @@
     cross_out = mix(cross_probs.astype(narrow), tval)
     gate_here = jnp.tanh(lax.dynamic_slice_in_dim(cross_gate, place * heads_here, heads_here, 0))
     combined = (self_out + gate_here[:, None] * cross_out).astype(narrow).reshape(tokens, span)
-    projected = scatter_tokens(dot(combined, w_out).reshape(items, seq_len, width))
+    projected = scatter_tokens(dot(combined, w_out), items, 4)
 
     unit_proj, inverse_proj = norm_parts(projected)
     norm_proj = unit_proj * gains[3]
     middle = states + gate_attn * norm_proj
     unit_mid, inverse_mid = norm_parts(middle)
     norm_mid = unit_mid * gains[4]
-    ffn_in = gather_tokens((norm_mid * (1.0 + scale_ffn)).astype(narrow)).reshape(tokens, width)
+    ffn_in = gather_tokens((norm_mid * (1.0 + scale_ffn)).astype(narrow), 5)
     gu_here = columns_here(w_gu, 2)
     gate_up = dot(ffn_in, gu_here)
     gate_part, up_part = jnp.split(gate_up, 2, axis=1)
     sigmoid = 1.0 / (1.0 + jnp.exp(-gate_part))
     inner_act = (gate_part * sigmoid * up_part).astype(narrow)
-    ffn_out = scatter_tokens(dot(inner_act, w_down).reshape(items, seq_len, width))
+    ffn_out = scatter_tokens(dot(inner_act, w_down), items, 6)
     unit_ffn, inverse_ffn = norm_parts(ffn_out)
     norm_ffn = unit_ffn * gains[5]
     output = live_mask * (middle + gate_ffn * norm_ffn)
@@ -657,8 +1060,8 @@
     grad_norm = gate_ffn * grad_result
     grad_five = over_tokens(grad_norm * unit_ffn)
     ffn_low = gather_tokens(
-        norm_back(unit_ffn, inverse_ffn, grad_norm * gains[5]).astype(narrow)
-    ).reshape(tokens, width)
+        norm_back(unit_ffn, inverse_ffn, grad_norm * gains[5]).astype(narrow), 7
+    )
     grad_down = weight_grad(inner_act, ffn_low)
     grad_inner = dot_back(ffn_low, w_down)
     gate_up_low = jnp.concatenate(
@@ -669,9 +1072,7 @@
         axis=1,
     ).astype(narrow)
     grad_gu = weight_grad(ffn_in, gate_up_low)
-    grad_ffn_in = scatter_tokens(
-        dot_back(gate_up_low, gu_here).reshape(items, seq_len, width)
-    )
+    grad_ffn_in = scatter_tokens(dot_back(gate_up_low, gu_here), items, 8)
     grad_scale_ffn = jnp.sum(grad_ffn_in * norm_mid, axis=1)
     grad_norm = grad_ffn_in * (1.0 + scale_ffn)
     grad_four = over_tokens(grad_norm * unit_mid)
@@ -681,8 +1082,8 @@
     grad_norm = gate_attn * grad_middle
     grad_three = over_tokens(grad_norm * unit_proj)
     projected_low = gather_tokens(
-        norm_back(unit_proj, inverse_proj, grad_norm * gains[3]).astype(narrow)
-    ).reshape(tokens, width)
+        norm_back(unit_proj, inverse_proj, grad_norm * gains[3]).astype(narrow), 9
+    )
     grad_out = weight_grad(combined, projected_low)
     grad_combined = by_head(dot_back(projected_low, w_out))
     self_low = grad_combined.astype(narrow)
@@ -714,60 +1115,42 @@
     grad_query = turn(grad_query, -1.0)
     grad_key = turn(grad_key, -1.0)
     scaled_q, scaled_k, scaled_t = grad_query * gain_q, grad_key * gain_k, grad_tkey * gain_t
-    means = (
-        lax.psum(
-            jnp.concatenate(
-                [
-                    jnp.sum(scaled_q * unit_q, axis=-1),
-                    jnp.sum(scaled_k * unit_k, axis=-1),
-                    jnp.sum(scaled_t * unit_t, axis=-1),
-                ]
-            ),
-            "rows",
-        )[:, None]
-        / width
+    mean_q, mean_k, mean_t = (
+        total[:, None] / width
+        for total in sum_vectors(
+            [
+                jnp.sum(scaled_q * unit_q, axis=-1),
+                jnp.sum(scaled_k * unit_k, axis=-1),
+                jnp.sum(scaled_t * unit_t, axis=-1),
+            ],
+            10,
+        )
     )
     qkv_low = jnp.concatenate(
         [
-            inverse_q * (scaled_q - unit_q * means[:tokens]),
-            inverse_k * (scaled_k - unit_k * means[tokens : 2 * tokens]),
+            inverse_q * (scaled_q - unit_q * mean_q),
+            inverse_k * (scaled_k - unit_k * mean_k),
             grad_value,
         ],
         axis=1,
     ).astype(narrow)
     text_low = jnp.concatenate(
-        [inverse_t * (scaled_t - unit_t * means[2 * tokens :]), grad_tval], axis=1
+        [inverse_t * (scaled_t - unit_t * mean_t), grad_tval], axis=1
     ).astype(narrow)
     grad_qkv = weight_grad(attn_in, qkv_low)
-    grad_attn_in = scatter_tokens(dot_back(qkv_low, qkv_here).reshape(items, seq_len, width))
+    grad_attn_in = scatter_tokens(dot_back(qkv_low, qkv_here), items, 11)
     grad_scale_attn = jnp.sum(grad_attn_in * norm_in, axis=1)
     grad_norm = grad_attn_in * (1.0 + scale_attn)
     grad_zero = over_tokens(grad_norm * unit_in)
     grad_x = grad_middle + norm_back(unit_in, inverse_in, grad_norm * gains[0])
 
-    grad_text = weight_grad(text_norm, text_low)
-    grad_text_gain = jnp.sum(dot_back(text_low, text_here) * text_unit, axis=0)
-    grad_modulation = jnp.concatenate(
-        [grad_scale_attn, grad_gate_attn, grad_scale_ffn, grad_gate_ffn], axis=-1
-    )
-    all_modulation = lax.all_gather(
-        lax.psum(grad_modulation, "rows"), "items", axis=0, tiled=True
-    )
-    all_time = lax.all_gather(time_here, "items", axis=0, tiled=True)
-    final_ada = jnp.einsum(
-        "tk,tn->kn",
-        all_time.astype(single),
-        all_modulation,
-        precision=lax.Precision.HIGHEST,
-        preferred_element_type=single,
-    )
-    total_bias = jnp.sum(all_modulation, axis=0)
-
-    def spread(part, whole):
-        return lax.dynamic_update_slice_in_dim(
-            jnp.zeros((whole,), single), part, place * part.shape[0], 0
-        )
-
+    text_low = text_low.reshape(items, ranks, text_local, 2 * span)
+    text_low = jnp.swapaxes(text_low, 0, 1).reshape(items * text_all, 2 * span)
+    all_low = gather_rows(text_low, 12, 0).reshape(ranks, -1, 2, span)
+    all_low = jnp.transpose(all_low, (1, 2, 0, 3)).reshape(items * text_all, 2 * width)
+    grad_text = weight_grad(text_norm, all_low)
+    grad_text_gain = jnp.sum(dot_back(all_low, w_text) * text_unit, axis=0)
+    grad_modulation = jnp.stack([grad_scale_attn, grad_gate_attn, grad_scale_ffn, grad_gate_ffn], 1)
     grad_gains = jnp.stack(
         [
             grad_zero,
@@ -779,15 +1162,45 @@
             spread(jnp.sum(grad_tkey * unit_t, axis=0), width),
         ]
     )
-    total_gains, total_gate, total_text_gain = lax.psum(
-        (grad_gains, spread(grad_gate, heads), grad_text_gain), ("items", "rows")
-    )
+    flat = jnp.concatenate(
+        [
+            grad_gains.reshape(-1),
+            spread(grad_text_gain, text_width),
+            spread(grad_gate, heads),
+        ]
+    )
+    lanes = ranks * 128
+    sum_depth = -(-flat.size // lanes)
+    flat = jnp.pad(flat, (0, sum_depth * lanes - flat.size)).reshape(ranks, sum_depth, 128)
+    keep_depth = grad_modulation.size // lanes
+    reduced = final_sums(
+        jnp.concatenate([flat, grad_modulation.reshape(ranks, keep_depth, 128)], axis=1),
+        sum_depth,
+        13,
+    )
+    flat = reduced[:, :sum_depth].reshape(-1)
+    total_gains = flat[: gains.size].reshape(gains.shape)
+    total_text_gain = flat[gains.size : gains.size + text_width]
+    total_gate = flat[gains.size + text_width : gains.size + text_width + heads]
+    groups = lax.axis_size("items")
+    all_modulation = jnp.swapaxes(
+        reduced[:, sum_depth:].reshape(ranks, groups, keep_depth * 128), 0, 1
+    ).reshape(groups * items, 4 * width)
+    all_time = lax.all_gather(time_here, "items", axis=0, tiled=True)
+    final_ada = jnp.einsum(
+        "tk,tn->kn",
+        all_time.astype(single),
+        all_modulation,
+        precision=lax.Precision.HIGHEST,
+        preferred_element_type=single,
+    )
+    total_bias = jnp.sum(all_modulation, axis=0)
     sums = [
         lax.psum(part.astype(narrow), "items").astype(single)
         for part in (
             rows_here(grad_qkv, 3),
             grad_out,
-            rows_here(grad_text, 2),
+            grad_text,
             rows_here(grad_gu, 2),
             grad_down,
         )

time: 1370 us -> 1010 us (0.74)
  waiting for transfers between devices: 661 us -> 135 us
  Pallas kernels: 0 us -> 501 us
  blocking collectives: 365 us -> 5.74 us
  other arithmetic: 55.5 us -> 70 us
    pallas_call x0 -> x14, Pallas kernels: none -> 501 us  [the longest x5 231 us: gather_rows(): pl.pallas_call(functools.partial(gather_kernel, axis), out_shape=jax.Shap...]
    psum x5 -> x0, blocking collectives: 272 us -> none  [the longest x1 98 us: head_parallel_plan(): modulation = lax.psum(dot(time_here, w_ada), 'rows') + ada_bias]
    reduce_scatter x4 -> x0, waiting for transfers between devices: 252 us -> none  [scatter_tokens(): lax.psum_scatter(partial.astype(jnp.bfloat16), 'rows', scatter_dimension=...]
    all_gather x5 -> x0, waiting for transfers between devices: 191 us -> none  [the longest x4 191 us: gather_tokens(): return lax.all_gather(block, 'rows', axis=1, tiled=True)]
    all_gather x2 -> x0, blocking collectives: 87.6 us -> none  [the longest x1 80.7 us: head_parallel_plan(): counts = lax.all_gather(counts_here, 'rows', axis=0, tiled=True)]
    all_to_all x3 -> x2, waiting for transfers between devices: 133 us -> 46.9 us  [rows_here(): moved = lax.all_to_all(low, 'rows', split_axis=0, concat_axis=2, tiled=True)]
    unnamed x242 -> x251, local copies, waits for them, and re-layouts: 34.5 us -> 23.9 us
  transfers between devices with their start and end apart: 16 -> 6, of which waited for: 9 -> 2; matrix products, arithmetic and copies ran while one was open for 15% -> 21% of each run, Pallas kernels for 0% -> 34%
where the time goes in v2:
time: 1010 us; the launch traced here: 1000 us
  Pallas kernels  501 us (50%)
  local copies, waits for them, and re-layouts  153 us (15%)
  waiting for transfers between devices  135 us (13%)
  matrix products  91.3 us (9%)
  other arithmetic  70 us (7%)
  starting transfers between devices  29.8 us (3%)
  between operations  16.1 us (2%)
    pallas_call x5, Pallas kernels, gather_rows(): pl.pallas_call(functools.partial(gather_kernel, axis), out_shape=jax.Shap...  231 us
    pallas_call x5, Pallas kernels, scatter_rows(): pl.pallas_call(functools.partial(scatter_kernel, axis), out_shape=jax.Sha...  177 us
    psum x1, waiting for transfers between devices, head_parallel_plan(): lax.psum(part.astype(narrow), 'items').astype(single)  87.8 us
    pallas_call x3, Pallas kernels, sum_rows(): pl.pallas_call(sum_kernel, out_shape=jax.ShapeDtypeStruct(own.shape, own....  75.5 us
    all_to_all x2, waiting for transfers between devices, rows_here(): moved = lax.all_to_all(low, 'rows', split_axis=0, concat_axis=2, tiled=True)  46.9 us
    unnamed x251, local copies, waits for them, and re-layouts  23.9 us
    dot_general x5, matrix products, dot_back(): return jnp.einsum('tn,kn->tk', left, weight, preferred_element_type=single)  21 us
  transfers between devices with their start and end apart: 6, of which 2 were waited for; matrix products, arithmetic and copies ran while one was open for 21% of the time, Pallas kernels for 34%

profile of v2, /device:TPU:0, one launch (start us, length us, event | category | flops | bytes accessed | tf_op | source)
XLA Modules:
  0.0 1001.4 jit_solution(8426595416426711529)
XLA Ops:
  9.2 7.3 all-to-all-start.1
  25.2 12.6 %sum_rows_0.1 = f32[104,128]{1,0:T(8,128)} custom-call(f32[104,128]{1,0:T(8,128)} %pad_bitcast_fusion.own), custom_call_target="tpu_custom_call" | custom-call | tf_op jit(solution)/shard_map/sum_rows_0/pallas_call | solution.py:721
  37.8 5.3 slice.120
  55.6 4.5 reshape.618
  60.0 4.6 copy.192
  64.7 42.3 %gather_rows_1.1 = bf16[2,8,64,1536]{3,2,1,0:T(8,128)(2,1)} custom-call(bf16[2,64,1536]{2,1,0:T(8,128)(2,1)} %multiply_convert_fusion.11.own), custom_call_target="tpu_custom_call" | custom-call | tf_op jit(solution)/shard_map/gather_rows_1/pallas_call | solution.py:560
  110.2 4.1 copy.214
  115.6 4.9 all-to-all-start
  153.1 28.1 %scatter_rows_2.1 = f32[256,384]{1,0:T(8,128)S(1)} custom-call(bf16[8,256,384]{2,1,0:T(8,128)(2,1)S(1)} %copy-done.5), custom_call_target="tpu_custom_call" | custom-call | tf_op jit(solution)/shard_map/scatter_rows_2/pallas_call | solution.py:677
  185.9 8.3 all-to-all-start.2
  194.2 4.4 copy.193
  198.6 4.7 reshape.619
  203.3 4.5 fusion.120
  210.0 54.5 %sum_rows_3.1 = f32[24,128]{1,0:T(8,128)} custom-call(f32[24,128]{1,0:T(8,128)} %fusion.90.own), custom_call_target="tpu_custom_call" | custom-call | tf_op jit(solution)/shard_map/sum_rows_3/pallas_call | solution.py:721
  276.0 3.5 fusion.106
  282.1 6.9 fusion.111
  289.0 3.9 fusion.21
  294.5 36.5 %scatter_rows_4.1 = f32[2,64,1536]{2,1,0:T(8,128)S(1)} custom-call(bf16[2,8,64,1536]{3,2,1,0:T(8,128)(2,1)S(1)} %bitcast.269), custom_call_target="tpu_custom_call" | custom-call | tf_op jit(solution)/shard_map/scatter_rows_4/pallas_call | solution.py:677
  334.0 36.6 %gather_rows_5.1 = bf16[2,8,64,1536]{3,2,1,0:T(8,128)(2,1)} custom-call(bf16[2,64,1536]{2,1,0:T(8,128)(2,1)} %multiply_convert_fusion.10.own), custom_call_target="tpu_custom_call" | custom-call | tf_op jit(solution)/shard_map/gather_rows_5/pallas_call | solution.py:560
  373.6 3.6 fusion.121
  382.7 37.8 %scatter_rows_6.1 = f32[2,64,1536]{2,1,0:T(8,128)S(1)} custom-call(bf16[2,8,64,1536]{3,2,1,0:T(8,128)(2,1)S(1)} %bitcast.272), custom_call_target="tpu_custom_call" | custom-call | tf_op jit(solution)/shard_map/scatter_rows_6/pallas_call | solution.py:677
  423.1 39.9 %gather_rows_7.1 = bf16[2,8,64,1536]{3,2,1,0:T(8,128)(2,1)} custom-call(bf16[2,64,1536]{2,1,0:T(8,128)(2,1)} %get-tuple-element.62.own), custom_call_target="tpu_custom_call" | custom-call | tf_op jit(solution)/shard_map/gather_rows_7/pallas_call | solution.py:560
  463.0 6.1 multiply_convert_fusion.2
  469.1 3.7 convolution_convert_fusion.6
  473.0 35.4 %scatter_rows_8.1 = f32[2,64,1536]{2,1,0:T(8,128)S(1)} custom-call(bf16[2,8,64,1536]{3,2,1,0:T(8,128)(2,1)S(1)} %bitcast.271), custom_call_target="tpu_custom_call" | custom-call | tf_op jit(solution)/shard_map/scatter_rows_8/pallas_call | solution.py:677
  512.5 33.9 %gather_rows_9.1 = bf16[2,8,64,1536]{3,2,1,0:T(8,128)(2,1)} custom-call(bf16[2,64,1536]{2,1,0:T(8,128)(2,1)} %multiply_convert_fusion.8.own), custom_call_target="tpu_custom_call" | custom-call | tf_op jit(solution)/shard_map/gather_rows_9/pallas_call | solution.py:560
  546.5 4.2 multiply_reduce_fusion.6
  550.7 4.9 fusion.27
  577.9 8.4 sum_rows_10.1
  592.8 5.5 copy.231
  598.3 4.8 all-to-all-start.3
  603.1 7.6 convolution_convert_fusion.5
  610.7 8.6 copy.238
  619.4 46.9 %all-to-all-done.3 = bf16[1536,3,1,192]{3,1,2,0:T(4,128)(2,1)} async-done(((bf16[1536,3,1,192]{3,1,2,0:T(4,128)(2,1)}), bf16[1536,3,1,192]{3,1,2,0:T(4,128)(2,1)}, u32[]{:S(2)}, u32[]{:S(2)}) %all-to-all-start.3) | async-done | bytes 1769504 | tf_op jit(solution)/shard_map/all_to_all | solution.py:844
  666.3 4.5 all-to-all-start.4
  683.1 78.2 %gather_rows_12.1 = bf16[8,256,384]{2,1,0:T(8,128)(2,1)} custom-call(bf16[256,384]{1,0:T(8,128)(2,1)} %bitcast.328), custom_call_target="tpu_custom_call" | custom-call | tf_op jit(solution)/shard_map/gather_rows_12/pallas_call | solution.py:560
  773.6 5.8 copy.232
  779.5 4.6 reshape.648
  789.9 5.9 reshape.654
  796.5 5.7 all-gather
  809.4 4.4 convolution_convert_fusion.2
  813.9 39.1 %scatter_rows_11.1 = f32[2,64,1536]{2,1,0:T(8,128)S(1)} custom-call(bf16[2,8,64,1536]{3,2,1,0:T(8,128)(2,1)S(1)} %bitcast.270), custom_call_target="tpu_custom_call" | custom-call | tf_op jit(solution)/shard_map/scatter_rows_11/pallas_call | solution.py:677
  859.5 17.4 %final_sums_13.1 = f32[8,63,128]{2,1,0:T(8,128)} custom-call(f32[8,27,128]{2,1,0:T(8,128)} %pad_maximum_fusion.12.own), custom_call_target="tpu_custom_call" | custom-call | tf_op jit(solution)/shard_map/final_sums_13/pallas_call | solution.py:787
  885.4 3.8 fusion.122
  890.3 87.8 %all-reduce.7.cloned.1.call-done = (bf16[192,4608]{1,0:T(8,128)(2,1)}, bf16[192,1536]{1,0:T(8,128)(2,1)}, bf16[512,3072]{1,0:T(8,128)(2,1)}, bf16[192,8192]{1,0:T(8,128)(2,1)}, bf16[512,1536]{1,0:T(8,128)(2,1)}) async-done(((bf16[192,4608]{1,0:T(8,128)(2,1)}, bf16[192,1536]{1,0:T(8,128)(2,1)}, bf16[512,3072]{1,0:T(8,128)(2,1)}, bf16[192,8192]{1,0:T(8,128)(2,1)}, bf16[512,1536]{1,0:T(8,128)(2,1)}), ...) | async-done | bytes 10223632 | tf_op jit(solution)/shard_map/psum | solution.py:1199
  980.5 3.7 convert_element_type.250
  987.2 3.5 convert_element_type.257
  990.7 3.4 convert_element_type.259
  (445 shorter events, 188.7 us)
Async XLA Ops:
  7.2 134.5 %copy-start = (bf16[512,3072]{1,0:T(8,128)(2,1)S(1)}, bf16[512,3072]{1,0:T(8,128)(2,1)}, u32[]{:S(2)}) copy-start(bf16[512,3072]{1,0:T(8,128)(2,1)} %param.26) | copy-start | bytes 9437188
  7.2 17.0 %copy-start.111 = (s32[1,1,2]{2,1,0:T(1,128)S(1)}, s32[1,1,2]{2,1,0:T(1,128)}, u32[]{:S(2)}) copy-start(s32[1,1,2]{2,1,0:T(1,128)} %param.21) | copy-start | bytes 28
  9.2 106.4 %all-to-all-start.1 = ((bf16[32,8,512]{2,0,1:T(8,128)(2,1)}), bf16[32,8,512]{2,0,1:T(8,128)(2,1)S(1)}, u32[]{:S(2)}, u32[]{:S(2)}) async-start(bf16[32,8,512]{2,0,1:T(8,128)(2,1)} %copy.195), calls=%async_computation.1 | async-start | bytes 524288 | tf_op jit(solution)/shard_map/all_to_all | solution.py:981
  22.4 23.3 %copy-start.84 = (f32[6144]{0:T(1024)S(1)}, f32[6144]{0:T(1024)}, u32[]{:S(2)}) copy-start(f32[6144]{0:T(1024)} %param.32) | copy-start | bytes 73732
  37.8 17.1 %copy-start.51 = (f32[104,128]{1,0:T(8,128)S(1)}, f32[104,128]{1,0:T(8,128)}, u32[]{:S(2)}) copy-start(f32[104,128]{1,0:T(8,128)} %sum_rows_0.1) | copy-start | bytes 159748
  46.5 18.1 %copy-start.58 = (f32[2,6144]{1,0:T(2,128)}, f32[2,6144]{1,0:T(2,128)S(1)}, u32[]{:S(2)}) copy-start(f32[2,6144]{1,0:T(2,128)S(1)} %broadcast_add_fusion) | copy-start | bytes 147460
  47.2 17.5 %copy-start.59 = (f32[2,1536]{1,0:T(2,128)}, f32[2,1536]{1,0:T(2,128)S(1)}, u32[]{:S(2)}) copy-start(f32[2,1536]{1,0:T(2,128)S(1)} %get-tuple-element.72) | copy-start | bytes 36868
  49.6 15.1 %copy-start.63 = (f32[1536]{0:T(1024)}, f32[1536]{0:T(1024)S(1)}, u32[]{:S(2)}) copy-start(f32[1536]{0:T(1024)S(1)} %get-tuple-element.78) | copy-start | bytes 18436
  115.6 24.5 %copy-start.35 = (bf16[32,8,512]{2,0,1:T(8,128)(2,1)}, bf16[32,8,512]{2,0,1:T(8,128)(2,1)S(1)}, u32[]{:S(2)}) copy-start(bf16[32,8,512]{2,0,1:T(8,128)(2,1)S(1)} %all-to-all-done.1) | copy-start | bytes 786436
  115.6 70.3 %all-to-all-start = ((bf16[192,3,8,192]{0,3,1,2:T(8,128)(2,1)}), bf16[192,3,8,192]{0,3,1,2:T(8,128)(2,1)}, u32[]{:S(2)}, u32[]{:S(2)}) async-start(bf16[192,3,8,192]{0,3,1,2:T(8,128)(2,1)} %copy.192), calls=%async_computation | async-start | bytes 4718592 | tf_op jit(solution)/shard_map/all_to_all | solution.py:836
  135.6 129.6 %copy-start.90 = (f32[1,192]{1,0:T(1,128)}, f32[1,192]{1,0:T(1,128)S(1)}, u32[]{:S(2)}) copy-start(f32[1,192]{1,0:T(1,128)S(1)} %get-tuple-element.103) | copy-start | bytes 2308
  185.9 184.8 %all-to-all-start.2 = ((bf16[192,2,8,512]{3,1,0,2:T(2,128)(2,1)}), bf16[192,2,8,512]{3,1,0,2:T(2,128)(2,1)}, u32[]{:S(2)}, u32[]{:S(2)}) async-start(bf16[192,2,8,512]{3,1,0,2:T(2,128)(2,1)} %copy.214), calls=%async_computation.2 | async-start | bytes 6291456 | tf_op jit(solution)/shard_map/all_to_all | solution.py:836
  294.4 37.5 %copy-start.6 = (f32[1,128,1536]{2,1,0:T(8,128)S(1)}, f32[1,128,1536]{2,1,0:T(8,128)}, u32[]{:S(2)}) copy-start(f32[1,128,1536]{2,1,0:T(8,128)} %param.17) | copy-start | bytes 2359300
  294.4 37.4 %copy-start.66 = (f32[1536]{0:T(1024)S(1)}, f32[1536]{0:T(1024)}, u32[]{:S(2)}) copy-start(f32[1536]{0:T(1024)} %get-tuple-element.79) | copy-start | bytes 18436
  294.4 38.7 %copy-start.61 = (f32[2,1536]{1,0:T(2,128)S(1)}, f32[2,1536]{1,0:T(2,128)}, u32[]{:S(2)}) copy-start(f32[2,1536]{1,0:T(2,128)} %get-tuple-element.71) | copy-start | bytes 36868
  294.4 38.7 %copy-start.68 = (f32[1536]{0:T(1024)S(1)}, f32[1536]{0:T(1024)}, u32[]{:S(2)}) copy-start(f32[1536]{0:T(1024)} %get-tuple-element.77) | copy-start | bytes 18436
  382.7 38.0 %copy-start.17 = (f32[1,128,1536]{2,1,0:T(8,128)S(1)}, f32[1,128,1536]{2,1,0:T(8,128)}, u32[]{:S(2)}) copy-start(f32[1,128,1536]{2,1,0:T(8,128)} %param.18) | copy-start | bytes 2359300
  382.7 38.0 %copy-start.70 = (f32[2,1536]{1,0:T(2,128)S(1)}, f32[2,1536]{1,0:T(2,128)}, u32[]{:S(2)}) copy-start(f32[2,1536]{1,0:T(2,128)} %get-tuple-element.70) | copy-start | bytes 36868
  382.7 38.0 %copy-start.72 = (f32[1536]{0:T(1024)S(1)}, f32[1536]{0:T(1024)}, u32[]{:S(2)}) copy-start(f32[1536]{0:T(1024)} %get-tuple-element.80) | copy-start | bytes 18436
  382.7 38.0 %copy-start.92 = (f32[2,64]{1,0:T(2,128)S(1)}, f32[2,64]{1,0:T(2,128)}, u32[]{:S(2)}) copy-start(f32[2,64]{1,0:T(2,128)} %compare_convert_fusion) | copy-start | bytes 1540
  382.7 39.0 %copy-start.10 = (f32[2,64,1536]{2,1,0:T(8,128)S(1)}, f32[2,64,1536]{2,1,0:T(8,128)}, u32[]{:S(2)}) copy-start(f32[2,64,1536]{2,1,0:T(8,128)} %copy-done.9) | copy-start | bytes 2359300
  472.9 35.5 %copy-start.11 = (f32[2,64,1536]{2,1,0:T(8,128)S(1)}, f32[2,64,1536]{2,1,0:T(8,128)}, u32[]{:S(2)}) copy-start(f32[2,64,1536]{2,1,0:T(8,128)} %copy-done.9) | copy-start | bytes 2359300
  472.9 35.5 %copy-start.62 = (f32[2,1536]{1,0:T(2,128)S(1)}, f32[2,1536]{1,0:T(2,128)}, u32[]{:S(2)}) copy-start(f32[2,1536]{1,0:T(2,128)} %get-tuple-element.71) | copy-start | bytes 36868
  472.9 35.5 %copy-start.69 = (f32[1536]{0:T(1024)S(1)}, f32[1536]{0:T(1024)}, u32[]{:S(2)}) copy-start(f32[1536]{0:T(1024)} %get-tuple-element.77) | copy-start | bytes 18436
  472.9 35.5 %copy-start.95 = (f32[2,64]{1,0:T(2,128)S(1)}, f32[2,64]{1,0:T(2,128)}, u32[]{:S(2)}) copy-start(f32[2,64]{1,0:T(2,128)} %copy-done.94) | copy-start | bytes 1540
  472.9 36.5 %copy-start.2 = (f32[2,64,1536]{2,1,0:T(8,128)S(1)}, f32[2,64,1536]{2,1,0:T(8,128)}, u32[]{:S(2)}) copy-start(f32[2,64,1536]{2,1,0:T(8,128)} %copy-done.1) | copy-start | bytes 2359300
  473.0 36.4 %copy-start.18 = (f32[1,128,1536]{2,1,0:T(8,128)S(1)}, f32[1,128,1536]{2,1,0:T(8,128)}, u32[]{:S(2)}) copy-start(f32[1,128,1536]{2,1,0:T(8,128)} %param.18) | copy-start | bytes 2359300
  473.0 36.4 %copy-start.67 = (f32[1536]{0:T(1024)S(1)}, f32[1536]{0:T(1024)}, u32[]{:S(2)}) copy-start(f32[1536]{0:T(1024)} %get-tuple-element.79) | copy-start | bytes 18436
  473.0 36.4 %copy-start.89 = (f32[2,64]{1,0:T(2,128)S(1)}, f32[2,64]{1,0:T(2,128)}, u32[]{:S(2)}) copy-start(f32[2,64]{1,0:T(2,128)} %copy-done.88) | copy-start | bytes 1540
  473.0 36.4 %copy-start.93 = (f32[2,64]{1,0:T(2,128)S(1)}, f32[2,64]{1,0:T(2,128)}, u32[]{:S(2)}) copy-start(f32[2,64]{1,0:T(2,128)} %compare_convert_fusion) | copy-start | bytes 1540
  598.3 68.0 %all-to-all-start.3 = ((bf16[1536,3,1,192]{3,1,2,0:T(4,128)(2,1)}), bf16[1536,3,1,192]{3,1,2,0:T(4,128)(2,1)}, u32[]{:S(2)}, u32[]{:S(2)}) async-start(bf16[1536,3,1,192]{3,1,2,0:T(4,128)(2,1)} %copy.231), calls=%async_computation.3 | async-start | bytes 6291456 | tf_op jit(solution)/shard_map/all_to_all | solution.py:844
  619.4 52.2 %copy-start.80 = (f32[512]{0:T(512)S(1)}, f32[512]{0:T(512)}, u32[]{:S(2)}) copy-start(f32[512]{0:T(512)} %copy-done.79) | copy-start | bytes 6148
  666.3 117.7 %all-to-all-start.4 = ((bf16[1536,2,1,512]{3,1,2,0:T(2,128)(2,1)}), bf16[1536,2,1,512]{3,1,2,0:T(2,128)(2,1)}, u32[]{:S(2)}, u32[]{:S(2)}) async-start(bf16[1536,2,1,512]{3,1,2,0:T(2,128)(2,1)} %copy.238), calls=%async_computation.4 | async-start | bytes 6291456 | tf_op jit(solution)/shard_map/all_to_all | solution.py:844
  670.8 307.4 %all-reduce.7.cloned.1.call-start = ((), (), s32[]{:S(2)}) async-start(), calls=%async_computation.5 | async-start | bytes 20447232 | tf_op jit(solution)/shard_map/psum | solution.py:1199
  795.7 13.7 %copy-start.53 = (bf16[1024,192]{0,1:T(8,128)(2,1)S(1)}, bf16[1024,192]{0,1:T(8,128)(2,1)}, u32[]{:S(2)}) copy-start(bf16[1024,192]{0,1:T(8,128)(2,1)} %copy-done.52) | copy-start | bytes 1179652
  813.8 40.1 %copy-start.7 = (f32[1,128,1536]{2,1,0:T(8,128)S(1)}, f32[1,128,1536]{2,1,0:T(8,128)}, u32[]{:S(2)}) copy-start(f32[1,128,1536]{2,1,0:T(8,128)} %param.17) | copy-start | bytes 2359300
  813.8 40.1 %copy-start.60 = (f32[2,1536]{1,0:T(2,128)S(1)}, f32[2,1536]{1,0:T(2,128)}, u32[]{:S(2)}) copy-start(f32[2,1536]{1,0:T(2,128)} %copy-done.59) | copy-start | bytes 36868
  813.8 40.1 %copy-start.64 = (f32[1536]{0:T(1024)S(1)}, f32[1536]{0:T(1024)}, u32[]{:S(2)}) copy-start(f32[1536]{0:T(1024)} %copy-done.63) | copy-start | bytes 18436
  813.8 40.1 %copy-start.100 = (f32[2,64]{1,0:T(2,128)S(1)}, f32[2,64]{1,0:T(2,128)}, u32[]{:S(2)}) copy-start(f32[2,64]{1,0:T(2,128)} %rsqrt.77) | copy-start | bytes 1540
  813.8 41.1 %copy-start.101 = (f32[192]{0:T(256)S(1)}, f32[192]{0:T(256)}, u32[]{:S(2)}) copy-start(f32[192]{0:T(256)} %get-tuple-element.32) | copy-start | bytes 2308
  813.8 41.3 %copy-start.104 = (f32[192]{0:T(256)S(1)}, f32[192]{0:T(256)}, u32[]{:S(2)}) copy-start(f32[192]{0:T(256)} %get-tuple-element.17) | copy-start | bytes 2308
  813.8 41.5 %copy-start.103 = (f32[192]{0:T(256)S(1)}, f32[192]{0:T(256)}, u32[]{:S(2)}) copy-start(f32[192]{0:T(256)} %get-tuple-element.12) | copy-start | bytes 2308
  813.9 41.7 %copy-start.81 = (f32[1,1536]{1,0:T(1,128)S(1)}, f32[1,1536]{1,0:T(1,128)}, u32[]{:S(2)}) copy-start(f32[1,1536]{1,0:T(1,128)} %stack.43) | copy-start | bytes 18436
  813.9 41.7 %copy-start.82 = (f32[1,1536]{1,0:T(1,128)S(1)}, f32[1,1536]{1,0:T(1,128)}, u32[]{:S(2)}) copy-start(f32[1,1536]{1,0:T(1,128)} %stack.42) | copy-start | bytes 18436
  813.9 41.7 %copy-start.83 = (f32[1,1536]{1,0:T(1,128)S(1)}, f32[1,1536]{1,0:T(1,128)}, u32[]{:S(2)}) copy-start(f32[1,1536]{1,0:T(1,128)} %stack.41) | copy-start | bytes 18436
  813.9 41.8 %copy-start.76 = (f32[2,1,1536]{2,1,0:T(1,128)S(1)}, f32[2,1,1536]{2,1,0:T(1,128)}, u32[]{:S(2)}) copy-start(f32[2,1,1536]{2,1,0:T(1,128)} %copy.242) | copy-start | bytes 36868
  813.9 41.8 %copy-start.77 = (f32[2,1,1536]{2,1,0:T(1,128)S(1)}, f32[2,1,1536]{2,1,0:T(1,128)}, u32[]{:S(2)}) copy-start(f32[2,1,1536]{2,1,0:T(1,128)} %mul.939) | copy-start | bytes 36868
  813.9 41.8 %copy-start.78 = (f32[2,1,1536]{2,1,0:T(1,128)S(1)}, f32[2,1,1536]{2,1,0:T(1,128)}, u32[]{:S(2)}) copy-start(f32[2,1,1536]{2,1,0:T(1,128)} %stack.47) | copy-start | bytes 36868
  (81 other events, 307.8 us)
Sparse Core Ops, SparseCore 0:
  795.9 182.2 all-reduce.6

commit v3 on v2

--- a/solution.py
+++ b/solution.py
@@ -490,7 +490,8 @@
     return ref.at[place] if axis == 0 else ref.at[:, place]
 
 
-def gather_kernel(axis, own, whole, local, z_send, z_recv, x_send, x_recv):
+def gather_kernel(axis, count, own, *rest):
+    whole, local, z_send, z_recv, x_send, x_recv = rest[count:]
     line, side = row_place()
     above, below, across = on_rows(line + 1, side), on_rows(line - 1, side), on_rows(line, 1 - side)
     has_above, has_below = line < DEPTH - 1, line > 0
@@ -553,14 +554,14 @@
             pass_on(own, at, 1, below).wait_send()
 
 
-def gather_rows(block, ident, axis):
+def gather_rows(block, ident, axis, after=()):
     ranks = DEPTH * BREADTH
     shape = block.shape[:axis] + (ranks,) + block.shape[axis:]
     anywhere = pl.BlockSpec(memory_space=pl.ANY)
     return pl.pallas_call(
-        functools.partial(gather_kernel, axis),
+        functools.partial(gather_kernel, axis, len(after)),
         out_shape=jax.ShapeDtypeStruct(shape, block.dtype),
-        in_specs=[anywhere],
+        in_specs=[anywhere] * (1 + len(after)),
         out_specs=anywhere,
         scratch_shapes=[
             pltpu.SemaphoreType.DMA,
@@ -571,10 +572,11 @@
         ],
         name=f"gather_rows_{ident}",
         compiler_params=pltpu.CompilerParams(collective_id=ident, has_side_effects=True),
-    )(block)
-
-
-def scatter_kernel(axis, parts, total, crossed, risen, sunk, up, down, x_send, x_recv, z_send, z_recv):
+    )(block, *after)
+
+
+def scatter_kernel(axis, count, parts, *rest):
+    total, crossed, risen, sunk, up, down, x_send, x_recv, z_send, z_recv = rest[count:]
     line, side = row_place()
     above, below, across = on_rows(line + 1, side), on_rows(line - 1, side), on_rows(line, 1 - side)
     has_above, has_below = line < DEPTH - 1, line > 0
@@ -670,14 +672,14 @@
             sink(at).wait_send()
 
 
-def scatter_rows(parts, ident, axis):
+def scatter_rows(parts, ident, axis, after=()):
     shape = parts.shape[:axis] + parts.shape[axis + 1 :]
     near = pl.BlockSpec(memory_space=pltpu.VMEM)
     slots = pltpu.VMEM((DEPTH,) + shape, parts.dtype)
     return pl.pallas_call(
-        functools.partial(scatter_kernel, axis),
+        functools.partial(scatter_kernel, axis, len(after)),
         out_shape=jax.ShapeDtypeStruct(shape, jnp.float32),
-        in_specs=[near],
+        in_specs=[near] + [pl.BlockSpec(memory_space=pl.ANY)] * len(after),
         out_specs=near,
         scratch_shapes=[slots] * 5
         + [
@@ -690,7 +692,7 @@
         compiler_params=pltpu.CompilerParams(
             collective_id=ident, has_side_effects=True, vmem_limit_bytes=32 << 20
         ),
-    )(parts)
+    )(parts, *after)
 
 
 def sum_kernel(own, total, held, send, receive):
@@ -805,44 +807,253 @@
     )(own)
 
 
-def gather_tokens(block, ident):
-    whole = gather_rows(block, ident, 1)
+def first_kernel(
+    ranks, quarters, own, qkv, text, total, qkv_out, text_out, held, packed, local,
+    s_send, s_recv, t_send, t_recv, a_send, a_recv, y_send, y_recv, c_send, c_recv,
+):
+    place, group = lax.axis_index("rows"), lax.axis_index("items")
+    others = [lax.rem(place + step, ranks) for step in range(1, ranks)]
+    far = lax.rem(group + 2, 4)
+    twin = group + 1 - 2 * lax.rem(group, 2)
+    depth = qkv.shape[0] // quarters
+    mine = pl.ds(pl.multiple_of(group * depth, 16), depth)
+    fars = pl.ds(pl.multiple_of(far * depth, 16), depth)
+    features = text_out.shape[-1]
+    span = qkv.shape[1] // (3 * ranks)
+
+    def columns(other):
+        return pl.ds(pl.multiple_of(other * features, features), features)
+
+    keeps = [pltpu.make_async_copy(text.at[:, :, columns(place)], text_out.at[place], local.at[0])]
+    keeps[0].start()
+    greet(
+        [(place >= 0, {"rows": other}) for other in others]
+        + [(place >= 0, {"items": far}), (place >= 0, {"items": twin})]
+    )
+
+    def sum_push(step, other, slot):
+        return remote(own, held.at[slot], s_send.at[step], s_recv.at[slot], {"rows": other})
+
+    def text_push(step, other, slot):
+        return remote(
+            text.at[:, :, columns(other)], text_out.at[slot], t_send.at[step], t_recv.at[slot], {"rows": other}
+        )
+
+    def push(step, other, slot):
+        return remote(
+            packed.at[other, mine], qkv_out.at[slot, mine], a_send.at[step], a_recv.at[slot], {"rows": other}
+        )
+
+    def pass_far(slot):
+        block = qkv_out.at[slot, mine]
+        return remote(block, block, y_send.at[slot], y_recv.at[slot], {"items": far})
+
+    def pass_twin(which, slot):
+        block = qkv_out.at[slot, fars if which else mine]
+        return remote(block, block, c_send.at[which, slot], c_recv.at[which, slot], {"items": twin})
+
+    for step, other in enumerate(others):
+        sum_push(step, other, place).start()
+    for rank in range(ranks):
+        packed[rank] = jnp.concatenate(
+            [
+                qkv[:, (part * ranks + rank) * span : (part * ranks + rank + 1) * span]
+                for part in range(3)
+            ],
+            axis=1,
+        )
+    for step, other in enumerate(others):
+        push(step, other, place).start()
+    for step, other in enumerate(others):
+        text_push(step, other, place).start()
+    keeps.append(pltpu.make_async_copy(packed.at[place], qkv_out.at[place], local.at[1]))
+    keeps[1].start()
+    held[pl.ds(place, 1)] = own[...][None]
+    for step, other in enumerate(others):
+        sum_push(step, other, other).wait_recv()
+    value = held[0]
+    for rank in range(1, ranks):
+        value = value + held[rank]
+    total[...] = value
+    for step, other in enumerate(others):
+        push(step, other, other).wait_recv()
+        pass_far(other).start()
+        pass_twin(0, other).start()
+    for other in others:
+        pass_far(other).wait_recv()
+        pass_twin(1, other).start()
+    for step, other in enumerate(others):
+        sum_push(step, other, place).wait_send()
+        text_push(step, other, other).wait_recv()
+        text_push(step, other, place).wait_send()
+        push(step, other, place).wait_send()
+        pass_far(other).wait_send()
+        for which in range(2):
+            pass_twin(which, other).wait_recv()
+            pass_twin(which, other).wait_send()
+    for copy in keeps:
+        copy.wait()
+
+
+def first_transfers(own, qkv, text, ident):
+    ranks, quarters = lax.axis_size("rows"), lax.axis_size("items")
+    depth = qkv.shape[0]
+    anywhere = pl.BlockSpec(memory_space=pl.ANY)
+    near = pl.BlockSpec(memory_space=pltpu.VMEM)
+    outs = [
+        jax.ShapeDtypeStruct(own.shape, own.dtype),
+        jax.ShapeDtypeStruct((ranks, depth, qkv.shape[1] // ranks), qkv.dtype),
+        jax.ShapeDtypeStruct((ranks,) + text.shape[:-1] + (text.shape[-1] // ranks,), text.dtype),
+    ]
+    wave = pltpu.SemaphoreType.DMA
+    return pl.pallas_call(
+        functools.partial(first_kernel, ranks, quarters),
+        out_shape=outs,
+        in_specs=[near, near, anywhere],
+        out_specs=[near, anywhere, anywhere],
+        scratch_shapes=[
+            pltpu.VMEM((ranks,) + own.shape, own.dtype),
+            pltpu.VMEM(outs[1].shape, qkv.dtype),
+            wave((2,)),
+        ]
+        + [wave((ranks,))] * 8
+        + [wave((2, ranks))] * 2,
+        name=f"first_transfers_{ident}",
+        compiler_params=pltpu.CompilerParams(
+            collective_id=ident, has_side_effects=True, vmem_limit_bytes=24 << 20
+        ),
+    )(own, qkv, text)
+
+
+def pack_kernel(pieces, whole, packed):
+    ranks, span = packed.shape[0], packed.shape[2] // pieces
+    for rank in range(ranks):
+        packed[rank] = jnp.concatenate(
+            [whole[:, (piece * ranks + rank) * span : (piece * ranks + rank + 1) * span] for piece in range(pieces)],
+            axis=1,
+        ).astype(packed.dtype)
+
+
+def pack_blocks(whole, pieces, ranks, dtype):
+    near = pl.BlockSpec(memory_space=pltpu.VMEM)
+    return pl.pallas_call(
+        functools.partial(pack_kernel, pieces),
+        out_shape=jax.ShapeDtypeStruct((ranks, whole.shape[0], whole.shape[1] // ranks), dtype),
+        in_specs=[near],
+        out_specs=near,
+        name="pack_blocks",
+        compiler_params=pltpu.CompilerParams(vmem_limit_bytes=24 << 20),
+    )(whole)
+
+
+def unpack_kernel(pieces, packed, whole):
+    ranks, span = packed.shape[0], packed.shape[2] // pieces
+    for piece in range(pieces):
+        for rank in range(0, ranks, 2):
+            start = (piece * ranks + rank) * span
+            whole[:, start : start + 2 * span] = jnp.concatenate(
+                [packed[rank + k, :, piece * span : (piece + 1) * span] for k in range(2)], axis=1
+            ).astype(whole.dtype)
+
+
+def unpack_blocks(packed, pieces, dtype):
+    near = pl.BlockSpec(memory_space=pltpu.VMEM)
+    ranks, rows, width = packed.shape
+    return pl.pallas_call(
+        functools.partial(unpack_kernel, pieces),
+        out_shape=jax.ShapeDtypeStruct((rows, ranks * width), dtype),
+        in_specs=[near],
+        out_specs=near,
+        name="unpack_blocks",
+        compiler_params=pltpu.CompilerParams(vmem_limit_bytes=24 << 20),
+    )(packed)
+
+
+def halves_kernel(pieces, own, other, whole):
+    ranks, half, span = own.shape[0], own.shape[1], own.shape[2] // pieces
+    first = lax.rem(lax.axis_index("items"), 2) == 0
+    for low in range(2):
+
+        @pl.when(first == (low == 0))
+        def _(low=low):
+            for source, start in ((own, low * half), (other, (1 - low) * half)):
+                for piece in range(pieces):
+                    for rank in range(0, ranks, 2):
+                        column = (piece * ranks + rank) * span
+                        whole[start : start + half, column : column + 2 * span] = jnp.concatenate(
+                            [source[rank + k, :, piece * span : (piece + 1) * span] for k in range(2)], axis=1
+                        ).astype(whole.dtype)
+
+
+def unpack_halves(own, other, pieces):
+    near = pl.BlockSpec(memory_space=pltpu.VMEM)
+    ranks, half, width = own.shape
+    return pl.pallas_call(
+        functools.partial(halves_kernel, pieces),
+        out_shape=jax.ShapeDtypeStruct((2 * half, ranks * width), jnp.float32),
+        in_specs=[near, near],
+        out_specs=near,
+        name="unpack_halves",
+        compiler_params=pltpu.CompilerParams(vmem_limit_bytes=32 << 20),
+    )(own, other)
+
+
+def gather_tokens(block, ident, after=()):
+    whole = gather_rows(block, ident, 1, after)
     return whole.reshape(-1, block.shape[-1])
 
 
-def scatter_tokens(partial, items, ident):
+def scatter_tokens(partial, items, ident, after=()):
     ranks = lax.axis_size("rows")
     blocks = partial.astype(jnp.bfloat16).reshape(items, ranks, -1, partial.shape[-1])
-    return scatter_rows(blocks, ident, 1)
-
-
-def sum_vectors(vectors, ident):
-    sizes = [vector.size for vector in vectors]
+    return scatter_rows(blocks, ident, 1, after)
+
+
+def lay_flat(vectors):
     flat = jnp.concatenate([vector.reshape(-1) for vector in vectors])
     rows = -(-flat.size // 1024) * 8
-    flat = jnp.pad(flat, (0, rows * 128 - flat.size))
-    total = sum_rows(flat.reshape(rows, 128), ident).reshape(-1)
-    parts, start = [], 0
-    for vector, size in zip(vectors, sizes):
-        parts.append(total[start : start + size].reshape(vector.shape))
-        start += size
+    return jnp.pad(flat, (0, rows * 128 - flat.size)).reshape(rows, 128)
+
+
+def take_apart(total, vectors):
+    flat, parts, start = total.reshape(-1), [], 0
+    for vector in vectors:
+        parts.append(flat[start : start + vector.size].reshape(vector.shape))
+        start += vector.size
     return parts
 
 
-def columns_here(weight, pieces):
-    ranks = lax.axis_size("rows")
-    depth, width = weight.shape
-    shaped = weight.reshape(depth, pieces, ranks, width // (pieces * ranks))
-    moved = lax.all_to_all(shaped, "rows", split_axis=2, concat_axis=0, tiled=True)
-    return moved.reshape(depth * ranks, width // ranks)
-
-
-def rows_here(grad, pieces):
-    ranks = lax.axis_size("rows")
-    depth, width = grad.shape
-    low = grad.astype(jnp.bfloat16).reshape(depth, pieces, 1, width // pieces)
-    moved = lax.all_to_all(low, "rows", split_axis=0, concat_axis=2, tiled=True)
-    return moved.reshape(depth // ranks, width * ranks)
+def sum_vectors(vectors, ident):
+    return take_apart(sum_rows(lay_flat(vectors), ident), vectors)
+
+
+def first_sums(vectors, qkv, text, ident):
+    total, qkv_here, text_in = first_transfers(lay_flat(vectors), qkv, text, ident)
+    return take_apart(total, vectors), qkv_here, text_in
+
+
+CORES = [(0, 1), (1, 0), (2, 3), (3, 2)]
+FARS = [(0, 2), (1, 3), (2, 0), (3, 1)]
+
+
+def swap(array, pairs):
+    return lax.ppermute(array, "items", pairs)
+
+
+def give_keep(grad, index, axis):
+    keep = lax.dynamic_index_in_dim(grad, index, axis, keepdims=False)
+    give = lax.dynamic_index_in_dim(grad, 1 - index, axis, keepdims=False)
+    return give, keep
+
+
+def add_low(one, other):
+    return (one.astype(jnp.float32) + other.astype(jnp.float32)).astype(jnp.bfloat16)
+
+
+def join(own, other, index, axis):
+    shape = own.shape[:axis] + (2,) + own.shape[axis:]
+    own, other = jnp.expand_dims(own, axis), jnp.expand_dims(other, axis)
+    return jnp.where(lax.broadcasted_iota(jnp.int32, shape, axis) == index, own, other)
 
 
 def head_parallel_plan(
@@ -901,17 +1112,22 @@
             jnp.zeros((whole,), single), part.reshape(-1), place * part.size, 0
         )
 
+    group = lax.axis_index("items")
+    core, far = lax.rem(group, 2), group // 2
     counts_here = live_rows[0]
     text_float = text_states[0].astype(single).reshape(items * text_local, text_width)
     text_inverse = norm_parts(text_float)[1]
-    modulation, counts, text_inverse = sum_vectors(
+    (modulation, counts, text_inverse), qkv_here, text_in = first_sums(
         [
             dot(time_here, w_ada),
             spread(counts_here.astype(single), ranks * items),
             spread(text_inverse, ranks * items * text_local),
         ],
+        w_qkv,
+        text_states[0],
         0,
     )
+    qkv_here = qkv_here.reshape(width, -1)
     modulation = modulation + ada_bias
     counts = counts.astype(jnp.int32).reshape(ranks, items)
     text_inverse = text_inverse.reshape(-1, 1)
@@ -973,31 +1189,32 @@
     unit_in, inverse_in = norm_parts(states)
     norm_in = unit_in * gains[0]
     attn_in = gather_tokens((norm_in * (1.0 + scale_attn)).astype(narrow), 1)
-    qkv_here = columns_here(w_qkv, 3)
+    hidden = w_down.shape[0]
+    gu_depth = w_gu.shape[0] // 4
+    gu_rows = lax.dynamic_slice_in_dim(w_gu, (2 * core + far) * gu_depth, gu_depth, 0)
+    gu_rows = jnp.transpose(gu_rows.reshape(gu_depth, 2, ranks, hidden), (2, 0, 1, 3))
+    gu_rows, attn_in = lax.optimization_barrier(
+        (gu_rows.reshape(ranks, gu_depth, 2 * hidden), attn_in)
+    )
+    gu_part = lax.all_to_all(gu_rows, "rows", 0, 0, tiled=True)
+    gu_pair = join(gu_part, swap(gu_part, FARS), far, 1)
+
     qkv_proj = dot(attn_in, qkv_here)
     query_proj, key_proj, value_proj = jnp.split(qkv_proj, 3, axis=1)
 
     features = text_width // ranks
-    text_in = lax.all_to_all(
-        text_states[0].reshape(items * text_local, ranks, features),
-        "rows",
-        split_axis=1,
-        concat_axis=0,
-        tiled=True,
-    ).reshape(items * text_all, features)
+    features = text_width // ranks
+    text_in = text_in.reshape(items * text_all, features)
     text_unit = text_in.astype(single) * text_inverse
     gain_text = lax.dynamic_slice_in_dim(text_gain, place * features, features, 0)
     text_norm = (text_unit * gain_text).astype(narrow)
 
-    def by_rank(values):
-        pieces = values.reshape(-1, 2, ranks, span)
-        return jnp.transpose(pieces, (2, 0, 1, 3)).reshape(ranks, -1, 2 * span)
-
     def text_rows(values):
         shaped = values.reshape(ranks, items, text_local, -1)
         return jnp.swapaxes(shaped, 0, 1).reshape(items * text_all, -1)
 
-    text_proj = scatter_rows(by_rank(dot(text_norm, w_text).astype(narrow)), 2, 0)
+    text_parts = pack_blocks(dot(text_norm, w_text).astype(narrow), 2, ranks, narrow)
+    text_proj = scatter_rows(text_parts, 2, 0)
     tkey_proj, tval_proj = jnp.split(text_rows(text_proj), 2, axis=1)
 
     def squares(values):
@@ -1042,7 +1259,8 @@
     unit_mid, inverse_mid = norm_parts(middle)
     norm_mid = unit_mid * gains[4]
     ffn_in = gather_tokens((norm_mid * (1.0 + scale_ffn)).astype(narrow), 5)
-    gu_here = columns_here(w_gu, 2)
+    gu_columns = join(gu_pair, swap(gu_pair, CORES), core, 1)
+    gu_here = gu_columns.reshape(width, 2 * w_down.shape[0])
     gate_up = dot(ffn_in, gu_here)
     gate_part, up_part = jnp.split(gate_up, 2, axis=1)
     sigmoid = 1.0 / (1.0 + jnp.exp(-gate_part))
@@ -1062,7 +1280,8 @@
     ffn_low = gather_tokens(
         norm_back(unit_ffn, inverse_ffn, grad_norm * gains[5]).astype(narrow), 7
     )
-    grad_down = weight_grad(inner_act, ffn_low)
+    grad_down = weight_grad(inner_act, ffn_low).astype(narrow).reshape(2, -1, width)
+    give_down, keep_down = give_keep(grad_down, core, 0)
     grad_inner = dot_back(ffn_low, w_down)
     gate_up_low = jnp.concatenate(
         [
@@ -1071,8 +1290,14 @@
         ],
         axis=1,
     ).astype(narrow)
-    grad_gu = weight_grad(ffn_in, gate_up_low)
-    grad_ffn_in = scatter_tokens(dot_back(gate_up_low, gu_here), items, 8)
+    grad_gu = weight_grad(ffn_in, gate_up_low).astype(narrow)
+    give_gu, keep_gu = give_keep(grad_gu.reshape(ranks, 2, -1, 2 * hidden), core, 1)
+    grad_ffn_in = scatter_tokens(
+        dot_back(gate_up_low, gu_here), items, 8, after=(give_down, give_gu)
+    )
+    half_down = add_low(keep_down, swap(give_down, CORES))
+    half_gu = add_low(keep_gu, swap(give_gu, CORES))
+    give_gu, keep_gu = give_keep(half_gu.reshape(ranks, 2, -1, 2 * hidden), far, 1)
     grad_scale_ffn = jnp.sum(grad_ffn_in * norm_mid, axis=1)
     grad_norm = grad_ffn_in * (1.0 + scale_ffn)
     grad_four = over_tokens(grad_norm * unit_mid)
@@ -1082,9 +1307,15 @@
     grad_norm = gate_attn * grad_middle
     grad_three = over_tokens(grad_norm * unit_proj)
     projected_low = gather_tokens(
-        norm_back(unit_proj, inverse_proj, grad_norm * gains[3]).astype(narrow), 9
-    )
-    grad_out = weight_grad(combined, projected_low)
+        norm_back(unit_proj, inverse_proj, grad_norm * gains[3]).astype(narrow),
+        9,
+        after=(half_down, give_gu),
+    )
+    sum_down = add_low(half_down, swap(half_down, FARS))
+    sum_gu = add_low(keep_gu, swap(give_gu, FARS))
+    rows_gu = lax.all_to_all(sum_gu, "rows", 0, 0, tiled=True)
+    grad_out = weight_grad(combined, projected_low).astype(narrow).reshape(2, -1, width)
+    give_out, keep_out = give_keep(grad_out, core, 0)
     grad_combined = by_head(dot_back(projected_low, w_out))
     self_low = grad_combined.astype(narrow)
     cross_grad_low = (gate_here[:, None] * grad_combined).astype(narrow)
@@ -1137,18 +1368,31 @@
     text_low = jnp.concatenate(
         [inverse_t * (scaled_t - unit_t * mean_t), grad_tval], axis=1
     ).astype(narrow)
-    grad_qkv = weight_grad(attn_in, qkv_low)
-    grad_attn_in = scatter_tokens(dot_back(qkv_low, qkv_here), items, 11)
+    grad_qkv = weight_grad(attn_in, qkv_low).astype(narrow)
+    give_qkv, keep_qkv = give_keep(grad_qkv.reshape(ranks, 2, -1, 3 * span), core, 1)
+
+    text_low = text_low.reshape(items, ranks, text_local, 2 * span)
+    text_low = jnp.swapaxes(text_low, 0, 1).reshape(items * text_all, 2 * span)
+    all_low = unpack_blocks(gather_rows(text_low, 12, 0, after=(give_qkv, give_out)), 2, narrow)
+    half_out = add_low(keep_out, swap(give_out, CORES))
+    half_qkv = add_low(keep_qkv, swap(give_qkv, CORES))
+    give_qkv, keep_qkv = give_keep(half_qkv.reshape(ranks, 2, -1, 3 * span), far, 1)
+    grad_text = weight_grad(text_norm, all_low).astype(narrow).reshape(2, -1, 2 * width)
+    give_text, keep_text = give_keep(grad_text, core, 0)
+    half_text = add_low(keep_text, swap(give_text, CORES))
+    pair_gu = join(rows_gu, swap(rows_gu, FARS), far, 1).reshape(ranks, -1, 2 * hidden)
+    sum_out = add_low(half_out, swap(half_out, FARS))
+    sum_qkv = add_low(keep_qkv, swap(give_qkv, FARS))
+    sum_text = add_low(half_text, swap(half_text, FARS))
+
+    grad_attn_in = scatter_tokens(
+        dot_back(qkv_low, qkv_here), items, 11, after=(half_out, give_qkv, half_text)
+    )
     grad_scale_attn = jnp.sum(grad_attn_in * norm_in, axis=1)
     grad_norm = grad_attn_in * (1.0 + scale_attn)
     grad_zero = over_tokens(grad_norm * unit_in)
     grad_x = grad_middle + norm_back(unit_in, inverse_in, grad_norm * gains[0])
 
-    text_low = text_low.reshape(items, ranks, text_local, 2 * span)
-    text_low = jnp.swapaxes(text_low, 0, 1).reshape(items * text_all, 2 * span)
-    all_low = gather_rows(text_low, 12, 0).reshape(ranks, -1, 2, span)
-    all_low = jnp.transpose(all_low, (1, 2, 0, 3)).reshape(items * text_all, 2 * width)
-    grad_text = weight_grad(text_norm, all_low)
     grad_text_gain = jnp.sum(dot_back(all_low, w_text) * text_unit, axis=0)
     grad_modulation = jnp.stack([grad_scale_attn, grad_gate_attn, grad_scale_ffn, grad_gate_ffn], 1)
     grad_gains = jnp.stack(
@@ -1195,15 +1439,19 @@
         preferred_element_type=single,
     )
     total_bias = jnp.sum(all_modulation, axis=0)
+    rows_qkv = lax.all_to_all(sum_qkv, "rows", 0, 0, tiled=True)
+    pair_qkv = join(rows_qkv, swap(rows_qkv, FARS), far, 1).reshape(ranks, -1, 3 * span)
+
+    def whole_rows(half):
+        both = join(half, swap(half, CORES), core, 0).astype(single)
+        return both.reshape(-1, half.shape[-1])
+
     sums = [
-        lax.psum(part.astype(narrow), "items").astype(single)
-        for part in (
-            rows_here(grad_qkv, 3),
-            grad_out,
-            grad_text,
-            rows_here(grad_gu, 2),
-            grad_down,
-        )
+        unpack_halves(pair_qkv, swap(pair_qkv, CORES), 3),
+        whole_rows(sum_out),
+        whole_rows(sum_text),
+        unpack_halves(pair_gu, swap(pair_gu, CORES), 2),
+        whole_rows(sum_down),
     ]
     return (
         output.reshape(1, items * slots, width),

time: 1010 us -> 823 us (0.81)
  waiting for transfers between devices: 135 us -> 43 us
  Pallas kernels: 501 us -> 446 us
  local copies, waits for them, and re-layouts: 153 us -> 110 us
  other arithmetic: 70 us -> 98.4 us
  between operations: 16.1 us -> 2.71 us
    psum x1 -> x0, waiting for transfers between devices: 87.8 us -> none  [head_parallel_plan(): lax.psum(part.astype(narrow), 'items').astype(single)]
    pallas_call x3 -> x2, Pallas kernels: 75.5 us -> 16.1 us  [sum_rows(): pl.pallas_call(sum_kernel, out_shape=jax.ShapeDtypeStruct(own.shape, own....]
    reshape x11 -> x3, local copies, waits for them, and re-layouts: 46.2 us -> 3.94 us  [the longest x1 3.24 us: head_parallel_plan(): gu_rows.reshape(ranks, gu_depth, 2 * hidden)]
    all_to_all x5 -> x3, waiting for transfers between devices: 46.9 us -> 9.89 us  [the longest x1 9.89 us: head_parallel_plan(): rows_gu = lax.all_to_all(sum_gu, 'rows', 0, 0, tiled=True)]
    ppermute x0 -> x19, waiting for transfers between devices: none -> 33.1 us  [swap(): return lax.ppermute(array, 'items', pairs)]
    all_to_all x4 -> x0, local copies, waits for them, and re-layouts: 16 us -> none  [the longest x3 11.6 us: rows_here(): moved = lax.all_to_all(low, 'rows', split_axis=0, concat_axis=2, tiled=True)]
    all_to_all x5 -> x3, starting transfers between devices: 29.7 us -> 14.4 us  [the longest x1 5.94 us: head_parallel_plan(): rows_qkv = lax.all_to_all(sum_qkv, 'rows', 0, 0, tiled=True)]
    convert_element_type x7 -> x13, other arithmetic: 16.8 us -> 32.1 us  [the longest x10 21.4 us: add_low(): (one.astype(jnp.float32) + other.astype(jnp.float32)).astype(jnp.bfloat16)]
  transfers between devices with their start and end apart: 6 -> 22, of which waited for: 2 -> 3; matrix products, arithmetic and copies ran while one was open for 21% -> 26% of each run, Pallas kernels for 34% -> 36%
where the time goes in v3:
time: 823 us; the launch traced here: 814 us
  Pallas kernels  446 us (54%)
  local copies, waits for them, and re-layouts  110 us (13%)
  other arithmetic  98.4 us (12%)
  matrix products  85.1 us (10%)
  waiting for transfers between devices  43 us (5%)
  starting transfers between devices  22.8 us (3%)
    pallas_call x5, Pallas kernels, gather_rows(): pl.pallas_call(functools.partial(gather_kernel, axis, len(after)), out_sh...  185 us
    pallas_call x5, Pallas kernels, scatter_rows(): pl.pallas_call(functools.partial(scatter_kernel, axis, len(after)), out_s...  184 us
    pallas_call x1, Pallas kernels, first_transfers(): pl.pallas_call(functools.partial(first_kernel, ranks, quarters), out_shap...  34.9 us
    ppermute x19, waiting for transfers between devices, swap(): return lax.ppermute(array, 'items', pairs)  33.1 us
    unnamed x285, local copies, waits for them, and re-layouts  26.8 us
    convert_element_type x10, other arithmetic, add_low(): (one.astype(jnp.float32) + other.astype(jnp.float32)).astype(jnp.bfloat16)  21.4 us
    dot_general x5, matrix products, dot_back(): return jnp.einsum('tn,kn->tk', left, weight, preferred_element_type=single)  20.5 us
    pallas_call x1, Pallas kernels, final_sums(): pl.pallas_call(functools.partial(final_kernel, ranks, groups, sums), out_...  17.1 us
  transfers between devices with their start and end apart: 22, of which 3 were waited for; matrix products, arithmetic and copies ran while one was open for 26% of the time, Pallas kernels for 36%

profile of v3, /device:TPU:0, one launch (start us, length us, event | category | flops | bytes accessed | tf_op | source)
XLA Modules:
  0.0 813.6 jit_solution(16682093055206377290)
XLA Ops:
  10.0 3.2 reshape.677
  15.7 34.9 %first_transfers_0.1 = (f32[104,128]{1,0:T(8,128)S(1)}, bf16[8,192,576]{2,1,0:T(8,128)(2,1)S(1)}, bf16[8,2,16,512]{3,2,1,0:T(8,128)(2,1)S(1)}) custom-call(f32[104,128]{1,0:T(8,128)S(1)} %pad_bitcast_fusion.own, bf16[192,4608]{1,0:T(8,128)(2,1)S(1)} %copy-done.8, bf16[2,16,4096]{2,1,0:T(8,128)(2,1)S(1)} %bitcast.306), custom_call_target="tpu_custom_call" | custom-call | tf_op jit(solution)/shard_map/first_transfers_0/pallas_call | solution.py:909
  57.5 48.5 %gather_rows_1.1 = bf16[2,8,64,1536]{3,2,1,0:T(8,128)(2,1)} custom-call(bf16[2,64,1536]{2,1,0:T(8,128)(2,1)} %multiply_convert_fusion.11.own), custom_call_target="tpu_custom_call" | custom-call | tf_op jit(solution)/shard_map/gather_rows_1/pallas_call | solution.py:561
  106.0 4.2 all-to-all-start
  112.5 31.1 %scatter_rows_2.1 = f32[256,384]{1,0:T(8,128)S(1)} custom-call(bf16[8,256,384]{2,1,0:T(8,128)(2,1)S(1)} %pack_blocks.1.parts), custom_call_target="tpu_custom_call" | custom-call | tf_op jit(solution)/shard_map/scatter_rows_2/pallas_call | solution.py:679
  146.2 5.2 slice.120
  153.0 4.5 fusion.131
  159.8 7.9 sum_rows_3.1
  218.1 3.5 fusion.117
  224.7 6.9 fusion.122
  231.6 3.8 fusion.28
  239.3 35.2 %scatter_rows_4.1 = f32[2,64,1536]{2,1,0:T(8,128)S(1)} custom-call(bf16[2,8,64,1536]{3,2,1,0:T(8,128)(2,1)S(1)} %bitcast.298), custom_call_target="tpu_custom_call" | custom-call | tf_op jit(solution)/shard_map/scatter_rows_4/pallas_call | solution.py:679
  274.8 2.8 broadcast_select_fusion.1
  279.8 41.5 %gather_rows_5.1 = bf16[2,8,64,1536]{3,2,1,0:T(8,128)(2,1)} custom-call(bf16[2,64,1536]{2,1,0:T(8,128)(2,1)} %multiply_convert_fusion.10.own), custom_call_target="tpu_custom_call" | custom-call | tf_op jit(solution)/shard_map/gather_rows_5/pallas_call | solution.py:561
  332.2 5.0 all-gather
  341.4 3.6 fusion.132
  350.3 38.8 %scatter_rows_6.1 = f32[2,64,1536]{2,1,0:T(8,128)S(1)} custom-call(bf16[2,8,64,1536]{3,2,1,0:T(8,128)(2,1)S(1)} %bitcast.301), custom_call_target="tpu_custom_call" | custom-call | tf_op jit(solution)/shard_map/scatter_rows_6/pallas_call | solution.py:679
  391.7 35.4 %gather_rows_7.1 = bf16[2,8,64,1536]{3,2,1,0:T(8,128)(2,1)} custom-call(bf16[2,64,1536]{2,1,0:T(8,128)(2,1)} %get-tuple-element.67.own), custom_call_target="tpu_custom_call" | custom-call | tf_op jit(solution)/shard_map/gather_rows_7/pallas_call | solution.py:561
  427.1 6.1 multiply_convert_fusion.2
  435.1 4.7 convolution_convert_fusion.5
  442.0 3.7 convolution_convert_fusion.6
  446.6 38.1 %scatter_rows_8.1 = f32[2,64,1536]{2,1,0:T(8,128)S(1)} custom-call(bf16[2,8,64,1536]{3,2,1,0:T(8,128)(2,1)S(1)} %bitcast.300, bf16[256,1536]{1,0:T(8,128)(2,1)S(1)} %dynamic-slice_bitcast_fusion.4.rest_0_, bf16[8,96,1024]{2,1,0:T(8,128)(2,1)S(1)} %dynamic-slice_bitcast_fusion.1.rest_1_), custom_call_target="tpu_custom_call" | custom-call | tf_op jit(solution)/shard_map/scatter_rows_8/pallas_call | solution.py:679
  496.9 34.7 %gather_rows_9.1 = bf16[2,8,64,1536]{3,2,1,0:T(8,128)(2,1)} custom-call(bf16[2,64,1536]{2,1,0:T(8,128)(2,1)} %multiply_convert_fusion.8.own, bf16[256,1536]{1,0:T(8,128)(2,1)} %fusion.12.rest_0_, bf16[8,48,1024]{2,1,0:T(8,128)(2,1)} %dynamic-slice_bitcast_fusion.3.rest_1_), custom_call_target="tpu_custom_call" | custom-call | tf_op jit(solution)/shard_map/gather_rows_9/pallas_call | solution.py:561
  531.6 4.2 multiply_reduce_fusion.6
  535.9 4.9 fusion.34
  545.3 2.6 fusion.52
  564.4 8.3 %sum_rows_10.1 = f32[24,128]{1,0:T(8,128)} custom-call(f32[24,128]{1,0:T(8,128)} %fusion.100.own), custom_call_target="tpu_custom_call" | custom-call | tf_op jit(solution)/shard_map/sum_rows_10/pallas_call | solution.py:723
  576.7 2.9 convolution_convert_fusion.9
  583.4 3.2 convolution_convert_fusion.7
  586.6 3.9 copy.161
  596.8 25.1 %gather_rows_12.1.packed = bf16[8,256,384]{2,1,0:T(8,128)(2,1)} custom-call(bf16[256,384]{1,0:T(8,128)(2,1)} %bitcast.366, bf16[8,96,576]{2,1,0:T(8,128)(2,1)} %dynamic-slice_bitcast_fusion.2.rest_0_, bf16[96,1536]{1,0:T(8,128)(2,1)} %dynamic-slice_bitcast_fusion.6.rest_1_), custom_call_target="tpu_custom_call" | custom-call | tf_op jit(solution)/shard_map/gather_rows_12/pallas_call | solution.py:561
  626.4 3.8 add_convert_fusion.1
  630.2 4.1 convolution_convert_fusion.2
  639.2 4.2 all-to-all-start.2
  643.5 3.8 fusion.3.rest_2_
  654.4 9.9 %all-to-all-done.2 = bf16[8,48,1024]{2,1,0:T(8,128)(2,1)} async-done(((bf16[8,48,1024]{2,1,0:T(8,128)(2,1)}), bf16[8,48,1024]{2,1,0:T(8,128)(2,1)}, u32[]{:S(2)}, u32[]{:S(2)}) %all-to-all-start.2) | async-done | bytes 786464 | tf_op jit(solution)/shard_map/all_to_all | solution.py:1316
  668.9 3.4 fusion.13
  674.6 20.8 %collective-permute-done.7 = bf16[8,48,576]{2,1,0:T(8,128)(2,1)} collective-permute-done((bf16[8,48,576]{2,1,0:T(8,128)(2,1)}, bf16[8,48,576]{2,1,0:T(8,128)(2,1)}, u32[]{:S(2)}, u32[]{:S(2)}) %collective-permute-start.7) | collective-permute-done | bytes 442400 | tf_op jit(solution)/shard_map/ppermute | solution.py:1040
  697.3 5.9 all-to-all-start.1
  705.1 40.5 %scatter_rows_11.1 = f32[2,64,1536]{2,1,0:T(8,128)S(1)} custom-call(bf16[2,8,64,1536]{3,2,1,0:T(8,128)(2,1)S(1)} %bitcast.299, bf16[96,1536]{1,0:T(8,128)(2,1)S(1)} %fusion.43.rest_0_, bf16[8,48,576]{2,1,0:T(8,128)(2,1)} %dynamic-slice_bitcast_fusion.5.rest_1_, bf16[256,3072]{1,0:T(8,128)(2,1)} %fusion.3.rest_2_), custom_call_target="tpu_custom_call" | custom-call | tf_op jit(solution)/shard_map/scatter_rows_11/pallas_call | solution.py:679
  746.2 2.7 bitcast_select_fusion.3.own
  749.1 3.6 add_convert_fusion
  754.7 12.3 %collective-permute-done.8 = bf16[8,48,576]{2,1,0:T(8,128)(2,1)} collective-permute-done((bf16[8,48,576]{2,1,0:T(8,128)(2,1)}, bf16[8,48,576]{2,1,0:T(8,128)(2,1)}, u32[]{:S(2)}, u32[]{:S(2)}) %collective-permute-start.8) | collective-permute-done | bytes 442400 | tf_op jit(solution)/shard_map/ppermute | solution.py:1040
  770.0 17.1 %final_sums_13.1 = f32[8,63,128]{2,1,0:T(8,128)} custom-call(f32[8,27,128]{2,1,0:T(8,128)} %pad_maximum_fusion.12.own), custom_call_target="tpu_custom_call" | custom-call | tf_op jit(solution)/shard_map/final_sums_13/pallas_call | solution.py:789
  794.6 3.9 fusion.133
  799.7 3.7 unpack_halves.2
  803.4 5.0 unpack_halves.3
  808.4 5.1 fusion.5
  (525 shorter events, 202.7 us)
Async XLA Ops:
  0.6 110.5 %copy-start = (bf16[512,3072]{1,0:T(8,128)(2,1)S(1)}, bf16[512,3072]{1,0:T(8,128)(2,1)}, u32[]{:S(2)}) copy-start(bf16[512,3072]{1,0:T(8,128)(2,1)} %param.26) | copy-start | bytes 9437188
  3.1 52.4 %copy-start.70 = (f32[1536]{0:T(1024)}, f32[1536]{0:T(1024)S(1)}, u32[]{:S(2)}) copy-start(f32[1536]{0:T(1024)S(1)} %get-tuple-element.83) | copy-start | bytes 18436
  10.0 42.6 %copy-start.97 = (f32[6144]{0:T(1024)S(1)}, f32[6144]{0:T(1024)}, u32[]{:S(2)}) copy-start(f32[6144]{0:T(1024)} %param.32) | copy-start | bytes 73732
  51.9 571.7 %copy-start.9 = (bf16[8,2,16,512]{3,2,1,0:T(8,128)(2,1)}, bf16[8,2,16,512]{3,2,1,0:T(8,128)(2,1)S(1)}, u32[]{:S(2)}) copy-start(bf16[8,2,16,512]{3,2,1,0:T(8,128)(2,1)S(1)} %get-tuple-element.20) | copy-start | bytes 786436
  53.5 52.5 %copy-start.64 = (f32[2,6144]{1,0:T(2,128)}, f32[2,6144]{1,0:T(2,128)S(1)}, u32[]{:S(2)}) copy-start(f32[2,6144]{1,0:T(2,128)S(1)} %broadcast_add_fusion) | copy-start | bytes 147460
  55.5 50.5 %copy-start.112 = (f32[2,64]{1,0:T(2,128)}, f32[2,64]{1,0:T(2,128)S(1)}, u32[]{:S(2)}) copy-start(f32[2,64]{1,0:T(2,128)S(1)} %rsqrt.77) | copy-start | bytes 1540
  106.0 130.6 %all-to-all-start = ((bf16[8,48,1024]{2,1,0:T(8,128)(2,1)}), bf16[8,48,1024]{2,1,0:T(8,128)(2,1)}, u32[]{:S(2)}, u32[]{:S(2)}) async-start(bf16[8,48,1024]{2,1,0:T(8,128)(2,1)} %reshape.677), calls=%async_computation | async-start | bytes 1572864 | tf_op jit(solution)/shard_map/all_to_all | solution.py:1199
  236.6 38.2 %collective-permute-start = (bf16[8,48,1024]{2,1,0:T(8,128)(2,1)}, bf16[8,48,1024]{2,1,0:T(8,128)(2,1)S(1)}, u32[]{:S(2)}, u32[]{:S(2)}) collective-permute-start(bf16[8,48,1024]{2,1,0:T(8,128)(2,1)} %all-to-all-done), channel_id=1, source_target_pairs={{0,16},{8,24},{16,0},{24,8},{1,17},{9,25},{17,1},{25,9},{2,18},{10... | collective-permute-start | bytes 2359304 | tf_op jit(solution)/shard_map/ppermute | solution.py:1040
  277.6 61.0 %collective-permute-start.1 = (bf16[8,2,48,1024]{3,2,1,0:T(8,128)(2,1)}, bf16[8,2,48,1024]{3,2,1,0:T(8,128)(2,1)}, u32[]{:S(2)}, u32[]{:S(2)}) collective-permute-start(bf16[8,2,48,1024]{3,2,1,0:T(8,128)(2,1)} %broadcast_select_fusion.1), channel_id=1, source_target_pairs={{0,8},{8,0},{16,24},{24,16},{1,9},{9,1},{17,25},{25,17},{2,10},{10... | collective-permute-start | bytes 4718600 | tf_op jit(solution)/shard_map/ppermute | solution.py:1040
  337.9 51.9 %copy-start.106 = (f32[2,64]{1,0:T(2,128)}, f32[2,64]{1,0:T(2,128)S(1)}, u32[]{:S(2)}) copy-start(f32[2,64]{1,0:T(2,128)S(1)} %compare_convert_fusion) | copy-start | bytes 1540
  350.3 39.0 %copy-start.28 = (f32[1,128,1536]{2,1,0:T(8,128)S(1)}, f32[1,128,1536]{2,1,0:T(8,128)}, u32[]{:S(2)}) copy-start(f32[1,128,1536]{2,1,0:T(8,128)} %param.18) | copy-start | bytes 2359300
  350.3 39.0 %copy-start.77 = (f32[2,1536]{1,0:T(2,128)S(1)}, f32[2,1536]{1,0:T(2,128)}, u32[]{:S(2)}) copy-start(f32[2,1536]{1,0:T(2,128)} %get-tuple-element.75) | copy-start | bytes 36868
  350.3 39.0 %copy-start.80 = (f32[1536]{0:T(1024)S(1)}, f32[1536]{0:T(1024)}, u32[]{:S(2)}) copy-start(f32[1536]{0:T(1024)} %get-tuple-element.85) | copy-start | bytes 18436
  446.0 45.6 %collective-permute-start.2 = (bf16[256,1536]{1,0:T(8,128)(2,1)S(1)}, bf16[256,1536]{1,0:T(8,128)(2,1)S(1)}, u32[]{:S(2)}, u32[]{:S(2)}) collective-permute-start(bf16[256,1536]{1,0:T(8,128)(2,1)S(1)} %dynamic-slice_bitcast_fusion.4.rest_0_), channel_id=1, source_target_pairs={{0,8},{8,0},{16,24},{24,16},{1,9},{9,1},{17,25},{25,17},{2,10},{10... | collective-permute-start | bytes 2359304 | tf_op jit(solution)/shard_map/ppermute | solution.py:1040
  446.1 48.0 %collective-permute-start.3 = (bf16[8,96,1024]{2,1,0:T(8,128)(2,1)S(1)}, bf16[8,96,1024]{2,1,0:T(8,128)(2,1)S(1)}, u32[]{:S(2)}, u32[]{:S(2)}) collective-permute-start(bf16[8,96,1024]{2,1,0:T(8,128)(2,1)S(1)} %dynamic-slice_bitcast_fusion.1.rest_1_), channel_id=1, source_target_pairs={{0,8},{8,0},{16,24},{24,16},{1,9},{9,1},{17,25},{25,17},{2,10},{10... | collective-permute-start | bytes 4718600 | tf_op jit(solution)/shard_map/ppermute | solution.py:1040
  446.6 38.2 %copy-start.19 = (f32[2,64,1536]{2,1,0:T(8,128)S(1)}, f32[2,64,1536]{2,1,0:T(8,128)}, u32[]{:S(2)}) copy-start(f32[2,64,1536]{2,1,0:T(8,128)} %copy-done.17) | copy-start | bytes 2359300
  446.6 38.2 %copy-start.69 = (f32[2,1536]{1,0:T(2,128)S(1)}, f32[2,1536]{1,0:T(2,128)}, u32[]{:S(2)}) copy-start(f32[2,1536]{1,0:T(2,128)} %get-tuple-element.76) | copy-start | bytes 36868
  446.6 38.2 %copy-start.76 = (f32[1536]{0:T(1024)S(1)}, f32[1536]{0:T(1024)}, u32[]{:S(2)}) copy-start(f32[1536]{0:T(1024)} %get-tuple-element.82) | copy-start | bytes 18436
  446.6 38.2 %copy-start.105 = (f32[2,64]{1,0:T(2,128)S(1)}, f32[2,64]{1,0:T(2,128)}, u32[]{:S(2)}) copy-start(f32[2,64]{1,0:T(2,128)} %copy-done.104) | copy-start | bytes 1540
  446.6 38.7 %copy-start.67 = (f32[2,1536]{1,0:T(2,128)S(1)}, f32[2,1536]{1,0:T(2,128)}, u32[]{:S(2)}) copy-start(f32[2,1536]{1,0:T(2,128)} %get-tuple-element.78) | copy-start | bytes 36868
  446.6 38.7 %copy-start.74 = (f32[1536]{0:T(1024)S(1)}, f32[1536]{0:T(1024)}, u32[]{:S(2)}) copy-start(f32[1536]{0:T(1024)} %get-tuple-element.84) | copy-start | bytes 18436
  446.6 38.7 %copy-start.101 = (f32[2,64]{1,0:T(2,128)S(1)}, f32[2,64]{1,0:T(2,128)}, u32[]{:S(2)}) copy-start(f32[2,64]{1,0:T(2,128)} %copy-done.100) | copy-start | bytes 1540
  446.6 38.7 %copy-start.107 = (f32[2,64]{1,0:T(2,128)S(1)}, f32[2,64]{1,0:T(2,128)}, u32[]{:S(2)}) copy-start(f32[2,64]{1,0:T(2,128)} %copy-done.106) | copy-start | bytes 1540
  492.6 133.7 %collective-permute-start.17 = (bf16[256,1536]{1,0:T(8,128)(2,1)}, bf16[256,1536]{1,0:T(8,128)(2,1)}, u32[]{:S(2)}, u32[]{:S(2)}) collective-permute-start(bf16[256,1536]{1,0:T(8,128)(2,1)} %fusion.12.rest_0_), channel_id=1, source_target_pairs={{0,16},{8,24},{16,0},{24,8},{1,17},{9,25},{17,1},{25,9},{2,18},{10... | collective-permute-start | bytes 2359304 | tf_op jit(solution)/shard_map/ppermute | solution.py:1040
  574.6 62.3 %collective-permute-start.14 = (bf16[8,48,1024]{2,1,0:T(8,128)(2,1)}, bf16[8,48,1024]{2,1,0:T(8,128)(2,1)}, u32[]{:S(2)}, u32[]{:S(2)}) collective-permute-start(bf16[8,48,1024]{2,1,0:T(8,128)(2,1)} %dynamic-slice_bitcast_fusion.3.rest_1_), channel_id=1, source_target_pairs={{0,16},{8,24},{16,0},{24,8},{1,17},{9,25},{17,1},{25,9},{2,18},{10... | collective-permute-start | bytes 2359304 | tf_op jit(solution)/shard_map/ppermute | solution.py:1040
  581.2 53.1 %collective-permute-start.4 = (bf16[96,1536]{1,0:T(8,128)(2,1)}, bf16[96,1536]{1,0:T(8,128)(2,1)}, u32[]{:S(2)}, u32[]{:S(2)}) collective-permute-start(bf16[96,1536]{1,0:T(8,128)(2,1)} %dynamic-slice_bitcast_fusion.6.rest_1_), channel_id=1, source_target_pairs={{0,8},{8,0},{16,24},{24,16},{1,9},{9,1},{17,25},{25,17},{2,10},{10... | collective-permute-start | bytes 884744 | tf_op jit(solution)/shard_map/ppermute | solution.py:1040
  592.7 56.8 %collective-permute-start.5 = (bf16[8,96,576]{2,1,0:T(8,128)(2,1)}, bf16[8,96,576]{2,1,0:T(8,128)(2,1)}, u32[]{:S(2)}, u32[]{:S(2)}) collective-permute-start(bf16[8,96,576]{2,1,0:T(8,128)(2,1)} %dynamic-slice_bitcast_fusion.2.rest_0_), channel_id=1, source_target_pairs={{0,8},{8,0},{16,24},{24,16},{1,9},{9,1},{17,25},{25,17},{2,10},{10... | collective-permute-start | bytes 2654216 | tf_op jit(solution)/shard_map/ppermute | solution.py:1040
  626.3 17.1 %collective-permute-start.6 = (bf16[256,3072]{1,0:T(8,128)(2,1)}, bf16[256,3072]{1,0:T(8,128)(2,1)}, u32[]{:S(2)}, u32[]{:S(2)}) collective-permute-start(bf16[256,3072]{1,0:T(8,128)(2,1)} %dynamic-slice_bitcast_fusion), channel_id=1, source_target_pairs={{0,8},{8,0},{16,24},{24,16},{1,9},{9,1},{17,25},{25,17},{2,10},{10... | collective-permute-start | bytes 4718600 | tf_op jit(solution)/shard_map/ppermute | solution.py:1040
  630.2 38.7 %collective-permute-start.18 = (bf16[256,1536]{1,0:T(8,128)(2,1)}, bf16[256,1536]{1,0:T(8,128)(2,1)}, u32[]{:S(2)}, u32[]{:S(2)}) collective-permute-start(bf16[256,1536]{1,0:T(8,128)(2,1)} %add_convert_fusion.1), channel_id=1, source_target_pairs={{0,8},{8,0},{16,24},{24,16},{1,9},{9,1},{17,25},{25,17},{2,10},{10... | collective-permute-start | bytes 2359304 | tf_op jit(solution)/shard_map/ppermute | solution.py:1040
  635.3 12.5 %collective-permute-start.10 = (bf16[96,1536]{1,0:T(8,128)(2,1)S(1)}, bf16[96,1536]{1,0:T(8,128)(2,1)}, u32[]{:S(2)}, u32[]{:S(2)}) collective-permute-start(bf16[96,1536]{1,0:T(8,128)(2,1)S(1)} %fusion.43.rest_0_), channel_id=1, source_target_pairs={{0,16},{8,24},{16,0},{24,8},{1,17},{9,25},{17,1},{25,9},{2,18},{10... | collective-permute-start | bytes 884744 | tf_op jit(solution)/shard_map/ppermute | solution.py:1040
  639.2 25.0 %all-to-all-start.2 = ((bf16[8,48,1024]{2,1,0:T(8,128)(2,1)}), bf16[8,48,1024]{2,1,0:T(8,128)(2,1)}, u32[]{:S(2)}, u32[]{:S(2)}) async-start(bf16[8,48,1024]{2,1,0:T(8,128)(2,1)} %fusion.11), calls=%async_computation.2 | async-start | bytes 1572864 | tf_op jit(solution)/shard_map/all_to_all | solution.py:1316
  647.3 101.8 %collective-permute-start.12 = (bf16[256,3072]{1,0:T(8,128)(2,1)}, bf16[256,3072]{1,0:T(8,128)(2,1)}, u32[]{:S(2)}, u32[]{:S(2)}) collective-permute-start(bf16[256,3072]{1,0:T(8,128)(2,1)} %fusion.3.rest_2_), channel_id=1, source_target_pairs={{0,16},{8,24},{16,0},{24,8},{1,17},{9,25},{17,1},{25,9},{2,18},{10... | collective-permute-start | bytes 4718600 | tf_op jit(solution)/shard_map/ppermute | solution.py:1040
  649.6 22.8 %collective-permute-start.11 = (bf16[96,1536]{1,0:T(8,128)(2,1)}, bf16[96,1536]{1,0:T(8,128)(2,1)}, u32[]{:S(2)}, u32[]{:S(2)}) collective-permute-start(bf16[96,1536]{1,0:T(8,128)(2,1)} %add_convert_fusion.2), channel_id=1, source_target_pairs={{0,8},{8,0},{16,24},{24,16},{1,9},{9,1},{17,25},{25,17},{2,10},{10... | collective-permute-start | bytes 884744 | tf_op jit(solution)/shard_map/ppermute | solution.py:1040
  652.8 15.7 %copy-start.131 = (f32[3]{0:T(128)S(1)}, f32[3]{0:T(128)}, u32[]{:S(2)}) copy-start(f32[3]{0:T(128)} %get-tuple-element.106) | copy-start | bytes 40
  652.8 16.1 %copy-start.120 = (pred[512]{0:T(512)(128)(4,1)S(1)}, pred[512]{0:T(512)(128)(4,1)}, u32[]{:S(2)}) copy-start(pred[512]{0:T(512)(128)(4,1)} %iota.115) | copy-start | bytes 1540
  652.8 42.5 %collective-permute-start.7 = (bf16[8,48,576]{2,1,0:T(8,128)(2,1)}, bf16[8,48,576]{2,1,0:T(8,128)(2,1)}, u32[]{:S(2)}, u32[]{:S(2)}) collective-permute-start(bf16[8,48,576]{2,1,0:T(8,128)(2,1)} %dynamic-slice_bitcast_fusion.5.rest_1_), channel_id=1, source_target_pairs={{0,16},{8,24},{16,0},{24,8},{1,17},{9,25},{17,1},{25,9},{2,18},{10... | collective-permute-start | bytes 1327112 | tf_op jit(solution)/shard_map/ppermute | solution.py:1040
  664.3 81.9 %collective-permute-start.15 = (bf16[8,48,1024]{2,1,0:T(8,128)(2,1)}, bf16[8,48,1024]{2,1,0:T(8,128)(2,1)}, u32[]{:S(2)}, u32[]{:S(2)}) collective-permute-start(bf16[8,48,1024]{2,1,0:T(8,128)(2,1)} %all-to-all-done.2), channel_id=1, source_target_pairs={{0,16},{8,24},{16,0},{24,8},{1,17},{9,25},{17,1},{25,9},{2,18},{10... | collective-permute-start | bytes 2359304 | tf_op jit(solution)/shard_map/ppermute | solution.py:1040
  668.9 26.4 %copy-start.38 = (bf16[8,96,576]{2,1,0:T(8,128)(2,1)S(1)}, bf16[8,96,576]{2,1,0:T(8,128)(2,1)}, u32[]{:S(2)}) copy-start(bf16[8,96,576]{2,1,0:T(8,128)(2,1)} %copy-done.37) | copy-start | bytes 2654212
  697.3 56.2 %all-to-all-start.1 = ((bf16[8,48,576]{2,1,0:T(8,128)(2,1)}), bf16[8,48,576]{2,1,0:T(8,128)(2,1)}, u32[]{:S(2)}, u32[]{:S(2)}) async-start(bf16[8,48,576]{2,1,0:T(8,128)(2,1)} %fusion.40), calls=%async_computation.1 | async-start | bytes 983040 | tf_op jit(solution)/shard_map/all_to_all | solution.py:1442
  705.1 40.6 %copy-start.15 = (f32[1,128,1536]{2,1,0:T(8,128)S(1)}, f32[1,128,1536]{2,1,0:T(8,128)}, u32[]{:S(2)}) copy-start(f32[1,128,1536]{2,1,0:T(8,128)} %param.17) | copy-start | bytes 2359300
  705.1 40.6 %copy-start.71 = (f32[1536]{0:T(1024)S(1)}, f32[1536]{0:T(1024)}, u32[]{:S(2)}) copy-start(f32[1536]{0:T(1024)} %copy-done.70) | copy-start | bytes 18436
  705.1 40.6 %copy-start.113 = (f32[2,64]{1,0:T(2,128)S(1)}, f32[2,64]{1,0:T(2,128)}, u32[]{:S(2)}) copy-start(f32[2,64]{1,0:T(2,128)} %copy-done.112) | copy-start | bytes 1540
  705.1 41.1 %copy-start.123 = (pred[96]{0:T(512)(128)(4,1)S(1)}, pred[96]{0:T(512)(128)(4,1)}, u32[]{:S(2)}) copy-start(pred[96]{0:T(512)(128)(4,1)} %iota.109) | copy-start | bytes 292
  749.0 18.0 %copy-start.124 = (pred[96]{0:T(512)(128)(4,1)S(1)}, pred[96]{0:T(512)(128)(4,1)}, u32[]{:S(2)}) copy-start(pred[96]{0:T(512)(128)(4,1)} %iota.109) | copy-start | bytes 292
  749.0 54.4 %collective-permute-start.16 = (bf16[8,96,1024]{2,1,0:T(8,128)(2,1)}, bf16[8,96,1024]{2,1,0:T(8,128)(2,1)}, u32[]{:S(2)}, u32[]{:S(2)}) collective-permute-start(bf16[8,96,1024]{2,1,0:T(8,128)(2,1)} %bitcast_select_fusion.3.own), channel_id=1, source_target_pairs={{0,8},{8,0},{16,24},{24,16},{1,9},{9,1},{17,25},{25,17},{2,10},{10... | collective-permute-start | bytes 4718600 | tf_op jit(solution)/shard_map/ppermute | solution.py:1040
  752.7 55.7 %collective-permute-start.13 = (bf16[256,3072]{1,0:T(8,128)(2,1)}, bf16[256,3072]{1,0:T(8,128)(2,1)}, u32[]{:S(2)}, u32[]{:S(2)}) collective-permute-start(bf16[256,3072]{1,0:T(8,128)(2,1)} %add_convert_fusion), channel_id=1, source_target_pairs={{0,8},{8,0},{16,24},{24,16},{1,9},{9,1},{17,25},{25,17},{2,10},{10... | collective-permute-start | bytes 4718600 | tf_op jit(solution)/shard_map/ppermute | solution.py:1040
  753.5 13.5 %collective-permute-start.8 = (bf16[8,48,576]{2,1,0:T(8,128)(2,1)}, bf16[8,48,576]{2,1,0:T(8,128)(2,1)}, u32[]{:S(2)}, u32[]{:S(2)}) collective-permute-start(bf16[8,48,576]{2,1,0:T(8,128)(2,1)} %all-to-all-done.1), channel_id=1, source_target_pairs={{0,16},{8,24},{16,0},{24,8},{1,17},{9,25},{17,1},{25,9},{2,18},{10... | collective-permute-start | bytes 1327112 | tf_op jit(solution)/shard_map/ppermute | solution.py:1040
  769.3 30.4 %collective-permute-start.9 = (bf16[8,96,576]{2,1,0:T(8,128)(2,1)}, bf16[8,96,576]{2,1,0:T(8,128)(2,1)}, u32[]{:S(2)}, u32[]{:S(2)}) collective-permute-start(bf16[8,96,576]{2,1,0:T(8,128)(2,1)} %bitcast_select_fusion.4.own), channel_id=1, source_target_pairs={{0,8},{8,0},{16,24},{24,16},{1,9},{9,1},{17,25},{25,17},{2,10},{10... | collective-permute-start | bytes 2654216 | tf_op jit(solution)/shard_map/ppermute | solution.py:1040
  (114 other events, 445.9 us)

commit v4 on v3

--- a/solution.py
+++ b/solution.py
@@ -1,4 +1,5 @@
 import functools
+import math
 
 import jax
 import jax.numpy as jnp
@@ -1009,6 +1010,515 @@
     return scatter_rows(blocks, ident, 1, after)
 
 
+NEAR = pl.BlockSpec(memory_space=pltpu.VMEM)
+SCALARS = pl.BlockSpec(memory_space=pltpu.SMEM)
+NT = (((1,), (1,)), ((), ()))
+
+
+def local_params():
+    return pltpu.CompilerParams(vmem_limit_bytes=48 << 20)
+
+
+def text_item(text, item):
+    block = text[:, item]
+    return block.reshape(block.shape[0] * block.shape[1], block.shape[2])
+
+
+def lanes_to_rows(columns, rows):
+    lane = lax.broadcasted_iota(jnp.int32, (128, 128), 1)
+    held = jnp.zeros((128, 128), jnp.float32)
+    for place, column in enumerate(columns):
+        held = jnp.where(lane == place, column, held)
+    return jnp.transpose(held)[:rows]
+
+
+def rows_to_lanes(rows):
+    missing = jnp.zeros((128 - rows.shape[0], 128), jnp.float32)
+    return jnp.transpose(jnp.concatenate([rows, missing], axis=0))
+
+
+def project_kernel(attn, weight, text, proj, squares):
+    span = text.shape[-1] // 2
+    tokens = attn.shape[0]
+    for start in range(0, tokens, 256):
+        proj[start : start + 256] = jnp.dot(
+            attn[start : start + 256], weight[...], preferred_element_type=jnp.float32
+        )
+    columns = []
+    for part in range(2):
+        for start in range(0, tokens, 128):
+            block = proj[start : start + 128, part * span : (part + 1) * span]
+            columns.append(jnp.sum(block * block, axis=1, keepdims=True))
+    for item in range(text.shape[1]):
+        block = text_item(text, item)[:, :span]
+        columns.append(jnp.sum(block * block, axis=1, keepdims=True))
+    squares[...] = lanes_to_rows(columns, squares.shape[0])
+
+
+def project(attn, weight, text):
+    count = 2 * attn.shape[0] // 128 + text.shape[1]
+    return pl.pallas_call(
+        project_kernel,
+        out_shape=[
+            jax.ShapeDtypeStruct((attn.shape[0], weight.shape[1]), jnp.float32),
+            jax.ShapeDtypeStruct((-(-count // 8) * 8, 128), jnp.float32),
+        ],
+        in_specs=[NEAR] * 3,
+        out_specs=[NEAR] * 2,
+        name="project",
+        compiler_params=local_params(),
+    )(attn, weight, text)
+
+
+def tile_lane():
+    return lax.broadcasted_iota(jnp.int32, (1, 128), 1)
+
+
+def swap_halves(tile):
+    low = lax.rem(tile_lane(), 64) < 32
+    return jnp.where(low, pltpu.roll(tile, 96, 1), pltpu.roll(tile, 32, 1))
+
+
+def block_tables(tab, block, frame_lanes):
+    by_row = lax.rem(tile_lane(), 32) < frame_lanes
+    rows = 128 // COLS
+    cosines, sines = [], []
+    for row in range(rows):
+        at = pl.ds(block * rows + row, 1)
+        cosines.append(jnp.where(by_row, tab[0, at], tab[2, :COLS]))
+        sines.append(jnp.where(by_row, tab[1, at], tab[3, :COLS]))
+    return jnp.concatenate(cosines, axis=0), jnp.concatenate(sines, axis=0)
+
+
+def block_inverse(inverse, block, blocks):
+    lane = lax.broadcasted_iota(jnp.int32, (128, 128), 1)
+
+    def column(place):
+        return jnp.sum(jnp.where(lane == place, inverse, 0.0), axis=1, keepdims=True)
+
+    query, key = column(block), column(blocks + block)
+    return [query, jnp.where(tile_lane() < 64, query, key), key]
+
+
+def attend_kernel(
+    scale, width, counts, heights, text_lens, proj, totals, text, gains, text_gain, gate, w_out,
+    parts, qkv, text_kv, tab, biases, text_biases,
+):
+    ranks, items = text.shape[0], text.shape[1]
+    span = gate.shape[-1]
+    heads, size = span // 64, 64
+    tokens = proj.shape[0]
+    blocks, item_blocks = tokens // 128, tokens // 128 // items
+    seq = tokens // items
+    slots = seq // ranks
+    row_slots = slots // COLS
+    frame_pairs = size // 8
+    space_pairs = (size // 2 - frame_pairs) // 2
+
+    place = lax.rem(tile_lane(), 32)
+    frame_rate = jnp.exp(place.astype(jnp.float32) * (-math.log(10000.0) / frame_pairs))
+    row_rate = jnp.exp((place - frame_pairs).astype(jnp.float32) * (-math.log(10000.0) / space_pairs))
+    column_rate = jnp.exp(
+        (place - frame_pairs - space_pairs).astype(jnp.float32) * (-math.log(10000.0) / space_pairs)
+    )
+    is_frame = place < frame_pairs
+    rows = items * ranks * row_slots
+    which = lax.broadcasted_iota(jnp.int32, (rows, 1), 0)
+    frame_index = jnp.zeros((rows, 1), jnp.float32)
+    frame_row = jnp.zeros((rows, 1), jnp.float32)
+    seq_place = lax.broadcasted_iota(jnp.int32, (seq, 128), 0)
+    for item in range(items):
+        below = jnp.int32(0)
+        bias = jnp.zeros((seq, 128), jnp.float32)
+        for rank in range(ranks):
+            live = counts[rank * items + item]
+            for row in range(row_slots):
+                index = below + row
+                at = which == (item * ranks + rank) * row_slots + row
+                frame_index = jnp.where(at, (index // heights[item]).astype(jnp.float32), frame_index)
+                frame_row = jnp.where(at, lax.rem(index, heights[item]).astype(jnp.float32), frame_row)
+            start = rank * slots
+            inside = (seq_place >= start + live * COLS) & (seq_place < start + slots)
+            bias = jnp.where(inside, masked_score, bias)
+            below = below + live
+        biases[item] = bias
+        text_place = lax.broadcasted_iota(jnp.int32, text_biases.shape[1:], 0)
+        text_biases[item] = jnp.where(text_place >= text_lens[item], masked_score, 0.0)
+    column = lax.broadcasted_iota(jnp.int32, (COLS, 1), 0).astype(jnp.float32)
+    row_angles = jnp.where(is_frame, frame_index * frame_rate, frame_row * row_rate)
+    column_angles = column * column_rate
+    sign = jnp.where(lax.rem(tile_lane(), 64) < 32, -1.0, 1.0)
+    tab[0, :rows] = jnp.cos(row_angles)
+    tab[1, :rows] = jnp.sin(row_angles) * sign
+    tab[2, :COLS] = jnp.cos(column_angles)
+    tab[3, :COLS] = jnp.sin(column_angles) * sign
+
+    inverse = rows_to_lanes(lax.rsqrt(totals[...] / width + epsilon))
+    for item in range(items):
+        block = text_item(text, item)
+        column = inverse[:, 2 * blocks + item : 2 * blocks + item + 1]
+        text_kv[item] = jnp.concatenate(
+            [block[:, :span] * column * text_gain[...], block[:, span:]], axis=1
+        ).astype(text_kv.dtype)
+
+    @pl.loop(0, blocks)
+    def _(block):
+        at = pl.ds(pl.multiple_of(block * 128, 128), 128)
+        cosine, sine = block_tables(tab, block, frame_pairs + space_pairs)
+        inverses = block_inverse(inverse, block, blocks)
+        tiles = []
+        for tile in range(3):
+            lanes = slice(tile * 128, (tile + 1) * 128)
+            value = proj[at, lanes] * inverses[tile] * gains[:, lanes]
+            tiles.append(value * cosine + swap_halves(value) * sine)
+        qkv[at] = jnp.concatenate(tiles + [proj[at, 2 * span :]], axis=1).astype(qkv.dtype)
+
+    @pl.loop(0, blocks)
+    def _(block):
+        at = pl.ds(pl.multiple_of(block * 128, 128), 128)
+        item = block // item_blocks
+        keys_at = pl.ds(pl.multiple_of(item * seq, seq), seq)
+        bias, text_bias = biases[item], text_biases[item]
+        mixed = []
+        for head in range(heads):
+            lanes = slice(head * size, (head + 1) * size)
+
+            def part_of(ref, rows, part):
+                start = part * span + head * size
+                return ref[rows, start : start + size]
+
+            query = part_of(qkv, at, 0)
+
+            def mix(keys, values, mask):
+                scores = lax.dot_general(keys, query, NT, preferred_element_type=jnp.float32)
+                scores = scores * scale + mask
+                terms = jnp.exp(scores - jnp.max(scores, axis=0, keepdims=True))
+                probs = terms * (1.0 / jnp.sum(terms, axis=0, keepdims=True))
+                return lax.dot_general(
+                    values,
+                    probs.astype(jnp.bfloat16),
+                    (((0,), (0,)), ((), ())),
+                    preferred_element_type=jnp.float32,
+                )
+
+            out = mix(part_of(qkv, keys_at, 1), part_of(qkv, keys_at, 2), bias)
+            text_keys = text_kv[item]
+            cross = mix(
+                text_keys[:, lanes], text_keys[:, span + head * size : span + (head + 1) * size], text_bias
+            )
+            mixed.append(jnp.transpose(out) + gate[:, lanes] * jnp.transpose(cross))
+        combined = jnp.concatenate(mixed, axis=1).astype(jnp.bfloat16)
+        parts[1][at] = combined
+        parts[0][at] = jnp.dot(combined, w_out[...], preferred_element_type=jnp.float32).astype(jnp.bfloat16)
+
+
+def attend(proj, totals, text, gains, text_gain, gate, w_out, counts, heights, text_lens, head_size):
+    tokens, span, width = proj.shape[0], gate.shape[-1], w_out.shape[1]
+    items, text_rows = text.shape[1], text.shape[0] * text.shape[2]
+    low = jnp.bfloat16
+
+    def body(*refs):
+        ins, outs, scratch = refs[:10], refs[10:15], refs[15:]
+        attend_kernel(
+            head_size**-0.5, width, *ins, (outs[0], outs[1]), outs[2], outs[3], outs[4], *scratch
+        )
+
+    return pl.pallas_call(
+        body,
+        out_shape=[
+            jax.ShapeDtypeStruct((tokens, width), low),
+            jax.ShapeDtypeStruct((tokens, span), low),
+            jax.ShapeDtypeStruct((tokens, 3 * span), low),
+            jax.ShapeDtypeStruct((items, text_rows, 2 * span), low),
+            jax.ShapeDtypeStruct((4, max(tokens // COLS, COLS), 128), jnp.float32),
+        ],
+        in_specs=[SCALARS] * 3 + [NEAR] * 7,
+        out_specs=[NEAR] * 5,
+        scratch_shapes=[
+            pltpu.VMEM((items, tokens // items, 128), jnp.float32),
+            pltpu.VMEM((items, text_rows, 128), jnp.float32),
+        ],
+        name="attend",
+        compiler_params=local_params(),
+    )(counts, heights, text_lens, proj, totals, text, gains, text_gain, gate, w_out)
+
+
+def attend_back_kernel(
+    scale, width, counts, text_lens, grad, w_out, qkv, text_kv, tab, proj, totals, text, gains, text_gain, gate,
+    scaled, grad_value, text_scaled, text_value, sums, gain_sums, gate_sums,
+    grad_query, key_sum, value_sum, text_key_sum, text_value_sum, biases, text_biases,
+):
+    ranks, items = text.shape[0], text.shape[1]
+    span = gate.shape[-1]
+    heads, size = span // 64, 64
+    tokens = proj.shape[0]
+    blocks, item_blocks = tokens // 128, tokens // 128 // items
+    seq = tokens // items
+    slots = seq // ranks
+    frame_pairs = size // 8
+    space_pairs = (size // 2 - frame_pairs) // 2
+    seq_place = lax.broadcasted_iota(jnp.int32, (seq, 128), 0)
+    for item in range(items):
+        bias = jnp.zeros((seq, 128), jnp.float32)
+        for rank in range(ranks):
+            start = rank * slots
+            live = counts[rank * items + item]
+            inside = (seq_place >= start + live * COLS) & (seq_place < start + slots)
+            bias = jnp.where(inside, masked_score, bias)
+        biases[item] = bias
+        text_place = lax.broadcasted_iota(jnp.int32, text_biases.shape[1:], 0)
+        text_biases[item] = jnp.where(text_place >= text_lens[item], masked_score, 0.0)
+    key_sum[...] = jnp.zeros_like(key_sum)
+    value_sum[...] = jnp.zeros_like(value_sum)
+    text_key_sum[...] = jnp.zeros_like(text_key_sum)
+    text_value_sum[...] = jnp.zeros_like(text_value_sum)
+    gate_sums[...] = jnp.zeros_like(gate_sums)
+    gain_sums[...] = jnp.zeros_like(gain_sums)
+
+    @pl.loop(0, blocks)
+    def _(block):
+        at = pl.ds(pl.multiple_of(block * 128, 128), 128)
+        item = block // item_blocks
+        keys_at = pl.ds(pl.multiple_of(item * seq, seq), seq)
+        bias, text_bias = biases[item], text_biases[item]
+        text_keys = text_kv[item]
+        grad_combined = lax.dot_general(grad[at], w_out[...], NT, preferred_element_type=jnp.float32)
+        self_low = grad_combined.astype(jnp.bfloat16)
+        cross_low = (gate[...] * grad_combined).astype(jnp.bfloat16)
+        queries, crossed = [], []
+        for head in range(heads):
+            lanes = slice(head * size, (head + 1) * size)
+            query = qkv[at, lanes]
+
+            def back(keys, values, low_grad, mask, key_total, value_total, rows):
+                scores = lax.dot_general(keys, query, NT, preferred_element_type=jnp.float32)
+                scores = scores * scale + mask
+                terms = jnp.exp(scores - jnp.max(scores, axis=0, keepdims=True))
+                probs = terms * (1.0 / jnp.sum(terms, axis=0, keepdims=True))
+                grad_probs = lax.dot_general(values, low_grad, NT, preferred_element_type=jnp.float32)
+                inner = jnp.sum(probs * grad_probs, axis=0, keepdims=True)
+                score_low = (probs * (grad_probs - inner)).astype(jnp.bfloat16)
+                probs_low = probs.astype(jnp.bfloat16)
+                key_total[head, rows] += jnp.dot(score_low, query, preferred_element_type=jnp.float32)
+                value_total[head, rows] += jnp.dot(probs_low, low_grad, preferred_element_type=jnp.float32)
+                to_query = lax.dot_general(
+                    keys, score_low, (((0,), (0,)), ((), ())), preferred_element_type=jnp.float32
+                )
+                return to_query, probs_low
+
+            to_query, _ = back(
+                qkv[keys_at, span + head * size : span + (head + 1) * size],
+                qkv[keys_at, 2 * span + head * size : 2 * span + (head + 1) * size],
+                self_low[:, lanes],
+                bias,
+                key_sum,
+                value_sum,
+                keys_at,
+            )
+            text_values = text_keys[:, span + head * size : span + (head + 1) * size]
+            text_rows = pl.ds(pl.multiple_of(item * 128, 128), 128)
+            cross_query, cross_probs = back(
+                text_keys[:, lanes],
+                text_values,
+                cross_low[:, lanes],
+                text_bias,
+                text_key_sum,
+                text_value_sum,
+                text_rows,
+            )
+            crossed.append(
+                jnp.transpose(
+                    lax.dot_general(
+                        text_values, cross_probs, (((0,), (0,)), ((), ())), preferred_element_type=jnp.float32
+                    )
+                )
+            )
+            queries.append(jnp.transpose(to_query + cross_query))
+        grad_query[at] = jnp.concatenate(queries, axis=1) * scale
+        gate_sums[...] += jnp.sum(
+            grad_combined * jnp.concatenate(crossed, axis=1), axis=0, keepdims=True
+        )
+
+    inverse = rows_to_lanes(lax.rsqrt(totals[...] / width + epsilon))
+    columns = [[], []]
+    for block in range(blocks):
+        at = slice(block * 128, (block + 1) * 128)
+        cosine, sine = block_tables(tab, block, frame_pairs + space_pairs)
+        inverses = block_inverse(inverse, block, blocks)
+        keys = jnp.concatenate([key_sum[head, at] for head in range(heads)], axis=1) * scale
+        both = jnp.concatenate([grad_query[at], keys], axis=1)
+        products = []
+        for tile in range(3):
+            lanes = slice(tile * 128, (tile + 1) * 128)
+            value = both[:, lanes]
+            value = value * cosine - swap_halves(value) * sine
+            unit = proj[at, lanes] * inverses[tile]
+            gain_sums[0:1, lanes] += jnp.sum(value * unit, axis=0, keepdims=True)
+            value = value * gains[:, lanes]
+            scaled[at, lanes] = value
+            products.append(value * unit)
+        first = tile_lane() < 64
+        query_part = products[0] + jnp.where(first, products[1], 0.0)
+        key_part = products[2] + jnp.where(first, 0.0, products[1])
+        columns[0].append(jnp.sum(query_part, axis=1, keepdims=True))
+        columns[1].append(jnp.sum(key_part, axis=1, keepdims=True))
+        grad_value[at] = jnp.concatenate([value_sum[head, at] for head in range(heads)], axis=1).astype(
+            grad_value.dtype
+        )
+    for item in range(items):
+        at = slice(item * 128, (item + 1) * 128)
+        unit = text_item(text, item)[:, :span] * inverse[:, 2 * blocks + item : 2 * blocks + item + 1]
+        value = jnp.concatenate([text_key_sum[head, at] for head in range(heads)], axis=1) * scale
+        gain_sums[1:2, :span] += jnp.sum(value * unit, axis=0, keepdims=True)
+        value = value * text_gain[...]
+        text_scaled[at] = value
+        text_value[at] = jnp.concatenate([text_value_sum[head, at] for head in range(heads)], axis=1).astype(
+            text_value.dtype
+        )
+        columns[1].append(jnp.sum(value * unit, axis=1, keepdims=True))
+    sums[...] = lanes_to_rows(columns[0] + columns[1], sums.shape[0])
+
+
+def attend_back(
+    grad, w_out, qkv, text_kv, tab, proj, totals, text, gains, text_gain, gate, counts, text_lens, head_size
+):
+    tokens, span, width = proj.shape[0], gate.shape[-1], w_out.shape[1]
+    items, text_rows = text.shape[1], text.shape[0] * text.shape[2]
+    heads = span // head_size
+    low, single = jnp.bfloat16, jnp.float32
+    return pl.pallas_call(
+        functools.partial(attend_back_kernel, head_size**-0.5, width),
+        out_shape=[
+            jax.ShapeDtypeStruct((tokens, 2 * span), single),
+            jax.ShapeDtypeStruct((tokens, span), low),
+            jax.ShapeDtypeStruct((items * text_rows, span), single),
+            jax.ShapeDtypeStruct((items * text_rows, span), low),
+            jax.ShapeDtypeStruct(totals.shape, single),
+            jax.ShapeDtypeStruct((8, 2 * span), single),
+            jax.ShapeDtypeStruct((1, span), single),
+        ],
+        in_specs=[SCALARS] * 2 + [NEAR] * 11,
+        out_specs=[NEAR] * 7,
+        scratch_shapes=[
+            pltpu.VMEM((tokens, span), single),
+            pltpu.VMEM((heads, tokens, head_size), single),
+            pltpu.VMEM((heads, tokens, head_size), single),
+            pltpu.VMEM((heads, items * text_rows, head_size), single),
+            pltpu.VMEM((heads, items * text_rows, head_size), single),
+            pltpu.VMEM((items, tokens // items, 128), single),
+            pltpu.VMEM((items, text_rows, 128), single),
+        ],
+        name="attend_back",
+        compiler_params=local_params(),
+    )(counts, text_lens, grad, w_out, qkv, text_kv, tab, proj, totals, text, gains, text_gain, gate)
+
+
+def norms_back_kernel(width, proj, totals, sums, scaled, grad_value, text, text_scaled, text_value, qkv_low, text_low):
+    items, span = text.shape[1], grad_value.shape[-1]
+    tokens = proj.shape[0]
+    blocks = tokens // 128
+    inverse = rows_to_lanes(lax.rsqrt(totals[...] / width + epsilon))
+    means = rows_to_lanes(sums[...] / width)
+    first = tile_lane() < 64
+    for block in range(blocks):
+        at = slice(block * 128, (block + 1) * 128)
+
+        def by_tile(columns):
+            query = columns[:, block : block + 1]
+            key = columns[:, blocks + block : blocks + block + 1]
+            return [query, jnp.where(first, query, key), key]
+
+        inverses, mean = by_tile(inverse), by_tile(means)
+        tiles = []
+        for tile in range(3):
+            lanes = slice(tile * 128, (tile + 1) * 128)
+            unit = proj[at, lanes] * inverses[tile]
+            tiles.append((inverses[tile] * (scaled[at, lanes] - unit * mean[tile])).astype(qkv_low.dtype))
+        qkv_low[at] = jnp.concatenate(tiles + [grad_value[at]], axis=1)
+    for item in range(items):
+        at = slice(item * 128, (item + 1) * 128)
+        place = 2 * blocks + item
+        column, mean = inverse[:, place : place + 1], means[:, place : place + 1]
+        unit = text_item(text, item)[:, :span] * column
+        low = (column * (text_scaled[at] - unit * mean)).astype(text_low.dtype)
+        low = jnp.concatenate([low, text_value[at]], axis=1)
+        text_low[:, item] = low.reshape(text_low.shape[0], text_low.shape[2], 2 * span)
+
+
+def norms_back(proj, totals, sums, scaled, grad_value, text, text_scaled, text_value, width):
+    low = jnp.bfloat16
+    return pl.pallas_call(
+        functools.partial(norms_back_kernel, width),
+        out_shape=[
+            jax.ShapeDtypeStruct(proj.shape, low),
+            jax.ShapeDtypeStruct(text.shape, low),
+        ],
+        in_specs=[NEAR] * 8,
+        out_specs=[NEAR] * 2,
+        name="norms_back",
+        compiler_params=local_params(),
+    )(proj, totals, sums, scaled, grad_value, text, text_scaled, text_value)
+
+
+def join_kernel(bit, own, other, out):
+    mine = pl.program_id(0) == bit()
+
+    @pl.when(mine)
+    def _():
+        out[0] = own[...].astype(out.dtype)
+
+    @pl.when(jnp.logical_not(mine))
+    def _():
+        out[0] = other[...].astype(out.dtype)
+
+
+def join_rows(own, other, bit, dtype):
+    rows, width = own.shape
+    step = min(rows, 128)
+    near = pl.BlockSpec((step, width), lambda half, at: (at, 0))
+    return pl.pallas_call(
+        functools.partial(join_kernel, bit),
+        grid=(2, rows // step),
+        out_shape=jax.ShapeDtypeStruct((2, rows, width), dtype),
+        in_specs=[near, near],
+        out_specs=pl.BlockSpec((1, step, width), lambda half, at: (half, at, 0)),
+        name="join_rows",
+        compiler_params=local_params(),
+    )(own, other)
+
+
+def core_bit():
+    return lax.rem(lax.axis_index("items"), 2)
+
+
+def far_bit():
+    return lax.axis_index("items") // 2
+
+
+def join_blocks(own, other, bit):
+    ranks, rows, width = own.shape
+    block = pl.BlockSpec((1, rows, width), lambda rank: (rank, 0, 0))
+
+    def kernel(one, two, out):
+        mine = bit()
+        for half in range(2):
+
+            @pl.when(mine == half)
+            def _(half=half):
+                out[0, half * rows : (half + 1) * rows] = one[0]
+                out[0, (1 - half) * rows : (2 - half) * rows] = two[0]
+
+    return pl.pallas_call(
+        kernel,
+        grid=(ranks,),
+        out_shape=jax.ShapeDtypeStruct((ranks, 2 * rows, width), own.dtype),
+        in_specs=[block, block],
+        out_specs=pl.BlockSpec((1, 2 * rows, width), lambda rank: (rank, 0, 0)),
+        name="join_blocks",
+        compiler_params=local_params(),
+    )(own, other)
+
+
 def lay_flat(vectors):
     flat = jnp.concatenate([vector.reshape(-1) for vector in vectors])
     rows = -(-flat.size // 1024) * 8
@@ -1048,12 +1558,6 @@
 
 def add_low(one, other):
     return (one.astype(jnp.float32) + other.astype(jnp.float32)).astype(jnp.bfloat16)
-
-
-def join(own, other, index, axis):
-    shape = own.shape[:axis] + (2,) + own.shape[axis:]
-    own, other = jnp.expand_dims(own, axis), jnp.expand_dims(other, axis)
-    return jnp.where(lax.broadcasted_iota(jnp.int32, shape, axis) == index, own, other)
 
 
 def head_parallel_plan(
@@ -1129,59 +1633,15 @@
     )
     qkv_here = qkv_here.reshape(width, -1)
     modulation = modulation + ada_bias
-    counts = counts.astype(jnp.int32).reshape(ranks, items)
+    counts = counts.astype(jnp.int32)
     text_inverse = text_inverse.reshape(-1, 1)
     scale_attn = modulation[:, None, 0:width]
     gate_attn = jnp.tanh(modulation[:, None, width : 2 * width])
     scale_ffn = modulation[:, None, 2 * width : 3 * width]
     gate_ffn = jnp.tanh(modulation[:, None, 3 * width :])
 
-    below = jnp.cumsum(counts, axis=0) - counts
-    slot_row = jnp.arange(row_slots)
-    row_index = jnp.transpose(below)[:, :, None] + slot_row
-    heights = frame_rows[0][:, None, None]
-    frame_pairs = head_size // 8
-    space_pairs = (head_size // 2 - frame_pairs) // 2
-    row_angles = jnp.concatenate(
-        [
-            (row_index // heights).astype(single)[..., None] * freq_rates(frame_pairs),
-            (row_index % heights).astype(single)[..., None] * freq_rates(space_pairs),
-        ],
-        axis=-1,
-    )
-    column_angles = jnp.arange(COLS).astype(single)[:, None] * freq_rates(space_pairs)
-
-    def table(function):
-        by_row = function(row_angles)
-        by_column = function(column_angles)
-        shape = (items, ranks, row_slots, COLS)
-        whole = jnp.concatenate(
-            [
-                jnp.broadcast_to(by_row[:, :, :, None, :], shape + by_row.shape[-1:]),
-                jnp.broadcast_to(by_column, shape + by_column.shape[-1:]),
-            ],
-            axis=-1,
-        )
-        return whole.reshape(tokens, 1, head_size // 2)
-
-    cos_table = table(jnp.cos)
-    sin_table = table(jnp.sin)
-
-    def turn(values, sign):
-        shaped = values.reshape(tokens, heads_here, head_size)
-        upper = shaped[..., : head_size // 2]
-        lower = shaped[..., head_size // 2 :]
-        sines = sign * sin_table
-        turned = jnp.concatenate(
-            [upper * cos_table - lower * sines, upper * sines + lower * cos_table], axis=-1
-        )
-        return turned.reshape(tokens, width // ranks)
-
     slot_in_row = jnp.arange(slots) // COLS
     live_mask = (slot_in_row[None, :] < counts_here[0][:, None]).astype(single)[..., None]
-    key_live = (slot_in_row < jnp.transpose(counts)[:, :, None]).reshape(items, seq_len)
-    text_live = jnp.arange(text_all)[None, :] < text_len[0][:, None]
-
     def gain_here(index):
         return lax.dynamic_slice_in_dim(gains[index], place * span, span, 0)
 
@@ -1197,10 +1657,7 @@
         (gu_rows.reshape(ranks, gu_depth, 2 * hidden), attn_in)
     )
     gu_part = lax.all_to_all(gu_rows, "rows", 0, 0, tiled=True)
-    gu_pair = join(gu_part, swap(gu_part, FARS), far, 1)
-
-    qkv_proj = dot(attn_in, qkv_here)
-    query_proj, key_proj, value_proj = jnp.split(qkv_proj, 3, axis=1)
+    gu_pair = join_blocks(gu_part, swap(gu_part, FARS), far_bit)
 
     features = text_width // ranks
     features = text_width // ranks
@@ -1209,49 +1666,28 @@
     gain_text = lax.dynamic_slice_in_dim(text_gain, place * features, features, 0)
     text_norm = (text_unit * gain_text).astype(narrow)
 
-    def text_rows(values):
-        shaped = values.reshape(ranks, items, text_local, -1)
-        return jnp.swapaxes(shaped, 0, 1).reshape(items * text_all, -1)
-
     text_parts = pack_blocks(dot(text_norm, w_text).astype(narrow), 2, ranks, narrow)
-    text_proj = scatter_rows(text_parts, 2, 0)
-    tkey_proj, tval_proj = jnp.split(text_rows(text_proj), 2, axis=1)
-
-    def squares(values):
-        return jnp.sum(values * values, axis=-1)
-
-    totals = sum_vectors([squares(query_proj), squares(key_proj), squares(tkey_proj)], 3)
-    inverse_q, inverse_k, inverse_t = (
-        lax.rsqrt(total / width + epsilon)[:, None] for total in totals
-    )
-    gain_q, gain_k, gain_t = gain_here(1), gain_here(2), gain_here(6)
-    unit_q, unit_k, unit_t = query_proj * inverse_q, key_proj * inverse_k, tkey_proj * inverse_t
-
-    def by_head(values):
-        return values.reshape(items, -1, heads_here, head_size)
-
-    query = by_head(turn(unit_q * gain_q, 1.0).astype(narrow))
-    key = by_head(turn(unit_k * gain_k, 1.0).astype(narrow))
-    value = by_head(value_proj.astype(narrow))
-    tkey = by_head((unit_t * gain_t).astype(narrow))
-    tval = by_head(tval_proj.astype(narrow))
-
-    def soft(keys, mask):
-        scores = jnp.einsum("iphe,ikhe->ihpk", query, keys, preferred_element_type=single)
-        scores = jnp.where(mask[:, None, None, :], scores * score_scale, masked_score)
-        terms = jnp.exp(scores - jnp.max(scores, axis=-1, keepdims=True))
-        return terms / jnp.sum(terms, axis=-1, keepdims=True)
-
-    def mix(weights, values):
-        return jnp.einsum("ihpk,ikhe->iphe", weights, values, preferred_element_type=single)
-
-    probs = soft(key, key_live)
-    self_out = mix(probs.astype(narrow), value)
-    cross_probs = soft(tkey, text_live)
-    cross_out = mix(cross_probs.astype(narrow), tval)
+    text_proj = scatter_rows(text_parts, 2, 0).reshape(ranks, items, text_local, 2 * span)
+    qkv_proj, squares = project(attn_in, qkv_here, text_proj)
+    totals = sum_rows(squares, 3)
+    gains_both = jnp.concatenate([gain_here(1), gain_here(2)])[None]
+    gain_t = gain_here(6)[None]
     gate_here = jnp.tanh(lax.dynamic_slice_in_dim(cross_gate, place * heads_here, heads_here, 0))
-    combined = (self_out + gate_here[:, None] * cross_out).astype(narrow).reshape(tokens, span)
-    projected = scatter_tokens(dot(combined, w_out), items, 4)
+    gate_lanes = jnp.repeat(gate_here, head_size)[None]
+    out_parts, combined, qkv_bf, text_kv, tables = attend(
+        qkv_proj,
+        totals,
+        text_proj,
+        gains_both,
+        gain_t,
+        gate_lanes,
+        w_out,
+        counts,
+        frame_rows[0],
+        text_len[0],
+        head_size,
+    )
+    projected = scatter_tokens(out_parts, items, 4)
 
     unit_proj, inverse_proj = norm_parts(projected)
     norm_proj = unit_proj * gains[3]
@@ -1259,7 +1695,7 @@
     unit_mid, inverse_mid = norm_parts(middle)
     norm_mid = unit_mid * gains[4]
     ffn_in = gather_tokens((norm_mid * (1.0 + scale_ffn)).astype(narrow), 5)
-    gu_columns = join(gu_pair, swap(gu_pair, CORES), core, 1)
+    gu_columns = join_blocks(gu_pair, swap(gu_pair, CORES), core_bit)
     gu_here = gu_columns.reshape(width, 2 * w_down.shape[0])
     gate_up = dot(ffn_in, gu_here)
     gate_part, up_part = jnp.split(gate_up, 2, axis=1)
@@ -1316,63 +1752,40 @@
     rows_gu = lax.all_to_all(sum_gu, "rows", 0, 0, tiled=True)
     grad_out = weight_grad(combined, projected_low).astype(narrow).reshape(2, -1, width)
     give_out, keep_out = give_keep(grad_out, core, 0)
-    grad_combined = by_head(dot_back(projected_low, w_out))
-    self_low = grad_combined.astype(narrow)
-    cross_grad_low = (gate_here[:, None] * grad_combined).astype(narrow)
-    grad_gate = (1.0 - gate_here * gate_here) * jnp.sum(grad_combined * cross_out, axis=(0, 1, 3))
-
-    def soft_back(weights, low_grad, keys, values):
-        grad_weights = jnp.einsum(
-            "iphe,ikhe->ihpk", low_grad, values, preferred_element_type=single
-        )
-        inner = jnp.sum(weights * grad_weights, axis=-1, keepdims=True)
-        score_low = (weights * (grad_weights - inner)).astype(narrow)
-        grad_values = jnp.einsum(
-            "ihpk,iphe->ikhe", weights.astype(narrow), low_grad, preferred_element_type=single
-        )
-        grad_keys = jnp.einsum(
-            "ihpk,iphe->ikhe", score_low, query, preferred_element_type=single
-        )
-        grad_queries = mix(score_low, keys)
-        return (
-            grad_queries * score_scale,
-            (grad_keys * score_scale).reshape(-1, span),
-            grad_values.reshape(-1, span),
-        )
-
-    grad_query, grad_key, grad_value = soft_back(probs, self_low, key, value)
-    grad_query_text, grad_tkey, grad_tval = soft_back(cross_probs, cross_grad_low, tkey, tval)
-    grad_query = (grad_query + grad_query_text).reshape(tokens, span)
-    grad_query = turn(grad_query, -1.0)
-    grad_key = turn(grad_key, -1.0)
-    scaled_q, scaled_k, scaled_t = grad_query * gain_q, grad_key * gain_k, grad_tkey * gain_t
-    mean_q, mean_k, mean_t = (
-        total[:, None] / width
-        for total in sum_vectors(
-            [
-                jnp.sum(scaled_q * unit_q, axis=-1),
-                jnp.sum(scaled_k * unit_k, axis=-1),
-                jnp.sum(scaled_t * unit_t, axis=-1),
-            ],
-            10,
-        )
-    )
-    qkv_low = jnp.concatenate(
-        [
-            inverse_q * (scaled_q - unit_q * mean_q),
-            inverse_k * (scaled_k - unit_k * mean_k),
-            grad_value,
-        ],
-        axis=1,
-    ).astype(narrow)
-    text_low = jnp.concatenate(
-        [inverse_t * (scaled_t - unit_t * mean_t), grad_tval], axis=1
-    ).astype(narrow)
+    scaled, grad_value, text_scaled, text_value, sums, gain_sums, gate_sums = attend_back(
+        projected_low,
+        w_out,
+        qkv_bf,
+        text_kv,
+        tables,
+        qkv_proj,
+        totals,
+        text_proj,
+        gains_both,
+        gain_t,
+        gate_lanes,
+        counts,
+        text_len[0],
+        head_size,
+    )
+    grad_gate = (1.0 - gate_here * gate_here) * jnp.sum(
+        gate_sums.reshape(heads_here, head_size), axis=1
+    )
+    qkv_low, text_low = norms_back(
+        qkv_proj,
+        totals,
+        sum_rows(sums, 10),
+        scaled,
+        grad_value,
+        text_proj,
+        text_scaled,
+        text_value,
+        width,
+    )
     grad_qkv = weight_grad(attn_in, qkv_low).astype(narrow)
     give_qkv, keep_qkv = give_keep(grad_qkv.reshape(ranks, 2, -1, 3 * span), core, 1)
 
-    text_low = text_low.reshape(items, ranks, text_local, 2 * span)
-    text_low = jnp.swapaxes(text_low, 0, 1).reshape(items * text_all, 2 * span)
+    text_low = text_low.reshape(items * text_all, 2 * span)
     all_low = unpack_blocks(gather_rows(text_low, 12, 0, after=(give_qkv, give_out)), 2, narrow)
     half_out = add_low(keep_out, swap(give_out, CORES))
     half_qkv = add_low(keep_qkv, swap(give_qkv, CORES))
@@ -1380,14 +1793,26 @@
     grad_text = weight_grad(text_norm, all_low).astype(narrow).reshape(2, -1, 2 * width)
     give_text, keep_text = give_keep(grad_text, core, 0)
     half_text = add_low(keep_text, swap(give_text, CORES))
-    pair_gu = join(rows_gu, swap(rows_gu, FARS), far, 1).reshape(ranks, -1, 2 * hidden)
-    sum_out = add_low(half_out, swap(half_out, FARS))
-    sum_qkv = add_low(keep_qkv, swap(give_qkv, FARS))
-    sum_text = add_low(half_text, swap(half_text, FARS))
-
+    got_gu, got_out, got_qkv, got_text, got_down = (
+        swap(rows_gu, FARS),
+        swap(half_out, FARS),
+        swap(give_qkv, FARS),
+        swap(half_text, FARS),
+        swap(sum_down, CORES),
+    )
     grad_attn_in = scatter_tokens(
-        dot_back(qkv_low, qkv_here), items, 11, after=(half_out, give_qkv, half_text)
-    )
+        dot_back(qkv_low, qkv_here),
+        items,
+        11,
+        after=(half_out, give_qkv, half_text, rows_gu, sum_down),
+    )
+    grad_attn_in, got_gu, got_out, got_qkv, got_text, got_down = lax.optimization_barrier(
+        (grad_attn_in, got_gu, got_out, got_qkv, got_text, got_down)
+    )
+    pair_gu = join_blocks(rows_gu, got_gu, far_bit)
+    sum_out = add_low(half_out, got_out)
+    sum_qkv = add_low(keep_qkv, got_qkv)
+    sum_text = add_low(half_text, got_text)
     grad_scale_attn = jnp.sum(grad_attn_in * norm_in, axis=1)
     grad_norm = grad_attn_in * (1.0 + scale_attn)
     grad_zero = over_tokens(grad_norm * unit_in)
@@ -1398,12 +1823,12 @@
     grad_gains = jnp.stack(
         [
             grad_zero,
-            spread(jnp.sum(grad_query * unit_q, axis=0), width),
-            spread(jnp.sum(grad_key * unit_k, axis=0), width),
+            spread(gain_sums[0, :span], width),
+            spread(gain_sums[0, span:], width),
             grad_three,
             grad_four,
             grad_five,
-            spread(jnp.sum(grad_tkey * unit_t, axis=0), width),
+            spread(gain_sums[1, :span], width),
         ]
     )
     flat = jnp.concatenate(
@@ -1416,9 +1841,11 @@
     lanes = ranks * 128
     sum_depth = -(-flat.size // lanes)
     flat = jnp.pad(flat, (0, sum_depth * lanes - flat.size)).reshape(ranks, sum_depth, 128)
-    keep_depth = grad_modulation.size // lanes
+    time_rows = spread(time_here.astype(single), ranks * time_here.size).reshape(ranks, -1, 128)
+    grad_depth, time_depth = grad_modulation.size // lanes, time_rows.shape[1]
+    keep_depth = grad_depth + time_depth
     reduced = final_sums(
-        jnp.concatenate([flat, grad_modulation.reshape(ranks, keep_depth, 128)], axis=1),
+        jnp.concatenate([flat, grad_modulation.reshape(ranks, grad_depth, 128), time_rows], axis=1),
         sum_depth,
         13,
     )
@@ -1427,31 +1854,30 @@
     total_text_gain = flat[gains.size : gains.size + text_width]
     total_gate = flat[gains.size + text_width : gains.size + text_width + heads]
     groups = lax.axis_size("items")
-    all_modulation = jnp.swapaxes(
-        reduced[:, sum_depth:].reshape(ranks, groups, keep_depth * 128), 0, 1
-    ).reshape(groups * items, 4 * width)
-    all_time = lax.all_gather(time_here, "items", axis=0, tiled=True)
+    kept = reduced[:, sum_depth:].reshape(ranks, groups, keep_depth, 128)
+    all_modulation = jnp.swapaxes(kept[:, :, :grad_depth], 0, 1).reshape(groups * items, 4 * width)
+    all_time = lax.dynamic_index_in_dim(kept[:, :, grad_depth:], place, 0, keepdims=False)
+    all_time = all_time.reshape(groups * items, ada_depth)
     final_ada = jnp.einsum(
         "tk,tn->kn",
-        all_time.astype(single),
+        all_time,
         all_modulation,
         precision=lax.Precision.HIGHEST,
         preferred_element_type=single,
     )
     total_bias = jnp.sum(all_modulation, axis=0)
     rows_qkv = lax.all_to_all(sum_qkv, "rows", 0, 0, tiled=True)
-    pair_qkv = join(rows_qkv, swap(rows_qkv, FARS), far, 1).reshape(ranks, -1, 3 * span)
-
-    def whole_rows(half):
-        both = join(half, swap(half, CORES), core, 0).astype(single)
-        return both.reshape(-1, half.shape[-1])
+    pair_qkv = join_blocks(rows_qkv, swap(rows_qkv, FARS), far_bit)
+
+    def whole_rows(half, got):
+        return join_rows(half, got, core_bit, single).reshape(-1, half.shape[-1])
 
     sums = [
         unpack_halves(pair_qkv, swap(pair_qkv, CORES), 3),
-        whole_rows(sum_out),
-        whole_rows(sum_text),
+        whole_rows(sum_out, swap(sum_out, CORES)),
+        whole_rows(sum_text, swap(sum_text, CORES)),
         unpack_halves(pair_gu, swap(pair_gu, CORES), 2),
-        whole_rows(sum_down),
+        whole_rows(sum_down, got_down),
     ]
     return (
         output.reshape(1, items * slots, width),

time: 823 us -> 782 us (0.950)
  Pallas kernels: 446 us -> 533 us
  other arithmetic: 98.4 us -> 46.7 us
  matrix products: 85.1 us -> 43.1 us
  local copies, waits for them, and re-layouts: 110 us -> 82.6 us
    pallas_call x0 -> x11, Pallas kernels: none -> 90 us  [the longest x1 28.7 us: attend_back(): pl.pallas_call(functools.partial(attend_back_kernel, head_size ** (-0.5),...]
    dot_general x11 -> x1, matrix products: 25.6 us -> 4.3 us  [head_parallel_plan(): jnp.einsum('tk,tn->kn', all_time, all_modulation, precision=lax.Precision...]
    convert_element_type x8 -> x1, other arithmetic: 16.1 us -> 0.69 us  [head_parallel_plan(): counts = counts.astype(jnp.int32)]
    unnamed x285 -> x256, local copies, waits for them, and re-layouts: 26.8 us -> 41.1 us
    select_n x5 -> x0, other arithmetic: 12.3 us -> none  [join(): jnp.where(lax.broadcasted_iota(jnp.int32, shape, axis) == index, own, other)]
    sub x2 -> x0, matrix products: 10.3 us -> none  [soft(): terms = jnp.exp(scores - jnp.max(scores, axis=-1, keepdims=True))]
    iota x8 -> x0, local copies, waits for them, and re-layouts: 9.6 us -> none  [join(): lax.broadcasted_iota(jnp.int32, shape, axis) == index]
    ppermute x19, waiting for transfers between devices: 33.1 us -> 24.8 us  [swap(): return lax.ppermute(array, 'items', pairs)]
  transfers between devices with their start and end apart: 22 -> 22, of which waited for: 3 -> 4; matrix products, arithmetic and copies ran while one was open for 26% -> 11% of each run, Pallas kernels for 36% -> 47%
where the time goes in v4:
time: 782 us; the launch traced here: 769 us
  Pallas kernels  533 us (68%)
  local copies, waits for them, and re-layouts  82.6 us (11%)
  other arithmetic  46.7 us (6%)
  matrix products  43.1 us (6%)
  waiting for transfers between devices  37.1 us (5%)
  starting transfers between devices  24.4 us (3%)
    pallas_call x5, Pallas kernels, gather_rows(): pl.pallas_call(functools.partial(gather_kernel, axis, len(after)), out_sh...  184 us
    pallas_call x5, Pallas kernels, scatter_rows(): pl.pallas_call(functools.partial(scatter_kernel, axis, len(after)), out_s...  179 us
    unnamed x256, local copies, waits for them, and re-layouts  41.1 us
    pallas_call x1, Pallas kernels, first_transfers(): pl.pallas_call(functools.partial(first_kernel, ranks, quarters), out_shap...  34.9 us
    pallas_call x1, Pallas kernels, attend_back(): pl.pallas_call(functools.partial(attend_back_kernel, head_size ** (-0.5),...  28.7 us
    ppermute x19, waiting for transfers between devices, swap(): return lax.ppermute(array, 'items', pairs)  24.8 us
    pallas_call x4, Pallas kernels, join_blocks(): pl.pallas_call(kernel, grid=(ranks,), out_shape=jax.ShapeDtypeStruct((ran...  22.6 us
    pallas_call x1, Pallas kernels, final_sums(): pl.pallas_call(functools.partial(final_kernel, ranks, groups, sums), out_...  20.3 us
  transfers between devices with their start and end apart: 22, of which 4 were waited for; matrix products, arithmetic and copies ran while one was open for 11% of the time, Pallas kernels for 47%

profile of v4, /device:TPU:0, one launch (start us, length us, event | category | flops | bytes accessed | tf_op | source)
XLA Modules:
  0.0 769.1 jit_solution(6673767388028903179)
XLA Ops:
  0.7 2.4 fusion.16
  10.0 3.2 reshape.334
  15.7 34.9 %first_transfers_0.1 = (f32[104,128]{1,0:T(8,128)S(1)}, bf16[8,192,576]{2,1,0:T(8,128)(2,1)S(1)}, bf16[8,2,16,512]{3,2,1,0:T(8,128)(2,1)S(1)}) custom-call(f32[104,128]{1,0:T(8,128)S(1)} %pad_bitcast_fusion.own, bf16[192,4608]{1,0:T(8,128)(2,1)S(1)} %copy-done.17, bf16[2,16,4096]{2,1,0:T(8,128)(2,1)S(1)} %bitcast.138), custom_call_target="tpu_custom_call" | custom-call | tf_op jit(solution)/shard_map/first_transfers_0/pallas_call | solution.py:910
  58.2 48.5 %gather_rows_1.1 = bf16[2,8,64,1536]{3,2,1,0:T(8,128)(2,1)} custom-call(bf16[2,64,1536]{2,1,0:T(8,128)(2,1)} %multiply_convert_fusion.6.own), custom_call_target="tpu_custom_call" | custom-call | tf_op jit(solution)/shard_map/gather_rows_1/pallas_call | solution.py:562
  106.6 4.2 all-to-all-start
  113.7 29.9 %scatter_rows_2.1 = f32[256,384]{1,0:T(8,128)S(1)} custom-call(bf16[8,256,384]{2,1,0:T(8,128)(2,1)S(1)} %pack_blocks.1.parts), custom_call_target="tpu_custom_call" | custom-call | tf_op jit(solution)/shard_map/scatter_rows_2/pallas_call | solution.py:680
  143.7 4.9 project.1
  150.7 7.9 %sum_rows_3.1.refs_4_.totals = f32[24,128]{1,0:T(8,128)} custom-call(f32[24,128]{1,0:T(8,128)} %copy-done.42), custom_call_target="tpu_custom_call" | custom-call | tf_op jit(solution)/shard_map/sum_rows_3/pallas_call | solution.py:724
  167.1 19.0 %attend.1 = (bf16[1024,1536]{1,0:T(8,128)(2,1)}, bf16[1024,192]{1,0:T(8,128)(2,1)S(1)}, bf16[1024,576]{1,0:T(8,128)(2,1)S(1)}, bf16[2,128,384]{2,1,0:T(8,128)(2,1)S(1)}, f32[4,32,128]{2,1,0:T(8,128)S(1)}) custom-call(s32[16]{0:T(128)S(1)} %slice_convert_fusion.refs_0_.counts, s32[2]{0:T(128)S(1)} %bitcast.144, s32[2]{0:T(128)S(1)} %bitcast.142, ...), custom_call_target="tpu_custom_call" | custom-call | tf_op jit(solution)/shard_map/attend/pallas_call | solution.py:1226
  189.3 34.8 %scatter_rows_4.1 = f32[2,64,1536]{2,1,0:T(8,128)S(1)} custom-call(bf16[2,8,64,1536]{3,2,1,0:T(8,128)(2,1)S(1)} %bitcast.131), custom_call_target="tpu_custom_call" | custom-call | tf_op jit(solution)/shard_map/scatter_rows_4/pallas_call | solution.py:680
  224.3 5.8 join_blocks.4.one
  232.3 41.2 %gather_rows_5.1 = bf16[2,8,64,1536]{3,2,1,0:T(8,128)(2,1)} custom-call(bf16[2,64,1536]{2,1,0:T(8,128)(2,1)} %multiply_convert_fusion.5.own), custom_call_target="tpu_custom_call" | custom-call | tf_op jit(solution)/shard_map/gather_rows_5/pallas_call | solution.py:562
  275.6 6.5 join_blocks.5
  282.1 5.5 fusion.18
  292.9 39.2 %scatter_rows_6.1 = f32[2,64,1536]{2,1,0:T(8,128)S(1)} custom-call(bf16[2,8,64,1536]{3,2,1,0:T(8,128)(2,1)S(1)} %bitcast.132), custom_call_target="tpu_custom_call" | custom-call | tf_op jit(solution)/shard_map/scatter_rows_6/pallas_call | solution.py:680
  334.7 35.7 %gather_rows_7.1 = bf16[2,8,64,1536]{3,2,1,0:T(8,128)(2,1)} custom-call(bf16[2,64,1536]{2,1,0:T(8,128)(2,1)} %get-tuple-element.87.own), custom_call_target="tpu_custom_call" | custom-call | tf_op jit(solution)/shard_map/gather_rows_7/pallas_call | solution.py:562
  370.4 6.1 multiply_convert_fusion.1
  378.5 3.7 convolution_convert_fusion.5
  382.2 4.6 convolution_convert_fusion.4
  387.6 37.9 %scatter_rows_8.1 = f32[2,64,1536]{2,1,0:T(8,128)S(1)} custom-call(bf16[2,8,64,1536]{3,2,1,0:T(8,128)(2,1)S(1)} %bitcast.129, bf16[256,1536]{1,0:T(8,128)(2,1)S(1)} %dynamic-slice_bitcast_fusion.4.rest_0_, bf16[8,96,1024]{2,1,0:T(8,128)(2,1)S(1)} %dynamic-slice_bitcast_fusion.1.rest_1_), custom_call_target="tpu_custom_call" | custom-call | tf_op jit(solution)/shard_map/scatter_rows_8/pallas_call | solution.py:680
  434.8 35.4 %gather_rows_9.1 = bf16[2,8,64,1536]{3,2,1,0:T(8,128)(2,1)} custom-call(bf16[2,64,1536]{2,1,0:T(8,128)(2,1)} %multiply_convert_fusion.3.own, bf16[256,1536]{1,0:T(8,128)(2,1)} %fusion.4.rest_0_, bf16[8,48,1024]{2,1,0:T(8,128)(2,1)} %dynamic-slice_bitcast_fusion.3.rest_1_), custom_call_target="tpu_custom_call" | custom-call | tf_op jit(solution)/shard_map/gather_rows_9/pallas_call | solution.py:562
  477.0 28.7 %attend_back.1 = (f32[1024,384]{1,0:T(8,128)S(1)}, bf16[1024,192]{1,0:T(8,128)(2,1)S(1)}, f32[256,192]{1,0:T(8,128)S(1)}, bf16[256,192]{1,0:T(8,128)(2,1)S(1)}, ...) custom-call(s32[16]{0:T(128)S(1)} %copy-done.50, s32[2]{0:T(128)S(1)} %bitcast.143, ...), custom_call_target="tpu_custom_call" | custom-call | tf_op jit(solution)/shard_map/attend_back/pallas_call | solution.py:1389
  510.8 7.9 %sum_rows_10.1.sums = f32[24,128]{1,0:T(8,128)} custom-call(f32[24,128]{1,0:T(8,128)} %copy-done.41), custom_call_target="tpu_custom_call" | custom-call | tf_op jit(solution)/shard_map/sum_rows_10/pallas_call | solution.py:724
  518.7 3.0 convolution_convert_fusion.8
  522.7 2.8 norms_back.1
  527.2 3.3 convolution_convert_fusion.6
  530.5 3.9 copy.32
  536.6 23.0 %gather_rows_12.1.packed = bf16[8,256,384]{2,1,0:T(8,128)(2,1)} custom-call(bf16[256,384]{1,0:T(8,128)(2,1)} %bitcast.139, bf16[8,96,576]{2,1,0:T(8,128)(2,1)} %dynamic-slice_bitcast_fusion.2.rest_0_, bf16[96,1536]{1,0:T(8,128)(2,1)} %dynamic-slice_bitcast_fusion.6.rest_1_), custom_call_target="tpu_custom_call" | custom-call | tf_op jit(solution)/shard_map/gather_rows_12/pallas_call | solution.py:562
  567.6 2.5 add_convert_fusion.1.rest_4_.own
  570.2 4.0 convolution_convert_fusion.2
  574.3 12.8 %collective-permute-done.7 = bf16[8,48,1024]{2,1,0:T(8,128)(2,1)S(1)} collective-permute-done((bf16[8,48,1024]{2,1,0:T(8,128)(2,1)S(1)}, bf16[8,48,1024]{2,1,0:T(8,128)(2,1)S(1)}, u32[]{:S(2)}, u32[]{:S(2)}) %collective-permute-start.7) | collective-permute-done | bytes 786464 | tf_op jit(solution)/shard_map/ppermute | solution.py:1550
  588.2 4.2 all-to-all-start.1
  592.5 3.7 fusion.rest_2_
  600.4 12.3 %all-to-all-done.1.rest_3_.one = bf16[8,48,1024]{2,1,0:T(8,128)(2,1)} async-done(((bf16[8,48,1024]{2,1,0:T(8,128)(2,1)}), bf16[8,48,1024]{2,1,0:T(8,128)(2,1)}, u32[]{:S(2)}, u32[]{:S(2)}) %all-to-all-start.1) | async-done | bytes 786464 | tf_op jit(solution)/shard_map/all_to_all | solution.py:1752
  623.5 36.8 %scatter_rows_11.1 = f32[2,64,1536]{2,1,0:T(8,128)S(1)} custom-call(bf16[2,8,64,1536]{3,2,1,0:T(8,128)(2,1)S(1)} %bitcast.130, bf16[96,1536]{1,0:T(8,128)(2,1)S(1)} %fusion.7.rest_0_, bf16[8,48,576]{2,1,0:T(8,128)(2,1)} %dynamic-slice_bitcast_fusion.5.rest_1_, bf16[256,3072]{1,0:T(8,128)(2,1)} %fusion.rest_2_, ...), custom_call_target="tpu_custom_call" | custom-call | tf_op jit(solution)/shard_map/scatter_rows_11/pallas_call | solution.py:680
  661.3 4.9 collective-permute-done.11
  668.1 5.6 all-to-all-start.2
  675.5 3.6 add_convert_fusion.own
  679.7 5.5 join_blocks.7.own
  693.8 20.3 %final_sums_13.1 = f32[8,71,128]{2,1,0:T(8,128)} custom-call(f32[8,29,128]{2,1,0:T(8,128)} %pad_maximum_fusion.3.own), custom_call_target="tpu_custom_call" | custom-call | tf_op jit(solution)/shard_map/final_sums_13/pallas_call | solution.py:790
  719.6 7.1 collective-permute-done.14.two
  726.7 4.8 join_blocks.6.own
  736.2 4.2 join_rows.5
  745.0 2.8 multiply_add_fusion
  747.8 4.3 fusion.19
  754.1 5.9 join_rows.4
  760.0 5.0 unpack_halves.3
  765.0 3.7 unpack_halves.2
  (413 shorter events, 128.8 us)
Async XLA Ops:
  0.6 111.7 %copy-start = (bf16[512,3072]{1,0:T(8,128)(2,1)S(1)}, bf16[512,3072]{1,0:T(8,128)(2,1)}, u32[]{:S(2)}) copy-start(bf16[512,3072]{1,0:T(8,128)(2,1)} %param.26) | copy-start | bytes 9437188
  3.1 53.0 %copy-start.92 = (f32[1536]{0:T(1024)}, f32[1536]{0:T(1024)S(1)}, u32[]{:S(2)}) copy-start(f32[1536]{0:T(1024)S(1)} %get-tuple-element.98) | copy-start | bytes 18436
  10.0 42.6 %copy-start.113 = (f32[6144]{0:T(1024)S(1)}, f32[6144]{0:T(1024)}, u32[]{:S(2)}) copy-start(f32[6144]{0:T(1024)} %param.32) | copy-start | bytes 73732
  51.9 59.0 %copy-start.40 = (f32[104,128]{1,0:T(8,128)}, f32[104,128]{1,0:T(8,128)S(1)}, u32[]{:S(2)}) copy-start(f32[104,128]{1,0:T(8,128)S(1)} %get-tuple-element.39) | copy-start | bytes 159748
  51.9 59.8 %copy-start.18 = (bf16[8,2,16,512]{3,2,1,0:T(8,128)(2,1)}, bf16[8,2,16,512]{3,2,1,0:T(8,128)(2,1)S(1)}, u32[]{:S(2)}) copy-start(bf16[8,2,16,512]{3,2,1,0:T(8,128)(2,1)S(1)} %get-tuple-element.42) | copy-start | bytes 786436
  54.7 51.9 %copy-start.87 = (f32[2,1536]{1,0:T(2,128)}, f32[2,1536]{1,0:T(2,128)S(1)}, u32[]{:S(2)}) copy-start(f32[2,1536]{1,0:T(2,128)S(1)} %get-tuple-element.93) | copy-start | bytes 36868
  56.1 50.5 %copy-start.121 = (f32[2,64]{1,0:T(2,128)}, f32[2,64]{1,0:T(2,128)S(1)}, u32[]{:S(2)}) copy-start(f32[2,64]{1,0:T(2,128)S(1)} %rsqrt.47) | copy-start | bytes 1540
  106.6 51.9 %all-to-all-start = ((bf16[8,48,1024]{2,1,0:T(8,128)(2,1)}), bf16[8,48,1024]{2,1,0:T(8,128)(2,1)}, u32[]{:S(2)}, u32[]{:S(2)}) async-start(bf16[8,48,1024]{2,1,0:T(8,128)(2,1)} %reshape.334), calls=%async_computation | async-start | bytes 1572864 | tf_op jit(solution)/shard_map/all_to_all | solution.py:1659
  158.6 65.7 %collective-permute-start = (bf16[8,48,1024]{2,1,0:T(8,128)(2,1)}, bf16[8,48,1024]{2,1,0:T(8,128)(2,1)}, u32[]{:S(2)}, u32[]{:S(2)}) collective-permute-start(bf16[8,48,1024]{2,1,0:T(8,128)(2,1)} %all-to-all-done.one), channel_id=1, source_target_pairs={{0,16},{8,24},{16,0},{24,8},{1,17},{9,25},{17,1},{25,9},{2,18},{10... | collective-permute-start | bytes 2359304 | tf_op jit(solution)/shard_map/ppermute | solution.py:1550
  160.0 64.1 %copy-start.45 = (f32[1,192]{1,0:T(1,128)}, f32[1,192]{1,0:T(1,128)S(1)}, u32[]{:S(2)}) copy-start(f32[1,192]{1,0:T(1,128)S(1)} %get-tuple-element.105.refs_7_.text_gain) | copy-start | bytes 2308
  162.2 61.9 %copy-start.43 = (f32[1,192]{1,0:T(1,128)}, f32[1,192]{1,0:T(1,128)S(1)}, u32[]{:S(2)}) copy-start(f32[1,192]{1,0:T(1,128)S(1)} %broadcast_in_dim_reshape.3.refs_8_.gate) | copy-start | bytes 2308
  187.1 37.2 %copy-start.31 = (bf16[2,128,384]{2,1,0:T(8,128)(2,1)}, bf16[2,128,384]{2,1,0:T(8,128)(2,1)S(1)}, u32[]{:S(2)}) copy-start(bf16[2,128,384]{2,1,0:T(8,128)(2,1)S(1)} %get-tuple-element.48.text_kv) | copy-start | bytes 589828
  187.1 37.2 %copy-start.37 = (f32[4,32,128]{2,1,0:T(8,128)}, f32[4,32,128]{2,1,0:T(8,128)S(1)}, u32[]{:S(2)}) copy-start(f32[4,32,128]{2,1,0:T(8,128)S(1)} %get-tuple-element.49.tab) | copy-start | bytes 196612
  230.2 45.5 %collective-permute-start.1 = (bf16[8,96,1024]{2,1,0:T(8,128)(2,1)}, bf16[8,96,1024]{2,1,0:T(8,128)(2,1)}, u32[]{:S(2)}, u32[]{:S(2)}) collective-permute-start(bf16[8,96,1024]{2,1,0:T(8,128)(2,1)} %join_blocks.4.one), channel_id=1, source_target_pairs={{0,8},{8,0},{16,24},{24,16},{1,9},{9,1},{17,25},{25,17},{2,10},{10... | collective-permute-start | bytes 4718600 | tf_op jit(solution)/shard_map/ppermute | solution.py:1550
  275.6 57.7 %copy-start.118 = (f32[2,64]{1,0:T(2,128)}, f32[2,64]{1,0:T(2,128)S(1)}, u32[]{:S(2)}) copy-start(f32[2,64]{1,0:T(2,128)S(1)} %compare_convert_fusion) | copy-start | bytes 1540
  292.8 39.4 %copy-start.64 = (f32[1,128,1536]{2,1,0:T(8,128)S(1)}, f32[1,128,1536]{2,1,0:T(8,128)}, u32[]{:S(2)}) copy-start(f32[1,128,1536]{2,1,0:T(8,128)} %param.18) | copy-start | bytes 2359300
  292.9 39.4 %copy-start.98 = (f32[2,1536]{1,0:T(2,128)S(1)}, f32[2,1536]{1,0:T(2,128)}, u32[]{:S(2)}) copy-start(f32[2,1536]{1,0:T(2,128)} %get-tuple-element.91) | copy-start | bytes 36868
  292.9 39.4 %copy-start.101 = (f32[1536]{0:T(1024)S(1)}, f32[1536]{0:T(1024)}, u32[]{:S(2)}) copy-start(f32[1536]{0:T(1024)} %get-tuple-element.100) | copy-start | bytes 18436
  387.0 42.2 %collective-permute-start.2 = (bf16[256,1536]{1,0:T(8,128)(2,1)S(1)}, bf16[256,1536]{1,0:T(8,128)(2,1)S(1)}, u32[]{:S(2)}, u32[]{:S(2)}) collective-permute-start(bf16[256,1536]{1,0:T(8,128)(2,1)S(1)} %dynamic-slice_bitcast_fusion.4.rest_0_), channel_id=1, source_target_pairs={{0,8},{8,0},{16,24},{24,16},{1,9},{9,1},{17,25},{25,17},{2,10},{10... | collective-permute-start | bytes 2359304 | tf_op jit(solution)/shard_map/ppermute | solution.py:1550
  387.1 44.8 %collective-permute-start.3 = (bf16[8,96,1024]{2,1,0:T(8,128)(2,1)S(1)}, bf16[8,96,1024]{2,1,0:T(8,128)(2,1)S(1)}, u32[]{:S(2)}, u32[]{:S(2)}) collective-permute-start(bf16[8,96,1024]{2,1,0:T(8,128)(2,1)S(1)} %dynamic-slice_bitcast_fusion.1.rest_1_), channel_id=1, source_target_pairs={{0,8},{8,0},{16,24},{24,16},{1,9},{9,1},{17,25},{25,17},{2,10},{10... | collective-permute-start | bytes 4718600 | tf_op jit(solution)/shard_map/ppermute | solution.py:1550
  387.6 38.0 %copy-start.62 = (f32[2,64,1536]{2,1,0:T(8,128)S(1)}, f32[2,64,1536]{2,1,0:T(8,128)}, u32[]{:S(2)}) copy-start(f32[2,64,1536]{2,1,0:T(8,128)} %copy-done.60) | copy-start | bytes 2359300
  387.6 38.0 %copy-start.97 = (f32[1536]{0:T(1024)S(1)}, f32[1536]{0:T(1024)}, u32[]{:S(2)}) copy-start(f32[1536]{0:T(1024)} %get-tuple-element.97) | copy-start | bytes 18436
  387.6 38.0 %copy-start.117 = (f32[2,64]{1,0:T(2,128)S(1)}, f32[2,64]{1,0:T(2,128)}, u32[]{:S(2)}) copy-start(f32[2,64]{1,0:T(2,128)} %copy-done.116) | copy-start | bytes 1540
  387.6 39.0 %copy-start.90 = (f32[2,1536]{1,0:T(2,128)S(1)}, f32[2,1536]{1,0:T(2,128)}, u32[]{:S(2)}) copy-start(f32[2,1536]{1,0:T(2,128)} %get-tuple-element.94) | copy-start | bytes 36868
  387.6 39.0 %copy-start.95 = (f32[1536]{0:T(1024)S(1)}, f32[1536]{0:T(1024)}, u32[]{:S(2)}) copy-start(f32[1536]{0:T(1024)} %get-tuple-element.99) | copy-start | bytes 18436
  387.6 39.0 %copy-start.115 = (f32[2,64]{1,0:T(2,128)S(1)}, f32[2,64]{1,0:T(2,128)}, u32[]{:S(2)}) copy-start(f32[2,64]{1,0:T(2,128)} %copy-done.114) | copy-start | bytes 1540
  387.6 39.0 %copy-start.119 = (f32[2,64]{1,0:T(2,128)S(1)}, f32[2,64]{1,0:T(2,128)}, u32[]{:S(2)}) copy-start(f32[2,64]{1,0:T(2,128)} %copy-done.118) | copy-start | bytes 1540
  430.4 137.2 %collective-permute-start.8 = (bf16[256,1536]{1,0:T(8,128)(2,1)}, bf16[256,1536]{1,0:T(8,128)(2,1)}, u32[]{:S(2)}, u32[]{:S(2)}) collective-permute-start(bf16[256,1536]{1,0:T(8,128)(2,1)} %fusion.4.rest_0_), channel_id=1, source_target_pairs={{0,16},{8,24},{16,0},{24,8},{1,17},{9,25},{17,1},{25,9},{2,18},{10... | collective-permute-start | bytes 2359304 | tf_op jit(solution)/shard_map/ppermute | solution.py:1550
  564.5 27.9 %collective-permute-start.6 = (bf16[256,3072]{1,0:T(8,128)(2,1)}, bf16[256,3072]{1,0:T(8,128)(2,1)}, u32[]{:S(2)}, u32[]{:S(2)}) collective-permute-start(bf16[256,3072]{1,0:T(8,128)(2,1)} %dynamic-slice_bitcast_fusion), channel_id=1, source_target_pairs={{0,8},{8,0},{16,24},{24,16},{1,9},{9,1},{17,25},{25,17},{2,10},{10... | collective-permute-start | bytes 4718600 | tf_op jit(solution)/shard_map/ppermute | solution.py:1550
  566.5 31.2 %collective-permute-start.4 = (bf16[96,1536]{1,0:T(8,128)(2,1)}, bf16[96,1536]{1,0:T(8,128)(2,1)}, u32[]{:S(2)}, u32[]{:S(2)}) collective-permute-start(bf16[96,1536]{1,0:T(8,128)(2,1)} %dynamic-slice_bitcast_fusion.6.rest_1_), channel_id=1, source_target_pairs={{0,8},{8,0},{16,24},{24,16},{1,9},{9,1},{17,25},{25,17},{2,10},{10... | collective-permute-start | bytes 884744 | tf_op jit(solution)/shard_map/ppermute | solution.py:1550
  567.0 46.2 %collective-permute-start.5 = (bf16[8,96,576]{2,1,0:T(8,128)(2,1)}, bf16[8,96,576]{2,1,0:T(8,128)(2,1)}, u32[]{:S(2)}, u32[]{:S(2)}) collective-permute-start(bf16[8,96,576]{2,1,0:T(8,128)(2,1)} %dynamic-slice_bitcast_fusion.2.rest_0_), channel_id=1, source_target_pairs={{0,8},{8,0},{16,24},{24,16},{1,9},{9,1},{17,25},{25,17},{2,10},{10... | collective-permute-start | bytes 2654216 | tf_op jit(solution)/shard_map/ppermute | solution.py:1550
  567.1 19.9 %collective-permute-start.7 = (bf16[8,48,1024]{2,1,0:T(8,128)(2,1)S(1)}, bf16[8,48,1024]{2,1,0:T(8,128)(2,1)S(1)}, u32[]{:S(2)}, u32[]{:S(2)}) collective-permute-start(bf16[8,48,1024]{2,1,0:T(8,128)(2,1)S(1)} %copy-done.72), channel_id=1, source_target_pairs={{0,16},{8,24},{16,0},{24,8},{1,17},{9,25},{17,1},{25,9},{2,18},{10... | collective-permute-start | bytes 2359304 | tf_op jit(solution)/shard_map/ppermute | solution.py:1550
  570.0 91.2 %collective-permute-start.13 = (bf16[256,1536]{1,0:T(8,128)(2,1)}, bf16[256,1536]{1,0:T(8,128)(2,1)}, u32[]{:S(2)}, u32[]{:S(2)}) collective-permute-start(bf16[256,1536]{1,0:T(8,128)(2,1)} %add_convert_fusion.1.rest_4_.own), channel_id=1, source_target_pairs={{0,8},{8,0},{16,24},{24,16},{1,9},{9,1},{17,25},{25,17},{2,10},{10... | collective-permute-start | bytes 2359304 | tf_op jit(solution)/shard_map/ppermute | solution.py:1550
  588.2 24.5 %all-to-all-start.1 = ((bf16[8,48,1024]{2,1,0:T(8,128)(2,1)}), bf16[8,48,1024]{2,1,0:T(8,128)(2,1)}, u32[]{:S(2)}, u32[]{:S(2)}) async-start(bf16[8,48,1024]{2,1,0:T(8,128)(2,1)} %fusion.3), calls=%async_computation.1 | async-start | bytes 1572864 | tf_op jit(solution)/shard_map/all_to_all | solution.py:1752
  596.2 70.0 %collective-permute-start.12 = (bf16[256,3072]{1,0:T(8,128)(2,1)}, bf16[256,3072]{1,0:T(8,128)(2,1)}, u32[]{:S(2)}, u32[]{:S(2)}) collective-permute-start(bf16[256,3072]{1,0:T(8,128)(2,1)} %fusion.rest_2_), channel_id=1, source_target_pairs={{0,16},{8,24},{16,0},{24,8},{1,17},{9,25},{17,1},{25,9},{2,18},{10... | collective-permute-start | bytes 4718600 | tf_op jit(solution)/shard_map/ppermute | solution.py:1550
  598.8 62.5 %collective-permute-start.10 = (bf16[96,1536]{1,0:T(8,128)(2,1)S(1)}, bf16[96,1536]{1,0:T(8,128)(2,1)}, u32[]{:S(2)}, u32[]{:S(2)}) collective-permute-start(bf16[96,1536]{1,0:T(8,128)(2,1)S(1)} %fusion.7.rest_0_), channel_id=1, source_target_pairs={{0,16},{8,24},{16,0},{24,8},{1,17},{9,25},{17,1},{25,9},{2,18},{10... | collective-permute-start | bytes 884744 | tf_op jit(solution)/shard_map/ppermute | solution.py:1550
  612.7 53.4 %collective-permute-start.9 = (bf16[8,48,1024]{2,1,0:T(8,128)(2,1)}, bf16[8,48,1024]{2,1,0:T(8,128)(2,1)}, u32[]{:S(2)}, u32[]{:S(2)}) collective-permute-start(bf16[8,48,1024]{2,1,0:T(8,128)(2,1)} %all-to-all-done.1.rest_3_.one), channel_id=1, source_target_pairs={{0,16},{8,24},{16,0},{24,8},{1,17},{9,25},{17,1},{25,9},{2,18},{10... | collective-permute-start | bytes 2359304 | tf_op jit(solution)/shard_map/ppermute | solution.py:1550
  616.7 49.5 %collective-permute-start.11 = (bf16[8,48,576]{2,1,0:T(8,128)(2,1)}, bf16[8,48,576]{2,1,0:T(8,128)(2,1)}, u32[]{:S(2)}, u32[]{:S(2)}) collective-permute-start(bf16[8,48,576]{2,1,0:T(8,128)(2,1)} %dynamic-slice_bitcast_fusion.5.rest_1_), channel_id=1, source_target_pairs={{0,16},{8,24},{16,0},{24,8},{1,17},{9,25},{17,1},{25,9},{2,18},{10... | collective-permute-start | bytes 1327112 | tf_op jit(solution)/shard_map/ppermute | solution.py:1550
  620.8 39.5 %copy-start.102 = (f32[4096]{0:T(1024)}, f32[4096]{0:T(1024)S(1)}, u32[]{:S(2)}) copy-start(f32[4096]{0:T(1024)S(1)} %dynamic_update_slice.32) | copy-start | bytes 49156
  621.2 39.2 %copy-start.112 = (f32[1,1536]{1,0:T(1,128)}, f32[1,1536]{1,0:T(1,128)S(1)}, u32[]{:S(2)}) copy-start(f32[1,1536]{1,0:T(1,128)S(1)} %dynamic_update_slice.30) | copy-start | bytes 18436
  621.6 38.8 %copy-start.123 = (f32[24]{0:T(128)}, f32[24]{0:T(128)S(1)}, u32[]{:S(2)}) copy-start(f32[24]{0:T(128)S(1)} %multiply_dynamic-update-slice_fusion) | copy-start | bytes 292
  623.5 42.7 %copy-start.71 = (bf16[8,96,576]{2,1,0:T(8,128)(2,1)S(1)}, bf16[8,96,576]{2,1,0:T(8,128)(2,1)}, u32[]{:S(2)}) copy-start(bf16[8,96,576]{2,1,0:T(8,128)(2,1)} %copy-done.70) | copy-start | bytes 2654212
  668.1 47.7 %all-to-all-start.2 = ((bf16[8,48,576]{2,1,0:T(8,128)(2,1)}), bf16[8,48,576]{2,1,0:T(8,128)(2,1)}, u32[]{:S(2)}, u32[]{:S(2)}) async-start(bf16[8,48,576]{2,1,0:T(8,128)(2,1)} %fusion.6), calls=%async_computation.2 | async-start | bytes 983040 | tf_op jit(solution)/shard_map/all_to_all | solution.py:1869
  675.5 76.6 %collective-permute-start.16 = (bf16[96,1536]{1,0:T(8,128)(2,1)}, bf16[96,1536]{1,0:T(8,128)(2,1)S(1)}, u32[]{:S(2)}, u32[]{:S(2)}) collective-permute-start(bf16[96,1536]{1,0:T(8,128)(2,1)} %add_convert_fusion.2.own), channel_id=1, source_target_pairs={{0,8},{8,0},{16,24},{24,16},{1,9},{9,1},{17,25},{25,17},{2,10},{10... | collective-permute-start | bytes 884744 | tf_op jit(solution)/shard_map/ppermute | solution.py:1550
  679.1 75.0 %collective-permute-start.17 = (bf16[256,3072]{1,0:T(8,128)(2,1)}, bf16[256,3072]{1,0:T(8,128)(2,1)}, u32[]{:S(2)}, u32[]{:S(2)}) collective-permute-start(bf16[256,3072]{1,0:T(8,128)(2,1)} %add_convert_fusion.own), channel_id=1, source_target_pairs={{0,8},{8,0},{16,24},{24,16},{1,9},{9,1},{17,25},{25,17},{2,10},{10... | collective-permute-start | bytes 4718600 | tf_op jit(solution)/shard_map/ppermute | solution.py:1550
  685.2 74.8 %collective-permute-start.18 = (bf16[8,96,1024]{2,1,0:T(8,128)(2,1)}, bf16[8,96,1024]{2,1,0:T(8,128)(2,1)}, u32[]{:S(2)}, u32[]{:S(2)}) collective-permute-start(bf16[8,96,1024]{2,1,0:T(8,128)(2,1)} %join_blocks.7.own), channel_id=1, source_target_pairs={{0,8},{8,0},{16,24},{24,16},{1,9},{9,1},{17,25},{25,17},{2,10},{10... | collective-permute-start | bytes 4718600 | tf_op jit(solution)/shard_map/ppermute | solution.py:1550
  715.8 10.9 %collective-permute-start.14 = (bf16[8,48,576]{2,1,0:T(8,128)(2,1)}, bf16[8,48,576]{2,1,0:T(8,128)(2,1)S(1)}, u32[]{:S(2)}, u32[]{:S(2)}) collective-permute-start(bf16[8,48,576]{2,1,0:T(8,128)(2,1)} %all-to-all-done.2.one), channel_id=1, source_target_pairs={{0,16},{8,24},{16,0},{24,8},{1,17},{9,25},{17,1},{25,9},{2,18},{10... | collective-permute-start | bytes 1327112 | tf_op jit(solution)/shard_map/ppermute | solution.py:1550
  731.5 33.5 %collective-permute-start.15 = (bf16[8,96,576]{2,1,0:T(8,128)(2,1)}, bf16[8,96,576]{2,1,0:T(8,128)(2,1)}, u32[]{:S(2)}, u32[]{:S(2)}) collective-permute-start(bf16[8,96,576]{2,1,0:T(8,128)(2,1)} %join_blocks.6.own), channel_id=1, source_target_pairs={{0,8},{8,0},{16,24},{24,16},{1,9},{9,1},{17,25},{25,17},{2,10},{10... | collective-permute-start | bytes 2654216 | tf_op jit(solution)/shard_map/ppermute | solution.py:1550
  (101 other events, 450.7 us)

commit v5 on v4

--- a/solution.py
+++ b/solution.py
@@ -491,212 +491,347 @@
     return ref.at[place] if axis == 0 else ref.at[:, place]
 
 
-def gather_kernel(axis, count, own, *rest):
-    whole, local, z_send, z_recv, x_send, x_recv = rest[count:]
+CHUNKS = 2
+
+
+def partner(kind):
+    group = lax.axis_index("items")
+    if kind == "core":
+        return {"items": group + 1 - 2 * lax.rem(group, 2)}
+    return {"items": lax.rem(group + 2, 4)}
+
+
+def chunk_part(ref, chunk, start, size):
+    rows = ref.shape[0] // CHUNKS
+    middle = (slice(None),) * (len(ref.shape) - 2)
+    return ref.at[(pl.ds(chunk * rows, rows),) + middle + (pl.ds(start, size),)]
+
+
+def streams_of(width):
+    first = split_lanes(width)
+    streams = [(0, chunk, 0, first) for chunk in range(CHUNKS)]
+    if first < width:
+        streams += [(which, chunk, first, width - first) for which in range(2) for chunk in range(CHUNKS)]
+    return streams
+
+
+class Swaps:
+    def __init__(self, pairs):
+        self.arrays = tuple(array for array, _ in pairs)
+        self.kinds = tuple(kind for _, kind in pairs)
+
+    def shapes(self):
+        return [jax.ShapeDtypeStruct(array.shape, array.dtype) for array in self.arrays]
+
+    def specs(self):
+        return [pl.BlockSpec(memory_space=pl.ANY)] * len(self.arrays)
+
+    def scratch(self):
+        return [pltpu.SemaphoreType.DMA((2, max(1, len(self.arrays))))]
+
+    def partners(self, always):
+        return [(always, partner(kind)) for kind in sorted(set(self.kinds))]
+
+    def copies(self, sources, targets, semaphores):
+        return [
+            remote(source, target, semaphores.at[0, at], semaphores.at[1, at], partner(kind))
+            for at, (source, target, kind) in enumerate(zip(sources, targets, self.kinds))
+        ]
+
+
+def split_lanes(width):
+    return width - 128 * round(width / 128 / 6)
+
+
+def gather_kernel(axis, swaps, count, own, *rest):
+    number = len(swaps.kinds)
+    sources, rest = rest[:number], rest[number + count :]
+    whole, targets, rest = rest[0], rest[1 : 1 + number], rest[1 + number :]
+    local, z_send, z_recv, x_send, x_recv, beside = rest
     line, side = row_place()
     above, below, across = on_rows(line + 1, side), on_rows(line - 1, side), on_rows(line, 1 - side)
-    has_above, has_below = line < DEPTH - 1, line > 0
-    greet([(has_above, above), (has_below, below), (line >= 0, across)])
-
-    def block(at, which):
-        return shard_of(whole, at * BREADTH + which, axis)
-
-    def pass_on(source, at, way, device):
-        return remote(source, block(at, side), z_send.at[way, at], z_recv.at[at], device)
-
-    def cross(source, at):
-        return remote(source, block(at, side), x_send.at[at], x_recv.at[at], across)
-
-    cross(own, line).start()
-
-    @pl.when(has_above)
-    def _():
-        pass_on(own, line, 0, above).start()
-
-    @pl.when(has_below)
-    def _():
-        pass_on(own, line, 1, below).start()
-
-    keep = pltpu.make_async_copy(own, block(line, side), local)
+    has_above, has_below, always = line < DEPTH - 1, line > 0, line >= 0
+    greet([(has_above, above), (has_below, below), (always, across)] + swaps.partners(always))
+    extra = swaps.copies(sources, targets, beside)
+    for copy in extra:
+        copy.start()
+    streams = streams_of(own.shape[-1])
+    along, over = range(CHUNKS), range(CHUNKS, len(streams))
+
+    def block(at, stream):
+        which, *piece = streams[stream]
+        return chunk_part(shard_of(whole, at * BREADTH + (1 - side if which else side), axis), *piece)
+
+    def mine(stream):
+        return chunk_part(own, *streams[stream][1:])
+
+    def pass_on(stream, source, at, way):
+        return remote(
+            source,
+            block(at, stream),
+            z_send.at[stream, way, at],
+            z_recv.at[stream, at],
+            below if way else above,
+        )
+
+    def cross(source, at, stream):
+        slot = stream * DEPTH + at if stream < CHUNKS else CHUNKS * DEPTH + stream - CHUNKS
+        return remote(source, block(at, stream), x_send.at[slot], x_recv.at[slot], across)
+
+    def onward(stream, source):
+        @pl.when(has_above)
+        def _():
+            pass_on(stream, source, line, 0).start()
+
+        @pl.when(has_below)
+        def _():
+            pass_on(stream, source, line, 1).start()
+
+    handed = [stream for stream in over if streams[stream][0] == 0]
+    for stream in handed + list(along):
+        cross(mine(stream), line, stream).start()
+    for stream in list(along) + handed:
+        onward(stream, mine(stream))
+    keep = pltpu.make_async_copy(own, shard_of(whole, line * BREADTH + side, axis), local)
     keep.start()
+    for stream in handed:
+        cross(mine(stream), line, stream).wait_recv()
+        onward(stream + CHUNKS, block(line, stream + CHUNKS))
     for step in range(1, DEPTH):
-
-        @pl.when(line - step >= 0)
-        def _(at=line - step):
-            pass_on(own, at, 0, below).wait_recv()
-
-            @pl.when(has_above)
-            def _():
-                pass_on(block(at, side), at, 0, above).start()
-
-            cross(block(at, side), at).start()
-
-        @pl.when(line + step < DEPTH)
-        def _(at=line + step):
-            pass_on(own, at, 1, above).wait_recv()
-
-            @pl.when(has_below)
-            def _():
-                pass_on(block(at, side), at, 1, below).start()
-
-            cross(block(at, side), at).start()
+        for way, at, there, more in (
+            (0, line - step, line - step >= 0, has_above),
+            (1, line + step, line + step < DEPTH, has_below),
+        ):
+
+            @pl.when(there)
+            def _(way=way, at=at, more=more):
+                for stream in range(len(streams)):
+                    pass_on(stream, block(at, stream), at, way).wait_recv()
+                    if stream in along:
+                        cross(block(at, stream), at, stream).start()
+
+                    @pl.when(more)
+                    def _(stream=stream):
+                        pass_on(stream, block(at, stream), at, way).start()
 
     keep.wait()
     for at in range(DEPTH):
-        cross(own, at).wait_recv()
-        cross(own, at).wait_send()
-
-        @pl.when(has_above & (at <= line))
-        def _(at=at):
-            pass_on(own, at, 0, above).wait_send()
-
-        @pl.when(has_below & (at >= line))
-        def _(at=at):
-            pass_on(own, at, 1, below).wait_send()
-
-
-def gather_rows(block, ident, axis, after=()):
+        for stream in along:
+            cross(mine(stream), at, stream).wait_recv()
+            cross(mine(stream), at, stream).wait_send()
+        for stream in range(len(streams)):
+
+            @pl.when(has_above & (at <= line))
+            def _(at=at, stream=stream):
+                pass_on(stream, block(at, stream), at, 0).wait_send()
+
+            @pl.when(has_below & (at >= line))
+            def _(at=at, stream=stream):
+                pass_on(stream, block(at, stream), at, 1).wait_send()
+
+    for stream in handed:
+        cross(mine(stream), line, stream).wait_send()
+    for copy in extra:
+        copy.wait()
+
+
+def gather_rows(block, ident, axis, after=(), swaps=()):
     ranks = DEPTH * BREADTH
+    swaps = Swaps(swaps)
     shape = block.shape[:axis] + (ranks,) + block.shape[axis:]
     anywhere = pl.BlockSpec(memory_space=pl.ANY)
-    return pl.pallas_call(
-        functools.partial(gather_kernel, axis, len(after)),
-        out_shape=jax.ShapeDtypeStruct(shape, block.dtype),
-        in_specs=[anywhere] * (1 + len(after)),
-        out_specs=anywhere,
+    wave = pltpu.SemaphoreType.DMA
+    whole, *others = pl.pallas_call(
+        functools.partial(gather_kernel, axis, swaps, len(after)),
+        out_shape=[jax.ShapeDtypeStruct(shape, block.dtype)] + swaps.shapes(),
+        in_specs=[anywhere] * (1 + len(swaps.kinds) + len(after)),
+        out_specs=[anywhere] + swaps.specs(),
         scratch_shapes=[
-            pltpu.SemaphoreType.DMA,
-            pltpu.SemaphoreType.DMA((2, DEPTH)),
-            pltpu.SemaphoreType.DMA((DEPTH,)),
-            pltpu.SemaphoreType.DMA((DEPTH,)),
-            pltpu.SemaphoreType.DMA((DEPTH,)),
-        ],
+            wave,
+            wave((3 * CHUNKS, 2, DEPTH)),
+            wave((3 * CHUNKS, DEPTH)),
+            wave((CHUNKS * (DEPTH + 1),)),
+            wave((CHUNKS * (DEPTH + 1),)),
+        ]
+        + swaps.scratch(),
         name=f"gather_rows_{ident}",
         compiler_params=pltpu.CompilerParams(collective_id=ident, has_side_effects=True),
-    )(block, *after)
-
-
-def scatter_kernel(axis, count, parts, *rest):
-    total, crossed, risen, sunk, up, down, x_send, x_recv, z_send, z_recv = rest[count:]
+    )(block, *swaps.arrays, *after)
+    return (whole, *others) if others else whole
+
+
+def scatter_kernel(axis, swaps, count, parts, *rest):
+    number = len(swaps.kinds)
+    sources, rest = rest[:number], rest[number + count :]
+    total, targets, rest = rest[0], rest[1 : 1 + number], rest[1 + number :]
+    crossed, flow, x_send, x_recv, z_send, z_recv, beside = rest[0], rest[1:-5], *rest[-5:]
     line, side = row_place()
     above, below, across = on_rows(line + 1, side), on_rows(line - 1, side), on_rows(line, 1 - side)
-    has_above, has_below = line < DEPTH - 1, line > 0
-    greet([(has_above, above), (has_below, below), (line >= 0, across)])
-
-    def part(at, which):
-        return shard_of(parts, at * BREADTH + which, axis)
-
-    def cross(at):
-        return remote(part(at, 1 - side), crossed.at[at], x_send.at[at], x_recv.at[at], across)
-
-    def rise(at):
-        return remote(up.at[at], risen.at[at], z_send.at[0, at], z_recv.at[0, at], above)
-
-    def sink(at):
-        return remote(down.at[at], sunk.at[at], z_send.at[1, at], z_recv.at[1, at], below)
-
-    def add_up(at, others, target):
-        mine = part(at, side)
-        whole = mine.shape
-        value = mine[...].astype(jnp.float32) + crossed[at].astype(jnp.float32)
+    has_above, has_below, always = line < DEPTH - 1, line > 0, line >= 0
+    greet([(has_above, above), (has_below, below), (always, across)] + swaps.partners(always))
+    extra = swaps.copies(sources, targets, beside)
+    for copy in extra:
+        copy.start()
+    streams = streams_of(parts.shape[-1])
+    along, over = range(CHUNKS), range(CHUNKS, len(streams))
+    handed = [stream for stream in over if streams[stream][0] == 1]
+
+    def part(at, stream, turned=False):
+        other, *piece = streams[stream]
+        return chunk_part(shard_of(parts, at * BREADTH + (1 - side if other or turned else side), axis), *piece)
+
+    def slot(ref, at, stream):
+        chunk = streams[stream][1]
+        rows = ref.shape[1] // CHUNKS
+        return ref.at[at, pl.ds(chunk * rows, rows)]
+
+    def cross(at, stream):
+        place = stream * DEPTH + at
+        return remote(
+            part(at, stream, True), slot(crossed, at, stream), x_send.at[place], x_recv.at[place], across
+        )
+
+    def hand(stream):
+        place = CHUNKS * DEPTH + stream - handed[0]
+        leave, arrive = flow[12], flow[13]
+        return remote(
+            slot(leave, 0, stream), slot(arrive, 0, stream), x_send.at[place], x_recv.at[place], across
+        )
+
+    def held(stream, way, leaving):
+        group = 0 if stream in along else 1 + streams[stream][0]
+        return flow[4 * group + 2 * way + leaving]
+
+    def moving(stream, at, way):
+        return remote(
+            slot(held(stream, way, 1), at, stream),
+            slot(held(stream, way, 0), at, stream),
+            z_send.at[stream, way, at],
+            z_recv.at[stream, way, at],
+            below if way else above,
+        )
+
+    def add_up(stream, at, ways, target, others=()):
+        value = part(at, stream)[...].astype(jnp.float32)
+        if stream in along:
+            value = value + slot(crossed, at, stream)[...].astype(jnp.float32)
+        for way in ways:
+            value = value + slot(held(stream, way, 0), at, stream)[...].astype(jnp.float32)
         for other in others:
-            value = value + other[at].astype(jnp.float32)
+            value = value + other[...].astype(jnp.float32)
         target[...] = value.astype(target.dtype)
+
+    def send_on(stream, at, way, comes):
+        leaving = slot(held(stream, way, 1), at, stream)
+
+        @pl.when(comes)
+        def _():
+            moving(stream, at, way).wait_recv()
+            add_up(stream, at, [way], leaving)
+
+        @pl.when(jnp.logical_not(comes))
+        def _():
+            add_up(stream, at, [], leaving)
+
+        moving(stream, at, way).start()
+
+    def finish(stream, target, others=()):
+        for below_there, above_there, ways in ((True, True, [0, 1]), (True, False, [0]), (False, True, [1])):
+
+            @pl.when((has_below == below_there) & (has_above == above_there))
+            def _(ways=ways):
+                for way in ways:
+                    moving(stream, line, way).wait_recv()
+                add_up(stream, line, ways, target, others)
 
     for step in range(DEPTH - 1, 0, -1):
         for at, there in ((line + step, line + step < DEPTH), (line - step, line - step >= 0)):
 
             @pl.when(there)
             def _(at=at):
-                cross(at).start()
-
-    cross(line).start()
-    for step in range(DEPTH - 1, 0, -1):
-
-        @pl.when(line + step < DEPTH)
-        def _(at=line + step):
-            cross(at).wait_recv()
-
-            @pl.when(has_below)
-            def _():
-                rise(at).wait_recv()
-                add_up(at, [risen], up.at[at])
-
-            @pl.when(jnp.logical_not(has_below))
-            def _():
-                add_up(at, [], up.at[at])
-
-            rise(at).start()
-
-        @pl.when(line - step >= 0)
-        def _(at=line - step):
-            cross(at).wait_recv()
-
-            @pl.when(has_above)
-            def _():
-                sink(at).wait_recv()
-                add_up(at, [sunk], down.at[at])
-
-            @pl.when(jnp.logical_not(has_above))
-            def _():
-                add_up(at, [], down.at[at])
-
-            sink(at).start()
-
-    cross(line).wait_recv()
-
-    @pl.when(has_below & has_above)
-    def _():
-        rise(line).wait_recv()
-        sink(line).wait_recv()
-        add_up(line, [risen, sunk], total)
-
-    @pl.when(jnp.logical_not(has_above))
-    def _():
-        rise(line).wait_recv()
-        add_up(line, [risen], total)
-
-    @pl.when(jnp.logical_not(has_below))
-    def _():
-        sink(line).wait_recv()
-        add_up(line, [sunk], total)
-
+                for stream in along:
+                    cross(at, stream).start()
+
+    for stream in along:
+        cross(line, stream).start()
+    for some in (over, along):
+        for step in range(DEPTH - 1, 0, -1):
+            for way, at, there, comes in (
+                (0, line + step, line + step < DEPTH, has_below),
+                (1, line - step, line - step >= 0, has_above),
+            ):
+                for stream in some:
+
+                    @pl.when(there)
+                    def _(way=way, at=at, comes=comes, stream=stream):
+                        if stream in along:
+                            cross(at, stream).wait_recv()
+                        send_on(stream, at, way, comes)
+
+        if some is over:
+            for stream in handed:
+                finish(stream, slot(flow[12], 0, stream))
+                hand(stream).start()
+
+    for stream in along:
+        cross(line, stream).wait_recv()
+        finish(stream, chunk_part(total, *streams[stream][1:]))
+    for stream in handed:
+        hand(stream).wait_recv()
+        mate = stream - CHUNKS
+        finish(mate, chunk_part(total, *streams[mate][1:]), (slot(flow[13], 0, stream),))
+        hand(stream).wait_send()
     for at in range(DEPTH):
-        cross(at).wait_send()
-
-        @pl.when(at > line)
-        def _(at=at):
-            rise(at).wait_send()
-
-        @pl.when(at < line)
-        def _(at=at):
-            sink(at).wait_send()
-
-
-def scatter_rows(parts, ident, axis, after=()):
+        for stream in along:
+            cross(at, stream).wait_send()
+        for stream in range(len(streams)):
+
+            @pl.when(at > line)
+            def _(at=at, stream=stream):
+                moving(stream, at, 0).wait_send()
+
+            @pl.when(at < line)
+            def _(at=at, stream=stream):
+                moving(stream, at, 1).wait_send()
+
+    for copy in extra:
+        copy.wait()
+
+
+def scatter_rows(parts, ident, axis, after=(), swaps=()):
+    swaps = Swaps(swaps)
     shape = parts.shape[:axis] + parts.shape[axis + 1 :]
+    width = shape[-1]
+    first = split_lanes(width)
     near = pl.BlockSpec(memory_space=pltpu.VMEM)
-    slots = pltpu.VMEM((DEPTH,) + shape, parts.dtype)
-    return pl.pallas_call(
-        functools.partial(scatter_kernel, axis, len(after)),
-        out_shape=jax.ShapeDtypeStruct(shape, jnp.float32),
-        in_specs=[near] + [pl.BlockSpec(memory_space=pl.ANY)] * len(after),
-        out_specs=near,
-        scratch_shapes=[slots] * 5
-        + [
-            pltpu.SemaphoreType.DMA((DEPTH,)),
-            pltpu.SemaphoreType.DMA((DEPTH,)),
-            pltpu.SemaphoreType.DMA((2, DEPTH)),
-            pltpu.SemaphoreType.DMA((2, DEPTH)),
-        ],
+    wave = pltpu.SemaphoreType.DMA
+
+    def slots(size, count=(DEPTH,)):
+        return pltpu.VMEM(count + shape[:-1] + (size,), parts.dtype)
+
+    flow = [slots(first)] * 4
+    if first < width:
+        flow = flow + [slots(width - first)] * 8 + [slots(width - first, (1,))] * 2
+    total, *others = pl.pallas_call(
+        functools.partial(scatter_kernel, axis, swaps, len(after)),
+        out_shape=[jax.ShapeDtypeStruct(shape, jnp.float32)] + swaps.shapes(),
+        in_specs=[near] + [pl.BlockSpec(memory_space=pl.ANY)] * (len(swaps.kinds) + len(after)),
+        out_specs=[near] + swaps.specs(),
+        scratch_shapes=[slots(first)]
+        + flow
+        + [wave((CHUNKS * (DEPTH + 1),))] * 2
+        + [wave((3 * CHUNKS, 2, DEPTH))] * 2
+        + swaps.scratch(),
         name=f"scatter_rows_{ident}",
         compiler_params=pltpu.CompilerParams(
             collective_id=ident, has_side_effects=True, vmem_limit_bytes=32 << 20
         ),
-    )(parts, *after)
-
-
-def sum_kernel(own, total, held, send, receive):
+    )(parts, *swaps.arrays, *after)
+    return (total, *others) if others else total
+
+
+def sum_kernel(count, own, *rest):
+    total, held, send, receive = rest[count:]
     ranks = DEPTH * BREADTH
     place = lax.axis_index("rows")
     others = [lax.rem(place + step, ranks) for step in range(1, ranks)]
@@ -718,13 +853,13 @@
         push(step, other, place).wait_send()
 
 
-def sum_rows(own, ident):
+def sum_rows(own, ident, after=()):
     ranks = DEPTH * BREADTH
     near = pl.BlockSpec(memory_space=pltpu.VMEM)
     return pl.pallas_call(
-        sum_kernel,
+        functools.partial(sum_kernel, len(after)),
         out_shape=jax.ShapeDtypeStruct(own.shape, own.dtype),
-        in_specs=[near],
+        in_specs=[near] + [pl.BlockSpec(memory_space=pl.ANY)] * len(after),
         out_specs=near,
         scratch_shapes=[
             pltpu.VMEM((ranks,) + own.shape, own.dtype),
@@ -733,14 +868,20 @@
         ],
         name=f"sum_rows_{ident}",
         compiler_params=pltpu.CompilerParams(collective_id=ident, has_side_effects=True),
-    )(own)
-
-
-def final_kernel(ranks, groups, sums, own, out, held, kept, part, h_send, h_recv, g_send, g_recv, o_send, o_recv):
+    )(own, *after)
+
+
+def final_kernel(ranks, groups, sums, swaps, own, *rest):
+    number = len(swaps.kinds)
+    sources, out, targets, rest = rest[:number], rest[number], rest[number + 1 : 2 * number + 1], rest[2 * number + 1 :]
+    held, kept, part, h_send, h_recv, g_send, g_recv, o_send, o_recv, beside = rest
     place, group = lax.axis_index("rows"), lax.axis_index("items")
     rows = [lax.rem(place + step, ranks) for step in range(1, ranks)]
     items = [lax.rem(group + step, groups) for step in range(1, groups)]
     greet([(place >= 0, {"rows": other}) for other in rows] + [(place >= 0, {"items": other}) for other in items])
+    extra = swaps.copies(sources, targets, beside)
+    for copy in extra:
+        copy.start()
 
     def push(step, other, slot):
         return remote(own.at[other], held.at[slot], h_send.at[step], h_recv.at[slot], {"rows": other})
@@ -781,17 +922,20 @@
         share(step, other, place).wait_send()
     for step, other in enumerate(items):
         swap(step, other, group).wait_send()
-
-
-def final_sums(own, sums, ident):
+    for copy in extra:
+        copy.wait()
+
+
+def final_sums(own, sums, ident, swaps=()):
     ranks, groups = lax.axis_size("rows"), lax.axis_size("items")
     near = pl.BlockSpec(memory_space=pltpu.VMEM)
     depth = own.shape[1]
+    swaps = Swaps(swaps)
     return pl.pallas_call(
-        functools.partial(final_kernel, ranks, groups, sums),
-        out_shape=jax.ShapeDtypeStruct((ranks, sums + groups * (depth - sums), 128), own.dtype),
-        in_specs=[near],
-        out_specs=near,
+        functools.partial(final_kernel, ranks, groups, sums, swaps),
+        out_shape=[jax.ShapeDtypeStruct((ranks, sums + groups * (depth - sums), 128), own.dtype)] + swaps.shapes(),
+        in_specs=[near] + swaps.specs(),
+        out_specs=[near] + swaps.specs(),
         scratch_shapes=[
             pltpu.VMEM(own.shape, own.dtype),
             pltpu.VMEM((groups,) + own.shape[1:], own.dtype),
@@ -802,10 +946,11 @@
             pltpu.SemaphoreType.DMA((groups,)),
             pltpu.SemaphoreType.DMA((ranks,)),
             pltpu.SemaphoreType.DMA((ranks,)),
-        ],
+        ]
+        + swaps.scratch(),
         name=f"final_sums_{ident}",
         compiler_params=pltpu.CompilerParams(collective_id=ident, has_side_effects=True),
-    )(own)
+    )(own, *swaps.arrays)
 
 
 def first_kernel(
@@ -926,6 +1071,31 @@
     )(own, qkv, text)
 
 
+def quarter_kernel(pieces, at, whole, packed):
+    ranks, span = packed.shape[0], packed.shape[2] // pieces
+    for rank in range(ranks):
+        for piece in range(pieces):
+            start = (piece * ranks + rank) * span
+            packed[rank, :, piece * span : (piece + 1) * span] = whole[:, start : start + span]
+
+
+def pack_quarter(whole, at, pieces, ranks):
+    rows, width = whole.shape[0] // 4, whole.shape[1]
+    out = (ranks, rows, width // ranks)
+    return pl.pallas_call(
+        functools.partial(quarter_kernel, pieces),
+        grid_spec=pltpu.PrefetchScalarGridSpec(
+            num_scalar_prefetch=1,
+            grid=(1,),
+            in_specs=[pl.BlockSpec((rows, width), lambda step, at: (at[0], 0))],
+            out_specs=pl.BlockSpec(out, lambda step, at: (0, 0, 0)),
+        ),
+        out_shape=jax.ShapeDtypeStruct(out, whole.dtype),
+        name="pack_quarter",
+        compiler_params=local_params(),
+    )(at, whole)
+
+
 def pack_kernel(pieces, whole, packed):
     ranks, span = packed.shape[0], packed.shape[2] // pieces
     for rank in range(ranks):
@@ -999,15 +1169,17 @@
     )(own, other)
 
 
-def gather_tokens(block, ident, after=()):
-    whole = gather_rows(block, ident, 1, after)
-    return whole.reshape(-1, block.shape[-1])
-
-
-def scatter_tokens(partial, items, ident, after=()):
+def gather_tokens(block, ident, swaps=()):
+    whole = gather_rows(block, ident, 1, swaps=swaps)
+    if not swaps:
+        return whole.reshape(-1, block.shape[-1])
+    return (whole[0].reshape(-1, block.shape[-1]), *whole[1:])
+
+
+def scatter_tokens(partial, items, ident, swaps=()):
     ranks = lax.axis_size("rows")
     blocks = partial.astype(jnp.bfloat16).reshape(items, ranks, -1, partial.shape[-1])
-    return scatter_rows(blocks, ident, 1, after)
+    return scatter_rows(blocks, ident, 1, swaps=swaps)
 
 
 NEAR = pl.BlockSpec(memory_space=pltpu.VMEM)
@@ -1380,14 +1552,18 @@
 
 
 def attend_back(
-    grad, w_out, qkv, text_kv, tab, proj, totals, text, gains, text_gain, gate, counts, text_lens, head_size
+    grad, w_out, qkv, text_kv, tab, proj, totals, text, gains, text_gain, gate, counts, text_lens, head_size, after
 ):
     tokens, span, width = proj.shape[0], gate.shape[-1], w_out.shape[1]
     items, text_rows = text.shape[1], text.shape[0] * text.shape[2]
     heads = span // head_size
     low, single = jnp.bfloat16, jnp.float32
+
+    def body(*refs):
+        attend_back_kernel(head_size**-0.5, width, *refs[:13], *refs[13 + len(after) :])
+
     return pl.pallas_call(
-        functools.partial(attend_back_kernel, head_size**-0.5, width),
+        body,
         out_shape=[
             jax.ShapeDtypeStruct((tokens, 2 * span), single),
             jax.ShapeDtypeStruct((tokens, span), low),
@@ -1397,7 +1573,7 @@
             jax.ShapeDtypeStruct((8, 2 * span), single),
             jax.ShapeDtypeStruct((1, span), single),
         ],
-        in_specs=[SCALARS] * 2 + [NEAR] * 11,
+        in_specs=[SCALARS] * 2 + [NEAR] * 11 + [pl.BlockSpec(memory_space=pl.ANY)] * len(after),
         out_specs=[NEAR] * 7,
         scratch_shapes=[
             pltpu.VMEM((tokens, span), single),
@@ -1410,7 +1586,7 @@
         ],
         name="attend_back",
         compiler_params=local_params(),
-    )(counts, text_lens, grad, w_out, qkv, text_kv, tab, proj, totals, text, gains, text_gain, gate)
+    )(counts, text_lens, grad, w_out, qkv, text_kv, tab, proj, totals, text, gains, text_gain, gate, *after)
 
 
 def norms_back_kernel(width, proj, totals, sums, scaled, grad_value, text, text_scaled, text_value, qkv_low, text_low):
@@ -1650,12 +1826,8 @@
     norm_in = unit_in * gains[0]
     attn_in = gather_tokens((norm_in * (1.0 + scale_attn)).astype(narrow), 1)
     hidden = w_down.shape[0]
-    gu_depth = w_gu.shape[0] // 4
-    gu_rows = lax.dynamic_slice_in_dim(w_gu, (2 * core + far) * gu_depth, gu_depth, 0)
-    gu_rows = jnp.transpose(gu_rows.reshape(gu_depth, 2, ranks, hidden), (2, 0, 1, 3))
-    gu_rows, attn_in = lax.optimization_barrier(
-        (gu_rows.reshape(ranks, gu_depth, 2 * hidden), attn_in)
-    )
+    gu_rows = pack_quarter(w_gu, (2 * core + far).reshape(1), 2, ranks)
+    gu_rows, attn_in = lax.optimization_barrier((gu_rows, attn_in))
     gu_part = lax.all_to_all(gu_rows, "rows", 0, 0, tiled=True)
     gu_pair = join_blocks(gu_part, swap(gu_part, FARS), far_bit)
 
@@ -1728,11 +1900,11 @@
     ).astype(narrow)
     grad_gu = weight_grad(ffn_in, gate_up_low).astype(narrow)
     give_gu, keep_gu = give_keep(grad_gu.reshape(ranks, 2, -1, 2 * hidden), core, 1)
-    grad_ffn_in = scatter_tokens(
-        dot_back(gate_up_low, gu_here), items, 8, after=(give_down, give_gu)
-    )
-    half_down = add_low(keep_down, swap(give_down, CORES))
-    half_gu = add_low(keep_gu, swap(give_gu, CORES))
+    grad_ffn_in, got_down, got_gu = scatter_tokens(
+        dot_back(gate_up_low, gu_here), items, 8, swaps=((give_down, "core"), (give_gu, "core"))
+    )
+    half_down = add_low(keep_down, got_down)
+    half_gu = add_low(keep_gu, got_gu)
     give_gu, keep_gu = give_keep(half_gu.reshape(ranks, 2, -1, 2 * hidden), far, 1)
     grad_scale_ffn = jnp.sum(grad_ffn_in * norm_mid, axis=1)
     grad_norm = grad_ffn_in * (1.0 + scale_ffn)
@@ -1742,13 +1914,12 @@
     grad_gate_attn = (1.0 - gate_attn * gate_attn)[:, 0] * jnp.sum(grad_middle * norm_proj, axis=1)
     grad_norm = gate_attn * grad_middle
     grad_three = over_tokens(grad_norm * unit_proj)
-    projected_low = gather_tokens(
+    projected_low, got_gu, got_down = gather_tokens(
         norm_back(unit_proj, inverse_proj, grad_norm * gains[3]).astype(narrow),
         9,
-        after=(half_down, give_gu),
-    )
-    sum_down = add_low(half_down, swap(half_down, FARS))
-    sum_gu = add_low(keep_gu, swap(give_gu, FARS))
+        swaps=((give_gu, "far"), (half_down, "far")),
+    )
+    sum_gu = add_low(keep_gu, got_gu)
     rows_gu = lax.all_to_all(sum_gu, "rows", 0, 0, tiled=True)
     grad_out = weight_grad(combined, projected_low).astype(narrow).reshape(2, -1, width)
     give_out, keep_out = give_keep(grad_out, core, 0)
@@ -1767,14 +1938,17 @@
         counts,
         text_len[0],
         head_size,
-    )
+        (sum_gu, give_out),
+    )
+    sum_down = add_low(half_down, got_down)
+    half_out = add_low(keep_out, swap(give_out, CORES))
     grad_gate = (1.0 - gate_here * gate_here) * jnp.sum(
         gate_sums.reshape(heads_here, head_size), axis=1
     )
     qkv_low, text_low = norms_back(
         qkv_proj,
         totals,
-        sum_rows(sums, 10),
+        sum_rows(sums, 10, after=(sum_down, half_out, rows_gu)),
         scaled,
         grad_value,
         text_proj,
@@ -1786,33 +1960,33 @@
     give_qkv, keep_qkv = give_keep(grad_qkv.reshape(ranks, 2, -1, 3 * span), core, 1)
 
     text_low = text_low.reshape(items * text_all, 2 * span)
-    all_low = unpack_blocks(gather_rows(text_low, 12, 0, after=(give_qkv, give_out)), 2, narrow)
-    half_out = add_low(keep_out, swap(give_out, CORES))
-    half_qkv = add_low(keep_qkv, swap(give_qkv, CORES))
-    give_qkv, keep_qkv = give_keep(half_qkv.reshape(ranks, 2, -1, 3 * span), far, 1)
+    all_low, got_gu, got_out, got_qkv, got_down = gather_rows(
+        text_low,
+        12,
+        0,
+        swaps=((rows_gu, "far"), (half_out, "far"), (give_qkv, "core"), (sum_down, "core")),
+    )
+    all_low = unpack_blocks(all_low, 2, narrow)
     grad_text = weight_grad(text_norm, all_low).astype(narrow).reshape(2, -1, 2 * width)
     give_text, keep_text = give_keep(grad_text, core, 0)
     half_text = add_low(keep_text, swap(give_text, CORES))
-    got_gu, got_out, got_qkv, got_text, got_down = (
-        swap(rows_gu, FARS),
-        swap(half_out, FARS),
-        swap(give_qkv, FARS),
-        swap(half_text, FARS),
-        swap(sum_down, CORES),
-    )
-    grad_attn_in = scatter_tokens(
+    middle_row = half_text.shape[0] // 2
+    pair_gu = join_blocks(rows_gu, got_gu, far_bit)
+    sum_out, half_qkv = add_low(half_out, got_out), add_low(keep_qkv, got_qkv)
+    grad_attn_in, got_qkv, got_text, got_out, got_gu = scatter_tokens(
         dot_back(qkv_low, qkv_here),
         items,
         11,
-        after=(half_out, give_qkv, half_text, rows_gu, sum_down),
-    )
-    grad_attn_in, got_gu, got_out, got_qkv, got_text, got_down = lax.optimization_barrier(
-        (grad_attn_in, got_gu, got_out, got_qkv, got_text, got_down)
-    )
-    pair_gu = join_blocks(rows_gu, got_gu, far_bit)
-    sum_out = add_low(half_out, got_out)
-    sum_qkv = add_low(keep_qkv, got_qkv)
-    sum_text = add_low(half_text, got_text)
+        swaps=(
+            (half_qkv, "far"),
+            (half_text[:middle_row], "far"),
+            (sum_out, "core"),
+            (pair_gu, "core"),
+        ),
+    )
+    sum_qkv = add_low(half_qkv, got_qkv)
+    rows_qkv = lax.all_to_all(sum_qkv, "rows", 0, 0, tiled=True)
+    sum_text = [add_low(half_text[:middle_row], got_text)]
     grad_scale_attn = jnp.sum(grad_attn_in * norm_in, axis=1)
     grad_norm = grad_attn_in * (1.0 + scale_attn)
     grad_zero = over_tokens(grad_norm * unit_in)
@@ -1844,11 +2018,15 @@
     time_rows = spread(time_here.astype(single), ranks * time_here.size).reshape(ranks, -1, 128)
     grad_depth, time_depth = grad_modulation.size // lanes, time_rows.shape[1]
     keep_depth = grad_depth + time_depth
-    reduced = final_sums(
+    reduced, got_text, other_text = final_sums(
         jnp.concatenate([flat, grad_modulation.reshape(ranks, grad_depth, 128), time_rows], axis=1),
         sum_depth,
         13,
-    )
+        swaps=((half_text[middle_row:], "far"), (sum_text[0], "core")),
+    )
+    sum_text.append(add_low(half_text[middle_row:], got_text))
+    sum_text = jnp.concatenate(sum_text)
+    got_text = jnp.concatenate([other_text, swap(sum_text[middle_row:], CORES)])
     flat = reduced[:, :sum_depth].reshape(-1)
     total_gains = flat[: gains.size].reshape(gains.shape)
     total_text_gain = flat[gains.size : gains.size + text_width]
@@ -1866,17 +2044,14 @@
         preferred_element_type=single,
     )
     total_bias = jnp.sum(all_modulation, axis=0)
-    rows_qkv = lax.all_to_all(sum_qkv, "rows", 0, 0, tiled=True)
-    pair_qkv = join_blocks(rows_qkv, swap(rows_qkv, FARS), far_bit)
-
     def whole_rows(half, got):
         return join_rows(half, got, core_bit, single).reshape(-1, half.shape[-1])
 
     sums = [
-        unpack_halves(pair_qkv, swap(pair_qkv, CORES), 3),
-        whole_rows(sum_out, swap(sum_out, CORES)),
+        unpack_halves(rows_qkv, swap(rows_qkv, CORES), 3),
+        whole_rows(sum_out, got_out),
         whole_rows(sum_text, swap(sum_text, CORES)),
-        unpack_halves(pair_gu, swap(pair_gu, CORES), 2),
+        unpack_halves(pair_gu, got_gu, 2),
         whole_rows(sum_down, got_down),
     ]
     return (

time: 782 us -> 728 us (0.931)
  waiting for transfers between devices: 37.1 us -> 0.02 us
  starting transfers between devices: 24.4 us -> 14.2 us
    ppermute x19 -> x6, waiting for transfers between devices: 24.8 us -> 0.02 us  [swap(): return lax.ppermute(array, 'items', pairs)]
    all_to_all x1, waiting for transfers between devices: 12.3 us -> 0.01 us  [head_parallel_plan(): rows_gu = lax.all_to_all(sum_gu, 'rows', 0, 0, tiled=True)]
    ppermute x19 -> x6, starting transfers between devices: 10.3 us -> 1.06 us  [swap(): return lax.ppermute(array, 'items', pairs)]
    pallas_call x4 -> x3, Pallas kernels: 22.6 us -> 16.2 us  [join_blocks(): pl.pallas_call(kernel, grid=(ranks,), out_shape=jax.ShapeDtypeStruct((ran...]
    pallas_call x14 -> x15, Pallas kernels: 427 us -> 433 us  [the longest x5 180 us: scatter_rows(): pl.pallas_call(functools.partial(scatter_kernel, axis, swaps, len(after))...]
    convert_element_type x10 -> x11, other arithmetic: 19.2 us -> 17.1 us  [add_low(): (one.astype(jnp.float32) + other.astype(jnp.float32)).astype(jnp.bfloat16)]
    unnamed x256 -> x279, local copies, waits for them, and re-layouts: 41.1 us -> 43.2 us
  transfers between devices with their start and end apart: 22 -> 9, of which waited for: 4 -> 0; matrix products, arithmetic and copies ran while one was open for 11% -> 9% of each run, Pallas kernels for 47% -> 29%
where the time goes in v5:
time: 728 us; the launch traced here: 719 us
  Pallas kernels  528 us (73%)
  local copies, waits for them, and re-layouts  88.9 us (12%)
  other arithmetic  43.8 us (6%)
  matrix products  42 us (6%)
  starting transfers between devices  14.2 us (2%)
    pallas_call x5, Pallas kernels, scatter_rows(): pl.pallas_call(functools.partial(scatter_kernel, axis, swaps, len(after))...  180 us
    pallas_call x5, Pallas kernels, gather_rows(): pl.pallas_call(functools.partial(gather_kernel, axis, swaps, len(after)),...  175 us
    unnamed x279, local copies, waits for them, and re-layouts  43.2 us
    pallas_call x1, Pallas kernels, first_transfers(): pl.pallas_call(functools.partial(first_kernel, ranks, quarters), out_shap...  34.9 us
    pallas_call x1, Pallas kernels, final_sums(): pl.pallas_call(functools.partial(final_kernel, ranks, groups, sums, swaps...  31.7 us
    pallas_call x1, Pallas kernels, attend_back(): pl.pallas_call(body, out_shape=[jax.ShapeDtypeStruct((tokens, 2 * span),...  28.8 us
    pallas_call x1, Pallas kernels, attend(): pl.pallas_call(body, out_shape=[jax.ShapeDtypeStruct((tokens, width), low...  19 us
    pallas_call x2, Pallas kernels, sum_rows(): pl.pallas_call(functools.partial(sum_kernel, len(after)), out_shape=jax.S...  17.4 us
  transfers between devices with their start and end apart: 9, of which 0 were waited for; matrix products, arithmetic and copies ran while one was open for 9% of the time, Pallas kernels for 29%

profile of v5, /device:TPU:0, one launch (start us, length us, event | category | flops | bytes accessed | tf_op | source)
XLA Modules:
  0.0 718.8 jit_solution(3150758763444140726)
XLA Ops:
  0.7 2.4 fusion.16
  9.5 34.9 %first_transfers_0.1 = (f32[104,128]{1,0:T(8,128)S(1)}, bf16[8,192,576]{2,1,0:T(8,128)(2,1)S(1)}, bf16[8,2,16,512]{3,2,1,0:T(8,128)(2,1)S(1)}) custom-call(f32[104,128]{1,0:T(8,128)S(1)} %pad_bitcast_fusion.own, bf16[192,4608]{1,0:T(8,128)(2,1)S(1)} %copy-done.19, bf16[2,16,4096]{2,1,0:T(8,128)(2,1)S(1)} %bitcast.126), custom_call_target="tpu_custom_call" | custom-call | tf_op jit(solution)/shard_map/first_transfers_0/pallas_call | solution.py:1055
  49.3 2.0 multiply_convert_fusion.6.own
  51.4 46.3 %gather_rows_1.1 = bf16[2,8,64,1536]{3,2,1,0:T(8,128)(2,1)} custom-call(bf16[2,64,1536]{2,1,0:T(8,128)(2,1)} %multiply_convert_fusion.6.own), custom_call_target="tpu_custom_call" | custom-call | tf_op jit(solution)/shard_map/gather_rows_1/pallas_call | solution.py:644
  97.7 1.9 copy-done.9
  100.5 4.2 all-to-all-start
  107.6 26.7 %scatter_rows_2.1 = f32[256,384]{1,0:T(8,128)S(1)} custom-call(bf16[8,256,384]{2,1,0:T(8,128)(2,1)S(1)} %pack_blocks.1.parts), custom_call_target="tpu_custom_call" | custom-call | tf_op jit(solution)/shard_map/scatter_rows_2/pallas_call | solution.py:815
  134.3 4.9 project.1
  141.3 8.1 %sum_rows_3.1.refs_4_.refs_8_.totals = f32[24,128]{1,0:T(8,128)} custom-call(f32[24,128]{1,0:T(8,128)} %copy-done.51), custom_call_target="tpu_custom_call" | custom-call | tf_op jit(solution)/shard_map/sum_rows_3/pallas_call | solution.py:859
  157.8 19.0 %attend.1 = (bf16[1024,1536]{1,0:T(8,128)(2,1)}, bf16[1024,192]{1,0:T(8,128)(2,1)S(1)}, bf16[1024,576]{1,0:T(8,128)(2,1)S(1)}, bf16[2,128,384]{2,1,0:T(8,128)(2,1)S(1)}, f32[4,32,128]{2,1,0:T(8,128)S(1)}) custom-call(s32[16]{0:T(128)S(1)} %slice_convert_fusion.refs_0_, s32[2]{0:T(128)S(1)} %bitcast.132, s32[2]{0:T(128)S(1)} %bitcast.130, ...), custom_call_target="tpu_custom_call" | custom-call | tf_op jit(solution)/shard_map/attend/pallas_call | solution.py:1398
  177.9 2.2 copy-done.13
  180.1 33.4 %scatter_rows_4.1 = f32[2,64,1536]{2,1,0:T(8,128)S(1)} custom-call(bf16[2,8,64,1536]{3,2,1,0:T(8,128)(2,1)S(1)} %bitcast.119), custom_call_target="tpu_custom_call" | custom-call | tf_op jit(solution)/shard_map/scatter_rows_4/pallas_call | solution.py:815
  213.7 5.8 join_blocks.3.one
  221.7 38.7 %gather_rows_5.1 = bf16[2,8,64,1536]{3,2,1,0:T(8,128)(2,1)} custom-call(bf16[2,64,1536]{2,1,0:T(8,128)(2,1)} %multiply_convert_fusion.5.own), custom_call_target="tpu_custom_call" | custom-call | tf_op jit(solution)/shard_map/gather_rows_5/pallas_call | solution.py:644
  261.4 6.5 join_blocks.4
  267.8 5.5 fusion.18
  273.3 2.0 copy-done.84
  276.7 1.8 convolution_convert_fusion.3
  278.6 40.7 %scatter_rows_6.1 = f32[2,64,1536]{2,1,0:T(8,128)S(1)} custom-call(bf16[2,8,64,1536]{3,2,1,0:T(8,128)(2,1)S(1)} %bitcast.120), custom_call_target="tpu_custom_call" | custom-call | tf_op jit(solution)/shard_map/scatter_rows_6/pallas_call | solution.py:815
  322.0 29.6 %gather_rows_7.1 = bf16[2,8,64,1536]{3,2,1,0:T(8,128)(2,1)} custom-call(bf16[2,64,1536]{2,1,0:T(8,128)(2,1)} %get-tuple-element.113.own), custom_call_target="tpu_custom_call" | custom-call | tf_op jit(solution)/shard_map/gather_rows_7/pallas_call | solution.py:644
  351.7 6.1 multiply_convert_fusion.1
  359.7 3.7 convolution_convert_fusion.5
  363.4 4.6 convolution_convert_fusion.4
  368.3 37.3 %scatter_rows_8.1 = (f32[2,64,1536]{2,1,0:T(8,128)S(1)}, bf16[256,1536]{1,0:T(8,128)(2,1)S(1)}, bf16[8,96,1024]{2,1,0:T(8,128)(2,1)S(1)}) custom-call(bf16[2,8,64,1536]{3,2,1,0:T(8,128)(2,1)S(1)} %bitcast.118, bf16[256,1536]{1,0:T(8,128)(2,1)S(1)} %dynamic-slice_bitcast_fusion.4.rest_0_, bf16[8,96,1024]{2,1,0:T(8,128)(2,1)S(1)} %dynamic-slice_bitcast_fusion.1.rest_1_), custom_call_target="tpu_custom_call" | custom-call | tf_op jit(solution)/shard_map/scatter_rows_8/pallas_call | solution.py:815
  412.1 32.9 %gather_rows_9.1 = (bf16[2,8,64,1536]{3,2,1,0:T(8,128)(2,1)}, bf16[8,48,1024]{2,1,0:T(8,128)(2,1)}, bf16[256,1536]{1,0:T(8,128)(2,1)}) custom-call(bf16[2,64,1536]{2,1,0:T(8,128)(2,1)} %multiply_convert_fusion.3.own, bf16[8,48,1024]{2,1,0:T(8,128)(2,1)} %dynamic-slice_bitcast_fusion.3.rest_0_, bf16[256,1536]{1,0:T(8,128)(2,1)} %fusion.4.rest_1_), custom_call_target="tpu_custom_call" | custom-call | tf_op jit(solution)/shard_map/gather_rows_9/pallas_call | solution.py:644
  445.1 2.7 add_convert_fusion.3.rest_0_.rest_3_.own
  449.0 4.2 all-to-all-start.1
  453.3 3.0 convolution_convert_fusion.8
  457.3 28.8 %attend_back.1 = (f32[1024,384]{1,0:T(8,128)S(1)}, bf16[1024,192]{1,0:T(8,128)(2,1)S(1)}, f32[256,192]{1,0:T(8,128)S(1)}, bf16[256,192]{1,0:T(8,128)(2,1)S(1)}, ...) custom-call(s32[16]{0:T(128)S(1)} %copy-done.60, s32[2]{0:T(128)S(1)} %bitcast.131, ...), custom_call_target="tpu_custom_call" | custom-call | tf_op jit(solution)/shard_map/attend_back/pallas_call | solution.py:1565
  510.0 9.4 %sum_rows_10.1.sums = f32[24,128]{1,0:T(8,128)} custom-call(f32[24,128]{1,0:T(8,128)} %copy-done.52, bf16[256,1536]{1,0:T(8,128)(2,1)} %add_convert_fusion.3.rest_0_.rest_3_.own, bf16[96,1536]{1,0:T(8,128)(2,1)} %fusion.6.rest_1_, bf16[8,48,1024]{2,1,0:T(8,128)(2,1)} %all-to-all-done.1.rest_2_.rest_0_.one), custom_call_target="tpu_custom_call" | custom-call | tf_op jit(solution)/shard_map/sum_rows_10/pallas_call | solution.py:859
  524.4 2.7 norms_back.1
  529.0 3.3 convolution_convert_fusion.6
  532.3 3.9 copy.32
  536.1 2.2 dynamic-slice_bitcast_fusion.2.rest_2_
  538.4 27.2 %gather_rows_12.1 = (bf16[8,256,384]{2,1,0:T(8,128)(2,1)}, bf16[8,48,1024]{2,1,0:T(8,128)(2,1)}, bf16[96,1536]{1,0:T(8,128)(2,1)}, bf16[8,96,576]{2,1,0:T(8,128)(2,1)}, bf16[256,1536]{1,0:T(8,128)(2,1)}) custom-call(bf16[256,384]{1,0:T(8,128)(2,1)} %bitcast.127, bf16[8,48,1024]{2,1,0:T(8,128)(2,1)} %all-to-all-done.1.rest_2_.rest_0_.one, ...), custom_call_target="tpu_custom_call" | custom-call | tf_op jit(solution)/shard_map/gather_rows_12/pallas_call | solution.py:644
  572.6 3.9 join_blocks.5.rest_3_.own
  576.6 2.0 fusion.2.rest_0_
  579.4 2.9 convolution_convert_fusion.2
  582.3 2.0 fusion
  585.7 42.4 %scatter_rows_11.1 = (f32[2,64,1536]{2,1,0:T(8,128)S(1)}, bf16[8,96,576]{2,1,0:T(8,128)(2,1)S(1)}, bf16[128,3072]{1,0:T(8,128)(2,1)S(1)}, bf16[96,1536]{1,0:T(8,128)(2,1)S(1)}, bf16[8,96,1024]{2,1,0:T(8,128)(2,1)S(1)}) custom-call(bf16[2,8,64,1536]{3,2,1,0:T(8,128)(2,1)S(1)} %bitcast.117, bf16[8,96,576]{2,1,0:T(8,128)(2,1)S(1)} %fusion.2.rest_0_, ...), custom_call_target="tpu_custom_call" | custom-call | tf_op jit(solution)/shard_map/scatter_rows_11/pallas_call | solution.py:815
  632.9 4.7 all-to-all-start.2
  645.5 2.5 add_convert_fusion.2.rest_1_
  648.7 31.7 %final_sums_13.1 = (f32[8,71,128]{2,1,0:T(8,128)}, bf16[128,3072]{1,0:T(8,128)(2,1)}, bf16[128,3072]{1,0:T(8,128)(2,1)}) custom-call(f32[8,29,128]{2,1,0:T(8,128)} %pad_maximum_fusion.4.own, bf16[128,3072]{1,0:T(8,128)(2,1)} %get-tuple-element.111.rest_0_, bf16[128,3072]{1,0:T(8,128)(2,1)} %add_convert_fusion.2.rest_1_), custom_call_target="tpu_custom_call" | custom-call | tf_op jit(solution)/shard_map/final_sums_13/pallas_call | solution.py:934
  685.6 2.1 join_rows.5
  697.2 3.3 unpack_halves.3
  703.6 4.3 fusion.19
  709.0 5.9 join_rows.4
  714.9 3.7 unpack_halves.2
  (409 shorter events, 116.5 us)
Async XLA Ops:
  0.6 105.5 %copy-start = (bf16[512,3072]{1,0:T(8,128)(2,1)S(1)}, bf16[512,3072]{1,0:T(8,128)(2,1)}, u32[]{:S(2)}) copy-start(bf16[512,3072]{1,0:T(8,128)(2,1)} %param.26) | copy-start | bytes 9437188
  3.1 46.2 %copy-start.106 = (f32[1536]{0:T(1024)}, f32[1536]{0:T(1024)S(1)}, u32[]{:S(2)}) copy-start(f32[1536]{0:T(1024)S(1)} %get-tuple-element.124) | copy-start | bytes 18436
  45.8 59.0 %copy-start.50 = (f32[104,128]{1,0:T(8,128)}, f32[104,128]{1,0:T(8,128)S(1)}, u32[]{:S(2)}) copy-start(f32[104,128]{1,0:T(8,128)S(1)} %get-tuple-element.51) | copy-start | bytes 159748
  45.8 59.9 %copy-start.20 = (bf16[8,2,16,512]{3,2,1,0:T(8,128)(2,1)}, bf16[8,2,16,512]{3,2,1,0:T(8,128)(2,1)S(1)}, u32[]{:S(2)}) copy-start(bf16[8,2,16,512]{3,2,1,0:T(8,128)(2,1)S(1)} %get-tuple-element.54) | copy-start | bytes 786436
  47.3 50.3 %copy-start.94 = (f32[2,6144]{1,0:T(2,128)}, f32[2,6144]{1,0:T(2,128)S(1)}, u32[]{:S(2)}) copy-start(f32[2,6144]{1,0:T(2,128)S(1)} %broadcast_add_fusion) | copy-start | bytes 147460
  48.0 49.7 %copy-start.100 = (f32[2,1536]{1,0:T(2,128)}, f32[2,1536]{1,0:T(2,128)S(1)}, u32[]{:S(2)}) copy-start(f32[2,1536]{1,0:T(2,128)S(1)} %get-tuple-element.119) | copy-start | bytes 36868
  49.3 48.4 %copy-start.133 = (f32[2,64]{1,0:T(2,128)}, f32[2,64]{1,0:T(2,128)S(1)}, u32[]{:S(2)}) copy-start(f32[2,64]{1,0:T(2,128)S(1)} %rsqrt.47) | copy-start | bytes 1540
  100.5 48.8 %all-to-all-start = ((bf16[8,48,1024]{2,1,0:T(8,128)(2,1)}), bf16[8,48,1024]{2,1,0:T(8,128)(2,1)}, u32[]{:S(2)}, u32[]{:S(2)}) async-start(bf16[8,48,1024]{2,1,0:T(8,128)(2,1)} %copy-done.12), calls=%async_computation | async-start | bytes 1572864 | tf_op jit(solution)/shard_map/all_to_all | solution.py:1831
  107.2 27.0 %copy-start.17 = (bf16[8,192,576]{2,1,0:T(8,128)(2,1)S(1)}, bf16[8,192,576]{2,1,0:T(8,128)(2,1)}, u32[]{:S(2)}) copy-start(bf16[8,192,576]{2,1,0:T(8,128)(2,1)} %copy-done.16) | copy-start | bytes 5308420
  134.3 19.4 %copy-start.57 = (s32[1,2]{1,0:T(1,128)S(1)}, s32[1,2]{1,0:T(1,128)}, u32[]{:S(2)}) copy-start(s32[1,2]{1,0:T(1,128)} %param.23) | copy-start | bytes 28
  149.4 64.3 %collective-permute-start = (bf16[8,48,1024]{2,1,0:T(8,128)(2,1)}, bf16[8,48,1024]{2,1,0:T(8,128)(2,1)}, u32[]{:S(2)}, u32[]{:S(2)}) collective-permute-start(bf16[8,48,1024]{2,1,0:T(8,128)(2,1)} %all-to-all-done.one), channel_id=1, source_target_pairs={{0,16},{8,24},{16,0},{24,8},{1,17},{9,25},{17,1},{25,9},{2,18},{10... | collective-permute-start | bytes 2359304 | tf_op jit(solution)/shard_map/ppermute | solution.py:1726
  150.7 62.7 %copy-start.55 = (f32[1,192]{1,0:T(1,128)}, f32[1,192]{1,0:T(1,128)S(1)}, u32[]{:S(2)}) copy-start(f32[1,192]{1,0:T(1,128)S(1)} %get-tuple-element.131.refs_7_.refs_11_) | copy-start | bytes 2308
  153.0 60.5 %copy-start.53 = (f32[1,192]{1,0:T(1,128)}, f32[1,192]{1,0:T(1,128)S(1)}, u32[]{:S(2)}) copy-start(f32[1,192]{1,0:T(1,128)S(1)} %broadcast_in_dim_reshape.3.refs_8_.refs_12_) | copy-start | bytes 2308
  153.7 59.8 %copy-start.59 = (s32[16]{0:T(128)}, s32[16]{0:T(128)S(1)}, u32[]{:S(2)}) copy-start(s32[16]{0:T(128)S(1)} %slice_convert_fusion.refs_0_) | copy-start | bytes 196
  177.9 35.8 %copy-start.33 = (bf16[1024,192]{1,0:T(8,128)(2,1)}, bf16[1024,192]{1,0:T(8,128)(2,1)S(1)}, u32[]{:S(2)}) copy-start(bf16[1024,192]{1,0:T(8,128)(2,1)S(1)} %get-tuple-element.67) | copy-start | bytes 1179652
  177.9 35.8 %copy-start.41 = (bf16[2,128,384]{2,1,0:T(8,128)(2,1)}, bf16[2,128,384]{2,1,0:T(8,128)(2,1)S(1)}, u32[]{:S(2)}) copy-start(bf16[2,128,384]{2,1,0:T(8,128)(2,1)S(1)} %get-tuple-element.64.refs_5_) | copy-start | bytes 589828
  177.9 35.8 %copy-start.47 = (f32[4,32,128]{2,1,0:T(8,128)}, f32[4,32,128]{2,1,0:T(8,128)S(1)}, u32[]{:S(2)}) copy-start(f32[4,32,128]{2,1,0:T(8,128)S(1)} %get-tuple-element.65.refs_6_) | copy-start | bytes 196612
  213.7 7.1 copy-start.104
  219.5 41.8 %collective-permute-start.1 = (bf16[8,96,1024]{2,1,0:T(8,128)(2,1)}, bf16[8,96,1024]{2,1,0:T(8,128)(2,1)}, u32[]{:S(2)}, u32[]{:S(2)}) collective-permute-start(bf16[8,96,1024]{2,1,0:T(8,128)(2,1)} %join_blocks.3.one), channel_id=1, source_target_pairs={{0,8},{8,0},{16,24},{24,16},{1,9},{9,1},{17,25},{25,17},{2,10},{10... | collective-permute-start | bytes 4718600 | tf_op jit(solution)/shard_map/ppermute | solution.py:1726
  221.7 39.6 %copy-start.137 = (s32[1,1,2]{2,1,0:T(1,128)S(1)}, s32[1,1,2]{2,1,0:T(1,128)}, u32[]{:S(2)}) copy-start(s32[1,1,2]{2,1,0:T(1,128)} %param.21) | copy-start | bytes 28
  261.4 59.2 %copy-start.130 = (f32[2,64]{1,0:T(2,128)}, f32[2,64]{1,0:T(2,128)S(1)}, u32[]{:S(2)}) copy-start(f32[2,64]{1,0:T(2,128)S(1)} %compare_convert_fusion) | copy-start | bytes 1540
  278.6 41.0 %copy-start.76 = (f32[1,128,1536]{2,1,0:T(8,128)S(1)}, f32[1,128,1536]{2,1,0:T(8,128)}, u32[]{:S(2)}) copy-start(f32[1,128,1536]{2,1,0:T(8,128)} %param.18) | copy-start | bytes 2359300
  278.6 40.9 %copy-start.112 = (f32[2,1536]{1,0:T(2,128)S(1)}, f32[2,1536]{1,0:T(2,128)}, u32[]{:S(2)}) copy-start(f32[2,1536]{1,0:T(2,128)} %get-tuple-element.117) | copy-start | bytes 36868
  278.6 40.9 %copy-start.115 = (f32[1536]{0:T(1024)S(1)}, f32[1536]{0:T(1024)}, u32[]{:S(2)}) copy-start(f32[1536]{0:T(1024)} %get-tuple-element.126) | copy-start | bytes 18436
  368.2 37.4 %copy-start.72 = (f32[2,64,1536]{2,1,0:T(8,128)S(1)}, f32[2,64,1536]{2,1,0:T(8,128)}, u32[]{:S(2)}) copy-start(f32[2,64,1536]{2,1,0:T(8,128)} %copy-done.70) | copy-start | bytes 2359300
  368.3 37.4 %copy-start.105 = (f32[2,1536]{1,0:T(2,128)S(1)}, f32[2,1536]{1,0:T(2,128)}, u32[]{:S(2)}) copy-start(f32[2,1536]{1,0:T(2,128)} %get-tuple-element.118) | copy-start | bytes 36868
  368.3 37.4 %copy-start.111 = (f32[1536]{0:T(1024)S(1)}, f32[1536]{0:T(1024)}, u32[]{:S(2)}) copy-start(f32[1536]{0:T(1024)} %get-tuple-element.123) | copy-start | bytes 18436
  368.3 37.4 %copy-start.129 = (f32[2,64]{1,0:T(2,128)S(1)}, f32[2,64]{1,0:T(2,128)}, u32[]{:S(2)}) copy-start(f32[2,64]{1,0:T(2,128)} %copy-done.128) | copy-start | bytes 1540
  368.3 38.3 %copy-start.103 = (f32[2,1536]{1,0:T(2,128)S(1)}, f32[2,1536]{1,0:T(2,128)}, u32[]{:S(2)}) copy-start(f32[2,1536]{1,0:T(2,128)} %get-tuple-element.120) | copy-start | bytes 36868
  368.3 38.3 %copy-start.109 = (f32[1536]{0:T(1024)S(1)}, f32[1536]{0:T(1024)}, u32[]{:S(2)}) copy-start(f32[1536]{0:T(1024)} %get-tuple-element.125) | copy-start | bytes 18436
  368.3 38.3 %copy-start.127 = (f32[2,64]{1,0:T(2,128)S(1)}, f32[2,64]{1,0:T(2,128)}, u32[]{:S(2)}) copy-start(f32[2,64]{1,0:T(2,128)} %copy-done.126) | copy-start | bytes 1540
  368.3 38.3 %copy-start.131 = (f32[2,64]{1,0:T(2,128)S(1)}, f32[2,64]{1,0:T(2,128)}, u32[]{:S(2)}) copy-start(f32[2,64]{1,0:T(2,128)} %copy-done.130) | copy-start | bytes 1540
  449.0 61.0 %all-to-all-start.1 = ((bf16[8,48,1024]{2,1,0:T(8,128)(2,1)}), bf16[8,48,1024]{2,1,0:T(8,128)(2,1)}, u32[]{:S(2)}, u32[]{:S(2)}) async-start(bf16[8,48,1024]{2,1,0:T(8,128)(2,1)} %fusion.3.refs_13_), calls=%async_computation.1 | async-start | bytes 1572864 | tf_op jit(solution)/shard_map/all_to_all | solution.py:1923
  457.1 51.0 %collective-permute-start.2 = (bf16[96,1536]{1,0:T(8,128)(2,1)}, bf16[96,1536]{1,0:T(8,128)(2,1)}, u32[]{:S(2)}, u32[]{:S(2)}) collective-permute-start(bf16[96,1536]{1,0:T(8,128)(2,1)} %dynamic-slice_bitcast_fusion.5.refs_14_), channel_id=1, source_target_pairs={{0,8},{8,0},{16,24},{24,16},{1,9},{9,1},{17,25},{25,17},{2,10},{10... | collective-permute-start | bytes 884744 | tf_op jit(solution)/shard_map/ppermute | solution.py:1726
  457.3 33.2 %copy-start.95 = (f32[2,6144]{1,0:T(2,128)S(1)}, f32[2,6144]{1,0:T(2,128)}, u32[]{:S(2)}) copy-start(f32[2,6144]{1,0:T(2,128)} %copy-done.94) | copy-start | bytes 147460
  457.3 33.2 %copy-start.118 = (f32[2,1536]{1,0:T(2,128)S(1)}, f32[2,1536]{1,0:T(2,128)}, u32[]{:S(2)}) copy-start(f32[2,1536]{1,0:T(2,128)} %get-tuple-element.98) | copy-start | bytes 36868
  457.3 33.2 %copy-start.119 = (f32[2,1536]{1,0:T(2,128)S(1)}, f32[2,1536]{1,0:T(2,128)}, u32[]{:S(2)}) copy-start(f32[2,1536]{1,0:T(2,128)} %get-tuple-element.100) | copy-start | bytes 36868
  457.3 34.5 %copy-start.120 = (f32[2,1536]{1,0:T(2,128)S(1)}, f32[2,1536]{1,0:T(2,128)}, u32[]{:S(2)}) copy-start(f32[2,1536]{1,0:T(2,128)} %get-tuple-element.101) | copy-start | bytes 36868
  570.2 12.1 %collective-permute-start.3 = (bf16[256,3072]{1,0:T(8,128)(2,1)}, bf16[256,3072]{1,0:T(8,128)(2,1)}, u32[]{:S(2)}, u32[]{:S(2)}) collective-permute-start(bf16[256,3072]{1,0:T(8,128)(2,1)} %dynamic-slice_bitcast_fusion), channel_id=1, source_target_pairs={{0,8},{8,0},{16,24},{24,16},{1,9},{9,1},{17,25},{25,17},{2,10},{10... | collective-permute-start | bytes 4718600 | tf_op jit(solution)/shard_map/ppermute | solution.py:1726
  576.6 9.1 %copy-start.5 = (bf16[8,96,1024]{2,1,0:T(8,128)(2,1)}, bf16[8,96,1024]{2,1,0:T(8,128)(2,1)S(1)}, u32[]{:S(2)}) copy-start(bf16[8,96,1024]{2,1,0:T(8,128)(2,1)S(1)} %join_blocks.5.rest_3_.own) | copy-start | bytes 4718596
  585.7 45.0 %copy-start.68 = (f32[1,128,1536]{2,1,0:T(8,128)S(1)}, f32[1,128,1536]{2,1,0:T(8,128)}, u32[]{:S(2)}) copy-start(f32[1,128,1536]{2,1,0:T(8,128)} %param.17) | copy-start | bytes 2359300
  585.7 45.0 %copy-start.101 = (f32[2,1536]{1,0:T(2,128)S(1)}, f32[2,1536]{1,0:T(2,128)}, u32[]{:S(2)}) copy-start(f32[2,1536]{1,0:T(2,128)} %copy-done.100) | copy-start | bytes 36868
  585.7 45.0 %copy-start.107 = (f32[1536]{0:T(1024)S(1)}, f32[1536]{0:T(1024)}, u32[]{:S(2)}) copy-start(f32[1536]{0:T(1024)} %copy-done.106) | copy-start | bytes 18436
  585.7 45.0 %copy-start.134 = (f32[2,64]{1,0:T(2,128)S(1)}, f32[2,64]{1,0:T(2,128)}, u32[]{:S(2)}) copy-start(f32[2,64]{1,0:T(2,128)} %copy-done.133) | copy-start | bytes 1540
  632.9 55.6 %all-to-all-start.2 = ((bf16[8,96,576]{2,1,0:T(8,128)(2,1)}), bf16[8,96,576]{2,1,0:T(8,128)(2,1)}, u32[]{:S(2)}, u32[]{:S(2)}) async-start(bf16[8,96,576]{2,1,0:T(8,128)(2,1)} %add_convert_fusion), calls=%async_computation.2 | async-start | bytes 1966080 | tf_op jit(solution)/shard_map/all_to_all | solution.py:1988
  639.7 8.3 %copy-start.125 = (f32[2048]{0:T(1024)S(1)}, f32[2048]{0:T(1024)}, u32[]{:S(2)}) copy-start(f32[2048]{0:T(1024)} %copy-done.124) | copy-start | bytes 24580
  683.3 25.7 %collective-permute-start.5 = (bf16[256,3072]{1,0:T(8,128)(2,1)}, bf16[256,3072]{1,0:T(8,128)(2,1)}, u32[]{:S(2)}, u32[]{:S(2)}) collective-permute-start(bf16[256,3072]{1,0:T(8,128)(2,1)} %pad_maximum_fusion.1.own), channel_id=1, source_target_pairs={{0,8},{8,0},{16,24},{24,16},{1,9},{9,1},{17,25},{25,17},{2,10},{10... | collective-permute-start | bytes 4718600 | tf_op jit(solution)/shard_map/ppermute | solution.py:1726
  688.5 26.4 %collective-permute-start.4 = (bf16[8,96,576]{2,1,0:T(8,128)(2,1)}, bf16[8,96,576]{2,1,0:T(8,128)(2,1)}, u32[]{:S(2)}, u32[]{:S(2)}) collective-permute-start(bf16[8,96,576]{2,1,0:T(8,128)(2,1)} %all-to-all-done.2.own), channel_id=1, source_target_pairs={{0,8},{8,0},{16,24},{24,16},{1,9},{9,1},{17,25},{25,17},{2,10},{10... | collective-permute-start | bytes 2654216 | tf_op jit(solution)/shard_map/ppermute | solution.py:1726
  (100 other events, 263.4 us)

commit v6 on v5

--- a/solution.py
+++ b/solution.py
@@ -1,4 +1,5 @@
 import functools
+import itertools
 import math
 
 import jax
@@ -1185,6 +1186,7 @@
 NEAR = pl.BlockSpec(memory_space=pltpu.VMEM)
 SCALARS = pl.BlockSpec(memory_space=pltpu.SMEM)
 NT = (((1,), (1,)), ((), ()))
+TN = (((0,), (0,)), ((), ()))
 
 
 def local_params():
@@ -1636,6 +1638,75 @@
     )(proj, totals, sums, scaled, grad_value, text, text_scaled, text_value)
 
 
+SUM_DEPTH = 16
+
+
+def finish_kernel(
+    grad, states, grad_middle, modulation, gains, vectors, gain_sums, gate_sums, text_gain, time, grad_x, small
+):
+    items, _, width = states.shape
+    ranks = small.shape[0]
+    place = lax.axis_index("rows")
+    scales, zero = [], jnp.zeros((1, width), jnp.float32)
+    for item in range(items):
+        unit, inverse = norm_unit(states[item])
+        value = grad[item]
+        scales.append(jnp.sum(value * (unit * gains[0:1]), axis=0, keepdims=True))
+        value = value * (1.0 + modulation[item : item + 1, :width])
+        zero = zero + jnp.sum(value * unit, axis=0, keepdims=True)
+        value = value * gains[0:1]
+        value = inverse * (value - unit * jnp.mean(value * unit, axis=-1, keepdims=True))
+        grad_x[item] = grad_middle[item] + value
+
+    def spread(part):
+        size = part.shape[1]
+        owner = lax.broadcasted_iota(jnp.int32, (1, ranks * size), 1) // size
+        return jnp.where(owner == place, jnp.concatenate([part] * ranks, axis=1), 0.0)
+
+    span = gate_sums.shape[1]
+    rows = [
+        zero,
+        spread(gain_sums[0:1, :span]),
+        spread(gain_sums[0:1, span:]),
+        vectors[8:9],
+        vectors[7:8],
+        vectors[6:7],
+        spread(gain_sums[1:2, :span]),
+        spread(text_gain[...]),
+        spread(gate_sums[...]),
+    ]
+    number = 0
+    for row in rows:
+        for start in range(0, row.shape[1], 128):
+            rank, depth = divmod(number, SUM_DEPTH)
+            small[rank, depth : depth + 1] = row[:, start : start + 128]
+            number += 1
+    for item in range(items):
+        kinds = (scales[item], vectors[4 + item : 5 + item], vectors[2 + item : 3 + item], vectors[item : item + 1])
+        for which, row in enumerate(kinds):
+            for at in range(width // 128):
+                depth = SUM_DEPTH + at
+                small[item * 4 + which, depth : depth + 1] = row[:, at * 128 : (at + 1) * 128]
+    for rank in range(ranks):
+        small[rank, SUM_DEPTH + width // 128 :] = jnp.where(rank == place, time[...], 0.0)
+
+
+def finish(grad, states, grad_middle, modulation, gains, vectors, gain_sums, gate_sums, text_gain, time):
+    ranks, width = lax.axis_size("rows"), states.shape[-1]
+    depth = SUM_DEPTH + width // 128 + time.shape[0]
+    return pl.pallas_call(
+        finish_kernel,
+        out_shape=[
+            jax.ShapeDtypeStruct(states.shape, jnp.float32),
+            jax.ShapeDtypeStruct((ranks, depth, 128), jnp.float32),
+        ],
+        in_specs=[NEAR] * 10,
+        out_specs=[NEAR] * 2,
+        name="finish",
+        compiler_params=local_params(),
+    )(grad, states, grad_middle, modulation, gains, vectors, gain_sums, gate_sums, text_gain, time)
+
+
 def join_kernel(bit, own, other, out):
     mine = pl.program_id(0) == bit()
 
@@ -1693,6 +1764,490 @@
         name="join_blocks",
         compiler_params=local_params(),
     )(own, other)
+
+
+ORDER = (
+    "gs", "wf", "sf", "wn", "sn", "t", "b0", "g1", "b1", "b2", "a0", "g2",
+    "a1", "h", "g3", "a2", "ge", "se",
+)
+LAST_ORDER = (
+    "gs", "wf", "sf", "wn", "sn", "t", "d0", "b0", "d1", "g1", "b1", "b2",
+    "u0", "a0", "u1", "g2", "a1", "u2", "h", "g3", "u3", "c", "a2", "ge",
+    "se",
+)
+END_ORDER = (
+    "gs", "t", "g1", "y", "g2", "g3", "ge",
+)
+
+
+def split_chain(width):
+    return width - 128 * round(width / 384)
+
+
+class Chain:
+    def __init__(self, place, width, flow, scatter_waves, gather_waves):
+        self.line, self.side = place
+        line = self.line
+        self.across = on_rows(line, 1 - self.side)
+        self.ways = (on_rows(line + 1, self.side), on_rows(line - 1, self.side))
+        self.more = (line < DEPTH - 1, line > 0)
+        low = line < 2
+        self.pair = jnp.where(low, 1, 0)
+        self.order = (jnp.where(low, 3, 0), jnp.where(low, 2, 1), line + 1 - 2 * lax.rem(line, 2))
+        even = lax.rem(line, 2) == 0
+        self.upward = (low, low, even)
+        first = split_chain(width)
+        self.pieces = ((0, 0, first), (0, first, width - first), (1, first, width - first))
+        self.crossed, self.flow = flow[0], flow[1:]
+        self.x_send, self.x_recv, self.z_send, self.z_recv = scatter_waves
+        self.gx_send, self.gx_recv, self.gz_send, self.gz_recv = gather_waves
+
+    def shard(self, ref, at, stream, turned=False):
+        which, start, size = self.pieces[stream]
+        other = which or turned
+        return ref.at[at * BREADTH + (1 - self.side if other else self.side), :, pl.ds(start, size)]
+
+
+    def cross(self, parts, at):
+        return remote(
+            self.shard(parts, at, 0, True), self.crossed.at[at], self.x_send.at[at], self.x_recv.at[at], self.across
+        )
+
+    def hand(self):
+        leave, arrive = self.flow[12], self.flow[13]
+        return remote(leave, arrive, self.x_send.at[DEPTH], self.x_recv.at[DEPTH], self.across)
+
+    def moving(self, stream, at, way):
+        return remote(
+            self.flow[4 * stream + 2 * way + 1].at[at],
+            self.flow[4 * stream + 2 * way].at[at],
+            self.z_send.at[stream, way, at],
+            self.z_recv.at[stream, way, at],
+            self.ways[way],
+        )
+
+    def add_up(self, parts, stream, at, ways, target, others=()):
+        value = self.shard(parts, at, stream)[...].astype(jnp.float32)
+        if stream == 0:
+            value = value + self.crossed[at].astype(jnp.float32)
+        for way in ways:
+            value = value + self.flow[4 * stream + 2 * way][at].astype(jnp.float32)
+        for other in others:
+            value = value + other[...].astype(jnp.float32)
+        target[...] = value.astype(target.dtype)
+
+    def send_on(self, parts, stream, number):
+        at = self.order[number]
+        for way in range(2):
+            going = self.upward[number] if way == 0 else jnp.logical_not(self.upward[number])
+            comes = self.more[1 - way]
+            leaving = self.flow[4 * stream + 2 * way + 1].at[at]
+
+            @pl.when(going & comes)
+            def _(way=way, leaving=leaving):
+                self.moving(stream, at, way).wait_recv()
+                self.add_up(parts, stream, at, [way], leaving)
+
+            @pl.when(going & jnp.logical_not(comes))
+            def _(leaving=leaving):
+                self.add_up(parts, stream, at, [], leaving)
+
+            @pl.when(going)
+            def _(way=way):
+                self.moving(stream, at, way).start()
+
+    def finish(self, parts, stream, target, others=()):
+        for above_there, below_there, ways in ((True, True, [0, 1]), (False, True, [0]), (True, False, [1])):
+
+            @pl.when((self.more[0] == above_there) & (self.more[1] == below_there))
+            def _(ways=ways):
+                for way in ways:
+                    self.moving(stream, self.line, way).wait_recv()
+                self.add_up(parts, stream, self.line, ways, target, others)
+
+    def scatter_start(self, parts, near):
+        for at in (self.order[2], self.line) if near else self.order[:2]:
+            self.cross(parts, at).start()
+
+    def scatter_over(self, parts, number):
+        for stream in (1, 2):
+            self.send_on(parts, stream, number)
+
+    def scatter_along(self, parts, number):
+        self.cross(parts, self.order[number]).wait_recv()
+        self.send_on(parts, 0, number)
+
+    def scatter_hand(self, parts):
+        self.finish(parts, 2, self.flow[12])
+        self.hand().start()
+
+    def scatter_end(self, parts, total):
+        first = self.pieces[0][2]
+        self.cross(parts, self.line).wait_recv()
+        self.finish(parts, 0, total.at[:, pl.ds(0, first)])
+        self.hand().wait_recv()
+        self.finish(parts, 1, total.at[:, pl.ds(*self.pieces[1][1:])], (self.flow[13],))
+        self.hand().wait_send()
+        for at in range(DEPTH):
+            self.cross(parts, at).wait_send()
+        for number in range(3):
+            for way in range(2):
+                going = self.upward[number] if way == 0 else jnp.logical_not(self.upward[number])
+
+                @pl.when(going)
+                def _(number=number, way=way):
+                    for stream in range(3):
+                        self.moving(stream, self.order[number], way).wait_send()
+
+
+    def mine(self, own, stream):
+        return own.at[:, pl.ds(*self.pieces[stream][1:])]
+
+    def pass_on(self, whole, stream, source, at, way):
+        return remote(
+            source,
+            self.shard(whole, at, stream),
+            self.gz_send.at[stream, way, at],
+            self.gz_recv.at[stream, at],
+            self.ways[way],
+        )
+
+    def give(self, whole, stream, source, at):
+        slot = DEPTH if stream else at
+        return remote(source, self.shard(whole, at, stream), self.gx_send.at[slot], self.gx_recv.at[slot], self.across)
+
+    def onward(self, whole, stream, source):
+        for way in range(2):
+
+            @pl.when(self.more[way])
+            def _(way=way):
+                self.pass_on(whole, stream, source, self.line, way).start()
+
+    def gather_start(self, own, whole):
+        self.give(whole, 1, self.mine(own, 1), self.line).start()
+        self.give(whole, 0, self.mine(own, 0), self.line).start()
+        for stream in range(2):
+            self.onward(whole, stream, self.mine(own, stream))
+        whole[self.line * BREADTH + self.side] = own[...]
+
+    def gather_turn(self, own, whole):
+        self.give(whole, 1, self.mine(own, 1), self.line).wait_recv()
+        self.onward(whole, 2, self.shard(whole, self.line, 2))
+
+    def gather_step(self, whole, step):
+        line = self.line
+        for way, at, there in ((0, line - step, line - step >= 0), (1, line + step, line + step < DEPTH)):
+
+            @pl.when(there)
+            def _(way=way, at=at):
+                for stream in range(3):
+                    block = self.shard(whole, at, stream)
+                    self.pass_on(whole, stream, block, at, way).wait_recv()
+                    if stream == 0:
+                        self.give(whole, 0, block, at).start()
+
+                    @pl.when(self.more[way])
+                    def _(stream=stream, block=block):
+                        self.pass_on(whole, stream, block, at, way).start()
+
+    def gather_end(self, own, whole):
+        for at in range(DEPTH):
+            self.give(whole, 0, self.mine(own, 0), at).wait_recv()
+            self.give(whole, 0, self.mine(own, 0), at).wait_send()
+            for stream in range(3):
+                for way, holds in ((0, at <= self.line), (1, at >= self.line)):
+
+                    @pl.when(self.more[way] & holds)
+                    def _(at=at, stream=stream, way=way):
+                        self.pass_on(whole, stream, self.shard(whole, at, stream), at, way).wait_send()
+
+        self.give(whole, 1, self.mine(own, 1), self.line).wait_send()
+
+
+def norm_unit(values):
+    inverse = lax.rsqrt(jnp.mean(values * values, axis=-1, keepdims=True) + epsilon)
+    return values * inverse, inverse
+
+
+def feed_forward_kernel(
+    parts, states, cotangent, live, modulation, gains, gu_part, w_down,
+    output, grad_middle, ffn_in, inner_act, ffn_low, gate_up_low, projected_low, vectors, sum_gu, half_down,
+    gate_up, projected, middle, result, own, partial, w_gu, grad_gu, grad_down, got_gu, got_down, half_gu,
+    far_gu, swap_send, swap_recv, *rest,
+):
+    items = states.shape[0]
+    width, hidden = states.shape[2], w_down.shape[0]
+    rows = states.shape[1]
+    half = 4 * rows
+    flows, waves = rest[: 15 * items], rest[15 * items :]
+    place = row_place()
+    line = place[0]
+    chains = [
+        Chain(place, width, flows[15 * item : 15 * item + 15], waves[8 * item : 8 * item + 4], waves[8 * item + 4 : 8 * item + 8])
+        for item in range(items)
+    ]
+    one = chains[0]
+    core, far = core_bit(), far_bit()
+    twin, across_y = partner("core"), partner("far")
+    greet(
+        [(one.more[0], one.ways[0]), (one.more[1], one.ways[1]), (line >= 0, one.across)]
+        + [(line >= 0, twin), (line >= 0, across_y)]
+    )
+
+    def quarter_on(number):
+        which = 2 * core + (far if number < 2 else 1 - far)
+        block = w_gu.at[:, which]
+        return remote(block, block, swap_send.at[number], swap_recv.at[number], across_y if number == 0 else twin)
+
+    w_gu[:, 2 * core + far] = gu_part[...]
+    quarter_on(0).start()
+    quarter_on(1).start()
+    vectors[...] = jnp.zeros_like(vectors)
+
+    def scale_of(item, which):
+        return modulation[item : item + 1, which * width : (which + 1) * width]
+
+    def over_rows(values):
+        return jnp.sum(values, axis=0, keepdims=True)
+
+    def middle_of(item):
+        projected[item] = result[item]
+        unit, _ = norm_unit(projected[item])
+        middle[item] = states[item] + jnp.tanh(scale_of(item, 1)) * (unit * gains[3:4])
+        unit, _ = norm_unit(middle[item])
+        own[item] = (unit * gains[4:5] * (1.0 + scale_of(item, 2))).astype(own.dtype)
+
+    def outcome(item):
+        mask = live[item][:, 0:1]
+        gate = jnp.tanh(scale_of(item, 3))
+        unit, inverse = norm_unit(result[item])
+        normed = unit * gains[5:6]
+        output[item] = mask * (middle[item] + gate * normed)
+        grad = mask * cotangent[item]
+        vectors[item : item + 1] = (1.0 - gate * gate) * over_rows(grad * normed)
+        grad = gate * grad
+        vectors[6:7] += over_rows(grad * unit)
+        grad = grad * gains[5:6]
+        grad = inverse * (grad - unit * jnp.mean(grad * unit, axis=-1, keepdims=True))
+        own[items + item] = grad.astype(own.dtype)
+
+    def back_to_attention(item):
+        unit, inverse = norm_unit(middle[item])
+        grad = result[item]
+        vectors[2 + item : 3 + item] = over_rows(grad * (unit * gains[4:5]))
+        grad = grad * (1.0 + scale_of(item, 2))
+        vectors[7:8] += over_rows(grad * unit)
+        grad = grad * gains[4:5]
+        grad = inverse * (grad - unit * jnp.mean(grad * unit, axis=-1, keepdims=True))
+        grad = live[item][:, 0:1] * cotangent[item] + grad
+        grad_middle[item] = grad
+        gate = jnp.tanh(scale_of(item, 1))
+        unit, inverse = norm_unit(projected[item])
+        vectors[4 + item : 5 + item] = (1.0 - gate * gate) * over_rows(grad * (unit * gains[3:4]))
+        grad = gate * grad
+        vectors[8:9] += over_rows(grad * unit)
+        grad = grad * gains[3:4]
+        grad = inverse * (grad - unit * jnp.mean(grad * unit, axis=-1, keepdims=True))
+        own[2 * items + item] = grad.astype(own.dtype)
+
+    def pair_of(near):
+        return jnp.where(near, 1 - one.pair, one.pair)
+
+    def forward(item, near):
+        pair = pair_of(near)
+        at = pl.ds(pl.multiple_of(item * 2 * half + pair * half, half), half)
+        tokens = ffn_in[item, pl.ds(pair * 4, 4)].reshape(half, width)
+
+        @pl.loop(0, hidden // 256)
+        def _(tile):
+            lanes = pl.ds(pl.multiple_of(tile * 256, 256), 256)
+            up_lanes = pl.ds(pl.multiple_of(hidden + tile * 256, 256), 256)
+            gate = jnp.dot(tokens, w_gu[:, :, :, lanes].reshape(width, 256), preferred_element_type=jnp.float32)
+            up = jnp.dot(tokens, w_gu[:, :, :, up_lanes].reshape(width, 256), preferred_element_type=jnp.float32)
+            gate_up[at, lanes] = gate
+            gate_up[at, up_lanes] = up
+            inner_act[at, lanes] = (gate * (1.0 / (1.0 + jnp.exp(-gate))) * up).astype(inner_act.dtype)
+
+        inner = inner_act[at]
+
+        @pl.loop(0, width // 256)
+        def _(tile):
+            lanes = pl.ds(pl.multiple_of(tile * 256, 256), 256)
+            out = jnp.dot(inner, w_down[:, lanes], preferred_element_type=jnp.float32)
+            partial[item, pl.ds(pair * 4, 4), :, lanes] = out.astype(partial.dtype).reshape(4, rows, 256)
+
+    def backward(item, near):
+        pair = pair_of(near)
+        at = pl.ds(pl.multiple_of(item * 2 * half + pair * half, half), half)
+        grads = ffn_low[item, pl.ds(pair * 4, 4)].reshape(half, width)
+
+        @pl.loop(0, hidden // 256)
+        def _(tile):
+            lanes = pl.ds(pl.multiple_of(tile * 256, 256), 256)
+            up_lanes = pl.ds(pl.multiple_of(hidden + tile * 256, 256), 256)
+            grad = lax.dot_general(grads, w_down[lanes], NT, preferred_element_type=jnp.float32)
+            gate, up = gate_up[at, lanes], gate_up[at, up_lanes]
+            sigmoid = 1.0 / (1.0 + jnp.exp(-gate))
+            gate_up_low[at, lanes] = (grad * up * sigmoid * (1.0 + gate * (1.0 - sigmoid))).astype(gate_up_low.dtype)
+            gate_up_low[at, up_lanes] = (grad * (gate * sigmoid)).astype(gate_up_low.dtype)
+
+        low = gate_up_low[at]
+
+        @pl.loop(0, 4)
+        def _(tile):
+            lanes = pl.ds(pl.multiple_of(tile * (width // 4), 128), width // 4)
+            weight = w_gu[pl.ds(tile * 2, 2)].reshape(width // 4, 2 * hidden)
+            out = lax.dot_general(low, weight, NT, preferred_element_type=jnp.float32)
+            partial[item, pl.ds(pair * 4, 4), :, lanes] = out.astype(partial.dtype).reshape(4, rows, width // 4)
+
+    def down_part(half):
+        at = slice(half * 256, (half + 1) * 256)
+        left = inner_act[:, at]
+        right = ffn_low[...].reshape(left.shape[0], width)
+        grad_down[half] = lax.dot_general(left, right, TN, preferred_element_type=jnp.float32).astype(grad_down.dtype)
+
+    def gu_columns(tile):
+        lanes = slice(tile * (width // 4), (tile + 1) * (width // 4))
+        left = ffn_in[:, :, :, lanes].reshape(gate_up_low.shape[0], width // 4)
+        out = lax.dot_general(left, gate_up_low[...], TN, preferred_element_type=jnp.float32)
+        grad_gu[2 * tile : 2 * tile + 2] = out.astype(grad_gu.dtype).reshape((2,) + grad_gu.shape[1:])
+
+    def to_twin(number):
+        pairs = ((grad_gu.at[:, pl.ds(2 * (1 - core), 2)], got_gu), (grad_down.at[1 - core], got_down))
+        return remote(*pairs[number], swap_send.at[3 + number], swap_recv.at[3 + number], twin)
+
+    def to_far():
+        return remote(half_gu.at[:, 1 - far], far_gu, swap_send.at[5], swap_recv.at[5], across_y)
+
+    def exchange():
+        to_twin(0).start()
+        to_twin(1).start()
+
+    def exchange_far():
+        to_twin(0).wait()
+        to_twin(1).wait()
+        mine = grad_gu[:, pl.ds(2 * core, 2)].astype(jnp.float32)
+        half_gu[...] = (mine + got_gu[...].astype(jnp.float32)).astype(half_gu.dtype)
+        to_far().start()
+        mine = grad_down[core].astype(jnp.float32)
+        half_down[...] = (mine + got_down[...].astype(jnp.float32)).astype(half_down.dtype)
+
+    def scatter(item, source):
+        chain, ref = chains[item], source.at[item]
+        steps = {
+            "sf": functools.partial(chain.scatter_start, ref, False),
+            "sn": functools.partial(chain.scatter_start, ref, True),
+            "h": functools.partial(chain.scatter_hand, ref),
+            "se": functools.partial(chain.scatter_end, ref, result.at[item]),
+        }
+        for number in range(3):
+            steps[f"b{number}"] = functools.partial(chain.scatter_over, ref, number)
+            steps[f"a{number}"] = functools.partial(chain.scatter_along, ref, number)
+        return steps
+
+    def gather(item, phase, target):
+        chain, mine, ref = chains[item], own.at[phase * items + item], target.at[item]
+        steps = {
+            "gs": functools.partial(chain.gather_start, mine, ref),
+            "t": functools.partial(chain.gather_turn, mine, ref),
+            "ge": functools.partial(chain.gather_end, mine, ref),
+        }
+        for step in range(1, DEPTH):
+            steps[f"g{step}"] = functools.partial(chain.gather_step, ref, step)
+        return steps
+
+    def working(item, work):
+        return {"wf": functools.partial(work, item, False), "wn": functools.partial(work, item, True)}
+
+    def run(order, *tables):
+        steps = {}
+        for table in tables:
+            steps.update(table)
+        for name in order:
+            if name in steps:
+                steps[name]()
+
+    weights = {f"d{half}": functools.partial(down_part, half) for half in range(2)}
+    weights.update({f"u{tile}": functools.partial(gu_columns, tile) for tile in range(4)})
+    weights.update({"c": exchange, "y": exchange_far})
+    run(ORDER, scatter(0, parts))
+    middle_of(0)
+    quarter_on(0).wait()
+    quarter_on(2).start()
+    run(ORDER, gather(0, 0, ffn_in), scatter(1, parts))
+    middle_of(1)
+    quarter_on(1).wait()
+    quarter_on(2).wait()
+    run(ORDER, gather(1, 0, ffn_in), scatter(0, partial), working(0, forward))
+    outcome(0)
+    run(ORDER, gather(0, 1, ffn_low), scatter(1, partial), working(1, forward))
+    outcome(1)
+    run(ORDER, gather(1, 1, ffn_low), scatter(0, partial), working(0, backward))
+    back_to_attention(0)
+    run(LAST_ORDER, gather(0, 2, projected_low), scatter(1, partial), working(1, backward), weights)
+    back_to_attention(1)
+    run(END_ORDER, gather(1, 2, projected_low), weights)
+    to_far().wait()
+    mine = half_gu[:, pl.ds(far, 1)][:, 0].astype(jnp.float32)
+    sum_gu[...] = (mine + far_gu[...].astype(jnp.float32)).astype(sum_gu.dtype)
+
+
+def feed_forward(parts, states, cotangent, live, modulation, gains, gu_part, w_down, ident):
+    items, ranks, rows, width = parts.shape
+    tokens, hidden = items * ranks * rows, w_down.shape[0]
+    low, single = parts.dtype, jnp.float32
+    first = split_chain(width)
+    wave = pltpu.SemaphoreType.DMA
+
+    def slots(size, count=(DEPTH,)):
+        return pltpu.VMEM(count + (rows, size), low)
+
+    flow = [slots(first)] * 5 + [slots(width - first)] * 8 + [slots(width - first, ())] * 2
+    waves = [wave((DEPTH + 1,))] * 2 + [wave((3, 2, DEPTH))] * 2
+    waves += [wave((DEPTH + 1,))] * 2 + [wave((3, 2, DEPTH)), wave((3, DEPTH))]
+    quarters, pair = ((ranks, count) + gu_part.shape[1:] for count in (4, 2))
+    local = jax.ShapeDtypeStruct(states.shape, single)
+    everywhere = jax.ShapeDtypeStruct(parts.shape, low)
+    return pl.pallas_call(
+        feed_forward_kernel,
+        out_shape=[
+            local,
+            local,
+            everywhere,
+            jax.ShapeDtypeStruct((tokens, hidden), low),
+            everywhere,
+            jax.ShapeDtypeStruct((tokens, 2 * hidden), low),
+            everywhere,
+            jax.ShapeDtypeStruct((16, width), single),
+            jax.ShapeDtypeStruct(gu_part.shape, low),
+            jax.ShapeDtypeStruct((hidden // 2, width), low),
+        ],
+        in_specs=[NEAR] * 8,
+        out_specs=[NEAR] * 10,
+        scratch_shapes=[
+            pltpu.VMEM((tokens, 2 * hidden), single),
+            pltpu.VMEM(states.shape, single),
+            pltpu.VMEM(states.shape, single),
+            pltpu.VMEM(states.shape, single),
+            pltpu.VMEM((3 * items, rows, width), low),
+            pltpu.VMEM(parts.shape, low),
+            pltpu.VMEM(quarters, low),
+            pltpu.VMEM(quarters, low),
+            pltpu.VMEM((2, hidden // 2, width), low),
+            pltpu.VMEM(pair, low),
+            pltpu.VMEM((hidden // 2, width), low),
+            pltpu.VMEM(pair, low),
+            pltpu.VMEM(gu_part.shape, low),
+            wave((6,)),
+            wave((6,)),
+        ]
+        + flow * items
+        + waves * items,
+        name=f"feed_forward_{ident}",
+        compiler_params=pltpu.CompilerParams(
+            collective_id=ident, has_side_effects=True, vmem_limit_bytes=58 << 20
+        ),
+    )(parts, states, cotangent, live, modulation, gains, gu_part, w_down)
 
 
 def lay_flat(vectors):
@@ -1812,9 +2367,6 @@
     counts = counts.astype(jnp.int32)
     text_inverse = text_inverse.reshape(-1, 1)
     scale_attn = modulation[:, None, 0:width]
-    gate_attn = jnp.tanh(modulation[:, None, width : 2 * width])
-    scale_ffn = modulation[:, None, 2 * width : 3 * width]
-    gate_ffn = jnp.tanh(modulation[:, None, 3 * width :])
 
     slot_in_row = jnp.arange(slots) // COLS
     live_mask = (slot_in_row[None, :] < counts_here[0][:, None]).astype(single)[..., None]
@@ -1827,9 +2379,6 @@
     attn_in = gather_tokens((norm_in * (1.0 + scale_attn)).astype(narrow), 1)
     hidden = w_down.shape[0]
     gu_rows = pack_quarter(w_gu, (2 * core + far).reshape(1), 2, ranks)
-    gu_rows, attn_in = lax.optimization_barrier((gu_rows, attn_in))
-    gu_part = lax.all_to_all(gu_rows, "rows", 0, 0, tiled=True)
-    gu_pair = join_blocks(gu_part, swap(gu_part, FARS), far_bit)
 
     features = text_width // ranks
     features = text_width // ranks
@@ -1840,6 +2389,8 @@
 
     text_parts = pack_blocks(dot(text_norm, w_text).astype(narrow), 2, ranks, narrow)
     text_proj = scatter_rows(text_parts, 2, 0).reshape(ranks, items, text_local, 2 * span)
+    gu_rows, text_proj = lax.optimization_barrier((gu_rows, text_proj))
+    gu_part = lax.all_to_all(gu_rows, "rows", 0, 0, tiled=True)
     qkv_proj, squares = project(attn_in, qkv_here, text_proj)
     totals = sum_rows(squares, 3)
     gains_both = jnp.concatenate([gain_here(1), gain_here(2)])[None]
@@ -1859,70 +2410,24 @@
         text_len[0],
         head_size,
     )
-    projected = scatter_tokens(out_parts, items, 4)
-
-    unit_proj, inverse_proj = norm_parts(projected)
-    norm_proj = unit_proj * gains[3]
-    middle = states + gate_attn * norm_proj
-    unit_mid, inverse_mid = norm_parts(middle)
-    norm_mid = unit_mid * gains[4]
-    ffn_in = gather_tokens((norm_mid * (1.0 + scale_ffn)).astype(narrow), 5)
-    gu_columns = join_blocks(gu_pair, swap(gu_pair, CORES), core_bit)
-    gu_here = gu_columns.reshape(width, 2 * w_down.shape[0])
-    gate_up = dot(ffn_in, gu_here)
-    gate_part, up_part = jnp.split(gate_up, 2, axis=1)
-    sigmoid = 1.0 / (1.0 + jnp.exp(-gate_part))
-    inner_act = (gate_part * sigmoid * up_part).astype(narrow)
-    ffn_out = scatter_tokens(dot(inner_act, w_down), items, 6)
-    unit_ffn, inverse_ffn = norm_parts(ffn_out)
-    norm_ffn = unit_ffn * gains[5]
-    output = live_mask * (middle + gate_ffn * norm_ffn)
-
-    def over_tokens(values):
-        return jnp.sum(values, axis=(0, 1))
-
-    grad_result = live_mask * cotangent[0].reshape(items, slots, width)
-    grad_gate_ffn = (1.0 - gate_ffn * gate_ffn)[:, 0] * jnp.sum(grad_result * norm_ffn, axis=1)
-    grad_norm = gate_ffn * grad_result
-    grad_five = over_tokens(grad_norm * unit_ffn)
-    ffn_low = gather_tokens(
-        norm_back(unit_ffn, inverse_ffn, grad_norm * gains[5]).astype(narrow), 7
-    )
-    grad_down = weight_grad(inner_act, ffn_low).astype(narrow).reshape(2, -1, width)
-    give_down, keep_down = give_keep(grad_down, core, 0)
-    grad_inner = dot_back(ffn_low, w_down)
-    gate_up_low = jnp.concatenate(
-        [
-            grad_inner * up_part * sigmoid * (1.0 + gate_part * (1.0 - sigmoid)),
-            grad_inner * gate_part * sigmoid,
-        ],
-        axis=1,
-    ).astype(narrow)
-    grad_gu = weight_grad(ffn_in, gate_up_low).astype(narrow)
-    give_gu, keep_gu = give_keep(grad_gu.reshape(ranks, 2, -1, 2 * hidden), core, 1)
-    grad_ffn_in, got_down, got_gu = scatter_tokens(
-        dot_back(gate_up_low, gu_here), items, 8, swaps=((give_down, "core"), (give_gu, "core"))
-    )
-    half_down = add_low(keep_down, got_down)
-    half_gu = add_low(keep_gu, got_gu)
-    give_gu, keep_gu = give_keep(half_gu.reshape(ranks, 2, -1, 2 * hidden), far, 1)
-    grad_scale_ffn = jnp.sum(grad_ffn_in * norm_mid, axis=1)
-    grad_norm = grad_ffn_in * (1.0 + scale_ffn)
-    grad_four = over_tokens(grad_norm * unit_mid)
-    grad_middle = grad_result + norm_back(unit_mid, inverse_mid, grad_norm * gains[4])
-
-    grad_gate_attn = (1.0 - gate_attn * gate_attn)[:, 0] * jnp.sum(grad_middle * norm_proj, axis=1)
-    grad_norm = gate_attn * grad_middle
-    grad_three = over_tokens(grad_norm * unit_proj)
-    projected_low, got_gu, got_down = gather_tokens(
-        norm_back(unit_proj, inverse_proj, grad_norm * gains[3]).astype(narrow),
-        9,
-        swaps=((give_gu, "far"), (half_down, "far")),
-    )
-    sum_gu = add_low(keep_gu, got_gu)
+    live_lanes = jnp.broadcast_to(live_mask, (items, slots, 128))
+    output, grad_middle, _, _, _, _, projected_low, vectors, sum_gu, half_down = feed_forward(
+        out_parts.reshape(items, ranks, slots, width),
+        states,
+        cotangent[0].reshape(items, slots, width),
+        live_lanes,
+        modulation,
+        gains,
+        gu_part,
+        w_down,
+        4,
+    )
+    projected_low = projected_low.reshape(tokens, width)
     rows_gu = lax.all_to_all(sum_gu, "rows", 0, 0, tiled=True)
+    got_down = swap(half_down, FARS)
     grad_out = weight_grad(combined, projected_low).astype(narrow).reshape(2, -1, width)
     give_out, keep_out = give_keep(grad_out, core, 0)
+
     scaled, grad_value, text_scaled, text_value, sums, gain_sums, gate_sums = attend_back(
         projected_low,
         w_out,
@@ -1938,17 +2443,14 @@
         counts,
         text_len[0],
         head_size,
-        (sum_gu, give_out),
-    )
+        (give_out,),
+    )
+    half_out = add_low(keep_out, swap(give_out, CORES))
     sum_down = add_low(half_down, got_down)
-    half_out = add_low(keep_out, swap(give_out, CORES))
-    grad_gate = (1.0 - gate_here * gate_here) * jnp.sum(
-        gate_sums.reshape(heads_here, head_size), axis=1
-    )
     qkv_low, text_low = norms_back(
         qkv_proj,
         totals,
-        sum_rows(sums, 10, after=(sum_down, half_out, rows_gu)),
+        sum_rows(sums, 10, after=(sum_down, half_out)),
         scaled,
         grad_value,
         text_proj,
@@ -1960,81 +2462,54 @@
     give_qkv, keep_qkv = give_keep(grad_qkv.reshape(ranks, 2, -1, 3 * span), core, 1)
 
     text_low = text_low.reshape(items * text_all, 2 * span)
-    all_low, got_gu, got_out, got_qkv, got_down = gather_rows(
+    half_qkv = add_low(keep_qkv, swap(give_qkv, CORES))
+    attn_parts = dot_back(qkv_low, qkv_here)
+    got_gu = swap(rows_gu, FARS)
+    all_low, got_out, got_qkv, got_down = gather_rows(
         text_low,
         12,
         0,
-        swaps=((rows_gu, "far"), (half_out, "far"), (give_qkv, "core"), (sum_down, "core")),
-    )
+        after=(got_gu, attn_parts),
+        swaps=((half_out, "far"), (half_qkv, "far"), (sum_down, "core")),
+    )
+    pair_gu = join_blocks(rows_gu, got_gu, far_bit)
     all_low = unpack_blocks(all_low, 2, narrow)
     grad_text = weight_grad(text_norm, all_low).astype(narrow).reshape(2, -1, 2 * width)
     give_text, keep_text = give_keep(grad_text, core, 0)
     half_text = add_low(keep_text, swap(give_text, CORES))
-    middle_row = half_text.shape[0] // 2
-    pair_gu = join_blocks(rows_gu, got_gu, far_bit)
-    sum_out, half_qkv = add_low(half_out, got_out), add_low(keep_qkv, got_qkv)
-    grad_attn_in, got_qkv, got_text, got_out, got_gu = scatter_tokens(
-        dot_back(qkv_low, qkv_here),
+    sum_out, sum_qkv = add_low(half_out, got_out), add_low(half_qkv, got_qkv)
+    grad_attn_in, got_text, got_out, got_gu = scatter_tokens(
+        attn_parts,
         items,
         11,
-        swaps=(
-            (half_qkv, "far"),
-            (half_text[:middle_row], "far"),
-            (sum_out, "core"),
-            (pair_gu, "core"),
-        ),
-    )
-    sum_qkv = add_low(half_qkv, got_qkv)
+        swaps=((half_text, "far"), (sum_out, "core"), (pair_gu, "core")),
+    )
+    sum_qkv, grad_attn_in = lax.optimization_barrier((sum_qkv, grad_attn_in))
     rows_qkv = lax.all_to_all(sum_qkv, "rows", 0, 0, tiled=True)
-    sum_text = [add_low(half_text[:middle_row], got_text)]
-    grad_scale_attn = jnp.sum(grad_attn_in * norm_in, axis=1)
-    grad_norm = grad_attn_in * (1.0 + scale_attn)
-    grad_zero = over_tokens(grad_norm * unit_in)
-    grad_x = grad_middle + norm_back(unit_in, inverse_in, grad_norm * gains[0])
-
+    sum_text = add_low(half_text, got_text)
     grad_text_gain = jnp.sum(dot_back(all_low, w_text) * text_unit, axis=0)
-    grad_modulation = jnp.stack([grad_scale_attn, grad_gate_attn, grad_scale_ffn, grad_gate_ffn], 1)
-    grad_gains = jnp.stack(
-        [
-            grad_zero,
-            spread(gain_sums[0, :span], width),
-            spread(gain_sums[0, span:], width),
-            grad_three,
-            grad_four,
-            grad_five,
-            spread(gain_sums[1, :span], width),
-        ]
-    )
-    flat = jnp.concatenate(
-        [
-            grad_gains.reshape(-1),
-            spread(grad_text_gain, text_width),
-            spread(grad_gate, heads),
-        ]
-    )
-    lanes = ranks * 128
-    sum_depth = -(-flat.size // lanes)
-    flat = jnp.pad(flat, (0, sum_depth * lanes - flat.size)).reshape(ranks, sum_depth, 128)
-    time_rows = spread(time_here.astype(single), ranks * time_here.size).reshape(ranks, -1, 128)
-    grad_depth, time_depth = grad_modulation.size // lanes, time_rows.shape[1]
-    keep_depth = grad_depth + time_depth
-    reduced, got_text, other_text = final_sums(
-        jnp.concatenate([flat, grad_modulation.reshape(ranks, grad_depth, 128), time_rows], axis=1),
-        sum_depth,
-        13,
-        swaps=((half_text[middle_row:], "far"), (sum_text[0], "core")),
-    )
-    sum_text.append(add_low(half_text[middle_row:], got_text))
-    sum_text = jnp.concatenate(sum_text)
-    got_text = jnp.concatenate([other_text, swap(sum_text[middle_row:], CORES)])
-    flat = reduced[:, :sum_depth].reshape(-1)
+    grad_x, small = finish(
+        grad_attn_in,
+        states,
+        grad_middle,
+        modulation,
+        gains,
+        vectors,
+        gain_sums,
+        gate_sums,
+        grad_text_gain[None],
+        time_here.astype(single),
+    )
+    reduced, got_text = final_sums(small, SUM_DEPTH, 13, swaps=((sum_text, "core"),))
+    flat = reduced[:, :SUM_DEPTH].reshape(-1)
     total_gains = flat[: gains.size].reshape(gains.shape)
     total_text_gain = flat[gains.size : gains.size + text_width]
-    total_gate = flat[gains.size + text_width : gains.size + text_width + heads]
+    total_gate = jnp.sum(flat[-width:].reshape(heads, head_size), axis=1)
+    total_gate = total_gate * (1.0 - jnp.tanh(cross_gate) ** 2)
     groups = lax.axis_size("items")
-    kept = reduced[:, sum_depth:].reshape(ranks, groups, keep_depth, 128)
-    all_modulation = jnp.swapaxes(kept[:, :, :grad_depth], 0, 1).reshape(groups * items, 4 * width)
-    all_time = lax.dynamic_index_in_dim(kept[:, :, grad_depth:], place, 0, keepdims=False)
+    kept = reduced[:, SUM_DEPTH:].reshape(ranks, groups, -1, 128)
+    all_modulation = jnp.swapaxes(kept[:, :, : width // 128], 0, 1).reshape(groups * items, 4 * width)
+    all_time = lax.dynamic_index_in_dim(kept[:, :, width // 128 :], place, 0, keepdims=False)
     all_time = all_time.reshape(groups * items, ada_depth)
     final_ada = jnp.einsum(
         "tk,tn->kn",
@@ -2050,7 +2525,7 @@
     sums = [
         unpack_halves(rows_qkv, swap(rows_qkv, CORES), 3),
         whole_rows(sum_out, got_out),
-        whole_rows(sum_text, swap(sum_text, CORES)),
+        whole_rows(sum_text, got_text),
         unpack_halves(pair_gu, got_gu, 2),
         whole_rows(sum_down, got_down),
     ]

time: 728 us -> 667 us (0.916)
  Pallas kernels: 528 us -> 501 us
  other arithmetic: 43.8 us -> 21.6 us
  matrix products: 42 us -> 24.4 us
  waiting for transfers between devices: 0.02 us -> 8.93 us
    pallas_call x0 -> x2, Pallas kernels: none -> 210 us  [the longest x1 209 us: feed_forward(): pl.pallas_call(feed_forward_kernel, out_shape=[local, local, everywhere,...]
    pallas_call x5 -> x2, Pallas kernels: 180 us -> 68.4 us  [scatter_rows(): pl.pallas_call(functools.partial(scatter_kernel, axis, swaps, len(after))...]
    pallas_call x5 -> x2, Pallas kernels: 175 us -> 70.4 us  [gather_rows(): pl.pallas_call(functools.partial(gather_kernel, axis, swaps, len(after)),...]
    pallas_call x3 -> x1, Pallas kernels: 16.2 us -> 4.15 us  [join_blocks(): pl.pallas_call(kernel, grid=(ranks,), out_shape=jax.ShapeDtypeStruct((ran...]
    unnamed x279 -> x194, local copies, waits for them, and re-layouts: 43.2 us -> 54.8 us
    ppermute x6, waiting for transfers between devices: 0.02 us -> 8.92 us  [swap(): return lax.ppermute(array, 'items', pairs)]
    another operation x12 -> x1, local copies, waits for them, and re-layouts: 8.87 us -> 0.01 us  [the longest x8 7.74 us: head_parallel_plan(): jnp.stack([grad_zero, spread(gain_sums[0, :span], width), spread(gain_sum...]
    dot_general x4 -> x2, matrix products: 10.1 us -> 2.75 us  [dot(): return jnp.dot(left, right, preferred_element_type=single)]
  transfers between devices with their start and end apart: 9 -> 9, of which waited for: 0 -> 1; matrix products, arithmetic and copies ran while one was open for 9% -> 10% of each run, Pallas kernels for 29% -> 23%
where the time goes in v6:
time: 667 us; the launch traced here: 655 us
  Pallas kernels  501 us (75%)
  local copies, waits for them, and re-layouts  81.9 us (12%)
  matrix products  24.4 us (4%)
  other arithmetic  21.6 us (3%)
  starting transfers between devices  15.3 us (2%)
  waiting for transfers between devices  8.93 us (1%)
    pallas_call x1, Pallas kernels, feed_forward(): pl.pallas_call(feed_forward_kernel, out_shape=[local, local, everywhere,...  209 us
    pallas_call x2, Pallas kernels, gather_rows(): pl.pallas_call(functools.partial(gather_kernel, axis, swaps, len(after)),...  70.4 us
    pallas_call x2, Pallas kernels, scatter_rows(): pl.pallas_call(functools.partial(scatter_kernel, axis, swaps, len(after))...  68.4 us
    unnamed x194, local copies, waits for them, and re-layouts  54.8 us
    pallas_call x1, Pallas kernels, first_transfers(): pl.pallas_call(functools.partial(first_kernel, ranks, quarters), out_shap...  34.9 us
    pallas_call x1, Pallas kernels, attend_back(): pl.pallas_call(body, out_shape=[jax.ShapeDtypeStruct((tokens, 2 * span),...  28.8 us
    pallas_call x1, Pallas kernels, final_sums(): pl.pallas_call(functools.partial(final_kernel, ranks, groups, sums, swaps...  27 us
    pallas_call x1, Pallas kernels, attend(): pl.pallas_call(body, out_shape=[jax.ShapeDtypeStruct((tokens, width), low...  19 us
  transfers between devices with their start and end apart: 9, of which 1 were waited for; matrix products, arithmetic and copies ran while one was open for 10% of the time, Pallas kernels for 23%

profile of v6, /device:TPU:0, one launch (start us, length us, event | category | flops | bytes accessed | tf_op | source)
XLA Modules:
  0.0 655.1 jit_solution(15910457599829303350)
XLA Ops:
  2.1 1.7 convolution_bitcast_fusion
  5.4 1.5 copy-done.19
  7.8 34.9 %first_transfers_0.1 = (f32[104,128]{1,0:T(8,128)S(1)}, bf16[8,192,576]{2,1,0:T(8,128)(2,1)S(1)}, bf16[8,2,16,512]{3,2,1,0:T(8,128)(2,1)S(1)}) custom-call(f32[104,128]{1,0:T(8,128)S(1)} %pad_bitcast_fusion.own, bf16[192,4608]{1,0:T(8,128)(2,1)S(1)} %copy-done.19, bf16[2,16,4096]{2,1,0:T(8,128)(2,1)S(1)} %bitcast.86), custom_call_target="tpu_custom_call" | custom-call | tf_op jit(solution)/shard_map/first_transfers_0/pallas_call | solution.py:1056
  47.5 30.1 %scatter_rows_2.1 = f32[256,384]{1,0:T(8,128)S(1)} custom-call(bf16[8,256,384]{2,1,0:T(8,128)(2,1)S(1)} %pack_blocks.1.parts), custom_call_target="tpu_custom_call" | custom-call | tf_op jit(solution)/shard_map/scatter_rows_2/pallas_call | solution.py:816
  77.7 1.9 copy-done.13
  80.5 4.2 all-to-all-start
  86.1 1.4 reshape.210
  89.0 2.2 fusion.11
  93.7 2.0 multiply_convert_fusion.own
  95.8 39.3 %gather_rows_1.1 = bf16[2,8,64,1536]{3,2,1,0:T(8,128)(2,1)} custom-call(bf16[2,64,1536]{2,1,0:T(8,128)(2,1)} %multiply_convert_fusion.own), custom_call_target="tpu_custom_call" | custom-call | tf_op jit(solution)/shard_map/gather_rows_1/pallas_call | solution.py:645
  135.1 1.5 copy-done.18
  136.6 4.9 project.1
  141.5 1.5 copy-done.1
  143.6 7.9 %sum_rows_3.1.refs_4_.refs_8_.totals = f32[24,128]{1,0:T(8,128)} custom-call(f32[24,128]{1,0:T(8,128)} %copy-done.65), custom_call_target="tpu_custom_call" | custom-call | tf_op jit(solution)/shard_map/sum_rows_3/pallas_call | solution.py:860
  155.9 1.7 copy-done.2
  160.1 19.0 %attend.1 = (bf16[1024,1536]{1,0:T(8,128)(2,1)}, bf16[1024,192]{1,0:T(8,128)(2,1)S(1)}, bf16[1024,576]{1,0:T(8,128)(2,1)S(1)}, bf16[2,128,384]{2,1,0:T(8,128)(2,1)S(1)}, f32[4,32,128]{2,1,0:T(8,128)S(1)}) custom-call(s32[16]{0:T(128)S(1)} %slice_convert_fusion.refs_0_, s32[2]{0:T(128)S(1)} %bitcast.93, s32[2]{0:T(128)S(1)} %bitcast.91, ...), custom_call_target="tpu_custom_call" | custom-call | tf_op jit(solution)/shard_map/attend/pallas_call | solution.py:1400
  183.7 208.6 %feed_forward_4.1 = (f32[2,64,1536]{2,1,0:T(8,128)}, f32[2,64,1536]{2,1,0:T(8,128)}, bf16[2,8,64,1536]{3,2,1,0:T(8,128)(2,1)}, bf16[1024,512]{1,0:T(8,128)(2,1)}...) custom-call(bf16[2,8,64,1536]{3,2,1,0:T(8,128)(2,1)} %bitcast.103, ...), custom_call_target="tpu_custom_call" | custom-call | tf_op jit(solution)/shard_map/feed_forward_4/pallas_call | solution.py:2211
  392.3 1.5 collective-permute-start
  393.8 2.7 convolution_convert_fusion.3
  398.1 4.2 all-to-all-start.1
  409.2 28.8 %attend_back.1 = (f32[1024,384]{1,0:T(8,128)S(1)}, bf16[1024,192]{1,0:T(8,128)(2,1)S(1)}, f32[256,192]{1,0:T(8,128)S(1)}, bf16[256,192]{1,0:T(8,128)(2,1)S(1)}, ...) custom-call(s32[16]{0:T(128)S(1)} %copy-done.74, s32[2]{0:T(128)S(1)} %bitcast.92, ...), custom_call_target="tpu_custom_call" | custom-call | tf_op jit(solution)/shard_map/attend_back/pallas_call | solution.py:1567
  443.0 1.7 fusion.3.rest_1_.rest_0_
  444.8 2.2 add_convert_fusion.2.rest_0_.rest_2_.own
  447.0 9.0 %sum_rows_10.1.sums = f32[24,128]{1,0:T(8,128)} custom-call(f32[24,128]{1,0:T(8,128)} %copy-done.64, bf16[256,1536]{1,0:T(8,128)(2,1)} %add_convert_fusion.2.rest_0_.rest_2_.own, bf16[96,1536]{1,0:T(8,128)(2,1)} %fusion.3.rest_1_.rest_0_), custom_call_target="tpu_custom_call" | custom-call | tf_op jit(solution)/shard_map/sum_rows_10/pallas_call | solution.py:860
  461.0 2.7 norms_back.1
  465.5 3.3 convolution_convert_fusion.2
  468.8 3.9 copy.29
  472.7 2.2 dynamic-slice_bitcast_fusion.1
  475.6 8.3 %fusion.12 = (bf16[1024,1536]{1,0:T(8,128)(2,1)}, f32[1024,1536]{1,0:T(8,128)}) fusion(bf16[1024,576]{1,0:T(8,128)(2,1)} %copy-done.78, bf16[1536,576]{1,0:T(8,128)(2,1)} %bitcast.81), kind=kOutput, calls=%fused_computation.54 | convolution fusion | flops 1813512192 | bytes 12386304 | tf_op jit(solution)/shard_map/tn,kn->tk/dot_general | solution.py:2336
  483.9 2.4 fusion.1.rest_1_
  486.3 8.9 %collective-permute-done.3.rest_3_.two = bf16[8,48,1024]{2,1,0:T(8,128)(2,1)} collective-permute-done((bf16[8,48,1024]{2,1,0:T(8,128)(2,1)}, bf16[8,48,1024]{2,1,0:T(8,128)(2,1)}, u32[]{:S(2)}, u32[]{:S(2)}) %collective-permute-start.3) | collective-permute-done | bytes 786464 | tf_op jit(solution)/shard_map/ppermute | solution.py:2281
  495.2 31.1 %gather_rows_12.1 = (bf16[8,256,384]{2,1,0:T(8,128)(2,1)}, bf16[96,1536]{1,0:T(8,128)(2,1)}, bf16[8,96,576]{2,1,0:T(8,128)(2,1)}, bf16[256,1536]{1,0:T(8,128)(2,1)}) custom-call(bf16[256,384]{1,0:T(8,128)(2,1)} %bitcast.87, bf16[96,1536]{1,0:T(8,128)(2,1)} %fusion.3.rest_1_.rest_0_, bf16[8,96,576]{2,1,0:T(8,128)(2,1)} %fusion.1.rest_1_, ...), custom_call_target="tpu_custom_call" | custom-call | tf_op jit(solution)/shard_map/gather_rows_12/pallas_call | solution.py:645
  526.3 1.4 copy-done.26
  529.8 4.2 join_blocks.1.rest_2_.own
  536.1 1.8 copy-done.12
  538.0 38.3 %scatter_rows_11.1 = (f32[2,64,1536]{2,1,0:T(8,128)S(1)}, bf16[256,3072]{1,0:T(8,128)(2,1)S(1)}, bf16[96,1536]{1,0:T(8,128)(2,1)S(1)}, bf16[8,96,1024]{2,1,0:T(8,128)(2,1)S(1)}) custom-call(bf16[2,8,64,1536]{3,2,1,0:T(8,128)(2,1)S(1)} %bitcast.80, bf16[256,3072]{1,0:T(8,128)(2,1)S(1)} %fusion.rest_0_, bf16[96,1536]{1,0:T(8,128)(2,1)S(1)} %add_convert_fusion.3.rest_1_.own, ...), custom_call_target="tpu_custom_call" | custom-call | tf_op jit(solution)/shard_map/scatter_rows_11/pallas_call | solution.py:816
  580.2 4.7 all-to-all-start.2
  587.1 2.1 join_rows.5
  591.1 1.5 finish.1
  592.5 1.7 add_convert_fusion.rest_0_.own
  594.3 27.0 %final_sums_13.1 = (f32[8,72,128]{2,1,0:T(8,128)}, bf16[256,3072]{1,0:T(8,128)(2,1)}) custom-call(f32[8,30,128]{2,1,0:T(8,128)} %copy-done.56, bf16[256,3072]{1,0:T(8,128)(2,1)} %add_convert_fusion.rest_0_.own), custom_call_target="tpu_custom_call" | custom-call | tf_op jit(solution)/shard_map/final_sums_13/pallas_call | solution.py:935
  621.3 1.6 slice.57
  628.5 1.7 reshape.229
  633.0 3.1 unpack_halves.3
  636.1 3.0 join_rows.4
  639.1 1.6 reduce_sum.49
  644.7 5.2 fusion.13
  650.0 3.8 unpack_halves.2
  (254 shorter events, 73.1 us)
Async XLA Ops:
  0.6 45.5 %copy-start = (bf16[512,3072]{1,0:T(8,128)(2,1)S(1)}, bf16[512,3072]{1,0:T(8,128)(2,1)}, u32[]{:S(2)}) copy-start(bf16[512,3072]{1,0:T(8,128)(2,1)} %param.26) | copy-start | bytes 9437188
  0.7 4.6 copy-start.94
  44.1 3.1 copy-start.20
  44.8 2.4 copy-start.92
  77.7 1.9 copy-start.13
  80.5 102.5 %all-to-all-start = ((bf16[8,48,1024]{2,1,0:T(8,128)(2,1)}), bf16[8,48,1024]{2,1,0:T(8,128)(2,1)}, u32[]{:S(2)}, u32[]{:S(2)}) async-start(bf16[8,48,1024]{2,1,0:T(8,128)(2,1)} %copy-done.14), calls=%async_computation | async-start | bytes 1572864 | tf_op jit(solution)/shard_map/all_to_all | solution.py:2393
  135.1 1.5 copy-start.18
  136.6 19.3 %copy-start.71 = (s32[1,2]{1,0:T(1,128)S(1)}, s32[1,2]{1,0:T(1,128)}, u32[]{:S(2)}) copy-start(s32[1,2]{1,0:T(1,128)} %param.23) | copy-start | bytes 28
  153.0 239.3 %copy-start.68 = (f32[1,192]{1,0:T(1,128)}, f32[1,192]{1,0:T(1,128)S(1)}, u32[]{:S(2)}) copy-start(f32[1,192]{1,0:T(1,128)S(1)} %get-tuple-element.102.refs_7_.refs_11_) | copy-start | bytes 2308
  155.2 237.1 %copy-start.66 = (f32[1,192]{1,0:T(1,128)}, f32[1,192]{1,0:T(1,128)S(1)}, u32[]{:S(2)}) copy-start(f32[1,192]{1,0:T(1,128)S(1)} %broadcast_in_dim_reshape.3.refs_8_.refs_12_) | copy-start | bytes 2308
  155.9 23.2 %copy-start.73 = (s32[16]{0:T(128)}, s32[16]{0:T(128)S(1)}, u32[]{:S(2)}) copy-start(s32[16]{0:T(128)S(1)} %slice_convert_fusion.refs_0_) | copy-start | bytes 196
  155.9 1.7 copy-start.2
  183.7 210.1 %copy-start.39 = (bf16[1024,192]{1,0:T(8,128)(2,1)S(1)}, bf16[1024,192]{1,0:T(8,128)(2,1)}, u32[]{:S(2)}) copy-start(bf16[1024,192]{1,0:T(8,128)(2,1)} %copy-done.38) | copy-start | bytes 1179652
  392.3 52.5 %collective-permute-start = (bf16[256,1536]{1,0:T(8,128)(2,1)}, bf16[256,1536]{1,0:T(8,128)(2,1)}, u32[]{:S(2)}, u32[]{:S(2)}) collective-permute-start(bf16[256,1536]{1,0:T(8,128)(2,1)} %get-tuple-element.68), channel_id=1, source_target_pairs={{0,16},{8,24},{16,0},{24,8},{1,17},{9,25},{17,1},{25,9},{2,18},{10... | collective-permute-start | bytes 2359304 | tf_op jit(solution)/shard_map/ppermute | solution.py:2281
  396.6 5.8 copy-start.53
  398.1 44.9 %collective-permute-start.1 = (bf16[96,1536]{1,0:T(8,128)(2,1)}, bf16[96,1536]{1,0:T(8,128)(2,1)}, u32[]{:S(2)}, u32[]{:S(2)}) collective-permute-start(bf16[96,1536]{1,0:T(8,128)(2,1)} %dynamic-slice_bitcast_fusion.2.refs_13_), channel_id=1, source_target_pairs={{0,8},{8,0},{16,24},{24,16},{1,9},{9,1},{17,25},{25,17},{2,10},{10... | collective-permute-start | bytes 884744 | tf_op jit(solution)/shard_map/ppermute | solution.py:2281
  398.1 76.8 %all-to-all-start.1 = ((bf16[8,48,1024]{2,1,0:T(8,128)(2,1)}), bf16[8,48,1024]{2,1,0:T(8,128)(2,1)}, u32[]{:S(2)}, u32[]{:S(2)}) async-start(bf16[8,48,1024]{2,1,0:T(8,128)(2,1)} %get-tuple-element.75), calls=%async_computation.1 | async-start | bytes 1572864 | tf_op jit(solution)/shard_map/all_to_all | solution.py:2426
  409.2 33.9 %copy-start.84 = (bf16[192,1536]{1,0:T(8,128)(2,1)S(1)}, bf16[192,1536]{1,0:T(8,128)(2,1)}, u32[]{:S(2)}) copy-start(bf16[192,1536]{1,0:T(8,128)(2,1)} %copy-done.83) | copy-start | bytes 1769476
  409.2 35.6 %copy-start.88 = (bf16[256,1536]{1,0:T(8,128)(2,1)S(1)}, bf16[256,1536]{1,0:T(8,128)(2,1)}, u32[]{:S(2)}) copy-start(bf16[256,1536]{1,0:T(8,128)(2,1)} %get-tuple-element.68) | copy-start | bytes 2359300
  461.0 4.5 copy-start.79
  474.9 9.0 %collective-permute-start.2 = (bf16[8,96,576]{2,1,0:T(8,128)(2,1)}, bf16[8,96,576]{2,1,0:T(8,128)(2,1)}, u32[]{:S(2)}, u32[]{:S(2)}) collective-permute-start(bf16[8,96,576]{2,1,0:T(8,128)(2,1)} %dynamic-slice_bitcast_fusion.1), channel_id=1, source_target_pairs={{0,8},{8,0},{16,24},{24,16},{1,9},{9,1},{17,25},{25,17},{2,10},{10... | collective-permute-start | bytes 2654216 | tf_op jit(solution)/shard_map/ppermute | solution.py:2281
  474.9 9.0 %copy-start.81 = (bf16[1536,576]{1,0:T(8,128)(2,1)S(1)}, bf16[1536,576]{1,0:T(8,128)(2,1)}, u32[]{:S(2)}) copy-start(bf16[1536,576]{1,0:T(8,128)(2,1)} %copy.29) | copy-start | bytes 5308420
  474.9 20.3 %collective-permute-start.3 = (bf16[8,48,1024]{2,1,0:T(8,128)(2,1)}, bf16[8,48,1024]{2,1,0:T(8,128)(2,1)}, u32[]{:S(2)}, u32[]{:S(2)}) collective-permute-start(bf16[8,48,1024]{2,1,0:T(8,128)(2,1)} %all-to-all-done.1.one), channel_id=1, source_target_pairs={{0,16},{8,24},{16,0},{24,8},{1,17},{9,25},{17,1},{25,9},{2,18},{10... | collective-permute-start | bytes 2359304 | tf_op jit(solution)/shard_map/ppermute | solution.py:2281
  526.3 1.8 copy-start.21
  529.7 4.3 copy-start.80
  529.7 4.3 copy-start.85
  529.7 5.8 collective-permute-start.4
  533.9 2.2 copy-start.3
  535.5 2.5 copy-start.12
  536.1 40.2 %copy-start.5 = (bf16[256,3072]{1,0:T(8,128)(2,1)}, bf16[256,3072]{1,0:T(8,128)(2,1)S(1)}, u32[]{:S(2)}) copy-start(bf16[256,3072]{1,0:T(8,128)(2,1)S(1)} %fusion.rest_0_) | copy-start | bytes 4718596
  580.2 46.6 %all-to-all-start.2 = ((bf16[8,96,576]{2,1,0:T(8,128)(2,1)}), bf16[8,96,576]{2,1,0:T(8,128)(2,1)}, u32[]{:S(2)}, u32[]{:S(2)}) async-start(bf16[8,96,576]{2,1,0:T(8,128)(2,1)} %add_convert_fusion.1), calls=%async_computation.2 | async-start | bytes 1966080 | tf_op jit(solution)/shard_map/all_to_all | solution.py:2488
  587.1 2.1 copy-start.11
  587.1 2.3 copy-start.22
  589.4 1.6 copy-start.37
  589.4 1.6 copy-start.43
  589.4 1.6 copy-start.44
  589.4 1.6 copy-start.57
  589.4 1.6 copy-start.63
  589.5 1.6 copy-start.70
  589.5 1.6 copy-start.76
  589.5 3.1 copy-start.28
  590.5 2.0 copy-start.6
  592.5 1.7 copy-start.56
  626.8 23.2 %collective-permute-start.5 = (bf16[8,96,576]{2,1,0:T(8,128)(2,1)}, bf16[8,96,576]{2,1,0:T(8,128)(2,1)}, u32[]{:S(2)}, u32[]{:S(2)}) collective-permute-start(bf16[8,96,576]{2,1,0:T(8,128)(2,1)} %all-to-all-done.2.own), channel_id=1, source_target_pairs={{0,8},{8,0},{16,24},{24,16},{1,9},{9,1},{17,25},{25,17},{2,10},{10... | collective-permute-start | bytes 2654216 | tf_op jit(solution)/shard_map/ppermute | solution.py:2281
  633.0 3.1 copy-start.7
  633.0 3.2 copy-start.25
  639.1 5.1 copy-start.95
  650.0 3.8 copy-start.87
  (57 other events, 53.3 us)

commit v7 on v6

--- a/solution.py
+++ b/solution.py
@@ -655,7 +655,6 @@
             wave((CHUNKS * (DEPTH + 1),)),
         ]
         + swaps.scratch(),
-        name=f"gather_rows_{ident}",
         compiler_params=pltpu.CompilerParams(collective_id=ident, has_side_effects=True),
     )(block, *swaps.arrays, *after)
     return (whole, *others) if others else whole
@@ -823,7 +822,6 @@
         + [wave((CHUNKS * (DEPTH + 1),))] * 2
         + [wave((3 * CHUNKS, 2, DEPTH))] * 2
         + swaps.scratch(),
-        name=f"scatter_rows_{ident}",
         compiler_params=pltpu.CompilerParams(
             collective_id=ident, has_side_effects=True, vmem_limit_bytes=32 << 20
         ),
@@ -867,7 +865,6 @@
             pltpu.SemaphoreType.DMA((ranks,)),
             pltpu.SemaphoreType.DMA((ranks,)),
         ],
-        name=f"sum_rows_{ident}",
         compiler_params=pltpu.CompilerParams(collective_id=ident, has_side_effects=True),
     )(own, *after)
 
@@ -949,34 +946,21 @@
             pltpu.SemaphoreType.DMA((ranks,)),
         ]
         + swaps.scratch(),
-        name=f"final_sums_{ident}",
         compiler_params=pltpu.CompilerParams(collective_id=ident, has_side_effects=True),
     )(own, *swaps.arrays)
 
 
-def first_kernel(
-    ranks, quarters, own, qkv, text, total, qkv_out, text_out, held, packed, local,
-    s_send, s_recv, t_send, t_recv, a_send, a_recv, y_send, y_recv, c_send, c_recv,
-):
-    place, group = lax.axis_index("rows"), lax.axis_index("items")
+def first_kernel(ranks, own, text, total, text_out, held, local, s_send, s_recv, t_send, t_recv):
+    place = lax.axis_index("rows")
     others = [lax.rem(place + step, ranks) for step in range(1, ranks)]
-    far = lax.rem(group + 2, 4)
-    twin = group + 1 - 2 * lax.rem(group, 2)
-    depth = qkv.shape[0] // quarters
-    mine = pl.ds(pl.multiple_of(group * depth, 16), depth)
-    fars = pl.ds(pl.multiple_of(far * depth, 16), depth)
     features = text_out.shape[-1]
-    span = qkv.shape[1] // (3 * ranks)
 
     def columns(other):
         return pl.ds(pl.multiple_of(other * features, features), features)
 
-    keeps = [pltpu.make_async_copy(text.at[:, :, columns(place)], text_out.at[place], local.at[0])]
-    keeps[0].start()
-    greet(
-        [(place >= 0, {"rows": other}) for other in others]
-        + [(place >= 0, {"items": far}), (place >= 0, {"items": twin})]
-    )
+    keep = pltpu.make_async_copy(text.at[:, :, columns(place)], text_out.at[place], local)
+    keep.start()
+    greet([(place >= 0, {"rows": other}) for other in others])
 
     def sum_push(step, other, slot):
         return remote(own, held.at[slot], s_send.at[step], s_recv.at[slot], {"rows": other})
@@ -986,35 +970,10 @@
             text.at[:, :, columns(other)], text_out.at[slot], t_send.at[step], t_recv.at[slot], {"rows": other}
         )
 
-    def push(step, other, slot):
-        return remote(
-            packed.at[other, mine], qkv_out.at[slot, mine], a_send.at[step], a_recv.at[slot], {"rows": other}
-        )
-
-    def pass_far(slot):
-        block = qkv_out.at[slot, mine]
-        return remote(block, block, y_send.at[slot], y_recv.at[slot], {"items": far})
-
-    def pass_twin(which, slot):
-        block = qkv_out.at[slot, fars if which else mine]
-        return remote(block, block, c_send.at[which, slot], c_recv.at[which, slot], {"items": twin})
-
     for step, other in enumerate(others):
         sum_push(step, other, place).start()
-    for rank in range(ranks):
-        packed[rank] = jnp.concatenate(
-            [
-                qkv[:, (part * ranks + rank) * span : (part * ranks + rank + 1) * span]
-                for part in range(3)
-            ],
-            axis=1,
-        )
-    for step, other in enumerate(others):
-        push(step, other, place).start()
     for step, other in enumerate(others):
         text_push(step, other, place).start()
-    keeps.append(pltpu.make_async_copy(packed.at[place], qkv_out.at[place], local.at[1]))
-    keeps[1].start()
     held[pl.ds(place, 1)] = own[...][None]
     for step, other in enumerate(others):
         sum_push(step, other, other).wait_recv()
@@ -1023,53 +982,28 @@
         value = value + held[rank]
     total[...] = value
     for step, other in enumerate(others):
-        push(step, other, other).wait_recv()
-        pass_far(other).start()
-        pass_twin(0, other).start()
-    for other in others:
-        pass_far(other).wait_recv()
-        pass_twin(1, other).start()
-    for step, other in enumerate(others):
         sum_push(step, other, place).wait_send()
         text_push(step, other, other).wait_recv()
         text_push(step, other, place).wait_send()
-        push(step, other, place).wait_send()
-        pass_far(other).wait_send()
-        for which in range(2):
-            pass_twin(which, other).wait_recv()
-            pass_twin(which, other).wait_send()
-    for copy in keeps:
-        copy.wait()
-
-
-def first_transfers(own, qkv, text, ident):
-    ranks, quarters = lax.axis_size("rows"), lax.axis_size("items")
-    depth = qkv.shape[0]
+    keep.wait()
+
+
+def first_transfers(own, text, ident):
+    ranks = lax.axis_size("rows")
     anywhere = pl.BlockSpec(memory_space=pl.ANY)
-    near = pl.BlockSpec(memory_space=pltpu.VMEM)
     outs = [
         jax.ShapeDtypeStruct(own.shape, own.dtype),
-        jax.ShapeDtypeStruct((ranks, depth, qkv.shape[1] // ranks), qkv.dtype),
         jax.ShapeDtypeStruct((ranks,) + text.shape[:-1] + (text.shape[-1] // ranks,), text.dtype),
     ]
     wave = pltpu.SemaphoreType.DMA
     return pl.pallas_call(
-        functools.partial(first_kernel, ranks, quarters),
+        functools.partial(first_kernel, ranks),
         out_shape=outs,
-        in_specs=[near, near, anywhere],
-        out_specs=[near, anywhere, anywhere],
-        scratch_shapes=[
-            pltpu.VMEM((ranks,) + own.shape, own.dtype),
-            pltpu.VMEM(outs[1].shape, qkv.dtype),
-            wave((2,)),
-        ]
-        + [wave((ranks,))] * 8
-        + [wave((2, ranks))] * 2,
-        name=f"first_transfers_{ident}",
-        compiler_params=pltpu.CompilerParams(
-            collective_id=ident, has_side_effects=True, vmem_limit_bytes=24 << 20
-        ),
-    )(own, qkv, text)
+        in_specs=[NEAR, anywhere],
+        out_specs=[NEAR, anywhere],
+        scratch_shapes=[pltpu.VMEM((ranks,) + own.shape, own.dtype), wave] + [wave((ranks,))] * 4,
+        compiler_params=pltpu.CompilerParams(collective_id=ident, has_side_effects=True),
+    )(own, text)
 
 
 def quarter_kernel(pieces, at, whole, packed):
@@ -1092,7 +1026,6 @@
             out_specs=pl.BlockSpec(out, lambda step, at: (0, 0, 0)),
         ),
         out_shape=jax.ShapeDtypeStruct(out, whole.dtype),
-        name="pack_quarter",
         compiler_params=local_params(),
     )(at, whole)
 
@@ -1113,7 +1046,6 @@
         out_shape=jax.ShapeDtypeStruct((ranks, whole.shape[0], whole.shape[1] // ranks), dtype),
         in_specs=[near],
         out_specs=near,
-        name="pack_blocks",
         compiler_params=pltpu.CompilerParams(vmem_limit_bytes=24 << 20),
     )(whole)
 
@@ -1136,7 +1068,6 @@
         out_shape=jax.ShapeDtypeStruct((rows, ranks * width), dtype),
         in_specs=[near],
         out_specs=near,
-        name="unpack_blocks",
         compiler_params=pltpu.CompilerParams(vmem_limit_bytes=24 << 20),
     )(packed)
 
@@ -1165,7 +1096,6 @@
         out_shape=jax.ShapeDtypeStruct((2 * half, ranks * width), jnp.float32),
         in_specs=[near, near],
         out_specs=near,
-        name="unpack_halves",
         compiler_params=pltpu.CompilerParams(vmem_limit_bytes=32 << 20),
     )(own, other)
 
@@ -1211,37 +1141,178 @@
     return jnp.transpose(jnp.concatenate([rows, missing], axis=0))
 
 
-def project_kernel(attn, weight, text, proj, squares):
-    span = text.shape[-1] // 2
-    tokens = attn.shape[0]
-    for start in range(0, tokens, 256):
-        proj[start : start + 256] = jnp.dot(
-            attn[start : start + 256], weight[...], preferred_element_type=jnp.float32
-        )
+def open_kernel(
+    total, states, gains, bias, text_parts, qkv,
+    attn, qkv_out, text_out, proj, totals, modulation,
+    own, squares, held, packed, flow, *waves,
+):
+    items, rows, width = states.shape
+    ranks, span = qkv_out.shape[0], text_out.shape[-1] // 2
+    chunks = bias.shape[0]
+    tokens = proj.shape[0]
+    place = lax.axis_index("rows")
+    group = lax.axis_index("items")
+    others = [lax.rem(place + step, ranks) for step in range(1, ranks)]
+    always = place >= 0
+    twin, across_y = partner("core"), partner("far")
+    depth = qkv.shape[0] // 4
+    mine = pl.ds(pl.multiple_of(group * depth, 16), depth)
+    fars = pl.ds(pl.multiple_of(lax.rem(group + 2, 4) * depth, 16), depth)
+    s_send, s_recv, a_send, a_recv, y_send, y_recv, c_send, c_recv = waves[:8]
+    greet([(always, {"rows": other}) for other in others] + [(always, twin), (always, across_y)])
+    text_chain = Chain(row_place(), text_out.shape[-1], flow, waves[8:12], (None,) * 4)
+    chains = [
+        Chain(row_place(), width, (None,) * 15, (None,) * 4, waves[12 + 4 * item : 16 + 4 * item])
+        for item in range(items)
+    ]
+
+    text_chain.scatter_start(text_parts, False)
+    text_chain.scatter_start(text_parts, True)
+    for item in range(items):
+        for chunk in range(chunks):
+            at = item * chunks + chunk
+            modulation[item : item + 1, chunk * 128 : (chunk + 1) * 128] = total[at : at + 1] + bias[chunk : chunk + 1]
+        unit, _ = norm_unit(states[item])
+        own[item] = (unit * gains[0:1] * (1.0 + modulation[item : item + 1, :width])).astype(own.dtype)
+        chains[item].gather_start(own.at[item], attn.at[item])
+
+    def push(step, other, slot):
+        return remote(
+            packed.at[other, mine], qkv_out.at[slot, mine], a_send.at[step], a_recv.at[slot], {"rows": other}
+        )
+
+    def pass_far(slot):
+        block = qkv_out.at[slot, mine]
+        return remote(block, block, y_send.at[slot], y_recv.at[slot], across_y)
+
+    def pass_twin(which, slot):
+        block = qkv_out.at[slot, fars if which else mine]
+        return remote(block, block, c_send.at[which, slot], c_recv.at[which, slot], twin)
+
+    head_span = qkv.shape[1] // (3 * ranks)
+    for rank in range(ranks):
+        packed[rank] = jnp.concatenate(
+            [
+                qkv[:, (part * ranks + rank) * head_span : (part * ranks + rank + 1) * head_span]
+                for part in range(3)
+            ],
+            axis=1,
+        )
+    for step, other in enumerate(others):
+        push(step, other, place).start()
+    qkv_out[pl.ds(place, 1)] = packed[pl.ds(place, 1)]
+
+    for item in range(items):
+        chains[item].gather_turn(own.at[item], attn.at[item])
+    text_chain.scatter_over(text_parts, 0)
+    for step in range(1, DEPTH):
+        for item in range(items):
+            chains[item].gather_step(attn.at[item], step)
+        if step == 1:
+            text_chain.scatter_over(text_parts, 1)
+            text_chain.scatter_over(text_parts, 2)
+        text_chain.scatter_along(text_parts, step - 1)
+        if step == 2:
+            text_chain.scatter_hand(text_parts)
+    for step, other in enumerate(others):
+        push(step, other, other).wait_recv()
+        pass_far(other).start()
+        pass_twin(0, other).start()
+    text_chain.scatter_end(text_parts, text_out)
+    for item in range(items):
+        chains[item].gather_end(own.at[item], attn.at[item])
+    for other in others:
+        pass_far(other).wait_recv()
+        pass_twin(1, other).start()
+    for step, other in enumerate(others):
+        push(step, other, place).wait_send()
+        pass_far(other).wait_send()
+        for which in range(2):
+            pass_twin(which, other).wait_recv()
+            pass_twin(which, other).wait_send()
+
+    weight = qkv_out[...].reshape(width, proj.shape[1])
+    half = tokens // (2 * items)
+    for block in range(2 * items):
+        item, pair = divmod(block, 2)
+        left = attn[item, pair * ranks // 2 : (pair + 1) * ranks // 2].reshape(half, width)
+        proj[block * half : (block + 1) * half] = jnp.dot(left, weight, preferred_element_type=jnp.float32)
     columns = []
     for part in range(2):
         for start in range(0, tokens, 128):
             block = proj[start : start + 128, part * span : (part + 1) * span]
             columns.append(jnp.sum(block * block, axis=1, keepdims=True))
-    for item in range(text.shape[1]):
-        block = text_item(text, item)[:, :span]
+    text_rows = text_out.shape[0] // (ranks * items)
+    for item in range(items):
+        block = text_out[...].reshape(ranks, items, text_rows, 2 * span)[:, item, :, :span]
+        block = block.reshape(ranks * text_rows, span)
         columns.append(jnp.sum(block * block, axis=1, keepdims=True))
     squares[...] = lanes_to_rows(columns, squares.shape[0])
 
-
-def project(attn, weight, text):
-    count = 2 * attn.shape[0] // 128 + text.shape[1]
+    def sum_push(step, other, slot):
+        return remote(squares, held.at[slot], s_send.at[step], s_recv.at[slot], {"rows": other})
+
+    for step, other in enumerate(others):
+        sum_push(step, other, place).start()
+    held[pl.ds(place, 1)] = squares[...][None]
+    for step, other in enumerate(others):
+        sum_push(step, other, other).wait_recv()
+    value = held[0]
+    for rank in range(1, ranks):
+        value = value + held[rank]
+    totals[...] = value
+    for step, other in enumerate(others):
+        sum_push(step, other, place).wait_send()
+
+
+def open_attention(total, states, gains, bias, text_parts, qkv, ident):
+    items, rows, width = states.shape
+    ranks, text_rows, text_width = text_parts.shape
+    low, single = text_parts.dtype, jnp.float32
+    tokens, depth, columns = items * ranks * rows, qkv.shape[0], qkv.shape[1] // ranks
+    count = 2 * tokens // 128 + items
+    squares = (-(-count // 8) * 8, 128)
+    first = split_chain(text_width)
+    wave = pltpu.SemaphoreType.DMA
+
+    def slots(size, count=(DEPTH,)):
+        return pltpu.VMEM(count + (text_rows, size), low)
+
+    flow = [slots(first)] * 5 + [slots(text_width - first)] * 8 + [slots(text_width - first, ())] * 2
+    scatter_waves = [wave((DEPTH + 1,))] * 2 + [wave((3, 2, DEPTH))] * 2
+    gather_waves = [wave((DEPTH + 1,))] * 2 + [wave((3, 2, DEPTH)), wave((3, DEPTH))]
+
+    def body(*refs):
+        ins, outs, rest = refs[:6], refs[6:12], refs[12:]
+        open_kernel(*ins, *outs, *rest[:4], rest[4:19], *rest[19:])
+
     return pl.pallas_call(
-        project_kernel,
+        body,
         out_shape=[
-            jax.ShapeDtypeStruct((attn.shape[0], weight.shape[1]), jnp.float32),
-            jax.ShapeDtypeStruct((-(-count // 8) * 8, 128), jnp.float32),
+            jax.ShapeDtypeStruct((items, ranks, rows, width), low),
+            jax.ShapeDtypeStruct((ranks, depth, columns), low),
+            jax.ShapeDtypeStruct((text_rows, text_width), single),
+            jax.ShapeDtypeStruct((tokens, columns), single),
+            jax.ShapeDtypeStruct(squares, single),
+            jax.ShapeDtypeStruct((items, bias.size), single),
         ],
-        in_specs=[NEAR] * 3,
-        out_specs=[NEAR] * 2,
-        name="project",
-        compiler_params=local_params(),
-    )(attn, weight, text)
+        in_specs=[NEAR] * 6,
+        out_specs=[NEAR] * 6,
+        scratch_shapes=[
+            pltpu.VMEM(states.shape, low),
+            pltpu.VMEM(squares, single),
+            pltpu.VMEM((ranks,) + squares, single),
+            pltpu.VMEM((ranks, depth, columns), low),
+        ]
+        + flow
+        + [wave((ranks,))] * 6
+        + [wave((2, ranks))] * 2
+        + scatter_waves
+        + gather_waves * items,
+        compiler_params=pltpu.CompilerParams(
+            collective_id=ident, has_side_effects=True, vmem_limit_bytes=48 << 20
+        ),
+    )(total, states, gains, bias, text_parts, qkv)
 
 
 def tile_lane():
@@ -1412,7 +1483,6 @@
             pltpu.VMEM((items, tokens // items, 128), jnp.float32),
             pltpu.VMEM((items, text_rows, 128), jnp.float32),
         ],
-        name="attend",
         compiler_params=local_params(),
     )(counts, heights, text_lens, proj, totals, text, gains, text_gain, gate, w_out)
 
@@ -1586,15 +1656,24 @@
             pltpu.VMEM((items, tokens // items, 128), single),
             pltpu.VMEM((items, text_rows, 128), single),
         ],
-        name="attend_back",
         compiler_params=local_params(),
     )(counts, text_lens, grad, w_out, qkv, text_kv, tab, proj, totals, text, gains, text_gain, gate, *after)
 
 
-def norms_back_kernel(width, proj, totals, sums, scaled, grad_value, text, text_scaled, text_value, qkv_low, text_low):
+def project_back_kernel(
+    width, proj, totals, sums, scaled, grad_value, text, text_scaled, text_value, attn, weight, rows_gu,
+    parts, text_low, half, got_gu,
+    qkv_low, grad_weight, got, send, receive,
+):
     items, span = text.shape[1], grad_value.shape[-1]
     tokens = proj.shape[0]
     blocks = tokens // 128
+    core = core_bit()
+    twin, across_y = partner("core"), partner("far")
+    always = lax.axis_index("rows") >= 0
+    greet([(always, twin), (always, across_y)])
+    far = remote(rows_gu, got_gu, send.at[0], receive.at[0], across_y)
+    far.start()
     inverse = rows_to_lanes(lax.rsqrt(totals[...] / width + epsilon))
     means = rows_to_lanes(sums[...] / width)
     first = tile_lane() < 64
@@ -1622,20 +1701,67 @@
         low = jnp.concatenate([low, text_value[at]], axis=1)
         text_low[:, item] = low.reshape(text_low.shape[0], text_low.shape[2], 2 * span)
 
-
-def norms_back(proj, totals, sums, scaled, grad_value, text, text_scaled, text_value, width):
+    quarter = width // 4
+
+    @pl.loop(0, 4)
+    def _(tile):
+        left = attn[:, :, :, pl.ds(pl.multiple_of(tile * quarter, 128), quarter)].reshape(tokens, quarter)
+        out = lax.dot_general(left, qkv_low[...], TN, preferred_element_type=jnp.float32)
+        grad_weight[pl.ds(2 * tile, 2)] = out.astype(grad_weight.dtype).reshape((2,) + grad_weight.shape[1:])
+
+    swap_halves_of = remote(grad_weight.at[:, 1 - core], got, send.at[1], receive.at[1], twin)
+    swap_halves_of.start()
+    groups = parts.shape[1] // 2
+
+    @pl.loop(0, 2 * items)
+    def _(block):
+        item, pair = block // 2, lax.rem(block, 2)
+        rows = tokens // (2 * items)
+        low = qkv_low[pl.ds(pl.multiple_of(block * rows, rows), rows)]
+
+        @pl.loop(0, 4)
+        def _(tile):
+            lanes = pl.ds(pl.multiple_of(tile * quarter, 128), quarter)
+            out = lax.dot_general(low, weight[lanes], NT, preferred_element_type=jnp.float32)
+            parts[item, pl.ds(pair * groups, groups), :, lanes] = out.astype(parts.dtype).reshape(
+                groups, parts.shape[2], quarter
+            )
+
+    swap_halves_of.wait()
+    mine = grad_weight[:, pl.ds(core, 1)][:, 0].astype(jnp.float32)
+    half[...] = (mine + got[...].astype(jnp.float32)).astype(half.dtype)
+    far.wait()
+
+
+def project_back(
+    proj, totals, sums, scaled, grad_value, text, text_scaled, text_value, attn, weight, rows_gu, ident
+):
     low = jnp.bfloat16
+    items, ranks, _, width = attn.shape
+    halves = (ranks, 2, width // ranks // 2, proj.shape[1])
+    half = (ranks,) + halves[2:]
+    anywhere = pl.BlockSpec(memory_space=pl.ANY)
     return pl.pallas_call(
-        functools.partial(norms_back_kernel, width),
+        functools.partial(project_back_kernel, width),
         out_shape=[
-            jax.ShapeDtypeStruct(proj.shape, low),
+            jax.ShapeDtypeStruct(attn.shape, low),
             jax.ShapeDtypeStruct(text.shape, low),
+            jax.ShapeDtypeStruct(half, low),
+            jax.ShapeDtypeStruct(rows_gu.shape, low),
         ],
-        in_specs=[NEAR] * 8,
-        out_specs=[NEAR] * 2,
-        name="norms_back",
-        compiler_params=local_params(),
-    )(proj, totals, sums, scaled, grad_value, text, text_scaled, text_value)
+        in_specs=[NEAR] * 10 + [anywhere],
+        out_specs=[NEAR] * 3 + [anywhere],
+        scratch_shapes=[
+            pltpu.VMEM(proj.shape, low),
+            pltpu.VMEM(halves, low),
+            pltpu.VMEM(half, low),
+            pltpu.SemaphoreType.DMA((2,)),
+            pltpu.SemaphoreType.DMA((2,)),
+        ],
+        compiler_params=pltpu.CompilerParams(
+            collective_id=ident, has_side_effects=True, vmem_limit_bytes=48 << 20
+        ),
+    )(proj, totals, sums, scaled, grad_value, text, text_scaled, text_value, attn, weight, rows_gu)
 
 
 SUM_DEPTH = 16
@@ -1702,7 +1828,6 @@
         ],
         in_specs=[NEAR] * 10,
         out_specs=[NEAR] * 2,
-        name="finish",
         compiler_params=local_params(),
     )(grad, states, grad_middle, modulation, gains, vectors, gain_sums, gate_sums, text_gain, time)
 
@@ -1729,7 +1854,6 @@
         out_shape=jax.ShapeDtypeStruct((2, rows, width), dtype),
         in_specs=[near, near],
         out_specs=pl.BlockSpec((1, step, width), lambda half, at: (half, at, 0)),
-        name="join_rows",
         compiler_params=local_params(),
     )(own, other)
 
@@ -1761,7 +1885,6 @@
         out_shape=jax.ShapeDtypeStruct((ranks, 2 * rows, width), own.dtype),
         in_specs=[block, block],
         out_specs=pl.BlockSpec((1, 2 * rows, width), lambda rank: (rank, 0, 0)),
-        name="join_blocks",
         compiler_params=local_params(),
     )(own, other)
 
@@ -2243,7 +2366,6 @@
         ]
         + flow * items
         + waves * items,
-        name=f"feed_forward_{ident}",
         compiler_params=pltpu.CompilerParams(
             collective_id=ident, has_side_effects=True, vmem_limit_bytes=58 << 20
         ),
@@ -2266,11 +2388,6 @@
 
 def sum_vectors(vectors, ident):
     return take_apart(sum_rows(lay_flat(vectors), ident), vectors)
-
-
-def first_sums(vectors, qkv, text, ident):
-    total, qkv_here, text_in = first_transfers(lay_flat(vectors), qkv, text, ident)
-    return take_apart(total, vectors), qkv_here, text_in
 
 
 CORES = [(0, 1), (1, 0), (2, 3), (3, 2)]
@@ -2352,21 +2469,15 @@
     counts_here = live_rows[0]
     text_float = text_states[0].astype(single).reshape(items * text_local, text_width)
     text_inverse = norm_parts(text_float)[1]
-    (modulation, counts, text_inverse), qkv_here, text_in = first_sums(
-        [
-            dot(time_here, w_ada),
-            spread(counts_here.astype(single), ranks * items),
-            spread(text_inverse, ranks * items * text_local),
-        ],
-        w_qkv,
-        text_states[0],
-        0,
-    )
-    qkv_here = qkv_here.reshape(width, -1)
-    modulation = modulation + ada_bias
+    small = [
+        dot(time_here, w_ada),
+        spread(counts_here.astype(single), ranks * items),
+        spread(text_inverse, ranks * items * text_local),
+    ]
+    total, text_in = first_transfers(lay_flat(small), text_states[0], 0)
+    _, counts, text_inverse = take_apart(total, small)
     counts = counts.astype(jnp.int32)
     text_inverse = text_inverse.reshape(-1, 1)
-    scale_attn = modulation[:, None, 0:width]
 
     slot_in_row = jnp.arange(slots) // COLS
     live_mask = (slot_in_row[None, :] < counts_here[0][:, None]).astype(single)[..., None]
@@ -2374,9 +2485,6 @@
         return lax.dynamic_slice_in_dim(gains[index], place * span, span, 0)
 
     states = hidden_in[0].reshape(items, slots, width)
-    unit_in, inverse_in = norm_parts(states)
-    norm_in = unit_in * gains[0]
-    attn_in = gather_tokens((norm_in * (1.0 + scale_attn)).astype(narrow), 1)
     hidden = w_down.shape[0]
     gu_rows = pack_quarter(w_gu, (2 * core + far).reshape(1), 2, ranks)
 
@@ -2388,11 +2496,13 @@
     text_norm = (text_unit * gain_text).astype(narrow)
 
     text_parts = pack_blocks(dot(text_norm, w_text).astype(narrow), 2, ranks, narrow)
-    text_proj = scatter_rows(text_parts, 2, 0).reshape(ranks, items, text_local, 2 * span)
-    gu_rows, text_proj = lax.optimization_barrier((gu_rows, text_proj))
+    attn_in, qkv_here, text_proj, qkv_proj, totals, modulation = open_attention(
+        total, states, gains, ada_bias.reshape(-1, 128), text_parts, w_qkv, 1
+    )
+    text_proj = text_proj.reshape(ranks, items, text_local, 2 * span)
+    qkv_here = qkv_here.reshape(width, -1)
+    gu_rows, totals = lax.optimization_barrier((gu_rows, totals))
     gu_part = lax.all_to_all(gu_rows, "rows", 0, 0, tiled=True)
-    qkv_proj, squares = project(attn_in, qkv_here, text_proj)
-    totals = sum_rows(squares, 3)
     gains_both = jnp.concatenate([gain_here(1), gain_here(2)])[None]
     gain_t = gain_here(6)[None]
     gate_here = jnp.tanh(lax.dynamic_slice_in_dim(cross_gate, place * heads_here, heads_here, 0))
@@ -2447,29 +2557,26 @@
     )
     half_out = add_low(keep_out, swap(give_out, CORES))
     sum_down = add_low(half_down, got_down)
-    qkv_low, text_low = norms_back(
+    attn_parts, text_low, half_qkv, got_gu = project_back(
         qkv_proj,
         totals,
-        sum_rows(sums, 10, after=(sum_down, half_out)),
+        sum_rows(sums, 10, after=(sum_down, half_out, rows_gu)),
         scaled,
         grad_value,
         text_proj,
         text_scaled,
         text_value,
-        width,
-    )
-    grad_qkv = weight_grad(attn_in, qkv_low).astype(narrow)
-    give_qkv, keep_qkv = give_keep(grad_qkv.reshape(ranks, 2, -1, 3 * span), core, 1)
+        attn_in,
+        qkv_here,
+        rows_gu,
+        14,
+    )
 
     text_low = text_low.reshape(items * text_all, 2 * span)
-    half_qkv = add_low(keep_qkv, swap(give_qkv, CORES))
-    attn_parts = dot_back(qkv_low, qkv_here)
-    got_gu = swap(rows_gu, FARS)
     all_low, got_out, got_qkv, got_down = gather_rows(
         text_low,
         12,
         0,
-        after=(got_gu, attn_parts),
         swaps=((half_out, "far"), (half_qkv, "far"), (sum_down, "core")),
     )
     pair_gu = join_blocks(rows_gu, got_gu, far_bit)
@@ -2478,10 +2585,10 @@
     give_text, keep_text = give_keep(grad_text, core, 0)
     half_text = add_low(keep_text, swap(give_text, CORES))
     sum_out, sum_qkv = add_low(half_out, got_out), add_low(half_qkv, got_qkv)
-    grad_attn_in, got_text, got_out, got_gu = scatter_tokens(
+    grad_attn_in, got_text, got_out, got_gu = scatter_rows(
         attn_parts,
-        items,
         11,
+        1,
         swaps=((half_text, "far"), (sum_out, "core"), (pair_gu, "core")),
     )
     sum_qkv, grad_attn_in = lax.optimization_barrier((sum_qkv, grad_attn_in))

time: 667 us -> 634 us (0.951)
  matrix products: 24.4 us -> 13.9 us
  local copies, waits for them, and re-layouts: 81.9 us -> 71.5 us
  waiting for transfers between devices: 8.93 us -> 0.02 us
    pallas_call x3, Pallas kernels: 42.6 us -> 125 us  [the longest x1 78.7 us: open_attention(): pl.pallas_call(body, out_shape=[jax.ShapeDtypeStruct((items, ranks, rows,...]
    pallas_call x2 -> x1, Pallas kernels: 70.4 us -> 31.3 us  [gather_rows(): pl.pallas_call(functools.partial(gather_kernel, axis, swaps, len(after)),...]
    pallas_call x2 -> x1, Pallas kernels: 68.4 us -> 37.7 us  [scatter_rows(): pl.pallas_call(functools.partial(scatter_kernel, axis, swaps, len(after))...]
    ppermute x6 -> x4, waiting for transfers between devices: 8.92 us -> 0.01 us  [swap(): return lax.ppermute(array, 'items', pairs)]
    dot_general x2 -> x1, matrix products: 9.35 us -> 1.04 us  [dot_back(): return jnp.einsum('tn,kn->tk', left, weight, preferred_element_type=single)]
    pallas_call x2 -> x1, Pallas kernels: 16.8 us -> 9.14 us  [sum_rows(): pl.pallas_call(functools.partial(sum_kernel, len(after)), out_shape=jax.S...]
    unnamed x194 -> x186, local copies, waits for them, and re-layouts: 54.8 us -> 53.6 us
  transfers between devices with their start and end apart: 9 -> 7, of which waited for: 1 -> 0; matrix products, arithmetic and copies ran while one was open for 10% -> 6% of each run, Pallas kernels for 23% -> 14%
where the time goes in v7:
time: 634 us; the launch traced here: 622 us
  Pallas kernels  505 us (80%)
  local copies, waits for them, and re-layouts  71.5 us (11%)
  starting transfers between devices  15.2 us (2%)
  other arithmetic  15.1 us (2%)
  matrix products  13.9 us (2%)
    pallas_call x1, Pallas kernels, feed_forward(): pl.pallas_call(feed_forward_kernel, out_shape=[local, local, everywhere,...  209 us
    pallas_call x1, Pallas kernels, open_attention(): pl.pallas_call(body, out_shape=[jax.ShapeDtypeStruct((items, ranks, rows,...  78.7 us
    unnamed x186, local copies, waits for them, and re-layouts  53.6 us
    pallas_call x1, Pallas kernels, scatter_rows(): pl.pallas_call(functools.partial(scatter_kernel, axis, swaps, len(after))...  37.7 us
    pallas_call x1, Pallas kernels, gather_rows(): pl.pallas_call(functools.partial(gather_kernel, axis, swaps, len(after)),...  31.3 us
    pallas_call x1, Pallas kernels, attend_back(): pl.pallas_call(body, out_shape=[jax.ShapeDtypeStruct((tokens, 2 * span),...  28.8 us
    pallas_call x1, Pallas kernels, final_sums(): pl.pallas_call(functools.partial(final_kernel, ranks, groups, sums, swaps...  25.8 us
    pallas_call x1, Pallas kernels, project_back(): pl.pallas_call(functools.partial(project_back_kernel, width), out_shape=[...  24.7 us
  transfers between devices with their start and end apart: 7, of which 0 were waited for; matrix products, arithmetic and copies ran while one was open for 6% of the time, Pallas kernels for 14%

profile of v7, /device:TPU:0, one launch (start us, length us, event | category | flops | bytes accessed | tf_op | source)
XLA Modules:
  0.0 622.1 jit_solution(2206169836212579412)
XLA Ops:
  2.1 1.7 convolution_bitcast_fusion
  6.0 21.5 %shard_map.256 = (f32[104,128]{1,0:T(8,128)}, bf16[8,2,16,512]{3,2,1,0:T(8,128)(2,1)}) custom-call(f32[104,128]{1,0:T(8,128)} %pad_bitcast_fusion.own, bf16[2,16,4096]{2,1,0:T(8,128)(2,1)} %bitcast.88), custom_call_target="tpu_custom_call" | custom-call | tf_op jit(solution)/shard_map/pallas_call | solution.py:999
  29.7 2.0 convolution_convert_fusion.1.whole
  32.0 1.1 copy-done.10
  33.1 1.9 copy-done.17
  35.1 1.3 copy-done.8
  37.0 1.5 copy-done.21
  38.5 78.7 %shard_map.258 = (bf16[2,8,64,1536]{3,2,1,0:T(8,128)(2,1)}, bf16[8,192,576]{2,1,0:T(8,128)(2,1)}, f32[256,384]{1,0:T(8,128)S(1)}, f32[1024,576]{1,0:T(8,128)}, f...) custom-call(f32[104,128]{1,0:T(8,128)S(1)} %copy-done.58, f32[2,64,1536]{2,1,0:T(8,128)S(1)} %bitcast.61, ...), custom_call_target="tpu_custom_call" | custom-call | tf_op jit(solution)/shard_map/pallas_call | solution.py:1289
  117.8 4.3 all-to-all-start
  125.2 1.3 broadcast_in_dim_reshape.3.refs_8_.refs_12_
  127.3 1.7 copy-done.1
  132.7 19.0 %shard_map.260 = (bf16[1024,1536]{1,0:T(8,128)(2,1)}, bf16[1024,192]{1,0:T(8,128)(2,1)S(1)}, bf16[1024,576]{1,0:T(8,128)(2,1)S(1)}, bf16[2,128,384]{2,1,0:T(8,128)(2,1)S(1)}, f32[4,32,128]{2,1,0:T(8,128)S(1)}) custom-call(s32[16]{0:T(128)S(1)} %slice_convert_fusion.refs_0_, s32[2]{0:T(128)S(1)} %bitcast.73, s32[2]{0:T(128)S(1)} %bitcast.71, ...), custom_call_target="tpu_custom_call" | custom-call | tf_op jit(solution)/shard_map/pallas_call | solution.py:1471
  154.9 1.3 compare_convert_fusion
  156.2 1.4 broadcast_in_dim.25.live
  157.6 208.7 %shard_map.261 = (f32[2,64,1536]{2,1,0:T(8,128)}, f32[2,64,1536]{2,1,0:T(8,128)}, bf16[2,8,64,1536]{3,2,1,0:T(8,128)(2,1)}, bf16[1024,512]{1,0:T(8,128)(2,1)}, b...) custom-call(bf16[2,8,64,1536]{3,2,1,0:T(8,128)(2,1)} %bitcast.79, ...), custom_call_target="tpu_custom_call" | custom-call | tf_op jit(solution)/shard_map/pallas_call | solution.py:2334
  366.3 1.4 collective-permute-start
  367.7 4.4 all-to-all-start.1
  372.1 2.9 convolution_convert_fusion.2
  377.6 1.3 copy-done.31
  383.4 28.8 %shard_map.262 = (f32[1024,384]{1,0:T(8,128)S(1)}, bf16[1024,192]{1,0:T(8,128)(2,1)S(1)}, f32[256,192]{1,0:T(8,128)S(1)}, bf16[256,192]{1,0:T(8,128)(2,1)S(1)}, ...) custom-call(s32[16]{0:T(128)S(1)} %copy-done.72, s32[2]{0:T(128)S(1)} %bitcast.72, ...), custom_call_target="tpu_custom_call" | custom-call | tf_op jit(solution)/shard_map/pallas_call | solution.py:1637
  412.2 1.1 copy-done.24
  417.3 1.7 fusion.2.rest_1_.rest_0_
  419.0 2.2 add_convert_fusion.2.rest_0_.rest_2_.own
  421.2 9.1 %shard_map.263.sums = f32[24,128]{1,0:T(8,128)} custom-call(f32[24,128]{1,0:T(8,128)} %copy-done.63, bf16[256,1536]{1,0:T(8,128)(2,1)} %add_convert_fusion.2.rest_0_.rest_2_.own, bf16[96,1536]{1,0:T(8,128)(2,1)} %fusion.2.rest_1_.rest_0_, bf16[8,48,1024]{2,1,0:T(8,128)(2,1)} %all-to-all-done.1.rest_2_.rows_gu.one), custom_call_target="tpu_custom_call" | custom-call | tf_op jit(solution)/shard_map/pallas_call | solution.py:858
  430.4 1.4 copy-done.25
  435.4 24.7 %shard_map.264 = (bf16[2,8,64,1536]{3,2,1,0:T(8,128)(2,1)}, bf16[8,2,16,384]{3,2,1,0:T(8,128)(2,1)S(1)}, bf16[8,96,576]{2,1,0:T(8,128)(2,1)S(1)}, bf16[8,48,1024]{2,1,0:T(8,128)(2,1)S(1)}) custom-call(f32[1024,576]{1,0:T(8,128)} %get-tuple-element.60.refs_3_.refs_7_.proj, f32[24,128]{1,0:T(8,128)S(1)} %get-tuple-element.62.refs_4_.refs_8_.totals, ...), custom_call_target="tpu_custom_call" | custom-call | tf_op jit(solution)/shard_map/pallas_call | solution.py:1744
  462.7 31.3 %shard_map.265 = (bf16[8,256,384]{2,1,0:T(8,128)(2,1)}, bf16[96,1536]{1,0:T(8,128)(2,1)}, bf16[8,96,576]{2,1,0:T(8,128)(2,1)}, bf16[256,1536]{1,0:T(8,128)(2,1)}) custom-call(bf16[256,384]{1,0:T(8,128)(2,1)} %bitcast.66, bf16[96,1536]{1,0:T(8,128)(2,1)} %fusion.2.rest_1_.rest_0_, bf16[8,96,576]{2,1,0:T(8,128)(2,1)} %copy-done.14, ...), custom_call_target="tpu_custom_call" | custom-call | tf_op jit(solution)/shard_map/pallas_call | solution.py:645
  494.0 1.4 copy-done.27
  498.7 3.8 shard_map.267.rest_2_.own
  502.5 1.2 add_convert_fusion.1
  504.6 1.8 copy-done.16
  506.5 37.7 %shard_map.268 = (f32[2,64,1536]{2,1,0:T(8,128)S(1)}, bf16[256,3072]{1,0:T(8,128)(2,1)S(1)}, bf16[96,1536]{1,0:T(8,128)(2,1)S(1)}, bf16[8,96,1024]{2,1,0:T(8,128)(2,1)S(1)}) custom-call(bf16[2,8,64,1536]{3,2,1,0:T(8,128)(2,1)S(1)} %copy-done.16, bf16[256,3072]{1,0:T(8,128)(2,1)S(1)} %fusion.rest_0_, bf16[96,1536]{1,0:T(8,128)(2,1)S(1)} %add_convert_fusion.3.rest_1_.own, ...), custom_call_target="tpu_custom_call" | custom-call | tf_op jit(solution)/shard_map/pallas_call | solution.py:815
  544.1 1.1 copy-done.22
  545.3 1.1 copy-done.28
  548.1 5.0 all-to-all-start.2
  555.3 2.1 shard_map.275
  559.2 1.5 shard_map.269
  560.7 1.7 add_convert_fusion.rest_0_.own
  562.5 25.8 %shard_map.272 = (f32[8,72,128]{2,1,0:T(8,128)}, bf16[256,3072]{1,0:T(8,128)(2,1)}) custom-call(f32[8,30,128]{2,1,0:T(8,128)} %copy-done.54, bf16[256,3072]{1,0:T(8,128)(2,1)} %add_convert_fusion.rest_0_.own), custom_call_target="tpu_custom_call" | custom-call | tf_op jit(solution)/shard_map/pallas_call | solution.py:932
  588.3 1.6 slice.44
  595.5 1.7 reshape.192
  597.2 1.4 copy-done.3
  598.6 1.4 copy-done.23
  600.0 3.1 shard_map.274
  603.2 3.0 shard_map.273
  606.2 1.6 reduce_sum.39
  611.8 5.2 fusion.11
  617.0 3.8 shard_map.270
  (226 shorter events, 55.2 us)
Async XLA Ops:
  0.6 29.0 %copy-start = (bf16[512,3072]{1,0:T(8,128)(2,1)S(1)}, bf16[512,3072]{1,0:T(8,128)(2,1)}, u32[]{:S(2)}) copy-start(bf16[512,3072]{1,0:T(8,128)(2,1)} %param.26) | copy-start | bytes 9437188
  0.7 4.6 copy-start.90
  28.3 3.3 copy-start.88
  33.1 1.9 copy-start.17
  35.0 1.4 copy-start.8
  35.0 1.9 copy-start.11
  35.0 1.9 copy-start.38
  35.0 1.9 copy-start.58
  35.0 1.9 copy-start.60
  35.1 82.0 %copy-start.18 = (bf16[8,48,1024]{2,1,0:T(8,128)(2,1)}, bf16[8,48,1024]{2,1,0:T(8,128)(2,1)S(1)}, u32[]{:S(2)}) copy-start(bf16[8,48,1024]{2,1,0:T(8,128)(2,1)S(1)} %shard_map.259) | copy-start | bytes 2359300
  37.0 1.5 copy-start.21
  117.8 38.4 %all-to-all-start = ((bf16[8,48,1024]{2,1,0:T(8,128)(2,1)}), bf16[8,48,1024]{2,1,0:T(8,128)(2,1)}, u32[]{:S(2)}, u32[]{:S(2)}) async-start(bf16[8,48,1024]{2,1,0:T(8,128)(2,1)} %copy-done.18), calls=%async_computation | async-start | bytes 1572864 | tf_op jit(solution)/shard_map/all_to_all | solution.py:2505
  127.3 24.5 %copy-start.71 = (s32[16]{0:T(128)}, s32[16]{0:T(128)S(1)}, u32[]{:S(2)}) copy-start(s32[16]{0:T(128)S(1)} %slice_convert_fusion.refs_0_) | copy-start | bytes 196
  127.3 1.7 copy-start.1
  366.3 52.7 %collective-permute-start = (bf16[256,1536]{1,0:T(8,128)(2,1)}, bf16[256,1536]{1,0:T(8,128)(2,1)}, u32[]{:S(2)}, u32[]{:S(2)}) collective-permute-start(bf16[256,1536]{1,0:T(8,128)(2,1)} %get-tuple-element.74), channel_id=1, source_target_pairs={{0,16},{8,24},{16,0},{24,8},{1,17},{9,25},{17,1},{25,9},{2,18},{10... | collective-permute-start | bytes 2359304 | tf_op jit(solution)/shard_map/ppermute | solution.py:2398
  367.7 53.5 %all-to-all-start.1 = ((bf16[8,48,1024]{2,1,0:T(8,128)(2,1)}), bf16[8,48,1024]{2,1,0:T(8,128)(2,1)}, u32[]{:S(2)}, u32[]{:S(2)}) async-start(bf16[8,48,1024]{2,1,0:T(8,128)(2,1)} %get-tuple-element.75), calls=%async_computation.1 | async-start | bytes 1572864 | tf_op jit(solution)/shard_map/all_to_all | solution.py:2536
  376.6 40.7 %collective-permute-start.1 = (bf16[96,1536]{1,0:T(8,128)(2,1)}, bf16[96,1536]{1,0:T(8,128)(2,1)}, u32[]{:S(2)}, u32[]{:S(2)}) collective-permute-start(bf16[96,1536]{1,0:T(8,128)(2,1)} %dynamic-slice_bitcast_fusion.1.refs_13_), channel_id=1, source_target_pairs={{0,8},{8,0},{16,24},{24,16},{1,9},{9,1},{17,25},{25,17},{2,10},{10... | collective-permute-start | bytes 884744 | tf_op jit(solution)/shard_map/ppermute | solution.py:2398
  383.4 33.9 %copy-start.78 = (bf16[192,1536]{1,0:T(8,128)(2,1)S(1)}, bf16[192,1536]{1,0:T(8,128)(2,1)}, u32[]{:S(2)}) copy-start(bf16[192,1536]{1,0:T(8,128)(2,1)} %copy-done.77) | copy-start | bytes 1769476
  383.4 35.6 %copy-start.84 = (bf16[256,1536]{1,0:T(8,128)(2,1)S(1)}, bf16[256,1536]{1,0:T(8,128)(2,1)}, u32[]{:S(2)}) copy-start(bf16[256,1536]{1,0:T(8,128)(2,1)} %get-tuple-element.74) | copy-start | bytes 2359300
  430.4 1.4 copy-start.25
  494.0 1.8 copy-start.89
  494.0 1.4 copy-start.27
  497.6 4.8 copy-start.15
  497.6 4.8 copy-start.81
  497.7 6.3 %collective-permute-start.2 = (bf16[256,3072]{1,0:T(8,128)(2,1)S(1)}, bf16[256,3072]{1,0:T(8,128)(2,1)S(1)}, u32[]{:S(2)}, u32[]{:S(2)}) collective-permute-start(bf16[256,3072]{1,0:T(8,128)(2,1)S(1)} %dynamic-slice_bitcast_fusion), channel_id=1, source_target_pairs={{0,8},{8,0},{16,24},{24,16},{1,9},{9,1},{17,25},{25,17},{2,10},{10... | collective-permute-start | bytes 4718600 | tf_op jit(solution)/shard_map/ppermute | solution.py:2398
  502.4 2.2 copy-start.2
  502.5 1.5 copy-start.85
  504.0 2.5 copy-start.16
  504.6 39.5 %copy-start.4 = (bf16[256,3072]{1,0:T(8,128)(2,1)}, bf16[256,3072]{1,0:T(8,128)(2,1)S(1)}, u32[]{:S(2)}) copy-start(bf16[256,3072]{1,0:T(8,128)(2,1)S(1)} %fusion.rest_0_) | copy-start | bytes 4718596
  548.1 45.8 %all-to-all-start.2 = ((bf16[8,96,576]{2,1,0:T(8,128)(2,1)}), bf16[8,96,576]{2,1,0:T(8,128)(2,1)}, u32[]{:S(2)}, u32[]{:S(2)}) async-start(bf16[8,96,576]{2,1,0:T(8,128)(2,1)} %add_convert_fusion.1), calls=%async_computation.2 | async-start | bytes 1966080 | tf_op jit(solution)/shard_map/all_to_all | solution.py:2595
  555.3 2.1 copy-start.13
  555.3 2.3 copy-start.80
  557.6 1.6 copy-start.35
  557.6 1.6 copy-start.39
  557.6 1.6 copy-start.48
  557.6 1.6 copy-start.55
  557.6 1.6 copy-start.62
  557.6 1.6 copy-start.68
  557.7 1.6 copy-start.74
  557.7 3.1 copy-start.29
  558.7 2.0 copy-start.5
  560.7 1.7 copy-start.54
  593.8 23.2 %collective-permute-start.3 = (bf16[8,96,576]{2,1,0:T(8,128)(2,1)}, bf16[8,96,576]{2,1,0:T(8,128)(2,1)}, u32[]{:S(2)}, u32[]{:S(2)}) collective-permute-start(bf16[8,96,576]{2,1,0:T(8,128)(2,1)} %all-to-all-done.2.own), channel_id=1, source_target_pairs={{0,8},{8,0},{16,24},{24,16},{1,9},{9,1},{17,25},{25,17},{2,10},{10... | collective-permute-start | bytes 2654216 | tf_op jit(solution)/shard_map/ppermute | solution.py:2398
  597.2 1.4 copy-start.3
  600.0 3.1 copy-start.6
  600.0 3.2 copy-start.26
  606.2 5.1 copy-start.91
  617.0 3.8 copy-start.83
  (51 other events, 45.1 us)
